TPU v7x, 32 devices: a whole 2x2x4 slice. The times are simulated.
32 devices in a mesh: grp: 2 (over x), row: 16 (over z, y, core).
Axes of the slice: x: 2, y: 2, z: 4, core: 2. Of those that a mesh axis runs over, the one named last changes fastest.
Arguments:
- cell_coeffs: float32 [6, 32, 384], P(None, 'row'), may hold values from 0.5 to 2
- z_factor: float32 [4, 64, 384, 128], P(None, ('grp', 'row')), parts along dimension 1, may hold values from -0.022552745 to 0.022552745
- noise_cols: float32 [4, 64, 384, 128], P(None, ('grp', 'row')), parts along dimension 1, may hold values from -0.022552745 to 0.022552745
- q_bar: float32 [4, 64, 384, 256], P(None, ('grp', 'row')), parts along dimension 1, may hold values from -10 to 10
- r_bar: float32 [512, 256], P('grp'), parts along dimension 0, may hold values from -11.085125 to 11.085125
Outputs:
- z_grad: float32 [4, 64, 384, 128], P(None, ('grp', 'row')), parts along dimension 1
- noise_grad: float32 [4, 64, 384, 128], P(None, ('grp', 'row')), parts along dimension 1
There are 2 independent parts, one for each index of `grp`. A program takes and returns all parts, laid end to end along the dimension named above; an argument that names none is the same for every part. Nothing has to cross between parts.
All inputs are finite; a program needn't handle non-finite values.
Results may differ from a plain program's by a relative error of at most 0.000061.
Values sent between devices are 32-bit elements; how exact they have to be, the bound alone decides.
No kernel may reach another device: no remote copies, remote signals or barrier semaphores. Data moves between devices by JAX's collectives and lax.ppermute only.
A program may use at most 64 MiB of HBM per device.

v0:
```python
import jax
import jax.numpy as jnp
from jax import lax
from jax.sharding import PartitionSpec as P

rate_scales = (0.4, 0.4, 0.1, 0.2, 0.1, 0.1)
exact = lax.Precision.HIGHEST


def padded(block, sides, width):
    for axis, dim in sides:
        count = lax.axis_size(axis)
        forward = [(i, i + 1) for i in range(count - 1)]
        backward = [(target, source) for source, target in forward]
        low = lax.ppermute(
            lax.slice_in_dim(block, block.shape[dim] - width, None, axis=dim), axis, forward
        )
        high = lax.ppermute(lax.slice_in_dim(block, 0, width, axis=dim), axis, backward)
        block = jnp.concatenate([low, block, high], axis=dim)
    return block


def local_part(values, scaled, transposed):
    detuning = scaled[0][..., None]
    mech_freq = scaled[1][..., None]
    coupling = scaled[2][..., None]
    cavity_loss = scaled[3][..., None]
    phonon_loss = scaled[4][..., None]
    light_x, light_p, motion_x, motion_p = (values[0], values[1], values[2], values[3])
    if transposed:
        return jnp.stack(
            [
                -0.5 * cavity_loss * light_x + detuning * light_p - 2.0 * coupling * motion_p,
                -detuning * light_x - 0.5 * cavity_loss * light_p,
                -2.0 * coupling * light_p - mech_freq * motion_p,
                mech_freq * motion_x - 0.5 * phonon_loss * motion_p,
            ]
        )
    return jnp.stack(
        [
            -0.5 * cavity_loss * light_x - detuning * light_p,
            detuning * light_x - 0.5 * cavity_loss * light_p - 2.0 * coupling * motion_x,
            mech_freq * motion_p,
            -mech_freq * motion_x - 0.5 * phonon_loss * motion_p - 2.0 * coupling * light_x,
        ]
    )


def hop_sources(values, scaled, transposed):
    hopping = scaled[5][..., None]
    if transposed:
        return jnp.stack([hopping * values[0], hopping * values[1]])
    return jnp.stack([values[1], values[0]])


def neighbours(source):
    middle = source[:, 1:-1]
    sideways = jnp.pad(middle, ((0, 0), (0, 0), (1, 1), (0, 0)))
    return source[:, :-2] + source[:, 2:] + sideways[:, :, :-2] + sideways[:, :, 2:]


def hop_add(local_term, hop_sums, scaled, transposed):
    hopping = scaled[5][..., None]
    if transposed:
        return jnp.stack(
            [local_term[0] + hop_sums[1], local_term[1] - hop_sums[0], local_term[2], local_term[3]]
        )
    return jnp.stack(
        [
            local_term[0] - hopping * hop_sums[0],
            local_term[1] + hopping * hop_sums[1],
            local_term[2],
            local_term[3],
        ]
    )


def rim_apply(values, scaled, transposed):
    source = hop_sources(values, scaled, transposed)
    extended = padded(source, (("row", 1),), 1)
    return hop_add(local_part(values, scaled, transposed), neighbours(extended), scaled, transposed)


def shallow_expand(values, scaled, transposed):
    first_term = rim_apply(values, scaled, transposed)
    second = rim_apply(first_term, scaled, transposed)
    return values + first_term + 0.5 * second


def on_device(cell_coeffs, z_factor, noise_cols, q_bar, r_bar):
    scaled = cell_coeffs * jnp.array(rate_scales, jnp.float32)[:, None, None]
    rank_cols = z_factor.shape[3]

    def expand(values, transposed):
        return shallow_expand(values, scaled, transposed)

    stacked = jnp.concatenate([expand(z_factor, False), noise_cols], axis=3)
    flat_rows = stacked.reshape(-1, stacked.shape[3])
    bar_rows = q_bar.reshape(-1, q_bar.shape[3])
    gram_matrix = lax.psum(jnp.einsum("ik,il->kl", flat_rows, flat_rows, precision=exact), "row")
    lower_factor = jnp.linalg.cholesky(gram_matrix)
    identity = jnp.eye(gram_matrix.shape[0], dtype=jnp.float32)
    r_inv = lax.linalg.triangular_solve(lower_factor, identity, left_side=True, lower=True).T
    upper_factor = lower_factor.T
    target = jnp.dot(upper_factor, jnp.triu(r_bar).T, precision=exact)
    q_fact = jnp.dot(flat_rows, r_inv, precision=exact)
    cross = lax.psum(jnp.einsum("ik,il->kl", bar_rows, q_fact, precision=exact), "row")
    middle = target - cross
    symmetric = jnp.tril(middle) + jnp.tril(middle, -1).T
    grad_rows = jnp.dot(
        bar_rows + jnp.dot(q_fact, symmetric, precision=exact), r_inv.T, precision=exact
    )
    grad_x = grad_rows.reshape(q_bar.shape)
    z_grad = expand(grad_x[..., :rank_cols], True)
    return (z_grad, grad_x[..., rank_cols:])


def solution(mesh):
    return jax.shard_map(
        on_device,
        mesh=mesh,
        in_specs=(
            P(None, "row", None),
            P(None, ("grp", "row"), None, None),
            P(None, ("grp", "row"), None, None),
            P(None, ("grp", "row"), None, None),
            P("grp", None),
        ),
        out_specs=(P(None, ("grp", "row"), None, None), P(None, ("grp", "row"), None, None)),
        check_vma=False,
    )
```

profile of v0, /device:TPU:9, one launch (start us, length us, event | category | flops | bytes accessed | tf_op | source)
XLA Modules:
  0.0 350.2 jit_solution(17974185893808140031)
XLA Ops:
  8.5 3.7 %collective-permute-start = (f32[2,1,384,128]{3,2,1,0:T(8,128)S(1)}, f32[2,1,384,128]{3,2,1,0:T(8,128)S(1)}, u32[]{:S(2)}, u32[]{:S(2)}) collective-permute-start(f32[2,1,384,128]{3,2,1,0:T(8,128)S(1)} %get-tuple-element.52), channel_id=1, source_target_pairs={{0,1},{1,2},{2,3},{3,4},{4,5},{5,6},{6,7},{7,8},{8,9},{9,10},{10,1... | collective-permute-start | bytes 1179656 | tf_op jit(solution)/shard_map/ppermute | solution.py:15
  12.2 1.9 collective-permute-start.1
  15.0 1.9 collective-permute-done
  16.9 5.8 %collective-permute-done.1 = f32[2,1,384,128]{3,2,1,0:T(8,128)S(1)} collective-permute-done((f32[2,1,384,128]{3,2,1,0:T(8,128)S(1)}, f32[2,1,384,128]{3,2,1,0:T(8,128)S(1)}, u32[]{:S(2)}, u32[]{:S(2)}) %collective-permute-start.1) | collective-permute-done | bytes 393248 | tf_op jit(solution)/shard_map/ppermute | solution.py:18
  24.4 1.9 collective-permute-start.2
  26.3 2.4 collective-permute-start.3
  29.5 1.8 collective-permute-done.2
  31.3 5.2 %collective-permute-done.3 = f32[2,1,384,128]{3,2,1,0:T(8,128)S(1)} collective-permute-done((f32[2,1,384,128]{3,2,1,0:T(8,128)}, f32[2,1,384,128]{3,2,1,0:T(8,128)S(1)}, u32[]{:S(2)}, u32[]{:S(2)}) %collective-permute-start.3) | collective-permute-done | bytes 393248 | tf_op jit(solution)/shard_map/ppermute | solution.py:18
  39.8 6.0 %convolution_bitcast_fusion.1 = f32[256,256]{0,1:T(8,128)} fusion(f32[4,2,384,128]{3,2,1,0:T(8,128)S(1)} %copy-done.4, f32[4,2,384,128]{3,2,1,0:T(8,128)S(1)} %fusion.1), kind=kOutput, calls=%fused_computation.12 | convolution fusion | flops 2416705536 | bytes 3407872 | tf_op jit(solution)/shard_map/ik,il->kl/dot_general | solution.py:100
  46.1 3.2 pad_maximum_fusion
  49.3 84.6 %all-reduce.8.cloned.1.call-done = f32[256,256]{0,1:T(8,128)} async-done(((f32[256,256]{0,1:T(8,128)}), f32[256,256]{0,1:T(8,128)}) %all-reduce.8.cloned.1.call-update) | async-done | bytes 262160 | tf_op jit(solution)/shard_map/psum | solution.py:100
  136.0 11.7 %cholesky.50 = f32[128,128]{1,0:T(8,128)S(1)} custom-call(f32[128,128]{1,0:T(8,128)S(1)} %cholesky.118), custom_call_target="Cholesky" | custom-call | tf_op jit(solution)/shard_map/jit(cholesky)/cholesky | solution.py:101
  147.7 9.8 %custom-call.14 = f32[1,128,128]{1,2,0:T(8,128)S(1)} custom-call(f32[1,128,128]{2,1,0:T(8,128)S(1)} %get-tuple-element.58), custom_call_target="InvertDiagBlocksLowerTriangular" | custom-call | tf_op jit(solution)/shard_map/jit(cholesky)/cholesky | solution.py:101
  158.1 11.7 %cholesky.105 = f32[128,128]{1,0:T(8,128)S(1)} custom-call(f32[128,128]{1,0:T(8,128)S(1)} %convolution_subtract_fusion.2), custom_call_target="Cholesky" | custom-call | tf_op jit(solution)/shard_map/jit(cholesky)/cholesky | solution.py:101
  172.0 5.3 %while.1 = (s32[]{:T(128)}, f32[256,256]{1,0:T(8,128)S(1)}, s32[2,2]{1,0:T(2,128)S(1)}, f32[2,128,128]{2,1,0:T(8,128)}, s32[]{:T(128)}) while((s32[]{:T(128)}, f32[256,256]{1,0:T(8,128)S(1)}, s32[2,2]{1,0:T(2,128)S(1)}, f32[2,128,128]{2,1,0:T(8,128)}, s32[]{:T(128)}) %tuple.56), condition=%wide.while_cond, body=%wide.while_body.sunk | while | flops 2 | bytes 132205 | solution.py:103
  172.6 2.0 bitcast_dynamic-update-slice_fusion.2
  175.3 2.1 bitcast_dynamic-update-slice_fusion.2
  177.3 20.7 %custom-call.15 = f32[2,128,128]{1,2,0:T(8,128)S(1)} custom-call(f32[2,128,128]{2,1,0:T(8,128)} %get-tuple-element.9), custom_call_target="InvertDiagBlocksLowerTriangular" | custom-call | tf_op jit(solution)/shard_map/triangular_solve | solution.py:103
  199.7 4.7 %fusion.33 = f32[3072,256]{1,0:T(8,128)S(1)} fusion(f32[3072,256]{1,0:T(8,128)} %bitcast.73, f32[128,256]{1,0:T(8,128)S(1)} %fusion.44, f32[128,256]{1,0:T(8,128)S(1)} %fusion.40), kind=kOutput, calls=%fused_computation.106 | convolution fusion | flops 2415984640 | bytes 6553600 | tf_op jit(solution)/shard_map/dot_general | solution.py:106
  204.4 5.9 %convolution_bitcast_fusion = f32[256,256]{0,1:T(8,128)} fusion(f32[3072,256]{1,0:T(8,128)S(1)} %fusion.33, f32[3072,256]{1,0:T(8,128)S(1)} %bitcast.72), kind=kOutput, calls=%fused_computation.11 | convolution fusion | flops 2415919104 | bytes 6553600 | tf_op jit(solution)/shard_map/ik,il->kl/dot_general | solution.py:107
  210.8 88.9 %all-reduce.10.cloned.1.call-done = f32[256,256]{0,1:T(8,128)} async-done(((f32[256,256]{0,1:T(8,128)}), f32[256,256]{0,1:T(8,128)}) %all-reduce.10.cloned.1.call-update) | async-done | bytes 262160 | tf_op jit(solution)/shard_map/psum | solution.py:107
  299.7 1.6 convolution_subtract_fusion
  302.1 4.9 %convolution_add_fusion = f32[3072,256]{1,0:T(8,128)S(1)} fusion(f32[3072,256]{1,0:T(8,128)} %bitcast.71, f32[3072,256]{1,0:T(8,128)S(1)} %fusion.33, f32[256,256]{1,0:T(8,128)} %copy.15, f32[256,256]{0,1:T(8,128)S(1)} %convolution_subtract_fusion, s32[256]{0:T(256)} %iota_add_fusion), kind=kOutput, calls=%fused_computation.2 | convolution fusion | flops 2417033216 | bytes 9962496 | tf_op jit(solution)/shard_map/dot_general | solution.py:111
  307.0 2.9 fusion.32
  310.2 4.7 %collective-permute-start.4 = (f32[2,1,384,128]{3,2,1,0:T(8,128)S(1)}, f32[2,1,384,128]{3,2,1,0:T(8,128)S(1)}, u32[]{:S(2)}, u32[]{:S(2)}) collective-permute-start(f32[2,1,384,128]{3,2,1,0:T(8,128)S(1)} %get-tuple-element.48), channel_id=1, source_target_pairs={{0,1},{1,2},{2,3},{3,4},{4,5},{5,6},{6,7},{7,8},{8,9},{9,10},{10,1... | collective-permute-start | bytes 1179656 | tf_op jit(solution)/shard_map/ppermute | solution.py:15
  314.9 1.9 collective-permute-start.5
  316.9 2.7 collective-permute-done.4
  319.6 6.7 %collective-permute-done.5 = f32[2,1,384,128]{3,2,1,0:T(8,128)S(1)} collective-permute-done((f32[2,1,384,128]{3,2,1,0:T(8,128)S(1)}, f32[2,1,384,128]{3,2,1,0:T(8,128)S(1)}, u32[]{:S(2)}, u32[]{:S(2)}) %collective-permute-start.5) | collective-permute-done | bytes 393248 | tf_op jit(solution)/shard_map/ppermute | solution.py:18
  327.4 1.9 collective-permute-start.6
  329.3 2.4 collective-permute-start.7
  331.8 6.4 %collective-permute-done.6 = f32[2,1,384,128]{3,2,1,0:T(8,128)S(1)} collective-permute-done((f32[2,1,384,128]{3,2,1,0:T(8,128)S(1)}, f32[2,1,384,128]{3,2,1,0:T(8,128)S(1)}, u32[]{:S(2)}, u32[]{:S(2)}) %collective-permute-start.6) | collective-permute-done | bytes 393248 | tf_op jit(solution)/shard_map/ppermute | solution.py:15
  340.9 2.1 fusion.58
  (94 shorter events, 19.6 us)
Async XLA Ops:
  7.2 7.0 %copy-start.19 = (f32[6]{0:T(128)S(1)}, f32[6]{0:T(128)}, u32[]{:S(2)}) copy-start(f32[6]{0:T(128)} %constant.100.clone) | copy-start | bytes 76
  7.2 7.0 %copy-start.17 = (f32[6,2,384]{2,1,0:T(2,128)S(1)}, f32[6,2,384]{2,1,0:T(2,128)}, u32[]{:S(2)}) copy-start(f32[6,2,384]{2,1,0:T(2,128)} %param.6) | copy-start | bytes 55300
  7.2 126.7 %all-reduce.8.cloned.1.call-start = ((), (), s32[]{:S(2)}) async-start(), calls=%async_computation | async-start | bytes 524288 | tf_op jit(solution)/shard_map/psum | solution.py:100
  8.5 8.4 %collective-permute-start = (f32[2,1,384,128]{3,2,1,0:T(8,128)S(1)}, f32[2,1,384,128]{3,2,1,0:T(8,128)S(1)}, u32[]{:S(2)}, u32[]{:S(2)}) collective-permute-start(f32[2,1,384,128]{3,2,1,0:T(8,128)S(1)} %get-tuple-element.52), channel_id=1, source_target_pairs={{0,1},{1,2},{2,3},{3,4},{4,5},{5,6},{6,7},{7,8},{8,9},{9,10},{10,1... | collective-permute-start | bytes 1179656 | tf_op jit(solution)/shard_map/ppermute | solution.py:15
  12.2 10.5 %collective-permute-start.1 = (f32[2,1,384,128]{3,2,1,0:T(8,128)S(1)}, f32[2,1,384,128]{3,2,1,0:T(8,128)S(1)}, u32[]{:S(2)}, u32[]{:S(2)}) collective-permute-start(f32[2,1,384,128]{3,2,1,0:T(8,128)S(1)} %get-tuple-element.53), channel_id=1, source_target_pairs={{1,0},{2,1},{3,2},{4,3},{5,4},{6,5},{7,6},{8,7},{9,8},{10,9},{11,1... | collective-permute-start | bytes 1179656 | tf_op jit(solution)/shard_map/ppermute | solution.py:18
  14.2 183.9 %copy-start.9 = (pred[256,256]{1,0:T(32,128)(4,1)}, pred[256,256]{1,0:T(32,128)(4,1)S(1)}, u32[]{:S(2)}) copy-start(pred[256,256]{1,0:T(32,128)(4,1)S(1)} %iota_compare_fusion.3) | copy-start | bytes 196612
  14.9 21.8 %copy-start.12 = (f32[2,384]{1,0:T(2,128)}, f32[2,384]{1,0:T(2,128)S(1)}, u32[]{:S(2)}) copy-start(f32[2,384]{1,0:T(2,128)S(1)} %get-tuple-element.64) | copy-start | bytes 9220
  14.9 21.8 %copy-start.14 = (f32[2,384]{1,0:T(2,128)}, f32[2,384]{1,0:T(2,128)S(1)}, u32[]{:S(2)}) copy-start(f32[2,384]{1,0:T(2,128)S(1)} %get-tuple-element.62) | copy-start | bytes 9220
  14.9 22.9 %copy-start.10 = (f32[2,384]{1,0:T(2,128)}, f32[2,384]{1,0:T(2,128)S(1)}, u32[]{:S(2)}) copy-start(f32[2,384]{1,0:T(2,128)S(1)} %get-tuple-element.61) | copy-start | bytes 9220
  15.0 7.9 %copy-start = (f32[4,2,384,128]{3,2,1,0:T(8,128)S(1)}, f32[4,2,384,128]{3,2,1,0:T(8,128)}, u32[]{:S(2)}) copy-start(f32[4,2,384,128]{3,2,1,0:T(8,128)} %param.7) | copy-start | bytes 4718596
  24.4 6.9 %collective-permute-start.2 = (f32[2,1,384,128]{3,2,1,0:T(8,128)}, f32[2,1,384,128]{3,2,1,0:T(8,128)S(1)}, u32[]{:S(2)}, u32[]{:S(2)}) collective-permute-start(f32[2,1,384,128]{3,2,1,0:T(8,128)} %get-tuple-element.50), channel_id=1, source_target_pairs={{0,1},{1,2},{2,3},{3,4},{4,5},{5,6},{6,7},{7,8},{8,9},{9,10},{10,1... | collective-permute-start | bytes 1179656 | tf_op jit(solution)/shard_map/ppermute | solution.py:15
  26.3 10.2 %collective-permute-start.3 = (f32[2,1,384,128]{3,2,1,0:T(8,128)}, f32[2,1,384,128]{3,2,1,0:T(8,128)S(1)}, u32[]{:S(2)}, u32[]{:S(2)}) collective-permute-start(f32[2,1,384,128]{3,2,1,0:T(8,128)} %get-tuple-element.51), channel_id=1, source_target_pairs={{1,0},{2,1},{3,2},{4,3},{5,4},{6,5},{7,6},{8,7},{9,8},{10,9},{11,1... | collective-permute-start | bytes 1179656 | tf_op jit(solution)/shard_map/ppermute | solution.py:18
  28.9 143.0 %copy-start.8 = (pred[256,256]{1,0:T(32,128)(4,1)}, pred[256,256]{1,0:T(32,128)(4,1)S(1)}, u32[]{:S(2)}) copy-start(pred[256,256]{1,0:T(32,128)(4,1)S(1)} %copy.12) | copy-start | bytes 196612
  38.3 1.6 copy-start.4
  38.7 1.1 copy-start.2
  39.8 6.2 %copy-start.5 = (f32[4,2,384,128]{3,2,1,0:T(8,128)S(1)}, f32[4,2,384,128]{3,2,1,0:T(8,128)}, u32[]{:S(2)}) copy-start(f32[4,2,384,128]{3,2,1,0:T(8,128)} %param.8) | copy-start | bytes 4718596
  45.8 253.9 %all-reduce.10.cloned.1.call-start = ((), (), s32[]{:S(2)}) async-start(), calls=%async_computation.1 | async-start | bytes 524288 | tf_op jit(solution)/shard_map/psum | solution.py:107
  169.8 29.8 %copy-start.3 = (f32[256,256]{1,0:T(8,128)}, f32[256,256]{1,0:T(8,128)S(1)}, u32[]{:S(2)}) copy-start(f32[256,256]{1,0:T(8,128)S(1)} %get-tuple-element.56) | copy-start | bytes 786436
  199.7 4.7 %copy-start.6 = (f32[128,256]{1,0:T(8,128)}, f32[128,256]{1,0:T(8,128)S(1)}, u32[]{:S(2)}) copy-start(f32[128,256]{1,0:T(8,128)S(1)} %fusion.44) | copy-start | bytes 393220
  199.7 4.7 %copy-start.1 = (f32[4,2,384,256]{3,2,1,0:T(8,128)S(1)}, f32[4,2,384,256]{3,2,1,0:T(8,128)}, u32[]{:S(2)}) copy-start(f32[4,2,384,256]{3,2,1,0:T(8,128)} %param.9) | copy-start | bytes 9437188
  302.1 4.9 %copy-start.7 = (f32[128,256]{1,0:T(8,128)S(1)}, f32[128,256]{1,0:T(8,128)}, u32[]{:S(2)}) copy-start(f32[128,256]{1,0:T(8,128)} %copy-done.6) | copy-start | bytes 393220
  307.0 2.9 copy-start.13
  310.2 9.4 %collective-permute-start.4 = (f32[2,1,384,128]{3,2,1,0:T(8,128)S(1)}, f32[2,1,384,128]{3,2,1,0:T(8,128)S(1)}, u32[]{:S(2)}, u32[]{:S(2)}) collective-permute-start(f32[2,1,384,128]{3,2,1,0:T(8,128)S(1)} %get-tuple-element.48), channel_id=1, source_target_pairs={{0,1},{1,2},{2,3},{3,4},{4,5},{5,6},{6,7},{7,8},{8,9},{9,10},{10,1... | collective-permute-start | bytes 1179656 | tf_op jit(solution)/shard_map/ppermute | solution.py:15
  314.9 11.4 %collective-permute-start.5 = (f32[2,1,384,128]{3,2,1,0:T(8,128)S(1)}, f32[2,1,384,128]{3,2,1,0:T(8,128)S(1)}, u32[]{:S(2)}, u32[]{:S(2)}) collective-permute-start(f32[2,1,384,128]{3,2,1,0:T(8,128)S(1)} %get-tuple-element.49), channel_id=1, source_target_pairs={{1,0},{2,1},{3,2},{4,3},{5,4},{6,5},{7,6},{8,7},{9,8},{10,9},{11,1... | collective-permute-start | bytes 1179656 | tf_op jit(solution)/shard_map/ppermute | solution.py:18
  316.9 9.6 %copy-start.16 = (f32[2,384]{1,0:T(2,128)S(1)}, f32[2,384]{1,0:T(2,128)}, u32[]{:S(2)}) copy-start(f32[2,384]{1,0:T(2,128)} %get-tuple-element.67) | copy-start | bytes 9220
  327.4 10.8 %collective-permute-start.6 = (f32[2,1,384,128]{3,2,1,0:T(8,128)S(1)}, f32[2,1,384,128]{3,2,1,0:T(8,128)S(1)}, u32[]{:S(2)}, u32[]{:S(2)}) collective-permute-start(f32[2,1,384,128]{3,2,1,0:T(8,128)S(1)} %get-tuple-element.46), channel_id=1, source_target_pairs={{0,1},{1,2},{2,3},{3,4},{4,5},{5,6},{6,7},{7,8},{8,9},{9,10},{10,1... | collective-permute-start | bytes 1179656 | tf_op jit(solution)/shard_map/ppermute | solution.py:15
  329.3 10.0 %collective-permute-start.7 = (f32[2,1,384,128]{3,2,1,0:T(8,128)S(1)}, f32[2,1,384,128]{3,2,1,0:T(8,128)S(1)}, u32[]{:S(2)}, u32[]{:S(2)}) collective-permute-start(f32[2,1,384,128]{3,2,1,0:T(8,128)S(1)} %get-tuple-element.47), channel_id=1, source_target_pairs={{1,0},{2,1},{3,2},{4,3},{5,4},{6,5},{7,6},{8,7},{9,8},{10,9},{11,1... | collective-permute-start | bytes 1179656 | tf_op jit(solution)/shard_map/ppermute | solution.py:18
  331.8 7.7 %copy-start.11 = (f32[2,384]{1,0:T(2,128)S(1)}, f32[2,384]{1,0:T(2,128)}, u32[]{:S(2)}) copy-start(f32[2,384]{1,0:T(2,128)} %copy-done.10) | copy-start | bytes 9220
  331.8 7.7 %copy-start.15 = (f32[2,384]{1,0:T(2,128)S(1)}, f32[2,384]{1,0:T(2,128)}, u32[]{:S(2)}) copy-start(f32[2,384]{1,0:T(2,128)} %copy-done.14) | copy-start | bytes 9220
  339.5 0.9 copy-start.18
Sparse Core Ops, SparseCore 0:
  46.0 87.8 all-reduce.7
  210.4 89.2 all-reduce.9
where the time goes:
time: 357 us; the launch traced here: 350 us
  waiting for transfers between devices  205 us (57%)
  other arithmetic  69.7 us (20%)
  matrix products  27.9 us (8%)
  starting transfers between devices  21.2 us (6%)
  between operations  16.4 us (5%)
  local copies, waits for them, and re-layouts  9.86 us (3%)
    psum x1, waiting for transfers between devices, on_device(): lax.psum(jnp.einsum('ik,il->kl', bar_rows, q_fact, precision=exact), 'row')  88.9 us
    psum x1, waiting for transfers between devices, on_device(): lax.psum(jnp.einsum('ik,il->kl', flat_rows, flat_rows, precision=exact),...  84.6 us
    another operation x6, other arithmetic, on_device(): lower_factor = jnp.linalg.cholesky(gram_matrix)  34 us
    another operation x4, other arithmetic, on_device(): lax.linalg.triangular_solve(lower_factor, identity, left_side=True, lower...  20.8 us
    ppermute x4, waiting for transfers between devices, padded(): lax.ppermute(lax.slice_in_dim(block, 0, width, axis=dim), axis, backward)  18.8 us
    ppermute x4, waiting for transfers between devices, padded(): lax.ppermute(lax.slice_in_dim(block, block.shape[dim] - width, None, axis...  12.8 us
    ppermute x4, starting transfers between devices, padded(): lax.ppermute(lax.slice_in_dim(block, block.shape[dim] - width, None, axis...  12.3 us
    ppermute x4, starting transfers between devices, padded(): lax.ppermute(lax.slice_in_dim(block, 0, width, axis=dim), axis, backward)  8.65 us
  transfers between devices with their start and end apart: 10, of which 10 were waited for; matrix products, arithmetic and copies ran while one was open for 2% of the time, Pallas kernels for 0%

commit v1 on v0

v1 whole, which is shorter than its diff:
```python
import jax
import jax.numpy as jnp
from jax import lax
from jax.experimental import pallas as pl
from jax.experimental.pallas import tpu as pltpu
from jax.sharding import PartitionSpec as P

rate_scales = (0.4, 0.4, 0.1, 0.2, 0.1, 0.1)
exact = lax.Precision.HIGHEST
f32 = jnp.float32
bf16 = jnp.bfloat16
VMEM = pl.BlockSpec(memory_space=pltpu.VMEM)
LIMIT = 56 * 1024 * 1024
PANEL = 16


def call(kernel, outs, flops, moved, scratch=()):
    return pl.pallas_call(
        kernel,
        out_shape=outs,
        scratch_shapes=list(scratch),
        compiler_params=pltpu.CompilerParams(vmem_limit_bytes=LIMIT),
        cost_estimate=pl.CostEstimate(flops=flops, bytes_accessed=moved, transcendentals=0),
    )


def split2(value):
    high = value.astype(bf16)
    low = (value - high.astype(f32)).astype(bf16)
    return high, low


def split3(value):
    high = value.astype(bf16)
    rest = value - high.astype(f32)
    mid = rest.astype(bf16)
    low = (rest - mid.astype(f32)).astype(bf16)
    return high, mid, low


def dot(a, b, contract):
    return lax.dot_general(a, b, ((contract[0], contract[1]), ((), ())), preferred_element_type=f32)


def coefficients(coeff_ref):
    table = coeff_ref[...]
    cols = jnp.transpose(table)
    out = []
    for r in range(2):
        out.append([cols[:, 2 * k + r : 2 * k + r + 1] * rate_scales[k] for k in range(6)])
    return out


def side(v):
    n = v.shape[0]
    place = lax.broadcasted_iota(jnp.int32, v.shape, 0)
    left = jnp.where(place == 0, 0.0, pltpu.roll(v, 1, 0))
    right = jnp.where(place == n - 1, 0.0, pltpu.roll(v, n - 1, 0))
    return left + right


def forward_light(c, xa, pa, xb, hop_x, hop_p):
    d, w, g, l, m, j = c
    return (
        -0.5 * l * xa - d * pa - j * hop_p,
        d * xa - 0.5 * l * pa - 2.0 * g * xb + j * hop_x,
    )


def forward_heavy(c, xa, xb, pb):
    d, w, g, l, m, j = c
    return w * pb, -w * xb - 0.5 * m * pb - 2.0 * g * xa


def backward_light(c, xa, pa, pb, hop_x, hop_p):
    d, w, g, l, m, j = c
    return (
        -0.5 * l * xa + d * pa - 2.0 * g * pb + hop_p,
        -d * xa - 0.5 * l * pa - hop_x,
    )


def backward_heavy(c, pa, xb, pb):
    d, w, g, l, m, j = c
    return -2.0 * g * pa - w * pb, w * xb - 0.5 * m * pb


def forward_rim(coeff_ref, z_ref, down_ref, up_ref):
    c = coefficients(coeff_ref)
    n = z_ref.shape[2]
    for r, out in ((0, down_ref), (1, up_ref)):
        xa, pa, xb = z_ref[0, r], z_ref[1, r], z_ref[2, r]
        hop_x = z_ref[0, 1 - r] + side(xa)
        hop_p = z_ref[1, 1 - r] + side(pa)
        bx, bp = forward_light(c[r], xa, pa, xb, hop_x, hop_p)
        out[0:n] = xa
        out[n : 2 * n] = pa
        out[2 * n : 3 * n] = bx
        out[3 * n : 4 * n] = bp
        hopping = coeff_ref[10 + r : 11 + r, :] * rate_scales[5]
        pieces = [hopping[:, k * 128 : (k + 1) * 128] for k in range(n // 128)]
        pieces.append(jnp.zeros((8 - n // 128, 128), f32))
        out[4 * n :] = jnp.concatenate(pieces, axis=0)


def far_hopping(recv_ref, n):
    tail = jnp.transpose(recv_ref[4 * n : 4 * n + 8])
    return jnp.concatenate([tail[:, k : k + 1] for k in range(n // 128)], axis=0)


def noise_products(noise_ref, q_ref, gram_ref, cross_ref, nh_ref, nl_ref, qh_ref, ql_ref):
    nh, nl = split2(noise_ref[...])
    qh, ql = split2(q_ref[...])
    nh_ref[...] = nh
    nl_ref[...] = nl
    qh_ref[...] = qh
    ql_ref[...] = ql
    down = ((0,), (0,))
    mixed = dot(nh, nl, down)
    gram_ref[...] = dot(nh, nh, down) + mixed + jnp.transpose(mixed)
    cross_ref[...] = dot(qh, nh, down) + dot(qh, nl, down) + dot(ql, nh, down)


def expand_products(
    coeff_ref, z_ref, low_ref, high_ref, nh_ref, nl_ref, qh_ref, ql_ref,
    gzz_ref, gzn_ref, cross_ref, xh_ref, xl_ref, first_ref,
):
    c = coefficients(coeff_ref)
    n = z_ref.shape[2]
    jlow = far_hopping(low_ref, n)
    jhigh = far_hopping(high_ref, n)
    low = [low_ref[k * n : (k + 1) * n] for k in range(4)]
    high = [high_ref[k * n : (k + 1) * n] for k in range(4)]
    far = ((low, jlow), (high, jhigh))
    for r in range(2):
        xa, pa, xb, pb = (z_ref[k, r] for k in range(4))
        hop_x = z_ref[0, 1 - r] + far[r][0][0] + side(xa)
        hop_p = z_ref[1, 1 - r] + far[r][0][1] + side(pa)
        first_ref[0, r], first_ref[1, r] = forward_light(c[r], xa, pa, xb, hop_x, hop_p)
        first_ref[2, r], first_ref[3, r] = forward_heavy(c[r], xa, xb, pb)
    for r in range(2):
        xa, pa, xb, pb = (first_ref[k, r] for k in range(4))
        beyond, jfar = far[r]
        far_x = beyond[2] - jfar * z_ref[1, r]
        far_p = beyond[3] + jfar * z_ref[0, r]
        hop_x = first_ref[0, 1 - r] + far_x + side(xa)
        hop_p = first_ref[1, 1 - r] + far_p + side(pa)
        second = forward_light(c[r], xa, pa, xb, hop_x, hop_p) + forward_heavy(c[r], xa, xb, pb)
        for k, (f, s) in enumerate(zip((xa, pa, xb, pb), second)):
            start = (2 * k + r) * n
            h, l = split2(z_ref[k, r] + f + 0.5 * s)
            xh_ref[start : start + n] = h
            xl_ref[start : start + n] = l
    down = ((0,), (0,))
    xh, xl = xh_ref[...], xl_ref[...]
    mixed = dot(xh, xl, down)
    gzz_ref[...] = dot(xh, xh, down) + mixed + jnp.transpose(mixed)
    gzn_ref[...] = dot(xh, nh_ref[...], down) + dot(xh, nl_ref[...], down) + dot(xl, nh_ref[...], down)
    cross_ref[...] = dot(qh_ref[...], xh, down) + dot(qh_ref[...], xl, down) + dot(ql_ref[...], xh, down)


def factor(sums_ref, r_bar_ref, nh_ref, nl_ref, sh_ref, sl_ref, a_ref, u_ref, inv_ref):
    size = 256
    tile = 128
    a_ref[0:tile, 0:tile] = sums_ref[0:tile]
    a_ref[0:tile, tile:size] = sums_ref[tile : 2 * tile]
    a_ref[tile:size, tile:size] = sums_ref[2 * tile : 3 * tile]
    row = lax.broadcasted_iota(jnp.int32, (size, size), 0)
    col = lax.broadcasted_iota(jnp.int32, (size, size), 1)
    a_ref[:, size : 2 * size] = jnp.where(row == col, 1.0, 0.0)
    u_ref[...] = jnp.zeros((size, size), f32)
    inv_ref[...] = jnp.zeros((size, size), f32)
    place = lax.broadcasted_iota(jnp.int32, (8, 3 * tile), 0)
    for start in range(0, size, PANEL):
        base = (start // tile) * tile
        lanes = slice(base, base + 3 * tile)
        offset = start - base
        rows = [jnp.broadcast_to(a_ref[start + i : start + i + 1, lanes], (8, 3 * tile)) for i in range(PANEL)]
        s = {}
        for i in range(PANEL):
            for m in range(i, PANEL):
                s[i, m] = jnp.broadcast_to(rows[i][:, offset + m : offset + m + 1], (8, tile))
        done = []
        for i in range(PANEL):
            inverse = pl.reciprocal(s[i, i])
            root = lax.rsqrt(s[i, i])
            root = root * (1.5 - 0.5 * s[i, i] * root * root)
            for k in range(i + 1, PANEL):
                factor_k = s[i, k] * inverse
                for m in range(k, PANEL):
                    s[k, m] = s[k, m] - factor_k * s[i, m]
                rows[k] = rows[k] - jnp.concatenate([factor_k] * 3, axis=1) * rows[i]
            done.append(rows[i] * jnp.concatenate([root] * 3, axis=1))
        groups = []
        for first in range(0, PANEL, 8):
            group = done[first]
            for i in range(1, 8):
                group = jnp.where(place == i, done[first + i], group)
            groups.append(group)
        panel = jnp.concatenate(groups, axis=0)
        stop = start + PANEL
        if base == 0:
            u_ref[start:stop, :] = panel[:, : 2 * tile]
            inv_ref[start:stop, :tile] = panel[:, 2 * tile :]
        else:
            u_ref[start:stop, tile:] = panel[:, :tile]
            inv_ref[start:stop, :] = panel[:, tile:]
        if stop < size:
            h, m, l = split3(panel)
            width = size - base
            left = jnp.concatenate([h, h, m, m, h, l], axis=0)[:, :width]
            right = jnp.concatenate([h, m, h, m, l, h], axis=0)
            change = dot(left, right, ((0,), (0,)))
            a_ref[stop:, lanes] = a_ref[stop:, lanes] - change[stop - base :]
    upper = jnp.where(row <= col, u_ref[...], 0.0)
    inv = jnp.where(row >= col, inv_ref[...], 0.0)
    bar = jnp.where(row <= col, r_bar_ref[...], 0.0)
    cross = jnp.concatenate([sums_ref[3 * tile : 5 * tile], sums_ref[5 * tile : 7 * tile]], axis=1)

    def product(a, b, contract):
        return lax.dot_general(a, b, ((contract[0], contract[1]), ((), ())), precision=exact, preferred_element_type=f32)

    across = ((1,), (1,))
    middle = product(upper, bar, across) - product(cross, inv, across)
    symmetric = jnp.where(row >= col, middle, 0.0) + jnp.transpose(jnp.where(row > col, middle, 0.0))
    spread = product(inv, product(symmetric, inv, ((1,), (0,))), ((0,), (0,)))
    nh_ref[...], nl_ref[...] = split2(inv)
    sh_ref[...], sl_ref[...] = split2(spread)


def gradient(
    coeff_ref, qh_ref, ql_ref, xh_ref, xl_ref, nh_ref, nl_ref, ih_ref, il_ref, sh_ref, sl_ref,
    w_ref, noise_ref, down_ref, up_ref,
):
    n = w_ref.shape[2]
    plain = ((1,), (0,))
    for k in range(4):
        for r in range(2):
            start = (2 * k + r) * n
            here = slice(start, start + n)
            qh, ql = qh_ref[here], ql_ref[here]
            xh = jnp.concatenate([xh_ref[here], nh_ref[here]], axis=1)
            xl = jnp.concatenate([xl_ref[here], nl_ref[here]], axis=1)
            grad = (
                dot(qh, ih_ref[...], plain) + dot(ql, ih_ref[...], plain) + dot(qh, il_ref[...], plain)
                + dot(xh, sh_ref[...], plain) + dot(xl, sh_ref[...], plain) + dot(xh, sl_ref[...], plain)
            )
            w_ref[k, r] = grad[:, :128]
            noise_ref[k, r] = grad[:, 128:]
    c = coefficients(coeff_ref)
    for r, out in ((0, down_ref), (1, up_ref)):
        xa, pa, pb = w_ref[0, r], w_ref[1, r], w_ref[3, r]
        j = c[r][5]
        jother = c[1 - r][5]
        jx, jp = j * xa, j * pa
        hop_x = jother * w_ref[0, 1 - r] + side(jx)
        hop_p = jother * w_ref[1, 1 - r] + side(jp)
        bx, bp = backward_light(c[r], xa, pa, pb, hop_x, hop_p)
        out[0:n] = jx
        out[n : 2 * n] = jp
        out[2 * n : 3 * n] = j * bx
        out[3 * n : 4 * n] = j * bp


def contract_back(coeff_ref, w_ref, low_ref, high_ref, flow_ref, fhigh_ref, out_ref, first_ref):
    c = coefficients(coeff_ref)
    n = w_ref.shape[2]
    far = ((low_ref, far_hopping(flow_ref, n)), (high_ref, far_hopping(fhigh_ref, n)))
    for r in range(2):
        xa, pa, xb, pb = (w_ref[k, r] for k in range(4))
        j, jother = c[r][5], c[1 - r][5]
        beyond = far[r][0]
        hop_x = jother * w_ref[0, 1 - r] + beyond[0:n] + side(j * xa)
        hop_p = jother * w_ref[1, 1 - r] + beyond[n : 2 * n] + side(j * pa)
        first_ref[0, r], first_ref[1, r] = backward_light(c[r], xa, pa, pb, hop_x, hop_p)
        first_ref[2, r], first_ref[3, r] = backward_heavy(c[r], pa, xb, pb)
    for r in range(2):
        xa, pa, xb, pb = (first_ref[k, r] for k in range(4))
        j, jother = c[r][5], c[1 - r][5]
        beyond, jfar = far[r]
        far_x = beyond[2 * n : 3 * n] + jfar * (j * w_ref[1, r])
        far_p = beyond[3 * n : 4 * n] - jfar * (j * w_ref[0, r])
        hop_x = jother * first_ref[0, 1 - r] + far_x + side(j * xa)
        hop_p = jother * first_ref[1, 1 - r] + far_p + side(j * pa)
        second = backward_light(c[r], xa, pa, pb, hop_x, hop_p) + backward_heavy(c[r], pa, xb, pb)
        for k, (f, s) in enumerate(zip((xa, pa, xb, pb), second)):
            out_ref[k, r] = w_ref[k, r] + f + 0.5 * s


def exchange(up, down):
    count = lax.axis_size("row")
    forward = [(i, i + 1) for i in range(count - 1)]
    backward = [(i + 1, i) for i in range(count - 1)]
    low = lax.ppermute(up, "row", forward)
    high = lax.ppermute(down, "row", backward)
    return low, high


def sum_over_rows(x):
    count = lax.axis_size("row")
    parts = lax.all_to_all(x.reshape((count, -1) + x.shape[1:]), "row", 0, 0)
    mine = parts.sum(0)
    whole = lax.all_to_all(jnp.broadcast_to(mine[None], parts.shape), "row", 0, 0)
    return whole.reshape(x.shape)


def on_device(cell_coeffs, z_factor, noise_cols, q_bar, r_bar):
    quads, lattice, n, rank = z_factor.shape
    flat = quads * lattice * n
    coeffs = cell_coeffs.reshape(12, n)
    noise = noise_cols.reshape(flat, -1)
    bar = q_bar.reshape(flat, -1)
    shape = jax.ShapeDtypeStruct
    rim = shape((4 * n + 8, rank), f32)
    up_down = call(forward_rim, (rim, rim), 10**6, 2 * 10**6)(coeffs, z_factor)
    low, high = exchange(up_down[1], up_down[0])
    half = shape((flat, 128), bf16)
    full = shape((flat, 256), bf16)
    block = shape((128, 128), f32)
    tall = shape((256, 128), f32)
    gnn, cross_n, nh, nl, qh, ql = call(
        noise_products, (block, tall, half, half, full, full), 2 * flat * 128 * 128 * 11, 9 * 10**6
    )(noise, bar)
    gzz, gzn, cross_z, xh, xl = call(
        expand_products, (block, block, tall, half, half), 2 * flat * 128 * 128 * 11, 9 * 10**6,
        [pltpu.VMEM(z_factor.shape, f32)],
    )(coeffs, z_factor, low, high, nh, nl, qh, ql)
    sums = sum_over_rows(jnp.concatenate([gzz, gzn, gnn, cross_z, cross_n], axis=0))
    square = shape((256, 256), bf16)
    ih, il, sh, sl = call(
        factor, (square,) * 4, 10**9, 10**6,
        [pltpu.VMEM((256, 512), f32), pltpu.VMEM((256, 256), f32), pltpu.VMEM((256, 256), f32)],
    )(sums, r_bar)
    rim = shape((4 * n, rank), f32)
    w, noise_grad, down, up = call(
        gradient, (shape(z_factor.shape, f32), shape(noise_cols.shape, f32), rim, rim),
        2 * flat * 256 * 256 * 6, 12 * 10**6,
    )(coeffs, qh, ql, xh, xl, nh, nl, ih, il, sh, sl)
    back_low, back_high = exchange(up, down)
    z_grad = call(
        contract_back, shape(z_factor.shape, f32), 10**7, 6 * 10**6, [pltpu.VMEM(z_factor.shape, f32)]
    )(coeffs, w, back_low, back_high, low, high)
    return z_grad, noise_grad


def solution(mesh):
    return jax.shard_map(
        on_device,
        mesh=mesh,
        in_specs=(
            P(None, "row", None),
            P(None, ("grp", "row"), None, None),
            P(None, ("grp", "row"), None, None),
            P(None, ("grp", "row"), None, None),
            P("grp", None),
        ),
        out_specs=(P(None, ("grp", "row"), None, None), P(None, ("grp", "row"), None, None)),
        check_vma=False,
    )
```

time: 357 us -> 125 us (0.35); the launches traced: 350 us -> 125 us
  waiting for transfers between devices: 205 us -> 29.2 us
  other arithmetic: 69.7 us -> 0.03 us
  Pallas kernels: 0 us -> 44.2 us
  blocking collectives: 0 us -> 34.7 us
  matrix products: 27.9 us -> 0 us
  between operations: 16.4 us -> 0.71 us
  starting transfers between devices: 21.2 us -> 10.1 us
  local copies, waits for them, and re-layouts: 9.86 us -> 5.8 us
    psum x2 -> x0, waiting for transfers between devices: 173 us -> none  [the longest x1 88.9 us: on_device(): lax.psum(jnp.einsum('ik,il->kl', bar_rows, q_fact, precision=exact), 'row')]
    another operation x18 -> x0, other arithmetic: 56.1 us -> none  [the longest x6 34 us: on_device(): lower_factor = jnp.linalg.cholesky(gram_matrix)]
    pallas_call x0 -> x6, Pallas kernels: none -> 44.2 us  [the longest x1 13.3 us: on_device(): call(factor, (square,) * 4, 10 ** 9, 10 ** 6, [pltpu.VMEM((256, 512), f32...]
    all_to_all x0 -> x2, blocking collectives: none -> 34.7 us  [the longest x1 17.6 us: sum_over_rows(): parts = lax.all_to_all(x.reshape((count, -1) + x.shape[1:]), 'row', 0, 0)]
    dot_general x6 -> x0, matrix products: 25.9 us -> none  [the longest x1 5.98 us: on_device(): jnp.einsum('ik,il->kl', flat_rows, flat_rows, precision=exact)]
    ppermute x8 -> x4, starting transfers between devices: 20.9 us -> 10.1 us  [the longest x2 6.28 us: exchange(): low = lax.ppermute(up, 'row', forward)]
    another operation x10 -> x0, local copies, waits for them, and re-layouts: 5.55 us -> none
    add x8 -> x0, other arithmetic: 3.72 us -> none  [the longest x1 1.08 us: hop_add(): local_term[1] + hopping * hop_sums[1]]
  transfers between devices with their start and end apart: 10 -> 4, of which waited for: 10 -> 4; matrix products, arithmetic and copies ran while one was open for 2% -> 0% of each run, Pallas kernels for 0% -> 4%
where the time goes in v1:
time: 125 us
  Pallas kernels  44.2 us (35%)
  blocking collectives  34.7 us (28%)
  waiting for transfers between devices  29.2 us (23%)
  starting transfers between devices  10.1 us (8%)
  local copies, waits for them, and re-layouts  5.8 us (5%)
    ppermute x2, waiting for transfers between devices, exchange(): low = lax.ppermute(up, 'row', forward)  26 us
    all_to_all x1, blocking collectives, sum_over_rows(): parts = lax.all_to_all(x.reshape((count, -1) + x.shape[1:]), 'row', 0, 0)  17.6 us
    all_to_all x1, blocking collectives, sum_over_rows(): lax.all_to_all(jnp.broadcast_to(mine[None], parts.shape), 'row', 0, 0)  17.1 us
    pallas_call x1, Pallas kernels, on_device(): call(factor, (square,) * 4, 10 ** 9, 10 ** 6, [pltpu.VMEM((256, 512), f32...  13.3 us
    pallas_call x1, Pallas kernels, on_device(): call(expand_products, (block, block, tall, half, half), 2 * flat * 128 *...  8.57 us
    pallas_call x1, Pallas kernels, on_device(): call(gradient, (shape(z_factor.shape, f32), shape(noise_cols.shape, f32),...  7.92 us
    ppermute x2, starting transfers between devices, exchange(): low = lax.ppermute(up, 'row', forward)  6.28 us
    pallas_call x1, Pallas kernels, on_device(): call(noise_products, (block, tall, half, half, full, full), 2 * flat * 12...  5.58 us
  transfers between devices with their start and end apart: 4, of which 4 were waited for; matrix products, arithmetic and copies ran while one was open for 0% of the time, Pallas kernels for 4%

profile of v1, /device:TPU:9, one launch (start us, length us, event | category | flops | bytes accessed | tf_op | source)
XLA Modules:
  0.0 124.8 jit_solution(10382607224140430393)
XLA Ops:
  0.6 1.3 %reshape.20.coeff_ref = f32[12,384]{1,0:T(8,128)} reshape(f32[6,2,384]{2,1,0:T(2,128)} %param.5) | data formatting | bytes 36864 | tf_op jit(solution)/shard_map/reshape | solution.py:310
  2.0 3.3 %shard_map.69 = (f32[1544,128]{1,0:T(8,128)}, f32[1544,128]{1,0:T(8,128)}) custom-call(f32[12,384]{1,0:T(8,128)} %reshape.20.coeff_ref, f32[4,2,384,128]{3,2,1,0:T(8,128)} %z_ref.3), custom_call_target="tpu_custom_call" | custom-call | flops 1000000 | bytes 2000000 | tf_op jit(solution)/shard_map/pallas_call | solution.py:315
  5.2 3.7 %collective-permute-start = (f32[1544,128]{1,0:T(8,128)}, f32[1544,128]{1,0:T(8,128)S(1)}, u32[]{:S(2)}, u32[]{:S(2)}) collective-permute-start(f32[1544,128]{1,0:T(8,128)} %get-tuple-element.25), channel_id=1, source_target_pairs={{0,1},{1,2},{2,3},{3,4},{4,5},{5,6},{6,7},{7,8},{8,9},{9,10},{10,1... | collective-permute-start | bytes 2371592 | tf_op jit(solution)/shard_map/ppermute | solution.py:294
  8.9 1.9 %collective-permute-start.1 = (f32[1544,128]{1,0:T(8,128)}, f32[1544,128]{1,0:T(8,128)S(1)}, u32[]{:S(2)}, u32[]{:S(2)}) collective-permute-start(f32[1544,128]{1,0:T(8,128)} %get-tuple-element.26), channel_id=1, source_target_pairs={{1,0},{2,1},{3,2},{4,3},{5,4},{6,5},{7,6},{8,7},{9,8},{10,9},{11,1... | collective-permute-start | bytes 2371592 | tf_op jit(solution)/shard_map/ppermute | solution.py:295
  10.9 5.6 %shard_map.68 = (f32[128,128]{1,0:T(8,128)}, f32[256,128]{1,0:T(8,128)}, bf16[3072,128]{1,0:T(8,128)(2,1)}, bf16[3072,128]{1,0:T(8,128)(2,1)}, bf16[3072,256]{1,0:T(8,128)(2,1)}, /*index=5*/bf16[3072,256]{1,0:T(8,128)(2,1)}) custom-call(f32[3072,128]{1,0:T(8,128)} %bitcast.5, f32[3072,256]{1,0:T(8,128)} %bitcast.4), custom_call_target="tpu_custom_call" | custom-call | flops 1107296256 | bytes 9000000 | tf_op jit(solution)/shard_map/pallas_call | solution.py:321
  16.5 10.2 %collective-permute-done.low_ref.flow_ref = f32[1544,128]{1,0:T(8,128)S(1)} collective-permute-done((f32[1544,128]{1,0:T(8,128)}, f32[1544,128]{1,0:T(8,128)S(1)}, u32[]{:S(2)}, u32[]{:S(2)}) %collective-permute-start) | collective-permute-done | bytes 790560 | tf_op jit(solution)/shard_map/ppermute | solution.py:294
  26.7 0.0 copy-start
  26.7 1.5 %collective-permute-done.1.high_ref.fhigh_ref = f32[1544,128]{1,0:T(8,128)S(1)} collective-permute-done((f32[1544,128]{1,0:T(8,128)}, f32[1544,128]{1,0:T(8,128)S(1)}, u32[]{:S(2)}, u32[]{:S(2)}) %collective-permute-start.1) | collective-permute-done | bytes 790560 | tf_op jit(solution)/shard_map/ppermute | solution.py:295
  28.2 0.0 copy-start.1
  28.2 0.0 copy-done
  28.2 0.9 copy-done.1
  29.0 0.0 copy-start.5
  29.0 0.0 copy-start.4
  29.0 8.6 %shard_map.70 = (f32[128,128]{1,0:T(8,128)}, f32[128,128]{1,0:T(8,128)}, f32[256,128]{1,0:T(8,128)}, bf16[3072,128]{1,0:T(8,128)(2,1)}, bf16[3072,128]{1,0:T(8,128)(2,1)}) custom-call(f32[12,384]{1,0:T(8,128)} %reshape.20.coeff_ref, f32[4,2,384,128]{3,2,1,0:T(8,128)} %z_ref.3, f32[1544,128]{1,0:T(8,128)} %copy-done, f32[1544,128]{1,0:T(8,128)} %copy-done.1, ...), custom_call_target="tpu_custom_call" | custom-call | flops 1107296256 | bytes 9000000 | tf_op jit(solution)/shard_map/pallas_call | solution.py:324
  37.6 0.8 constant_dynamic-update-slice_fusion.4
  38.5 0.8 constant_dynamic-update-slice_fusion.3
  39.3 0.0 copy-done.5
  39.3 0.9 constant_dynamic-update-slice_fusion.1
  40.2 0.0 copy-done.4
  40.3 17.6 %all_to_all.10 = f32[16,56,128]{2,1,0:T(8,128)S(1)} all-to-all(f32[16,56,128]{2,1,0:T(8,128)S(1)} %bitcast.6), channel_id=1, replica_groups=mesh['grp'=2,'row'=16] {'row'}, dimensions={0} | all-to-all | bytes 917504 | tf_op jit(solution)/shard_map/all_to_all | solution.py:301
  58.0 17.1 %all_to_all.11 = f32[16,56,128]{2,1,0:T(8,128)} all-to-all(f32[16,56,128]{2,1,0:T(8,128)S(1)} %broadcast_in_dim.2), channel_id=1, replica_groups=mesh['grp'=2,'row'=16] {'row'}, dimensions={0} | all-to-all | bytes 917504 | tf_op jit(solution)/shard_map/all_to_all | solution.py:303
  75.0 13.3 %shard_map.71 = (bf16[256,256]{1,0:T(8,128)(2,1)}, bf16[256,256]{1,0:T(8,128)(2,1)}, bf16[256,256]{1,0:T(8,128)(2,1)}, bf16[256,256]{1,0:T(8,128)(2,1)}) custom-call(f32[896,128]{1,0:T(8,128)} %bitcast.7, f32[256,256]{1,0:T(8,128)} %r_bar_ref.1), custom_call_target="tpu_custom_call" | custom-call | flops 1000000000 | bytes 1000000 | tf_op jit(solution)/shard_map/pallas_call | solution.py:330
  88.3 7.9 %shard_map.72 = (f32[4,2,384,128]{3,2,1,0:T(8,128)}, f32[4,2,384,128]{3,2,1,0:T(8,128)}, f32[1536,128]{1,0:T(8,128)}, f32[1536,128]{1,0:T(8,128)}) custom-call(f32[12,384]{1,0:T(8,128)} %reshape.20.coeff_ref, bf16[3072,256]{1,0:T(8,128)(2,1)} %get-tuple-element.23.qh_ref, bf16[3072,256]{1,0:T(8,128)(2,1)} %get-tuple-element.24.ql_ref, ...), custom_call_target="tpu_custom_call" | custom-call | flops 2415919104 | bytes 12000000 | tf_op jit(solution)/shard_map/pallas_call | solution.py:335
  96.3 2.6 %collective-permute-start.2 = (f32[1536,128]{1,0:T(8,128)}, f32[1536,128]{1,0:T(8,128)S(1)}, u32[]{:S(2)}, u32[]{:S(2)}) collective-permute-start(f32[1536,128]{1,0:T(8,128)} %get-tuple-element.41), channel_id=1, source_target_pairs={{0,1},{1,2},{2,3},{3,4},{4,5},{5,6},{6,7},{7,8},{8,9},{9,10},{10,1... | collective-permute-start | bytes 2359304 | tf_op jit(solution)/shard_map/ppermute | solution.py:294
  98.9 1.9 %collective-permute-start.3 = (f32[1536,128]{1,0:T(8,128)}, f32[1536,128]{1,0:T(8,128)S(1)}, u32[]{:S(2)}, u32[]{:S(2)}) collective-permute-start(f32[1536,128]{1,0:T(8,128)} %get-tuple-element.42), channel_id=1, source_target_pairs={{1,0},{2,1},{3,2},{4,3},{5,4},{6,5},{7,6},{8,7},{9,8},{10,9},{11,1... | collective-permute-start | bytes 2359304 | tf_op jit(solution)/shard_map/ppermute | solution.py:295
  100.8 15.7 %collective-permute-done.2.low_ref = f32[1536,128]{1,0:T(8,128)S(1)} collective-permute-done((f32[1536,128]{1,0:T(8,128)}, f32[1536,128]{1,0:T(8,128)S(1)}, u32[]{:S(2)}, u32[]{:S(2)}) %collective-permute-start.2) | collective-permute-done | bytes 786464 | tf_op jit(solution)/shard_map/ppermute | solution.py:294
  116.5 0.0 copy-start.2
  116.5 1.8 %collective-permute-done.3.high_ref = f32[1536,128]{1,0:T(8,128)S(1)} collective-permute-done((f32[1536,128]{1,0:T(8,128)}, f32[1536,128]{1,0:T(8,128)S(1)}, u32[]{:S(2)}, u32[]{:S(2)}) %collective-permute-start.3) | collective-permute-done | bytes 786464 | tf_op jit(solution)/shard_map/ppermute | solution.py:295
  118.3 0.0 copy-start.3
  118.3 0.0 copy-done.2
  118.3 0.9 copy-done.3
  119.2 5.6 %shard_map.73 = f32[4,2,384,128]{3,2,1,0:T(8,128)} custom-call(f32[12,384]{1,0:T(8,128)} %reshape.20.coeff_ref, f32[4,2,384,128]{3,2,1,0:T(8,128)} %get-tuple-element.40.w_ref, f32[1536,128]{1,0:T(8,128)} %copy-done.2, f32[1536,128]{1,0:T(8,128)} %copy-done.3, f32[1544,128]{1,0:T(8,128)} %copy-done, f32[1544,128]{1,0:T(8,128)} %copy-done.1), custom_call_target="tpu_custom_call" | custom-call | flops 10000000 | bytes 6000000 | tf_op jit(solution)/shard_map/pallas_call | solution.py:340
  (4 shorter events, 0.1 us)
Async XLA Ops:
  5.2 21.4 %collective-permute-start = (f32[1544,128]{1,0:T(8,128)}, f32[1544,128]{1,0:T(8,128)S(1)}, u32[]{:S(2)}, u32[]{:S(2)}) collective-permute-start(f32[1544,128]{1,0:T(8,128)} %get-tuple-element.25), channel_id=1, source_target_pairs={{0,1},{1,2},{2,3},{3,4},{4,5},{5,6},{6,7},{7,8},{8,9},{9,10},{10,1... | collective-permute-start | bytes 2371592 | tf_op jit(solution)/shard_map/ppermute | solution.py:294
  8.9 19.2 %collective-permute-start.1 = (f32[1544,128]{1,0:T(8,128)}, f32[1544,128]{1,0:T(8,128)S(1)}, u32[]{:S(2)}, u32[]{:S(2)}) collective-permute-start(f32[1544,128]{1,0:T(8,128)} %get-tuple-element.26), channel_id=1, source_target_pairs={{1,0},{2,1},{3,2},{4,3},{5,4},{6,5},{7,6},{8,7},{9,8},{10,9},{11,1... | collective-permute-start | bytes 2371592 | tf_op jit(solution)/shard_map/ppermute | solution.py:295
  26.7 1.5 %copy-start = (f32[1544,128]{1,0:T(8,128)}, f32[1544,128]{1,0:T(8,128)S(1)}, u32[]{:S(2)}) copy-start(f32[1544,128]{1,0:T(8,128)S(1)} %collective-permute-done.low_ref.flow_ref) | copy-start | bytes 2371588
  28.2 0.9 copy-start.1
  29.0 10.3 %copy-start.5 = (f32[128,128]{1,0:T(8,128)S(1)}, f32[128,128]{1,0:T(8,128)}, u32[]{:S(2)}) copy-start(f32[128,128]{1,0:T(8,128)} %get-tuple-element.33) | copy-start | bytes 196612
  29.0 11.2 %copy-start.4 = (f32[256,128]{1,0:T(8,128)S(1)}, f32[256,128]{1,0:T(8,128)}, u32[]{:S(2)}) copy-start(f32[256,128]{1,0:T(8,128)} %get-tuple-element.35) | copy-start | bytes 393220
  96.3 20.2 %collective-permute-start.2 = (f32[1536,128]{1,0:T(8,128)}, f32[1536,128]{1,0:T(8,128)S(1)}, u32[]{:S(2)}, u32[]{:S(2)}) collective-permute-start(f32[1536,128]{1,0:T(8,128)} %get-tuple-element.41), channel_id=1, source_target_pairs={{0,1},{1,2},{2,3},{3,4},{4,5},{5,6},{6,7},{7,8},{8,9},{9,10},{10,1... | collective-permute-start | bytes 2359304 | tf_op jit(solution)/shard_map/ppermute | solution.py:294
  98.9 19.5 %collective-permute-start.3 = (f32[1536,128]{1,0:T(8,128)}, f32[1536,128]{1,0:T(8,128)S(1)}, u32[]{:S(2)}, u32[]{:S(2)}) collective-permute-start(f32[1536,128]{1,0:T(8,128)} %get-tuple-element.42), channel_id=1, source_target_pairs={{1,0},{2,1},{3,2},{4,3},{5,4},{6,5},{7,6},{8,7},{9,8},{10,9},{11,1... | collective-permute-start | bytes 2359304 | tf_op jit(solution)/shard_map/ppermute | solution.py:295
  116.5 1.8 %copy-start.2 = (f32[1536,128]{1,0:T(8,128)}, f32[1536,128]{1,0:T(8,128)S(1)}, u32[]{:S(2)}) copy-start(f32[1536,128]{1,0:T(8,128)S(1)} %collective-permute-done.2.low_ref) | copy-start | bytes 2359300
  118.3 0.9 copy-start.3

commit v2 on v1

--- a/solution.py
+++ b/solution.py
@@ -10,18 +10,25 @@
 f32 = jnp.float32
 bf16 = jnp.bfloat16
 VMEM = pl.BlockSpec(memory_space=pltpu.VMEM)
-LIMIT = 56 * 1024 * 1024
+LIMIT = 24 * 1024 * 1024
 PANEL = 16
 
 
-def call(kernel, outs, flops, moved, scratch=()):
-    return pl.pallas_call(
-        kernel,
-        out_shape=outs,
-        scratch_shapes=list(scratch),
-        compiler_params=pltpu.CompilerParams(vmem_limit_bytes=LIMIT),
-        cost_estimate=pl.CostEstimate(flops=flops, bytes_accessed=moved, transcendentals=0),
-    )
+def call(kernel, outs, flops, moved, scratch=(), scalar=False):
+    def run(*args):
+        specs = [pl.BlockSpec() for _ in args]
+        if scalar:
+            specs[0] = pl.BlockSpec(memory_space=pltpu.SMEM)
+        return pl.pallas_call(
+            kernel,
+            out_shape=outs,
+            in_specs=specs,
+            scratch_shapes=list(scratch),
+            compiler_params=pltpu.CompilerParams(vmem_limit_bytes=LIMIT),
+            cost_estimate=pl.CostEstimate(flops=flops, bytes_accessed=moved, transcendentals=0),
+        )(*args)
+
+    return run
 
 
 def split2(value):
@@ -43,8 +50,7 @@
 
 
 def coefficients(coeff_ref):
-    table = coeff_ref[...]
-    cols = jnp.transpose(table)
+    cols = jnp.transpose(jnp.concatenate([coeff_ref[k] for k in range(6)], axis=0))
     out = []
     for r in range(2):
         out.append([cols[:, 2 * k + r : 2 * k + r + 1] * rate_scales[k] for k in range(6)])
@@ -97,7 +103,7 @@
         out[n : 2 * n] = pa
         out[2 * n : 3 * n] = bx
         out[3 * n : 4 * n] = bp
-        hopping = coeff_ref[10 + r : 11 + r, :] * rate_scales[5]
+        hopping = coeff_ref[5, r : r + 1, :] * rate_scales[5]
         pieces = [hopping[:, k * 128 : (k + 1) * 128] for k in range(n // 128)]
         pieces.append(jnp.zeros((8 - n // 128, 128), f32))
         out[4 * n :] = jnp.concatenate(pieces, axis=0)
@@ -108,7 +114,14 @@
     return jnp.concatenate([tail[:, k : k + 1] for k in range(n // 128)], axis=0)
 
 
-def noise_products(noise_ref, q_ref, gram_ref, cross_ref, nh_ref, nl_ref, qh_ref, ql_ref):
+def packed(gram, cross):
+    row = lax.broadcasted_iota(jnp.int32, gram.shape, 0)
+    col = lax.broadcasted_iota(jnp.int32, gram.shape, 1)
+    diagonal = jnp.sum(jnp.where(row == col, cross, 0.0), axis=0, keepdims=True)
+    return jnp.where(row <= col, gram, cross), jnp.broadcast_to(diagonal, (8, gram.shape[1]))
+
+
+def noise_products(noise_ref, q_ref, pack_ref, nh_ref, nl_ref, qh_ref, ql_ref):
     nh, nl = split2(noise_ref[...])
     qh, ql = split2(q_ref[...])
     nh_ref[...] = nh
@@ -117,13 +130,15 @@
     ql_ref[...] = ql
     down = ((0,), (0,))
     mixed = dot(nh, nl, down)
-    gram_ref[...] = dot(nh, nh, down) + mixed + jnp.transpose(mixed)
-    cross_ref[...] = dot(qh, nh, down) + dot(qh, nl, down) + dot(ql, nh, down)
+    gram = dot(nh, nh, down) + mixed + jnp.transpose(mixed)
+    qh, ql = qh[:, 128:], ql[:, 128:]
+    cross = dot(qh, nh, down) + dot(qh, nl, down) + dot(ql, nh, down)
+    pack_ref[0:128], pack_ref[128:] = packed(gram, cross)
 
 
 def expand_products(
-    coeff_ref, z_ref, low_ref, high_ref, nh_ref, nl_ref, qh_ref, ql_ref,
-    gzz_ref, gzn_ref, cross_ref, xh_ref, xl_ref, first_ref,
+    core_ref, coeff_ref, z_ref, low_ref, high_ref, pack_ref, nh_ref, nl_ref, qh_ref, ql_ref,
+    mine_ref, other_ref, xh_ref, xl_ref, first_ref, sums_ref,
 ):
     c = coefficients(coeff_ref)
     n = z_ref.shape[2]
@@ -154,17 +169,29 @@
     down = ((0,), (0,))
     xh, xl = xh_ref[...], xl_ref[...]
     mixed = dot(xh, xl, down)
-    gzz_ref[...] = dot(xh, xh, down) + mixed + jnp.transpose(mixed)
-    gzn_ref[...] = dot(xh, nh_ref[...], down) + dot(xh, nl_ref[...], down) + dot(xl, nh_ref[...], down)
-    cross_ref[...] = dot(qh_ref[...], xh, down) + dot(qh_ref[...], xl, down) + dot(ql_ref[...], xh, down)
-
-
-def factor(sums_ref, r_bar_ref, nh_ref, nl_ref, sh_ref, sl_ref, a_ref, u_ref, inv_ref):
+    gram = dot(xh, xh, down) + mixed + jnp.transpose(mixed)
+    cross = dot(qh_ref[...], xh, down) + dot(qh_ref[...], xl, down) + dot(ql_ref[...], xh, down)
+    sums_ref[0:128], sums_ref[512:520] = packed(gram, cross[:128])
+    sums_ref[128:256] = dot(xh, nh_ref[...], down) + dot(xh, nl_ref[...], down) + dot(xl, nh_ref[...], down)
+    sums_ref[256:384] = cross[128:]
+    sums_ref[384:512] = pack_ref[0:128]
+    sums_ref[520:528] = pack_ref[128:136]
+    core = core_ref[0]
+    mine_ref[...] = sums_ref[pl.ds(pl.multiple_of(core * 264, 8), 264)]
+    other_ref[...] = sums_ref[pl.ds(pl.multiple_of((1 - core) * 264, 8), 264)]
+
+
+def factor(
+    core_ref, mine_ref, other_ref, r_bar_ref, nh_ref, nl_ref, sh_ref, sl_ref, sums_ref, a_ref, u_ref, inv_ref
+):
     size = 256
     tile = 128
+    core = core_ref[0]
+    sums_ref[pl.ds(pl.multiple_of(core * 264, 8), 264)] = mine_ref[...]
+    sums_ref[pl.ds(pl.multiple_of((1 - core) * 264, 8), 264)] = other_ref[...]
     a_ref[0:tile, 0:tile] = sums_ref[0:tile]
     a_ref[0:tile, tile:size] = sums_ref[tile : 2 * tile]
-    a_ref[tile:size, tile:size] = sums_ref[2 * tile : 3 * tile]
+    a_ref[tile:size, tile:size] = sums_ref[3 * tile : 4 * tile]
     row = lax.broadcasted_iota(jnp.int32, (size, size), 0)
     col = lax.broadcasted_iota(jnp.int32, (size, size), 1)
     a_ref[:, size : 2 * size] = jnp.where(row == col, 1.0, 0.0)
@@ -215,7 +242,12 @@
     upper = jnp.where(row <= col, u_ref[...], 0.0)
     inv = jnp.where(row >= col, inv_ref[...], 0.0)
     bar = jnp.where(row <= col, r_bar_ref[...], 0.0)
-    cross = jnp.concatenate([sums_ref[3 * tile : 5 * tile], sums_ref[5 * tile : 7 * tile]], axis=1)
+    corner = jnp.zeros((tile, tile), f32)
+    top = jnp.concatenate([sums_ref[0:tile], corner], axis=1)
+    bottom = jnp.concatenate([sums_ref[2 * tile : 3 * tile], sums_ref[3 * tile : 4 * tile]], axis=1)
+    cross = jnp.concatenate([top, bottom], axis=0)
+    diagonal = jnp.concatenate([sums_ref[512:513], sums_ref[520:521]], axis=1)
+    cross = jnp.where(row > col, cross, jnp.where(row == col, diagonal, 0.0))
 
     def product(a, b, contract):
         return lax.dot_general(a, b, ((contract[0], contract[1]), ((), ())), precision=exact, preferred_element_type=f32)
@@ -296,18 +328,22 @@
     return low, high
 
 
-def sum_over_rows(x):
+def sum_over_rows(mine, other):
     count = lax.axis_size("row")
-    parts = lax.all_to_all(x.reshape((count, -1) + x.shape[1:]), "row", 0, 0)
-    mine = parts.sum(0)
-    whole = lax.all_to_all(jnp.broadcast_to(mine[None], parts.shape), "row", 0, 0)
-    return whole.reshape(x.shape)
+    bits = count.bit_length() - 1
+    swap = [(i, i ^ 1) for i in range(count)]
+    mine = mine + lax.ppermute(other, "row", swap)
+    for step in range(bits - 1):
+        turn = [1 + step, 1 + (step + 1) % (bits - 1)]
+        mine = mine + lax.ppermute(mine, "row", [(i, i ^ (1 << turn[i & 1])) for i in range(count)])
+    return mine, lax.ppermute(mine, "row", swap)
 
 
 def on_device(cell_coeffs, z_factor, noise_cols, q_bar, r_bar):
     quads, lattice, n, rank = z_factor.shape
     flat = quads * lattice * n
-    coeffs = cell_coeffs.reshape(12, n)
+    coeffs = cell_coeffs
+    core = (lax.axis_index("row") & 1).reshape(1)
     noise = noise_cols.reshape(flat, -1)
     bar = q_bar.reshape(flat, -1)
     shape = jax.ShapeDtypeStruct
@@ -316,21 +352,21 @@
     low, high = exchange(up_down[1], up_down[0])
     half = shape((flat, 128), bf16)
     full = shape((flat, 256), bf16)
-    block = shape((128, 128), f32)
-    tall = shape((256, 128), f32)
-    gnn, cross_n, nh, nl, qh, ql = call(
-        noise_products, (block, tall, half, half, full, full), 2 * flat * 128 * 128 * 11, 9 * 10**6
+    pack, nh, nl, qh, ql = call(
+        noise_products, (shape((136, 128), f32), half, half, full, full), 2 * flat * 128 * 128 * 11, 9 * 10**6
     )(noise, bar)
-    gzz, gzn, cross_z, xh, xl = call(
-        expand_products, (block, block, tall, half, half), 2 * flat * 128 * 128 * 11, 9 * 10**6,
-        [pltpu.VMEM(z_factor.shape, f32)],
-    )(coeffs, z_factor, low, high, nh, nl, qh, ql)
-    sums = sum_over_rows(jnp.concatenate([gzz, gzn, gnn, cross_z, cross_n], axis=0))
+    part = shape((264, 128), f32)
+    mine, other, xh, xl = call(
+        expand_products, (part, part, half, half), 2 * flat * 128 * 128 * 11, 9 * 10**6,
+        [pltpu.VMEM(z_factor.shape, f32), pltpu.VMEM((528, 128), f32)], scalar=True,
+    )(core, coeffs, z_factor, low, high, pack, nh, nl, qh, ql)
+    mine, other = sum_over_rows(mine, other)
     square = shape((256, 256), bf16)
     ih, il, sh, sl = call(
         factor, (square,) * 4, 10**9, 10**6,
-        [pltpu.VMEM((256, 512), f32), pltpu.VMEM((256, 256), f32), pltpu.VMEM((256, 256), f32)],
-    )(sums, r_bar)
+        [pltpu.VMEM((528, 128), f32), pltpu.VMEM((256, 512), f32), pltpu.VMEM((256, 256), f32), pltpu.VMEM((256, 256), f32)],
+        scalar=True,
+    )(core, mine, other, r_bar)
     rim = shape((4 * n, rank), f32)
     w, noise_grad, down, up = call(
         gradient, (shape(z_factor.shape, f32), shape(noise_cols.shape, f32), rim, rim),

time: 125 us -> 95.1 us (0.76)
  blocking collectives: 34.7 us -> 0 us
  Pallas kernels: 44.2 us -> 27.8 us
  waiting for transfers between devices: 29.2 us -> 44.9 us
  starting transfers between devices: 10.1 us -> 16.5 us
  local copies, waits for them, and re-layouts: 5.8 us -> 4.03 us
    all_to_all x2 -> x0, blocking collectives: 34.7 us -> none  [the longest x1 17.6 us: sum_over_rows(): parts = lax.all_to_all(x.reshape((count, -1) + x.shape[1:]), 'row', 0, 0)]
    pallas_call x6, Pallas kernels: 44.2 us -> 27.8 us  [run(): pl.pallas_call(kernel, out_shape=outs, in_specs=specs, scratch_shapes=lis...]
    ppermute x0 -> x5, waiting for transfers between devices: none -> 13.6 us  [the longest x3 11.3 us: sum_over_rows(): lax.ppermute(mine, 'row', [(i, i ^ 1 << turn[i & 1]) for i in range(count)])]
    ppermute x0 -> x5, starting transfers between devices: none -> 6.11 us  [the longest x1 3.53 us: sum_over_rows(): return (mine, lax.ppermute(mine, 'row', swap))]
    ppermute x2, waiting for transfers between devices: 26 us -> 27.7 us  [exchange(): low = lax.ppermute(up, 'row', forward)]
    reshape x1 -> x0, local copies, waits for them, and re-layouts: 1.35 us -> none  [on_device(): coeffs = cell_coeffs.reshape(12, n)]
    unnamed x16 -> x14, local copies, waits for them, and re-layouts: 4.41 us -> 4.03 us
  transfers between devices with their start and end apart: 4 -> 9, of which waited for: 4 -> 9; matrix products, arithmetic and copies ran while one was open for 0% -> 0% of each run, Pallas kernels for 4% -> 2%
where the time goes in v2:
time: 95.1 us; the launch traced here: 94 us
  waiting for transfers between devices  44.9 us (47%)
  Pallas kernels  27.8 us (29%)
  starting transfers between devices  16.5 us (17%)
  local copies, waits for them, and re-layouts  4.03 us (4%)
    pallas_call x6, Pallas kernels, run(): pl.pallas_call(kernel, out_shape=outs, in_specs=specs, scratch_shapes=lis...  27.8 us
    ppermute x2, waiting for transfers between devices, exchange(): low = lax.ppermute(up, 'row', forward)  27.7 us
    ppermute x3, waiting for transfers between devices, sum_over_rows(): lax.ppermute(mine, 'row', [(i, i ^ 1 << turn[i & 1]) for i in range(count)])  11.3 us
    ppermute x2, starting transfers between devices, exchange(): low = lax.ppermute(up, 'row', forward)  6.52 us
    unnamed x14, local copies, waits for them, and re-layouts  4.03 us
    ppermute x2, starting transfers between devices, exchange(): high = lax.ppermute(down, 'row', backward)  3.84 us
    ppermute x2, waiting for transfers between devices, exchange(): high = lax.ppermute(down, 'row', backward)  3.59 us
    ppermute x1, starting transfers between devices, sum_over_rows(): return (mine, lax.ppermute(mine, 'row', swap))  3.53 us
  transfers between devices with their start and end apart: 9, of which 9 were waited for; matrix products, arithmetic and copies ran while one was open for 0% of the time, Pallas kernels for 2%

profile of v2, /device:TPU:9, one launch (start us, length us, event | category | flops | bytes accessed | tf_op | source)
XLA Modules:
  0.0 94.0 jit_solution(3665147414564147234)
XLA Ops:
  0.6 0.0 copy-start
  0.6 1.4 %copy-done = f32[4,2,384,128]{3,2,1,0:T(8,128)S(1)} copy-done((f32[4,2,384,128]{3,2,1,0:T(8,128)S(1)}, f32[4,2,384,128]{3,2,1,0:T(8,128)}, u32[]{:S(2)}) %copy-start) | copy-done | bytes 1572888
  2.0 0.7 copy-done.4
  2.8 1.7 %shard_map.69 = (f32[1544,128]{1,0:T(8,128)}, f32[1544,128]{1,0:T(8,128)}) custom-call(f32[6,2,384]{2,1,0:T(2,128)S(1)} %copy-done.4, f32[4,2,384,128]{3,2,1,0:T(8,128)S(1)} %copy-done), custom_call_target="tpu_custom_call" | custom-call | flops 1000000 | bytes 2000000 | tf_op jit(solution)/shard_map/pallas_call | solution.py:22
  4.5 3.7 %collective-permute-start = (f32[1544,128]{1,0:T(8,128)}, f32[1544,128]{1,0:T(8,128)S(1)}, u32[]{:S(2)}, u32[]{:S(2)}) collective-permute-start(f32[1544,128]{1,0:T(8,128)} %get-tuple-element.23), channel_id=1, source_target_pairs={{0,1},{1,2},{2,3},{3,4},{4,5},{5,6},{6,7},{7,8},{8,9},{9,10},{10,1... | collective-permute-start | bytes 2371592 | tf_op jit(solution)/shard_map/ppermute | solution.py:326
  8.2 1.9 %collective-permute-start.1 = (f32[1544,128]{1,0:T(8,128)}, f32[1544,128]{1,0:T(8,128)S(1)}, u32[]{:S(2)}, u32[]{:S(2)}) collective-permute-start(f32[1544,128]{1,0:T(8,128)} %get-tuple-element.24), channel_id=1, source_target_pairs={{1,0},{2,1},{3,2},{4,3},{5,4},{6,5},{7,6},{8,7},{9,8},{10,9},{11,1... | collective-permute-start | bytes 2371592 | tf_op jit(solution)/shard_map/ppermute | solution.py:327
  10.1 0.0 copy-done.3
  10.1 0.0 copy-start.2
  10.2 1.9 %copy-done.2 = f32[4,2,384,256]{3,2,1,0:T(8,128)S(1)} copy-done((f32[4,2,384,256]{3,2,1,0:T(8,128)S(1)}, f32[4,2,384,256]{3,2,1,0:T(8,128)}, u32[]{:S(2)}) %copy-start.2) | copy-done | bytes 3145752
  12.0 1.7 %shard_map.68 = (f32[136,128]{1,0:T(8,128)S(1)}, bf16[3072,128]{1,0:T(8,128)(2,1)S(1)}, bf16[3072,128]{1,0:T(8,128)(2,1)S(1)}, bf16[3072,256]{1,0:T(8,128)(2,1)S(1)}, bf16[3072,256]{1,0:T(8,128)(2,1)S(1)}) custom-call(f32[3072,128]{1,0:T(8,128)S(1)} %bitcast.4, f32[3072,256]{1,0:T(8,128)S(1)} %bitcast.3), custom_call_target="tpu_custom_call" | custom-call | flops 1107296256 | bytes 9000000 | tf_op jit(solution)/shard_map/pallas_call | solution.py:22
  13.7 12.2 %collective-permute-done.low_ref.flow_ref = f32[1544,128]{1,0:T(8,128)S(1)} collective-permute-done((f32[1544,128]{1,0:T(8,128)}, f32[1544,128]{1,0:T(8,128)S(1)}, u32[]{:S(2)}, u32[]{:S(2)}) %collective-permute-start) | collective-permute-done | bytes 790560 | tf_op jit(solution)/shard_map/ppermute | solution.py:326
  25.9 1.5 %collective-permute-done.1.high_ref.fhigh_ref = f32[1544,128]{1,0:T(8,128)S(1)} collective-permute-done((f32[1544,128]{1,0:T(8,128)}, f32[1544,128]{1,0:T(8,128)S(1)}, u32[]{:S(2)}, u32[]{:S(2)}) %collective-permute-start.1) | collective-permute-done | bytes 790560 | tf_op jit(solution)/shard_map/ppermute | solution.py:327
  27.4 5.1 %shard_map.70 = (f32[264,128]{1,0:T(8,128)S(1)}, f32[264,128]{1,0:T(8,128)S(1)}, bf16[3072,128]{1,0:T(8,128)(2,1)S(1)}, bf16[3072,128]{1,0:T(8,128)(2,1)S(1)}) custom-call(s32[1]{0:T(128)} %bitcast.2.core_ref, f32[6,2,384]{2,1,0:T(2,128)S(1)} %copy-done.5, f32[4,2,384,128]{3,2,1,0:T(8,128)S(1)} %copy-done.1, ...), custom_call_target="tpu_custom_call" | custom-call | flops 1107296256 | bytes 9000000 | tf_op jit(solution)/shard_map/pallas_call | solution.py:22
  32.5 0.0 copy-start.6
  32.5 0.1 collective-permute-start.2
  32.6 1.3 %collective-permute-done.2 = f32[264,128]{1,0:T(8,128)S(1)} collective-permute-done((f32[264,128]{1,0:T(8,128)S(1)}, f32[264,128]{1,0:T(8,128)S(1)}, u32[]{:S(2)}, u32[]{:S(2)}) %collective-permute-start.2) | collective-permute-done | bytes 135200 | tf_op jit(solution)/shard_map/ppermute | solution.py:335
  34.0 0.1 collective-permute-start.3
  34.0 4.1 %collective-permute-done.3 = f32[264,128]{1,0:T(8,128)S(1)} collective-permute-done((f32[264,128]{1,0:T(8,128)S(1)}, f32[264,128]{1,0:T(8,128)S(1)}, u32[]{:S(2)}, u32[]{:S(2)}) %collective-permute-start.3) | collective-permute-done | bytes 135200 | tf_op jit(solution)/shard_map/ppermute | solution.py:338
  38.2 2.4 %collective-permute-start.4 = (f32[264,128]{1,0:T(8,128)S(1)}, f32[264,128]{1,0:T(8,128)S(1)}, u32[]{:S(2)}, u32[]{:S(2)}) collective-permute-start(f32[264,128]{1,0:T(8,128)S(1)} %add.13), channel_id=1, source_target_pairs={{0,4},{1,9},{2,6},{3,11},{4,0},{5,13},{6,2},{7,15},{8,12},{9,1},{1... | collective-permute-start | bytes 405512 | tf_op jit(solution)/shard_map/ppermute | solution.py:338
  40.6 3.3 %collective-permute-done.4 = f32[264,128]{1,0:T(8,128)S(1)} collective-permute-done((f32[264,128]{1,0:T(8,128)S(1)}, f32[264,128]{1,0:T(8,128)S(1)}, u32[]{:S(2)}, u32[]{:S(2)}) %collective-permute-start.4) | collective-permute-done | bytes 135200 | tf_op jit(solution)/shard_map/ppermute | solution.py:338
  43.9 0.1 collective-permute-start.5
  44.0 3.8 %collective-permute-done.5 = f32[264,128]{1,0:T(8,128)S(1)} collective-permute-done((f32[264,128]{1,0:T(8,128)S(1)}, f32[264,128]{1,0:T(8,128)S(1)}, u32[]{:S(2)}, u32[]{:S(2)}) %collective-permute-start.5) | collective-permute-done | bytes 135200 | tf_op jit(solution)/shard_map/ppermute | solution.py:338
  47.8 3.5 %collective-permute-start.6 = (f32[264,128]{1,0:T(8,128)S(1)}, f32[264,128]{1,0:T(8,128)S(1)}, u32[]{:S(2)}, u32[]{:S(2)}) collective-permute-start(f32[264,128]{1,0:T(8,128)S(1)} %add.15.mine_ref), channel_id=1, source_target_pairs={{0,1},{1,0},{2,3},{3,2},{4,5},{5,4},{6,7},{7,6},{8,9},{9,8},{10,11... | collective-permute-start | bytes 405512 | tf_op jit(solution)/shard_map/ppermute | solution.py:339
  51.4 1.0 %collective-permute-done.6.other_ref = f32[264,128]{1,0:T(8,128)S(1)} collective-permute-done((f32[264,128]{1,0:T(8,128)S(1)}, f32[264,128]{1,0:T(8,128)S(1)}, u32[]{:S(2)}, u32[]{:S(2)}) %collective-permute-start.6) | collective-permute-done | bytes 135200 | tf_op jit(solution)/shard_map/ppermute | solution.py:339
  52.4 0.0 copy-done.6
  52.4 11.7 %shard_map.71 = (bf16[256,256]{1,0:T(8,128)(2,1)S(1)}, bf16[256,256]{1,0:T(8,128)(2,1)S(1)}, bf16[256,256]{1,0:T(8,128)(2,1)S(1)}, bf16[256,256]{1,0:T(8,128)(2,1)S(1)}) custom-call(s32[1]{0:T(128)} %bitcast.2.core_ref, f32[264,128]{1,0:T(8,128)S(1)} %add.15.mine_ref, f32[264,128]{1,0:T(8,128)S(1)} %collective-permute-done.6.other_ref, f32[256,256]{1,0:T(8,128)S(1)} %copy-done.6), custom_call_target="tpu_custom_call" | custom-call | flops 1000000000 | bytes 1000000 | tf_op jit(solution)/shard_map/pallas_call | solution.py:22
  64.1 4.1 %shard_map.72 = (f32[4,2,384,128]{3,2,1,0:T(8,128)S(1)}, f32[4,2,384,128]{3,2,1,0:T(8,128)}, f32[1536,128]{1,0:T(8,128)S(1)}, f32[1536,128]{1,0:T(8,128)S(1)}) custom-call(f32[6,2,384]{2,1,0:T(2,128)S(1)} %copy-done.5, bf16[3072,256]{1,0:T(8,128)(2,1)S(1)} %get-tuple-element.21.qh_ref, bf16[3072,256]{1,0:T(8,128)(2,1)S(1)} %get-tuple-element.22.ql_ref, ...), custom_call_target="tpu_custom_call" | custom-call | flops 2415919104 | bytes 12000000 | tf_op jit(solution)/shard_map/pallas_call | solution.py:22
  68.2 2.8 %collective-permute-start.7 = (f32[1536,128]{1,0:T(8,128)S(1)}, f32[1536,128]{1,0:T(8,128)S(1)}, u32[]{:S(2)}, u32[]{:S(2)}) collective-permute-start(f32[1536,128]{1,0:T(8,128)S(1)} %get-tuple-element.37), channel_id=1, source_target_pairs={{0,1},{1,2},{2,3},{3,4},{4,5},{5,6},{6,7},{7,8},{8,9},{9,10},{10,1... | collective-permute-start | bytes 2359304 | tf_op jit(solution)/shard_map/ppermute | solution.py:326
  71.0 1.9 %collective-permute-start.8 = (f32[1536,128]{1,0:T(8,128)S(1)}, f32[1536,128]{1,0:T(8,128)S(1)}, u32[]{:S(2)}, u32[]{:S(2)}) collective-permute-start(f32[1536,128]{1,0:T(8,128)S(1)} %get-tuple-element.38), channel_id=1, source_target_pairs={{1,0},{2,1},{3,2},{4,3},{5,4},{6,5},{7,6},{8,7},{9,8},{10,9},{11,1... | collective-permute-start | bytes 2359304 | tf_op jit(solution)/shard_map/ppermute | solution.py:327
  72.9 15.4 %collective-permute-done.7.low_ref = f32[1536,128]{1,0:T(8,128)S(1)} collective-permute-done((f32[1536,128]{1,0:T(8,128)S(1)}, f32[1536,128]{1,0:T(8,128)S(1)}, u32[]{:S(2)}, u32[]{:S(2)}) %collective-permute-start.7) | collective-permute-done | bytes 786464 | tf_op jit(solution)/shard_map/ppermute | solution.py:326
  88.3 2.1 %collective-permute-done.8.high_ref = f32[1536,128]{1,0:T(8,128)S(1)} collective-permute-done((f32[1536,128]{1,0:T(8,128)S(1)}, f32[1536,128]{1,0:T(8,128)S(1)}, u32[]{:S(2)}, u32[]{:S(2)}) %collective-permute-start.8) | collective-permute-done | bytes 786464 | tf_op jit(solution)/shard_map/ppermute | solution.py:327
  90.5 3.6 %shard_map.73 = f32[4,2,384,128]{3,2,1,0:T(8,128)} custom-call(f32[6,2,384]{2,1,0:T(2,128)S(1)} %copy-done.5, f32[4,2,384,128]{3,2,1,0:T(8,128)S(1)} %get-tuple-element.36.w_ref, f32[1536,128]{1,0:T(8,128)S(1)} %collective-permute-done.7.low_ref, f32[1536,128]{1,0:T(8,128)S(1)} %collective-permute-done.8.high_ref, ...), custom_call_target="tpu_custom_call" | custom-call | flops 10000000 | bytes 6000000 | tf_op jit(solution)/shard_map/pallas_call | solution.py:22
  (10 shorter events, 0.1 us)
Async XLA Ops:
  0.6 1.4 %copy-start = (f32[4,2,384,128]{3,2,1,0:T(8,128)S(1)}, f32[4,2,384,128]{3,2,1,0:T(8,128)}, u32[]{:S(2)}) copy-start(f32[4,2,384,128]{3,2,1,0:T(8,128)} %z_ref.3) | copy-start | bytes 4718596
  2.0 0.7 copy-start.4
  2.8 7.4 %copy-start.3 = (f32[4,2,384,128]{3,2,1,0:T(8,128)S(1)}, f32[4,2,384,128]{3,2,1,0:T(8,128)}, u32[]{:S(2)}) copy-start(f32[4,2,384,128]{3,2,1,0:T(8,128)} %param.7) | copy-start | bytes 4718596
  4.5 21.4 %collective-permute-start = (f32[1544,128]{1,0:T(8,128)}, f32[1544,128]{1,0:T(8,128)S(1)}, u32[]{:S(2)}, u32[]{:S(2)}) collective-permute-start(f32[1544,128]{1,0:T(8,128)} %get-tuple-element.23), channel_id=1, source_target_pairs={{0,1},{1,2},{2,3},{3,4},{4,5},{5,6},{6,7},{7,8},{8,9},{9,10},{10,1... | collective-permute-start | bytes 2371592 | tf_op jit(solution)/shard_map/ppermute | solution.py:326
  8.2 19.2 %collective-permute-start.1 = (f32[1544,128]{1,0:T(8,128)}, f32[1544,128]{1,0:T(8,128)S(1)}, u32[]{:S(2)}, u32[]{:S(2)}) collective-permute-start(f32[1544,128]{1,0:T(8,128)} %get-tuple-element.24), channel_id=1, source_target_pairs={{1,0},{2,1},{3,2},{4,3},{5,4},{6,5},{7,6},{8,7},{9,8},{10,9},{11,1... | collective-permute-start | bytes 2371592 | tf_op jit(solution)/shard_map/ppermute | solution.py:327
  10.1 1.9 %copy-start.2 = (f32[4,2,384,256]{3,2,1,0:T(8,128)S(1)}, f32[4,2,384,256]{3,2,1,0:T(8,128)}, u32[]{:S(2)}) copy-start(f32[4,2,384,256]{3,2,1,0:T(8,128)} %param.8) | copy-start | bytes 9437188
  12.0 15.4 %copy-start.1 = (f32[4,2,384,128]{3,2,1,0:T(8,128)S(1)}, f32[4,2,384,128]{3,2,1,0:T(8,128)}, u32[]{:S(2)}) copy-start(f32[4,2,384,128]{3,2,1,0:T(8,128)} %z_ref.3) | copy-start | bytes 4718596
  12.0 15.4 %copy-start.5 = (f32[6,2,384]{2,1,0:T(2,128)S(1)}, f32[6,2,384]{2,1,0:T(2,128)}, u32[]{:S(2)}) copy-start(f32[6,2,384]{2,1,0:T(2,128)} %coeff_ref.7) | copy-start | bytes 55300
  32.5 19.8 %copy-start.6 = (f32[256,256]{1,0:T(8,128)S(1)}, f32[256,256]{1,0:T(8,128)}, u32[]{:S(2)}) copy-start(f32[256,256]{1,0:T(8,128)} %r_bar_ref.1) | copy-start | bytes 786436
  32.5 1.4 %collective-permute-start.2 = (f32[264,128]{1,0:T(8,128)S(1)}, f32[264,128]{1,0:T(8,128)S(1)}, u32[]{:S(2)}, u32[]{:S(2)}) collective-permute-start(f32[264,128]{1,0:T(8,128)S(1)} %get-tuple-element.31), channel_id=1, source_target_pairs={{0,1},{1,0},{2,3},{3,2},{4,5},{5,4},{6,7},{7,6},{8,9},{9,8},{10,11... | collective-permute-start | bytes 405512 | tf_op jit(solution)/shard_map/ppermute | solution.py:335
  34.0 4.2 %collective-permute-start.3 = (f32[264,128]{1,0:T(8,128)S(1)}, f32[264,128]{1,0:T(8,128)S(1)}, u32[]{:S(2)}, u32[]{:S(2)}) collective-permute-start(f32[264,128]{1,0:T(8,128)S(1)} %add.12), channel_id=1, source_target_pairs={{0,2},{1,5},{2,0},{3,7},{4,6},{5,1},{6,4},{7,3},{8,10},{9,13},{10,... | collective-permute-start | bytes 405512 | tf_op jit(solution)/shard_map/ppermute | solution.py:338
  38.2 5.7 %collective-permute-start.4 = (f32[264,128]{1,0:T(8,128)S(1)}, f32[264,128]{1,0:T(8,128)S(1)}, u32[]{:S(2)}, u32[]{:S(2)}) collective-permute-start(f32[264,128]{1,0:T(8,128)S(1)} %add.13), channel_id=1, source_target_pairs={{0,4},{1,9},{2,6},{3,11},{4,0},{5,13},{6,2},{7,15},{8,12},{9,1},{1... | collective-permute-start | bytes 405512 | tf_op jit(solution)/shard_map/ppermute | solution.py:338
  43.9 3.9 %collective-permute-start.5 = (f32[264,128]{1,0:T(8,128)S(1)}, f32[264,128]{1,0:T(8,128)S(1)}, u32[]{:S(2)}, u32[]{:S(2)}) collective-permute-start(f32[264,128]{1,0:T(8,128)S(1)} %add.14), channel_id=1, source_target_pairs={{0,8},{1,3},{2,10},{3,1},{4,12},{5,7},{6,14},{7,5},{8,0},{9,11},{1... | collective-permute-start | bytes 405512 | tf_op jit(solution)/shard_map/ppermute | solution.py:338
  47.8 4.5 %collective-permute-start.6 = (f32[264,128]{1,0:T(8,128)S(1)}, f32[264,128]{1,0:T(8,128)S(1)}, u32[]{:S(2)}, u32[]{:S(2)}) collective-permute-start(f32[264,128]{1,0:T(8,128)S(1)} %add.15.mine_ref), channel_id=1, source_target_pairs={{0,1},{1,0},{2,3},{3,2},{4,5},{5,4},{6,7},{7,6},{8,9},{9,8},{10,11... | collective-permute-start | bytes 405512 | tf_op jit(solution)/shard_map/ppermute | solution.py:339
  68.2 20.2 %collective-permute-start.7 = (f32[1536,128]{1,0:T(8,128)S(1)}, f32[1536,128]{1,0:T(8,128)S(1)}, u32[]{:S(2)}, u32[]{:S(2)}) collective-permute-start(f32[1536,128]{1,0:T(8,128)S(1)} %get-tuple-element.37), channel_id=1, source_target_pairs={{0,1},{1,2},{2,3},{3,4},{4,5},{5,6},{6,7},{7,8},{8,9},{9,10},{10,1... | collective-permute-start | bytes 2359304 | tf_op jit(solution)/shard_map/ppermute | solution.py:326
  71.0 19.5 %collective-permute-start.8 = (f32[1536,128]{1,0:T(8,128)S(1)}, f32[1536,128]{1,0:T(8,128)S(1)}, u32[]{:S(2)}, u32[]{:S(2)}) collective-permute-start(f32[1536,128]{1,0:T(8,128)S(1)} %get-tuple-element.38), channel_id=1, source_target_pairs={{1,0},{2,1},{3,2},{4,3},{5,4},{6,5},{7,6},{8,7},{9,8},{10,9},{11,1... | collective-permute-start | bytes 2359304 | tf_op jit(solution)/shard_map/ppermute | solution.py:327

commit v3 on v2

--- a/solution.py
+++ b/solution.py
@@ -11,20 +11,22 @@
 bf16 = jnp.bfloat16
 VMEM = pl.BlockSpec(memory_space=pltpu.VMEM)
 LIMIT = 24 * 1024 * 1024
+FAR_LIMIT = 63 * 1024 * 1024
 PANEL = 16
 
 
-def call(kernel, outs, flops, moved, scratch=(), scalar=False):
+def call(kernel, outs, flops, moved, scratch=(), scalar=False, far=False):
     def run(*args):
-        specs = [pl.BlockSpec() for _ in args]
+        specs = [pl.BlockSpec(memory_space=pltpu.HBM) if far else pl.BlockSpec() for _ in args]
         if scalar:
             specs[0] = pl.BlockSpec(memory_space=pltpu.SMEM)
         return pl.pallas_call(
             kernel,
             out_shape=outs,
             in_specs=specs,
+            **({"out_specs": (pl.BlockSpec(memory_space=pltpu.HBM),) * len(outs)} if far else {}),
             scratch_shapes=list(scratch),
-            compiler_params=pltpu.CompilerParams(vmem_limit_bytes=LIMIT),
+            compiler_params=pltpu.CompilerParams(vmem_limit_bytes=FAR_LIMIT if far else LIMIT),
             cost_estimate=pl.CostEstimate(flops=flops, bytes_accessed=moved, transcendentals=0),
         )(*args)
 
@@ -89,6 +91,16 @@
 def backward_heavy(c, pa, xb, pb):
     d, w, g, l, m, j = c
     return -2.0 * g * pa - w * pb, w * xb - 0.5 * m * pb
+
+
+def light_rows(z_ref, down_ref, up_ref, sems):
+    copies = [
+        pltpu.make_async_copy(z_ref.at[0:2, r], out, sems.at[r]) for r, out in ((0, down_ref), (1, up_ref))
+    ]
+    for copy in copies:
+        copy.start()
+    for copy in copies:
+        copy.wait()
 
 
 def forward_rim(coeff_ref, z_ref, down_ref, up_ref):
@@ -98,19 +110,15 @@
         xa, pa, xb = z_ref[0, r], z_ref[1, r], z_ref[2, r]
         hop_x = z_ref[0, 1 - r] + side(xa)
         hop_p = z_ref[1, 1 - r] + side(pa)
-        bx, bp = forward_light(c[r], xa, pa, xb, hop_x, hop_p)
-        out[0:n] = xa
-        out[n : 2 * n] = pa
-        out[2 * n : 3 * n] = bx
-        out[3 * n : 4 * n] = bp
+        out[0:n], out[n : 2 * n] = forward_light(c[r], xa, pa, xb, hop_x, hop_p)
         hopping = coeff_ref[5, r : r + 1, :] * rate_scales[5]
         pieces = [hopping[:, k * 128 : (k + 1) * 128] for k in range(n // 128)]
         pieces.append(jnp.zeros((8 - n // 128, 128), f32))
-        out[4 * n :] = jnp.concatenate(pieces, axis=0)
+        out[2 * n :] = jnp.concatenate(pieces, axis=0)
 
 
 def far_hopping(recv_ref, n):
-    tail = jnp.transpose(recv_ref[4 * n : 4 * n + 8])
+    tail = jnp.transpose(recv_ref[2 * n : 2 * n + 8])
     return jnp.concatenate([tail[:, k : k + 1] for k in range(n // 128)], axis=0)
 
 
@@ -121,59 +129,94 @@
     return jnp.where(row <= col, gram, cross), jnp.broadcast_to(diagonal, (8, gram.shape[1]))
 
 
-def noise_products(noise_ref, q_ref, pack_ref, nh_ref, nl_ref, qh_ref, ql_ref):
+def noise_products(noise_ref, q_ref, pack_ref, nh_ref, nl_ref, qh_ref, ql_ref, nht_ref, nlt_ref, qht_ref, qlt_ref):
     nh, nl = split2(noise_ref[...])
     qh, ql = split2(q_ref[...])
     nh_ref[...] = nh
     nl_ref[...] = nl
     qh_ref[...] = qh
     ql_ref[...] = ql
-    down = ((0,), (0,))
-    mixed = dot(nh, nl, down)
-    gram = dot(nh, nh, down) + mixed + jnp.transpose(mixed)
-    qh, ql = qh[:, 128:], ql[:, 128:]
-    cross = dot(qh, nh, down) + dot(qh, nl, down) + dot(ql, nh, down)
+    for value, out in ((nh, nht_ref), (nl, nlt_ref), (qh, qht_ref), (ql, qlt_ref)):
+        out[...] = jnp.transpose(value)
+    plain = ((1,), (0,))
+    high = dot(jnp.concatenate([nht_ref[...], qht_ref[128:]], axis=0), jnp.concatenate([nh, nl], axis=1), plain)
+    low = dot(qlt_ref[128:], nh, plain)
+    mixed = high[:128, 128:]
+    gram = high[:128, :128] + mixed + jnp.transpose(mixed)
+    cross = high[128:, :128] + high[128:, 128:] + low
     pack_ref[0:128], pack_ref[128:] = packed(gram, cross)
 
 
-def expand_products(
-    core_ref, coeff_ref, z_ref, low_ref, high_ref, pack_ref, nh_ref, nl_ref, qh_ref, ql_ref,
-    mine_ref, other_ref, xh_ref, xl_ref, first_ref, sums_ref,
+def row_products(xh, xl, nht, nlt, qht, qlt):
+    plain = ((1,), (0,))
+    left = jnp.concatenate([jnp.transpose(xh), nht, qht], axis=0)
+    high = dot(left, jnp.concatenate([xh, xl], axis=1), plain)
+    low = dot(jnp.concatenate([nlt, qlt], axis=0), xh, plain)
+    mixed = high[:128, 128:]
+    return (
+        high[:128, :128] + mixed + jnp.transpose(mixed),
+        high[128:, :128] + high[128:, 128:] + low,
+    )
+
+
+def expand_first(
+    coeff_ref, z_ref, low_ref, high_ref, nht_ref, nlt_ref, qht_ref, qlt_ref,
+    light_ref, xh_ref, xl_ref, gram_ref, rest_ref, first_ref,
 ):
     c = coefficients(coeff_ref)
     n = z_ref.shape[2]
-    jlow = far_hopping(low_ref, n)
-    jhigh = far_hopping(high_ref, n)
-    low = [low_ref[k * n : (k + 1) * n] for k in range(4)]
-    high = [high_ref[k * n : (k + 1) * n] for k in range(4)]
-    far = ((low, jlow), (high, jhigh))
+    far = (low_ref, high_ref)
     for r in range(2):
         xa, pa, xb, pb = (z_ref[k, r] for k in range(4))
-        hop_x = z_ref[0, 1 - r] + far[r][0][0] + side(xa)
-        hop_p = z_ref[1, 1 - r] + far[r][0][1] + side(pa)
+        hop_x = z_ref[0, 1 - r] + far[r][0] + side(xa)
+        hop_p = z_ref[1, 1 - r] + far[r][1] + side(pa)
         first_ref[0, r], first_ref[1, r] = forward_light(c[r], xa, pa, xb, hop_x, hop_p)
         first_ref[2, r], first_ref[3, r] = forward_heavy(c[r], xa, xb, pb)
     for r in range(2):
         xa, pa, xb, pb = (first_ref[k, r] for k in range(4))
-        beyond, jfar = far[r]
-        far_x = beyond[2] - jfar * z_ref[1, r]
-        far_p = beyond[3] + jfar * z_ref[0, r]
-        hop_x = first_ref[0, 1 - r] + far_x + side(xa)
-        hop_p = first_ref[1, 1 - r] + far_p + side(pa)
-        second = forward_light(c[r], xa, pa, xb, hop_x, hop_p) + forward_heavy(c[r], xa, xb, pb)
-        for k, (f, s) in enumerate(zip((xa, pa, xb, pb), second)):
+        for k, (f, s) in enumerate(zip((xb, pb), forward_heavy(c[r], xa, xb, pb))):
             start = (2 * k + r) * n
-            h, l = split2(z_ref[k, r] + f + 0.5 * s)
+            h, l = split2(z_ref[2 + k, r] + f + 0.5 * s)
             xh_ref[start : start + n] = h
             xl_ref[start : start + n] = l
-    down = ((0,), (0,))
-    xh, xl = xh_ref[...], xl_ref[...]
-    mixed = dot(xh, xl, down)
-    gram = dot(xh, xh, down) + mixed + jnp.transpose(mixed)
-    cross = dot(qh_ref[...], xh, down) + dot(qh_ref[...], xl, down) + dot(ql_ref[...], xh, down)
-    sums_ref[0:128], sums_ref[512:520] = packed(gram, cross[:128])
-    sums_ref[128:256] = dot(xh, nh_ref[...], down) + dot(xh, nl_ref[...], down) + dot(xl, nh_ref[...], down)
-    sums_ref[256:384] = cross[128:]
+    half = 4 * n
+    gram_ref[...], rest_ref[...] = row_products(
+        xh_ref[...], xl_ref[...], nht_ref[:, half:], nlt_ref[:, half:], qht_ref[:, half:], qlt_ref[:, half:]
+    )
+    for r in range(2):
+        xa, pa, xb, pb = (first_ref[k, r] for k in range(4))
+        hop_x = first_ref[0, 1 - r] + side(xa)
+        hop_p = first_ref[1, 1 - r] + side(pa)
+        second = forward_light(c[r], xa, pa, xb, hop_x, hop_p)
+        for k, (f, s) in enumerate(zip((xa, pa), second)):
+            light_ref[k, r] = z_ref[k, r] + f + 0.5 * s
+
+
+def expand_last(
+    core_ref, coeff_ref, z_ref, low_ref, high_ref, light_ref, gram_ref, rest_ref, pack_ref,
+    nht_ref, nlt_ref, qht_ref, qlt_ref, mine_ref, other_ref, xh_ref, xl_ref, sums_ref,
+):
+    c = coefficients(coeff_ref)
+    n = z_ref.shape[2]
+    for r, far in enumerate((low_ref, high_ref)):
+        jfar = far_hopping(far, n)
+        far_x = far[0:n] - jfar * z_ref[1, r]
+        far_p = far[n : 2 * n] + jfar * z_ref[0, r]
+        j = 0.5 * c[r][5]
+        for k, value in enumerate((light_ref[0, r] - j * far_p, light_ref[1, r] + j * far_x)):
+            start = (2 * k + r) * n
+            h, l = split2(value)
+            xh_ref[start : start + n] = h
+            xl_ref[start : start + n] = l
+    half = 4 * n
+    gram, rest = row_products(
+        xh_ref[...], xl_ref[...], nht_ref[:, :half], nlt_ref[:, :half], qht_ref[:, :half], qlt_ref[:, :half]
+    )
+    gram = gram + gram_ref[...]
+    rest = rest + rest_ref[...]
+    sums_ref[0:128], sums_ref[512:520] = packed(gram, rest[128:256])
+    sums_ref[128:256] = jnp.transpose(rest[:128])
+    sums_ref[256:384] = rest[256:]
     sums_ref[384:512] = pack_ref[0:128]
     sums_ref[520:528] = pack_ref[128:136]
     core = core_ref[0]
@@ -260,63 +303,101 @@
     sh_ref[...], sl_ref[...] = split2(spread)
 
 
-def gradient(
-    coeff_ref, qh_ref, ql_ref, xh_ref, xl_ref, nh_ref, nl_ref, ih_ref, il_ref, sh_ref, sl_ref,
-    w_ref, noise_ref, down_ref, up_ref,
-):
-    n = w_ref.shape[2]
+def columns(qh, ql, nh, nl, xh, xl, ih, il, sh, sl):
     plain = ((1,), (0,))
-    for k in range(4):
-        for r in range(2):
-            start = (2 * k + r) * n
-            here = slice(start, start + n)
-            qh, ql = qh_ref[here], ql_ref[here]
-            xh = jnp.concatenate([xh_ref[here], nh_ref[here]], axis=1)
-            xl = jnp.concatenate([xl_ref[here], nl_ref[here]], axis=1)
-            grad = (
-                dot(qh, ih_ref[...], plain) + dot(ql, ih_ref[...], plain) + dot(qh, il_ref[...], plain)
-                + dot(xh, sh_ref[...], plain) + dot(xl, sh_ref[...], plain) + dot(xh, sl_ref[...], plain)
-            )
-            w_ref[k, r] = grad[:, :128]
-            noise_ref[k, r] = grad[:, 128:]
-    c = coefficients(coeff_ref)
-    for r, out in ((0, down_ref), (1, up_ref)):
-        xa, pa, pb = w_ref[0, r], w_ref[1, r], w_ref[3, r]
-        j = c[r][5]
-        jother = c[1 - r][5]
-        jx, jp = j * xa, j * pa
-        hop_x = jother * w_ref[0, 1 - r] + side(jx)
-        hop_p = jother * w_ref[1, 1 - r] + side(jp)
-        bx, bp = backward_light(c[r], xa, pa, pb, hop_x, hop_p)
-        out[0:n] = jx
-        out[n : 2 * n] = jp
-        out[2 * n : 3 * n] = j * bx
-        out[3 * n : 4 * n] = j * bp
-
-
-def contract_back(coeff_ref, w_ref, low_ref, high_ref, flow_ref, fhigh_ref, out_ref, first_ref):
+    xh = jnp.concatenate([xh, nh], axis=1)
+    xl = jnp.concatenate([xl, nl], axis=1)
+    high = dot(qh, jnp.concatenate([ih, il], axis=1), plain) + dot(xh, jnp.concatenate([sh, sl], axis=1), plain)
+    return high[:, :128] + high[:, 128:] + dot(ql, ih, plain) + dot(xl, sh, plain)
+
+
+def gradient_light(
+    coeff_ref, qh_ref, ql_ref, nh_ref, nl_ref, xh_ref, xl_ref, ih_ref, il_ref, sh_ref, sl_ref,
+    w_ref, down_ref, up_ref,
+):
     c = coefficients(coeff_ref)
     n = w_ref.shape[2]
-    far = ((low_ref, far_hopping(flow_ref, n)), (high_ref, far_hopping(fhigh_ref, n)))
+    weights = [ref[:, :128] for ref in (ih_ref, il_ref, sh_ref, sl_ref)]
+    for k in range(2):
+        for r, out in ((0, down_ref), (1, up_ref)):
+            here = slice((2 * k + r) * n, (2 * k + r + 1) * n)
+            parts = [ref[here] for ref in (qh_ref, ql_ref, nh_ref, nl_ref, xh_ref, xl_ref)]
+            w = columns(*parts, *weights)
+            w_ref[k, r] = w
+            out[k] = c[r][5] * w
+
+
+def gradient_heavy(
+    coeff_ref, light_ref, jdown_ref, jup_ref, qh_ref, ql_ref, nh_ref, nl_ref, xh_ref, xl_ref,
+    ih_ref, il_ref, sh_ref, sl_ref, w_ref, down_ref, up_ref,
+):
+    c = coefficients(coeff_ref)
+    n = w_ref.shape[2]
+    weights = [ref[:, :128] for ref in (ih_ref, il_ref, sh_ref, sl_ref)]
+    half = 4 * n
+    for k in (1, 0):
+        for r in range(2):
+            here = slice((2 * k + r) * n, (2 * k + r + 1) * n)
+            there = slice(half + here.start, half + here.stop)
+            parts = [ref[there] for ref in (qh_ref, ql_ref, nh_ref, nl_ref)] + [xh_ref[here], xl_ref[here]]
+            w_ref[k, r] = columns(*parts, *weights)
+    hops = (jdown_ref, jup_ref)
+    for r, out in ((0, down_ref), (1, up_ref)):
+        j = c[r][5]
+        hop_x = hops[1 - r][0] + side(hops[r][0])
+        hop_p = hops[1 - r][1] + side(hops[r][1])
+        bx, bp = backward_light(c[r], light_ref[0, r], light_ref[1, r], w_ref[1, r], hop_x, hop_p)
+        out[0] = j * bx
+        out[1] = j * bp
+
+
+def gradient_noise(
+    qh_ref, ql_ref, nh_ref, nl_ref, xlight_h, xlight_l, xheavy_h, xheavy_l, ih_ref, il_ref, sh_ref, sl_ref, out_ref
+):
+    n = out_ref.shape[2]
+    weights = [ref[:, 128:] for ref in (ih_ref, il_ref, sh_ref, sl_ref)]
+    for k in range(4):
+        xh_ref, xl_ref = (xlight_h, xlight_l) if k < 2 else (xheavy_h, xheavy_l)
+        for r in range(2):
+            here = slice((2 * k + r) * n, (2 * k + r + 1) * n)
+            there = slice((2 * (k % 2) + r) * n, (2 * (k % 2) + r + 1) * n)
+            parts = [ref[here] for ref in (qh_ref, ql_ref, nh_ref, nl_ref)] + [xh_ref[there], xl_ref[there]]
+            out_ref[k, r] = columns(*parts, *weights)
+
+
+def contract_first(
+    coeff_ref, light_ref, heavy_ref, jdown_ref, jup_ref, low_ref, high_ref, flow_ref, fhigh_ref,
+    out_light_ref, out_heavy_ref, first_ref,
+):
+    c = coefficients(coeff_ref)
+    n = light_ref.shape[2]
+    hops = (jdown_ref, jup_ref)
+    far = (low_ref, high_ref)
     for r in range(2):
-        xa, pa, xb, pb = (w_ref[k, r] for k in range(4))
-        j, jother = c[r][5], c[1 - r][5]
-        beyond = far[r][0]
-        hop_x = jother * w_ref[0, 1 - r] + beyond[0:n] + side(j * xa)
-        hop_p = jother * w_ref[1, 1 - r] + beyond[n : 2 * n] + side(j * pa)
+        xa, pa, xb, pb = light_ref[0, r], light_ref[1, r], heavy_ref[0, r], heavy_ref[1, r]
+        hop_x = hops[1 - r][0] + far[r][0] + side(hops[r][0])
+        hop_p = hops[1 - r][1] + far[r][1] + side(hops[r][1])
         first_ref[0, r], first_ref[1, r] = backward_light(c[r], xa, pa, pb, hop_x, hop_p)
         first_ref[2, r], first_ref[3, r] = backward_heavy(c[r], pa, xb, pb)
-    for r in range(2):
+    for r, fref in enumerate((flow_ref, fhigh_ref)):
         xa, pa, xb, pb = (first_ref[k, r] for k in range(4))
+        jfar = far_hopping(fref, n)
         j, jother = c[r][5], c[1 - r][5]
-        beyond, jfar = far[r]
-        far_x = beyond[2 * n : 3 * n] + jfar * (j * w_ref[1, r])
-        far_p = beyond[3 * n : 4 * n] - jfar * (j * w_ref[0, r])
-        hop_x = jother * first_ref[0, 1 - r] + far_x + side(j * xa)
-        hop_p = jother * first_ref[1, 1 - r] + far_p + side(j * pa)
-        second = backward_light(c[r], xa, pa, pb, hop_x, hop_p) + backward_heavy(c[r], pa, xb, pb)
-        for k, (f, s) in enumerate(zip((xa, pa, xb, pb), second)):
-            out_ref[k, r] = w_ref[k, r] + f + 0.5 * s
+        hop_x = jother * first_ref[0, 1 - r] + jfar * hops[r][1] + side(j * xa)
+        hop_p = jother * first_ref[1, 1 - r] - jfar * hops[r][0] + side(j * pa)
+        light = backward_light(c[r], xa, pa, pb, hop_x, hop_p)
+        heavy = backward_heavy(c[r], pa, xb, pb)
+        for k in range(2):
+            out_light_ref[k, r] = light_ref[k, r] + first_ref[k, r] + 0.5 * light[k]
+            out_heavy_ref[k, r] = heavy_ref[k, r] + first_ref[2 + k, r] + 0.5 * heavy[k]
+
+
+def contract_last(light_ref, heavy_ref, low_ref, high_ref, out_ref):
+    for r, far in enumerate((low_ref, high_ref)):
+        out_ref[0, r] = light_ref[0, r] + 0.5 * far[1]
+        out_ref[1, r] = light_ref[1, r] - 0.5 * far[0]
+        out_ref[2, r] = heavy_ref[0, r]
+        out_ref[3, r] = heavy_ref[1, r]
 
 
 def exchange(up, down):
@@ -347,35 +428,62 @@
     noise = noise_cols.reshape(flat, -1)
     bar = q_bar.reshape(flat, -1)
     shape = jax.ShapeDtypeStruct
-    rim = shape((4 * n + 8, rank), f32)
-    up_down = call(forward_rim, (rim, rim), 10**6, 2 * 10**6)(coeffs, z_factor)
-    low, high = exchange(up_down[1], up_down[0])
-    half = shape((flat, 128), bf16)
-    full = shape((flat, 256), bf16)
-    pack, nh, nl, qh, ql = call(
-        noise_products, (shape((136, 128), f32), half, half, full, full), 2 * flat * 128 * 128 * 11, 9 * 10**6
+    hops = shape((2, n, rank), f32)
+    down, up = call(
+        light_rows, (hops, hops), 0, 2 * 10**6, [pltpu.SemaphoreType.DMA((2,))], far=True
+    )(z_factor)
+    low, high = exchange(up, down)
+    rim = shape((2 * n + 8, rank), f32)
+    down, up = call(forward_rim, (rim, rim), 10**6, 2 * 10**6)(coeffs, z_factor)
+    far_low, far_high = exchange(up, down)
+    wide, tall = shape((flat, 256), bf16), shape((flat, 128), bf16)
+    wide_t, tall_t = shape((256, flat), bf16), shape((128, flat), bf16)
+    work = 2 * flat * 128 * 128
+    pack, nh, nl, qh, ql, nht, nlt, qht, qlt = call(
+        noise_products, (shape((136, 128), f32), tall, tall, wide, wide, tall_t, tall_t, wide_t, wide_t),
+        work * 5, 9 * 10**6,
     )(noise, bar)
+    transposed = (nht, nlt, qht, qlt)
+    half = shape((flat // 2, 128), bf16)
+    pair = shape((2, lattice, n, rank), f32)
+    light, xh_heavy, xl_heavy, gram, rest = call(
+        expand_first, (pair, half, half, shape((128, 128), f32), shape((384, 128), f32)), work * 6, 9 * 10**6,
+        [pltpu.VMEM(z_factor.shape, f32)],
+    )(coeffs, z_factor, low, high, *transposed)
     part = shape((264, 128), f32)
-    mine, other, xh, xl = call(
-        expand_products, (part, part, half, half), 2 * flat * 128 * 128 * 11, 9 * 10**6,
-        [pltpu.VMEM(z_factor.shape, f32), pltpu.VMEM((528, 128), f32)], scalar=True,
-    )(core, coeffs, z_factor, low, high, pack, nh, nl, qh, ql)
+    mine, other, xh_light, xl_light = call(
+        expand_last, (part, part, half, half), work * 6, 9 * 10**6, [pltpu.VMEM((528, 128), f32)], scalar=True
+    )(core, coeffs, z_factor, far_low, far_high, light, gram, rest, pack, *transposed)
     mine, other = sum_over_rows(mine, other)
     square = shape((256, 256), bf16)
-    ih, il, sh, sl = call(
+    weights = call(
         factor, (square,) * 4, 10**9, 10**6,
-        [pltpu.VMEM((528, 128), f32), pltpu.VMEM((256, 512), f32), pltpu.VMEM((256, 256), f32), pltpu.VMEM((256, 256), f32)],
+        [
+            pltpu.VMEM((528, 128), f32),
+            pltpu.VMEM((256, 512), f32),
+            pltpu.VMEM((256, 256), f32),
+            pltpu.VMEM((256, 256), f32),
+        ],
         scalar=True,
     )(core, mine, other, r_bar)
-    rim = shape((4 * n, rank), f32)
-    w, noise_grad, down, up = call(
-        gradient, (shape(z_factor.shape, f32), shape(noise_cols.shape, f32), rim, rim),
-        2 * flat * 256 * 256 * 6, 12 * 10**6,
-    )(coeffs, qh, ql, xh, xl, nh, nl, ih, il, sh, sl)
-    back_low, back_high = exchange(up, down)
-    z_grad = call(
-        contract_back, shape(z_factor.shape, f32), 10**7, 6 * 10**6, [pltpu.VMEM(z_factor.shape, f32)]
-    )(coeffs, w, back_low, back_high, low, high)
+    left = (qh, ql, nh, nl)
+    w_light, jdown, jup = call(gradient_light, (pair, hops, hops), work * 6, 6 * 10**6)(
+        coeffs, *left, xh_light, xl_light, *weights
+    )
+    low, high = exchange(jup, jdown)
+    w_heavy, down, up = call(gradient_heavy, (pair, hops, hops), work * 6, 6 * 10**6)(
+        coeffs, w_light, jdown, jup, *left, xh_heavy, xl_heavy, *weights
+    )
+    last_low, last_high = exchange(up, down)
+    noise_grad = call(gradient_noise, shape(noise_cols.shape, f32), work * 12, 9 * 10**6)(
+        *left, xh_light, xl_light, xh_heavy, xl_heavy, *weights
+    )
+    out_light, out_heavy = call(contract_first, (pair, pair), 10**7, 6 * 10**6, [pltpu.VMEM(z_factor.shape, f32)])(
+        coeffs, w_light, w_heavy, jdown, jup, low, high, far_low, far_high
+    )
+    z_grad = call(contract_last, shape(z_factor.shape, f32), 10**6, 6 * 10**6)(
+        out_light, out_heavy, last_low, last_high
+    )
     return z_grad, noise_grad
 
 

time: 95.1 us -> 108 us (1.14)
  Pallas kernels: 27.8 us -> 53.3 us
  waiting for transfers between devices: 44.9 us -> 22.1 us
  starting transfers between devices: 16.5 us -> 27.2 us
    ppermute x2 -> x4, waiting for transfers between devices: 27.7 us -> 1.76 us  [exchange(): low = lax.ppermute(up, 'row', forward)]
    pallas_call x6 -> x11, Pallas kernels: 27.8 us -> 53.3 us  [run(): pl.pallas_call(kernel, out_shape=outs, in_specs=specs, **{'out_specs': (p...]
    ppermute x2 -> x4, starting transfers between devices: 6.52 us -> 12.5 us  [exchange(): low = lax.ppermute(up, 'row', forward)]
    ppermute x2 -> x4, starting transfers between devices: 3.84 us -> 8.52 us  [exchange(): high = lax.ppermute(down, 'row', backward)]
    ppermute x2 -> x4, waiting for transfers between devices: 3.59 us -> 6.71 us  [exchange(): high = lax.ppermute(down, 'row', backward)]
    unnamed x14 -> x12, local copies, waits for them, and re-layouts: 4.03 us -> 3.31 us
  transfers between devices with their start and end apart: 9 -> 13, of which waited for: 9 -> 9; matrix products, arithmetic and copies ran while one was open for 0% -> 0% of each run, Pallas kernels for 2% -> 12%
where the time goes in v3:
time: 108 us; the launch traced here: 107 us
  Pallas kernels  53.3 us (49%)
  starting transfers between devices  27.2 us (25%)
  waiting for transfers between devices  22.1 us (20%)
  local copies, waits for them, and re-layouts  3.31 us (3%)
    pallas_call x11, Pallas kernels, run(): pl.pallas_call(kernel, out_shape=outs, in_specs=specs, **{'out_specs': (p...  53.3 us
    ppermute x4, starting transfers between devices, exchange(): low = lax.ppermute(up, 'row', forward)  12.5 us
    ppermute x3, waiting for transfers between devices, sum_over_rows(): lax.ppermute(mine, 'row', [(i, i ^ 1 << turn[i & 1]) for i in range(count)])  11.3 us
    ppermute x4, starting transfers between devices, exchange(): high = lax.ppermute(down, 'row', backward)  8.52 us
    ppermute x4, waiting for transfers between devices, exchange(): high = lax.ppermute(down, 'row', backward)  6.71 us
    ppermute x1, starting transfers between devices, sum_over_rows(): return (mine, lax.ppermute(mine, 'row', swap))  3.53 us
    unnamed x12, local copies, waits for them, and re-layouts  3.31 us
    ppermute x3, starting transfers between devices, sum_over_rows(): lax.ppermute(mine, 'row', [(i, i ^ 1 << turn[i & 1]) for i in range(count)])  2.52 us
  transfers between devices with their start and end apart: 13, of which 9 were waited for; matrix products, arithmetic and copies ran while one was open for 0% of the time, Pallas kernels for 12%

profile of v3, /device:TPU:9, one launch (start us, length us, event | category | flops | bytes accessed | tf_op | source)
XLA Modules:
  0.0 106.9 jit_solution(3427955474720994213)
XLA Ops:
  0.6 24.9 %shard_map.70 = (f32[2,384,128]{2,1,0:T(8,128)}, f32[2,384,128]{2,1,0:T(8,128)}) custom-call(f32[4,2,384,128]{3,2,1,0:T(8,128)} %z_ref.7), custom_call_target="tpu_custom_call" | custom-call | bytes 2000000 | tf_op jit(solution)/shard_map/pallas_call | solution.py:23
  25.6 3.7 %collective-permute-start.2 = (f32[2,384,128]{2,1,0:T(8,128)}, f32[2,384,128]{2,1,0:T(8,128)S(1)}, u32[]{:S(2)}, u32[]{:S(2)}) collective-permute-start(f32[2,384,128]{2,1,0:T(8,128)} %get-tuple-element.42), channel_id=1, source_target_pairs={{0,1},{1,2},{2,3},{3,4},{4,5},{5,6},{6,7},{7,8},{8,9},{9,10},{10,1... | collective-permute-start | bytes 1179656 | tf_op jit(solution)/shard_map/ppermute | solution.py:407
  29.3 1.9 %collective-permute-start.3 = (f32[2,384,128]{2,1,0:T(8,128)}, f32[2,384,128]{2,1,0:T(8,128)S(1)}, u32[]{:S(2)}, u32[]{:S(2)}) collective-permute-start(f32[2,384,128]{2,1,0:T(8,128)} %get-tuple-element.43), channel_id=1, source_target_pairs={{1,0},{2,1},{3,2},{4,3},{5,4},{6,5},{7,6},{8,7},{9,8},{10,9},{11,1... | collective-permute-start | bytes 1179656 | tf_op jit(solution)/shard_map/ppermute | solution.py:408
  31.3 1.4 %copy-done = f32[4,2,384,128]{3,2,1,0:T(8,128)S(1)} copy-done((f32[4,2,384,128]{3,2,1,0:T(8,128)S(1)}, f32[4,2,384,128]{3,2,1,0:T(8,128)}, u32[]{:S(2)}) %copy-start) | copy-done | bytes 1572888
  32.7 1.6 %shard_map.69 = (f32[776,128]{1,0:T(8,128)}, f32[776,128]{1,0:T(8,128)}) custom-call(f32[6,2,384]{2,1,0:T(2,128)S(1)} %copy-done.4, f32[4,2,384,128]{3,2,1,0:T(8,128)S(1)} %copy-done), custom_call_target="tpu_custom_call" | custom-call | flops 1000000 | bytes 2000000 | tf_op jit(solution)/shard_map/pallas_call | solution.py:23
  34.3 3.6 %collective-permute-start = (f32[776,128]{1,0:T(8,128)}, f32[776,128]{1,0:T(8,128)S(1)}, u32[]{:S(2)}, u32[]{:S(2)}) collective-permute-start(f32[776,128]{1,0:T(8,128)} %get-tuple-element.40), channel_id=1, source_target_pairs={{0,1},{1,2},{2,3},{3,4},{4,5},{5,6},{6,7},{7,8},{8,9},{9,10},{10,1... | collective-permute-start | bytes 1191944 | tf_op jit(solution)/shard_map/ppermute | solution.py:407
  37.9 1.9 %collective-permute-start.1 = (f32[776,128]{1,0:T(8,128)}, f32[776,128]{1,0:T(8,128)S(1)}, u32[]{:S(2)}, u32[]{:S(2)}) collective-permute-start(f32[776,128]{1,0:T(8,128)} %get-tuple-element.41), channel_id=1, source_target_pairs={{1,0},{2,1},{3,2},{4,3},{5,4},{6,5},{7,6},{8,7},{9,8},{10,9},{11,1... | collective-permute-start | bytes 1191944 | tf_op jit(solution)/shard_map/ppermute | solution.py:408
  39.9 1.9 %copy-done.2 = f32[4,2,384,256]{3,2,1,0:T(8,128)S(1)} copy-done((f32[4,2,384,256]{3,2,1,0:T(8,128)S(1)}, f32[4,2,384,256]{3,2,1,0:T(8,128)}, u32[]{:S(2)}) %copy-start.2) | copy-done | bytes 3145752
  41.7 1.8 %shard_map.68 = (f32[136,128]{1,0:T(8,128)S(1)}, bf16[3072,128]{1,0:T(8,128)(2,1)S(1)}, bf16[3072,128]{1,0:T(8,128)(2,1)S(1)}, bf16[3072,256]{1,0:T(8,128)(2,1)S...) custom-call(f32[3072,128]{1,0:T(8,128)S(1)} %bitcast.4, ...), custom_call_target="tpu_custom_call" | custom-call | flops 503316480 | bytes 9000000 | tf_op jit(solution)/shard_map/pallas_call | solution.py:23
  43.6 2.7 %shard_map.71 = (f32[2,2,384,128]{3,2,1,0:T(8,128)S(1)}, bf16[1536,128]{1,0:T(8,128)(2,1)S(1)}, bf16[1536,128]{1,0:T(8,128)(2,1)S(1)}, f32[128,128]{1,0:T(8,128)S(1)}, f32[384,128]{1,0:T(8,128)S(1)}) custom-call(f32[6,2,384]{2,1,0:T(2,128)S(1)} %copy-done.4, f32[4,2,384,128]{3,2,1,0:T(8,128)S(1)} %copy-done.1, ...), custom_call_target="tpu_custom_call" | custom-call | flops 603979776 | bytes 9000000 | tf_op jit(solution)/shard_map/pallas_call | solution.py:23
  46.3 3.3 %collective-permute-done.1.high_ref.fhigh_ref = f32[776,128]{1,0:T(8,128)S(1)} collective-permute-done((f32[776,128]{1,0:T(8,128)}, f32[776,128]{1,0:T(8,128)S(1)}, u32[]{:S(2)}, u32[]{:S(2)}) %collective-permute-start.1) | collective-permute-done | bytes 397344 | tf_op jit(solution)/shard_map/ppermute | solution.py:408
  49.6 1.5 %shard_map.72 = (f32[264,128]{1,0:T(8,128)S(1)}, f32[264,128]{1,0:T(8,128)S(1)}, bf16[1536,128]{1,0:T(8,128)(2,1)S(1)}, bf16[1536,128]{1,0:T(8,128)(2,1)S(1)}) custom-call(s32[1]{0:T(128)} %bitcast.2.core_ref, f32[6,2,384]{2,1,0:T(2,128)S(1)} %copy-done.4, f32[4,2,384,128]{3,2,1,0:T(8,128)S(1)} %copy-done.1, ...), custom_call_target="tpu_custom_call" | custom-call | flops 603979776 | bytes 9000000 | tf_op jit(solution)/shard_map/pallas_call | solution.py:23
  51.2 1.3 %collective-permute-done.4 = f32[264,128]{1,0:T(8,128)S(1)} collective-permute-done((f32[264,128]{1,0:T(8,128)S(1)}, f32[264,128]{1,0:T(8,128)S(1)}, u32[]{:S(2)}, u32[]{:S(2)}) %collective-permute-start.4) | collective-permute-done | bytes 135200 | tf_op jit(solution)/shard_map/ppermute | solution.py:416
  52.7 4.1 %collective-permute-done.5 = f32[264,128]{1,0:T(8,128)S(1)} collective-permute-done((f32[264,128]{1,0:T(8,128)S(1)}, f32[264,128]{1,0:T(8,128)S(1)}, u32[]{:S(2)}, u32[]{:S(2)}) %collective-permute-start.5) | collective-permute-done | bytes 135200 | tf_op jit(solution)/shard_map/ppermute | solution.py:419
  56.8 2.4 %collective-permute-start.6 = (f32[264,128]{1,0:T(8,128)S(1)}, f32[264,128]{1,0:T(8,128)S(1)}, u32[]{:S(2)}, u32[]{:S(2)}) collective-permute-start(f32[264,128]{1,0:T(8,128)S(1)} %add.13), channel_id=1, source_target_pairs={{0,4},{1,9},{2,6},{3,11},{4,0},{5,13},{6,2},{7,15},{8,12},{9,1},{1... | collective-permute-start | bytes 405512 | tf_op jit(solution)/shard_map/ppermute | solution.py:419
  59.2 3.3 %collective-permute-done.6 = f32[264,128]{1,0:T(8,128)S(1)} collective-permute-done((f32[264,128]{1,0:T(8,128)S(1)}, f32[264,128]{1,0:T(8,128)S(1)}, u32[]{:S(2)}, u32[]{:S(2)}) %collective-permute-start.6) | collective-permute-done | bytes 135200 | tf_op jit(solution)/shard_map/ppermute | solution.py:419
  62.6 3.8 %collective-permute-done.7 = f32[264,128]{1,0:T(8,128)S(1)} collective-permute-done((f32[264,128]{1,0:T(8,128)S(1)}, f32[264,128]{1,0:T(8,128)S(1)}, u32[]{:S(2)}, u32[]{:S(2)}) %collective-permute-start.7) | collective-permute-done | bytes 135200 | tf_op jit(solution)/shard_map/ppermute | solution.py:419
  66.5 3.5 %collective-permute-start.8 = (f32[264,128]{1,0:T(8,128)S(1)}, f32[264,128]{1,0:T(8,128)S(1)}, u32[]{:S(2)}, u32[]{:S(2)}) collective-permute-start(f32[264,128]{1,0:T(8,128)S(1)} %add.15.mine_ref), channel_id=1, source_target_pairs={{0,1},{1,0},{2,3},{3,2},{4,5},{5,4},{6,7},{7,6},{8,9},{9,8},{10,11... | collective-permute-start | bytes 405512 | tf_op jit(solution)/shard_map/ppermute | solution.py:420
  70.0 1.0 collective-permute-done.8.other_ref
  71.0 11.7 %shard_map.73 = (bf16[256,256]{1,0:T(8,128)(2,1)S(1)}, bf16[256,256]{1,0:T(8,128)(2,1)S(1)}, bf16[256,256]{1,0:T(8,128)(2,1)S(1)}, bf16[256,256]{1,0:T(8,128)(2,1)S(1)}) custom-call(s32[1]{0:T(128)} %bitcast.2.core_ref, f32[264,128]{1,0:T(8,128)S(1)} %add.15.mine_ref, f32[264,128]{1,0:T(8,128)S(1)} %collective-permute-done.8.other_ref, f32[256,256]{1,0:T(8,128)S(1)} %copy-done.5), custom_call_target="tpu_custom_call" | custom-call | flops 1000000000 | bytes 1000000 | tf_op jit(solution)/shard_map/pallas_call | solution.py:23
  82.7 1.1 %shard_map.74 = (f32[2,2,384,128]{3,2,1,0:T(8,128)S(1)}, f32[2,384,128]{2,1,0:T(8,128)S(1)}, f32[2,384,128]{2,1,0:T(8,128)S(1)}) custom-call(f32[6,2,384]{2,1,0:T(2,128)S(1)} %copy-done.4, bf16[3072,256]{1,0:T(8,128)(2,1)S(1)} %get-tuple-element.36.qh_ref, bf16[3072,256]{1,0:T(8,128)(2,1)S(1)} %get-tuple-element.37.ql_ref, ...), custom_call_target="tpu_custom_call" | custom-call | flops 603979776 | bytes 6000000 | tf_op jit(solution)/shard_map/pallas_call | solution.py:23
  83.8 2.3 %collective-permute-start.10 = (f32[2,384,128]{2,1,0:T(8,128)S(1)}, f32[2,384,128]{2,1,0:T(8,128)S(1)}, u32[]{:S(2)}, u32[]{:S(2)}) collective-permute-start(f32[2,384,128]{2,1,0:T(8,128)S(1)} %get-tuple-element.61.jdown_ref), channel_id=1, source_target_pairs={{1,0},{2,1},{3,2},{4,3},{5,4},{6,5},{7,6},{8,7},{9,8},{10,9},{11,1... | collective-permute-start | bytes 1179656 | tf_op jit(solution)/shard_map/ppermute | solution.py:408
  86.1 3.3 %collective-permute-start.9 = (f32[2,384,128]{2,1,0:T(8,128)S(1)}, f32[2,384,128]{2,1,0:T(8,128)S(1)}, u32[]{:S(2)}, u32[]{:S(2)}) collective-permute-start(f32[2,384,128]{2,1,0:T(8,128)S(1)} %get-tuple-element.62.jup_ref), channel_id=1, source_target_pairs={{0,1},{1,2},{2,3},{3,4},{4,5},{5,6},{6,7},{7,8},{8,9},{9,10},{10,1... | collective-permute-start | bytes 1179656 | tf_op jit(solution)/shard_map/ppermute | solution.py:407
  89.4 1.4 %shard_map.75 = (f32[2,2,384,128]{3,2,1,0:T(8,128)S(1)}, f32[2,384,128]{2,1,0:T(8,128)S(1)}, f32[2,384,128]{2,1,0:T(8,128)S(1)}) custom-call(f32[6,2,384]{2,1,0:T(2,128)S(1)} %copy-done.4, f32[2,2,384,128]{3,2,1,0:T(8,128)S(1)} %get-tuple-element.60.light_ref, f32[2,384,128]{2,1,0:T(8,128)S(1)} %get-tuple-element.61.jdown_ref, ...), custom_call_target="tpu_custom_call" | custom-call | flops 603979776 | bytes 6000000 | tf_op jit(solution)/shard_map/pallas_call | solution.py:23
  90.8 1.9 %collective-permute-start.11 = (f32[2,384,128]{2,1,0:T(8,128)S(1)}, f32[2,384,128]{2,1,0:T(8,128)S(1)}, u32[]{:S(2)}, u32[]{:S(2)}) collective-permute-start(f32[2,384,128]{2,1,0:T(8,128)S(1)} %get-tuple-element.68), channel_id=1, source_target_pairs={{0,1},{1,2},{2,3},{3,4},{4,5},{5,6},{6,7},{7,8},{8,9},{9,10},{10,1... | collective-permute-start | bytes 1179656 | tf_op jit(solution)/shard_map/ppermute | solution.py:407
  92.8 2.4 %collective-permute-start.12 = (f32[2,384,128]{2,1,0:T(8,128)S(1)}, f32[2,384,128]{2,1,0:T(8,128)S(1)}, u32[]{:S(2)}, u32[]{:S(2)}) collective-permute-start(f32[2,384,128]{2,1,0:T(8,128)S(1)} %get-tuple-element.69), channel_id=1, source_target_pairs={{1,0},{2,1},{3,2},{4,3},{5,4},{6,5},{7,6},{8,7},{9,8},{10,9},{11,1... | collective-permute-start | bytes 1179656 | tf_op jit(solution)/shard_map/ppermute | solution.py:408
  95.2 3.0 %shard_map.78 = f32[4,2,384,128]{3,2,1,0:T(8,128)} custom-call(bf16[3072,256]{1,0:T(8,128)(2,1)S(1)} %get-tuple-element.36.qh_ref, bf16[3072,256]{1,0:T(8,128)(2,1)S(1)} %get-tuple-element.37.ql_ref, bf16[3072,128]{1,0:T(8,128)(2,1)S(1)} %get-tuple-element.38.nh_ref, bf16[3072,128]{1,0:T(8,128)(2,1)S(1)} %get-tuple-element.39.nl_ref, ...), custom_call_target="tpu_custom_call" | custom-call | flops 1207959552 | bytes 9000000 | tf_op jit(solution)/shard_map/pallas_call | solution.py:23
  98.2 3.1 %collective-permute-done.10.high_ref = f32[2,384,128]{2,1,0:T(8,128)S(1)} collective-permute-done((f32[2,384,128]{2,1,0:T(8,128)S(1)}, f32[2,384,128]{2,1,0:T(8,128)S(1)}, u32[]{:S(2)}, u32[]{:S(2)}) %collective-permute-start.10) | collective-permute-done | bytes 393248 | tf_op jit(solution)/shard_map/ppermute | solution.py:408
  101.3 2.2 %shard_map.76 = (f32[2,2,384,128]{3,2,1,0:T(8,128)S(1)}, f32[2,2,384,128]{3,2,1,0:T(8,128)S(1)}) custom-call(f32[6,2,384]{2,1,0:T(2,128)S(1)} %copy-done.4, f32[2,2,384,128]{3,2,1,0:T(8,128)S(1)} %get-tuple-element.60.light_ref, f32[2,2,384,128]{3,2,1,0:T(8,128)S(1)} %get-tuple-element.65.heavy_ref, f32[2,384,128]{2,1,0:T(8,128)S(1)} %get-tuple-element.61.jdown_ref, ...), custom_call_target="tpu_custom_call" | custom-call | flops 10000000 | bytes 6000000 | tf_op jit(solution)/shard_map/pallas_call | solution.py:23
  103.5 1.8 %collective-permute-done.11.low_ref = f32[2,384,128]{2,1,0:T(8,128)S(1)} collective-permute-done((f32[2,384,128]{2,1,0:T(8,128)S(1)}, f32[2,384,128]{2,1,0:T(8,128)S(1)}, u32[]{:S(2)}, u32[]{:S(2)}) %collective-permute-start.11) | collective-permute-done | bytes 393248 | tf_op jit(solution)/shard_map/ppermute | solution.py:407
  105.3 0.3 collective-permute-done.12.high_ref
  105.6 1.3 %shard_map.77 = f32[4,2,384,128]{3,2,1,0:T(8,128)} custom-call(f32[2,2,384,128]{3,2,1,0:T(8,128)S(1)} %get-tuple-element.66.light_ref, f32[2,2,384,128]{3,2,1,0:T(8,128)S(1)} %get-tuple-element.67.heavy_ref, f32[2,384,128]{2,1,0:T(8,128)S(1)} %collective-permute-done.11.low_ref, f32[2,384,128]{2,1,0:T(8,128)S(1)} %collective-permute-done.12.high_ref), custom_call_target="tpu_custom_call" | custom-call | flops 1000000 | bytes 6000000 | tf_op jit(solution)/shard_map/pallas_call | solution.py:23
  (21 shorter events, 0.3 us)
Async XLA Ops:
  0.6 30.6 %copy-start.4 = (f32[6,2,384]{2,1,0:T(2,128)S(1)}, f32[6,2,384]{2,1,0:T(2,128)}, u32[]{:S(2)}) copy-start(f32[6,2,384]{2,1,0:T(2,128)} %coeff_ref.11) | copy-start | bytes 55300
  25.6 18.0 %collective-permute-start.2 = (f32[2,384,128]{2,1,0:T(8,128)}, f32[2,384,128]{2,1,0:T(8,128)S(1)}, u32[]{:S(2)}, u32[]{:S(2)}) collective-permute-start(f32[2,384,128]{2,1,0:T(8,128)} %get-tuple-element.42), channel_id=1, source_target_pairs={{0,1},{1,2},{2,3},{3,4},{4,5},{5,6},{6,7},{7,8},{8,9},{9,10},{10,1... | collective-permute-start | bytes 1179656 | tf_op jit(solution)/shard_map/ppermute | solution.py:407
  29.3 14.2 %collective-permute-start.3 = (f32[2,384,128]{2,1,0:T(8,128)}, f32[2,384,128]{2,1,0:T(8,128)S(1)}, u32[]{:S(2)}, u32[]{:S(2)}) collective-permute-start(f32[2,384,128]{2,1,0:T(8,128)} %get-tuple-element.43), channel_id=1, source_target_pairs={{1,0},{2,1},{3,2},{4,3},{5,4},{6,5},{7,6},{8,7},{9,8},{10,9},{11,1... | collective-permute-start | bytes 1179656 | tf_op jit(solution)/shard_map/ppermute | solution.py:408
  31.2 1.4 %copy-start = (f32[4,2,384,128]{3,2,1,0:T(8,128)S(1)}, f32[4,2,384,128]{3,2,1,0:T(8,128)}, u32[]{:S(2)}) copy-start(f32[4,2,384,128]{3,2,1,0:T(8,128)} %z_ref.7) | copy-start | bytes 4718596
  32.7 7.2 %copy-start.3 = (f32[4,2,384,128]{3,2,1,0:T(8,128)S(1)}, f32[4,2,384,128]{3,2,1,0:T(8,128)}, u32[]{:S(2)}) copy-start(f32[4,2,384,128]{3,2,1,0:T(8,128)} %param.7) | copy-start | bytes 4718596
  34.3 12.0 %collective-permute-start = (f32[776,128]{1,0:T(8,128)}, f32[776,128]{1,0:T(8,128)S(1)}, u32[]{:S(2)}, u32[]{:S(2)}) collective-permute-start(f32[776,128]{1,0:T(8,128)} %get-tuple-element.40), channel_id=1, source_target_pairs={{0,1},{1,2},{2,3},{3,4},{4,5},{5,6},{6,7},{7,8},{8,9},{9,10},{10,1... | collective-permute-start | bytes 1191944 | tf_op jit(solution)/shard_map/ppermute | solution.py:407
  37.9 11.7 %collective-permute-start.1 = (f32[776,128]{1,0:T(8,128)}, f32[776,128]{1,0:T(8,128)S(1)}, u32[]{:S(2)}, u32[]{:S(2)}) collective-permute-start(f32[776,128]{1,0:T(8,128)} %get-tuple-element.41), channel_id=1, source_target_pairs={{1,0},{2,1},{3,2},{4,3},{5,4},{6,5},{7,6},{8,7},{9,8},{10,9},{11,1... | collective-permute-start | bytes 1191944 | tf_op jit(solution)/shard_map/ppermute | solution.py:408
  39.9 1.9 %copy-start.2 = (f32[4,2,384,256]{3,2,1,0:T(8,128)S(1)}, f32[4,2,384,256]{3,2,1,0:T(8,128)}, u32[]{:S(2)}) copy-start(f32[4,2,384,256]{3,2,1,0:T(8,128)} %param.8) | copy-start | bytes 9437188
  41.7 1.8 %copy-start.1 = (f32[4,2,384,128]{3,2,1,0:T(8,128)S(1)}, f32[4,2,384,128]{3,2,1,0:T(8,128)}, u32[]{:S(2)}) copy-start(f32[4,2,384,128]{3,2,1,0:T(8,128)} %z_ref.7) | copy-start | bytes 4718596
  51.1 19.9 %copy-start.5 = (f32[256,256]{1,0:T(8,128)S(1)}, f32[256,256]{1,0:T(8,128)}, u32[]{:S(2)}) copy-start(f32[256,256]{1,0:T(8,128)} %r_bar_ref.1) | copy-start | bytes 786436
  51.1 1.4 %collective-permute-start.4 = (f32[264,128]{1,0:T(8,128)S(1)}, f32[264,128]{1,0:T(8,128)S(1)}, u32[]{:S(2)}, u32[]{:S(2)}) collective-permute-start(f32[264,128]{1,0:T(8,128)S(1)} %get-tuple-element.55), channel_id=1, source_target_pairs={{0,1},{1,0},{2,3},{3,2},{4,5},{5,4},{6,7},{7,6},{8,9},{9,8},{10,11... | collective-permute-start | bytes 405512 | tf_op jit(solution)/shard_map/ppermute | solution.py:416
  52.6 4.2 %collective-permute-start.5 = (f32[264,128]{1,0:T(8,128)S(1)}, f32[264,128]{1,0:T(8,128)S(1)}, u32[]{:S(2)}, u32[]{:S(2)}) collective-permute-start(f32[264,128]{1,0:T(8,128)S(1)} %add.12), channel_id=1, source_target_pairs={{0,2},{1,5},{2,0},{3,7},{4,6},{5,1},{6,4},{7,3},{8,10},{9,13},{10,... | collective-permute-start | bytes 405512 | tf_op jit(solution)/shard_map/ppermute | solution.py:419
  56.8 5.7 %collective-permute-start.6 = (f32[264,128]{1,0:T(8,128)S(1)}, f32[264,128]{1,0:T(8,128)S(1)}, u32[]{:S(2)}, u32[]{:S(2)}) collective-permute-start(f32[264,128]{1,0:T(8,128)S(1)} %add.13), channel_id=1, source_target_pairs={{0,4},{1,9},{2,6},{3,11},{4,0},{5,13},{6,2},{7,15},{8,12},{9,1},{1... | collective-permute-start | bytes 405512 | tf_op jit(solution)/shard_map/ppermute | solution.py:419
  62.5 3.9 %collective-permute-start.7 = (f32[264,128]{1,0:T(8,128)S(1)}, f32[264,128]{1,0:T(8,128)S(1)}, u32[]{:S(2)}, u32[]{:S(2)}) collective-permute-start(f32[264,128]{1,0:T(8,128)S(1)} %add.14), channel_id=1, source_target_pairs={{0,8},{1,3},{2,10},{3,1},{4,12},{5,7},{6,14},{7,5},{8,0},{9,11},{1... | collective-permute-start | bytes 405512 | tf_op jit(solution)/shard_map/ppermute | solution.py:419
  66.5 4.5 %collective-permute-start.8 = (f32[264,128]{1,0:T(8,128)S(1)}, f32[264,128]{1,0:T(8,128)S(1)}, u32[]{:S(2)}, u32[]{:S(2)}) collective-permute-start(f32[264,128]{1,0:T(8,128)S(1)} %add.15.mine_ref), channel_id=1, source_target_pairs={{0,1},{1,0},{2,3},{3,2},{4,5},{5,4},{6,7},{7,6},{8,9},{9,8},{10,11... | collective-permute-start | bytes 405512 | tf_op jit(solution)/shard_map/ppermute | solution.py:420
  83.8 17.5 %collective-permute-start.10 = (f32[2,384,128]{2,1,0:T(8,128)S(1)}, f32[2,384,128]{2,1,0:T(8,128)S(1)}, u32[]{:S(2)}, u32[]{:S(2)}) collective-permute-start(f32[2,384,128]{2,1,0:T(8,128)S(1)} %get-tuple-element.61.jdown_ref), channel_id=1, source_target_pairs={{1,0},{2,1},{3,2},{4,3},{5,4},{6,5},{7,6},{8,7},{9,8},{10,9},{11,1... | collective-permute-start | bytes 1179656 | tf_op jit(solution)/shard_map/ppermute | solution.py:408
  86.1 15.2 %collective-permute-start.9 = (f32[2,384,128]{2,1,0:T(8,128)S(1)}, f32[2,384,128]{2,1,0:T(8,128)S(1)}, u32[]{:S(2)}, u32[]{:S(2)}) collective-permute-start(f32[2,384,128]{2,1,0:T(8,128)S(1)} %get-tuple-element.62.jup_ref), channel_id=1, source_target_pairs={{0,1},{1,2},{2,3},{3,4},{4,5},{5,6},{6,7},{7,8},{8,9},{9,10},{10,1... | collective-permute-start | bytes 1179656 | tf_op jit(solution)/shard_map/ppermute | solution.py:407
  90.8 14.4 %collective-permute-start.11 = (f32[2,384,128]{2,1,0:T(8,128)S(1)}, f32[2,384,128]{2,1,0:T(8,128)S(1)}, u32[]{:S(2)}, u32[]{:S(2)}) collective-permute-start(f32[2,384,128]{2,1,0:T(8,128)S(1)} %get-tuple-element.68), channel_id=1, source_target_pairs={{0,1},{1,2},{2,3},{3,4},{4,5},{5,6},{6,7},{7,8},{8,9},{9,10},{10,1... | collective-permute-start | bytes 1179656 | tf_op jit(solution)/shard_map/ppermute | solution.py:407
  92.8 12.8 %collective-permute-start.12 = (f32[2,384,128]{2,1,0:T(8,128)S(1)}, f32[2,384,128]{2,1,0:T(8,128)S(1)}, u32[]{:S(2)}, u32[]{:S(2)}) collective-permute-start(f32[2,384,128]{2,1,0:T(8,128)S(1)} %get-tuple-element.69), channel_id=1, source_target_pairs={{1,0},{2,1},{3,2},{4,3},{5,4},{6,5},{7,6},{8,7},{9,8},{10,9},{11,1... | collective-permute-start | bytes 1179656 | tf_op jit(solution)/shard_map/ppermute | solution.py:408

commit v4 on v3

--- a/solution.py
+++ b/solution.py
@@ -24,7 +24,6 @@
             kernel,
             out_shape=outs,
             in_specs=specs,
-            **({"out_specs": (pl.BlockSpec(memory_space=pltpu.HBM),) * len(outs)} if far else {}),
             scratch_shapes=list(scratch),
             compiler_params=pltpu.CompilerParams(vmem_limit_bytes=FAR_LIMIT if far else LIMIT),
             cost_estimate=pl.CostEstimate(flops=flops, bytes_accessed=moved, transcendentals=0),

time: 108 us -> 85.1 us (0.79)
  Pallas kernels: 53.3 us -> 30.4 us
    pallas_call x11, Pallas kernels: 53.3 us -> 30.4 us  [run(): pl.pallas_call(kernel, out_shape=outs, in_specs=specs, scratch_shapes=lis...]
  transfers between devices with their start and end apart: 13 -> 13, of which waited for: 9 -> 9; matrix products, arithmetic and copies ran while one was open for 0% -> 0% of each run, Pallas kernels for 12% -> 15%
where the time goes in v4:
time: 85.1 us; the launch traced here: 83.9 us
  Pallas kernels  30.4 us (36%)
  starting transfers between devices  27.2 us (32%)
  waiting for transfers between devices  22.1 us (26%)
  local copies, waits for them, and re-layouts  3.31 us (4%)
  between operations  0.86 us (1%)
    pallas_call x11, Pallas kernels, run(): pl.pallas_call(kernel, out_shape=outs, in_specs=specs, scratch_shapes=lis...  30.4 us
    ppermute x4, starting transfers between devices, exchange(): low = lax.ppermute(up, 'row', forward)  12.5 us
    ppermute x3, waiting for transfers between devices, sum_over_rows(): lax.ppermute(mine, 'row', [(i, i ^ 1 << turn[i & 1]) for i in range(count)])  11.3 us
    ppermute x4, starting transfers between devices, exchange(): high = lax.ppermute(down, 'row', backward)  8.52 us
    ppermute x4, waiting for transfers between devices, exchange(): high = lax.ppermute(down, 'row', backward)  6.71 us
    ppermute x1, starting transfers between devices, sum_over_rows(): return (mine, lax.ppermute(mine, 'row', swap))  3.53 us
    unnamed x12, local copies, waits for them, and re-layouts  3.31 us
    ppermute x3, starting transfers between devices, sum_over_rows(): lax.ppermute(mine, 'row', [(i, i ^ 1 << turn[i & 1]) for i in range(count)])  2.51 us
  transfers between devices with their start and end apart: 13, of which 9 were waited for; matrix products, arithmetic and copies ran while one was open for 0% of the time, Pallas kernels for 15%

profile of v4, /device:TPU:9, one launch (start us, length us, event | category | flops | bytes accessed | tf_op | source)
XLA Modules:
  0.0 83.9 jit_solution(17065660543698135239)
XLA Ops:
  0.6 2.0 %shard_map.70 = (f32[2,384,128]{2,1,0:T(8,128)}, f32[2,384,128]{2,1,0:T(8,128)}) custom-call(f32[4,2,384,128]{3,2,1,0:T(8,128)} %z_ref.7), custom_call_target="tpu_custom_call" | custom-call | bytes 2000000 | tf_op jit(solution)/shard_map/pallas_call | solution.py:23
  2.7 3.7 %collective-permute-start.2 = (f32[2,384,128]{2,1,0:T(8,128)}, f32[2,384,128]{2,1,0:T(8,128)S(1)}, u32[]{:S(2)}, u32[]{:S(2)}) collective-permute-start(f32[2,384,128]{2,1,0:T(8,128)} %get-tuple-element.42), channel_id=1, source_target_pairs={{0,1},{1,2},{2,3},{3,4},{4,5},{5,6},{6,7},{7,8},{8,9},{9,10},{10,1... | collective-permute-start | bytes 1179656 | tf_op jit(solution)/shard_map/ppermute | solution.py:406
  6.4 1.9 %collective-permute-start.3 = (f32[2,384,128]{2,1,0:T(8,128)}, f32[2,384,128]{2,1,0:T(8,128)S(1)}, u32[]{:S(2)}, u32[]{:S(2)}) collective-permute-start(f32[2,384,128]{2,1,0:T(8,128)} %get-tuple-element.43), channel_id=1, source_target_pairs={{1,0},{2,1},{3,2},{4,3},{5,4},{6,5},{7,6},{8,7},{9,8},{10,9},{11,1... | collective-permute-start | bytes 1179656 | tf_op jit(solution)/shard_map/ppermute | solution.py:407
  8.3 1.4 %copy-done = f32[4,2,384,128]{3,2,1,0:T(8,128)S(1)} copy-done((f32[4,2,384,128]{3,2,1,0:T(8,128)S(1)}, f32[4,2,384,128]{3,2,1,0:T(8,128)}, u32[]{:S(2)}) %copy-start) | copy-done | bytes 1572888
  9.7 1.6 %shard_map.69 = (f32[776,128]{1,0:T(8,128)}, f32[776,128]{1,0:T(8,128)}) custom-call(f32[6,2,384]{2,1,0:T(2,128)S(1)} %copy-done.4, f32[4,2,384,128]{3,2,1,0:T(8,128)S(1)} %copy-done), custom_call_target="tpu_custom_call" | custom-call | flops 1000000 | bytes 2000000 | tf_op jit(solution)/shard_map/pallas_call | solution.py:23
  11.3 3.6 %collective-permute-start = (f32[776,128]{1,0:T(8,128)}, f32[776,128]{1,0:T(8,128)S(1)}, u32[]{:S(2)}, u32[]{:S(2)}) collective-permute-start(f32[776,128]{1,0:T(8,128)} %get-tuple-element.40), channel_id=1, source_target_pairs={{0,1},{1,2},{2,3},{3,4},{4,5},{5,6},{6,7},{7,8},{8,9},{9,10},{10,1... | collective-permute-start | bytes 1191944 | tf_op jit(solution)/shard_map/ppermute | solution.py:406
  15.0 1.9 %collective-permute-start.1 = (f32[776,128]{1,0:T(8,128)}, f32[776,128]{1,0:T(8,128)S(1)}, u32[]{:S(2)}, u32[]{:S(2)}) collective-permute-start(f32[776,128]{1,0:T(8,128)} %get-tuple-element.41), channel_id=1, source_target_pairs={{1,0},{2,1},{3,2},{4,3},{5,4},{6,5},{7,6},{8,7},{9,8},{10,9},{11,1... | collective-permute-start | bytes 1191944 | tf_op jit(solution)/shard_map/ppermute | solution.py:407
  16.9 1.9 %copy-done.2 = f32[4,2,384,256]{3,2,1,0:T(8,128)S(1)} copy-done((f32[4,2,384,256]{3,2,1,0:T(8,128)S(1)}, f32[4,2,384,256]{3,2,1,0:T(8,128)}, u32[]{:S(2)}) %copy-start.2) | copy-done | bytes 3145752
  18.8 1.8 %shard_map.68 = (f32[136,128]{1,0:T(8,128)S(1)}, bf16[3072,128]{1,0:T(8,128)(2,1)S(1)}, bf16[3072,128]{1,0:T(8,128)(2,1)S(1)}, bf16[3072,256]{1,0:T(8,128)(2,1)S...) custom-call(f32[3072,128]{1,0:T(8,128)S(1)} %bitcast.4, ...), custom_call_target="tpu_custom_call" | custom-call | flops 503316480 | bytes 9000000 | tf_op jit(solution)/shard_map/pallas_call | solution.py:23
  20.7 2.7 %shard_map.71 = (f32[2,2,384,128]{3,2,1,0:T(8,128)S(1)}, bf16[1536,128]{1,0:T(8,128)(2,1)S(1)}, bf16[1536,128]{1,0:T(8,128)(2,1)S(1)}, f32[128,128]{1,0:T(8,128)S(1)}, f32[384,128]{1,0:T(8,128)S(1)}) custom-call(f32[6,2,384]{2,1,0:T(2,128)S(1)} %copy-done.4, f32[4,2,384,128]{3,2,1,0:T(8,128)S(1)} %copy-done.1, ...), custom_call_target="tpu_custom_call" | custom-call | flops 603979776 | bytes 9000000 | tf_op jit(solution)/shard_map/pallas_call | solution.py:23
  23.4 3.3 %collective-permute-done.1.high_ref.fhigh_ref = f32[776,128]{1,0:T(8,128)S(1)} collective-permute-done((f32[776,128]{1,0:T(8,128)}, f32[776,128]{1,0:T(8,128)S(1)}, u32[]{:S(2)}, u32[]{:S(2)}) %collective-permute-start.1) | collective-permute-done | bytes 397344 | tf_op jit(solution)/shard_map/ppermute | solution.py:407
  26.7 1.5 %shard_map.72 = (f32[264,128]{1,0:T(8,128)S(1)}, f32[264,128]{1,0:T(8,128)S(1)}, bf16[1536,128]{1,0:T(8,128)(2,1)S(1)}, bf16[1536,128]{1,0:T(8,128)(2,1)S(1)}) custom-call(s32[1]{0:T(128)} %bitcast.2.core_ref, f32[6,2,384]{2,1,0:T(2,128)S(1)} %copy-done.4, f32[4,2,384,128]{3,2,1,0:T(8,128)S(1)} %copy-done.1, ...), custom_call_target="tpu_custom_call" | custom-call | flops 603979776 | bytes 9000000 | tf_op jit(solution)/shard_map/pallas_call | solution.py:23
  28.3 1.3 %collective-permute-done.4 = f32[264,128]{1,0:T(8,128)S(1)} collective-permute-done((f32[264,128]{1,0:T(8,128)S(1)}, f32[264,128]{1,0:T(8,128)S(1)}, u32[]{:S(2)}, u32[]{:S(2)}) %collective-permute-start.4) | collective-permute-done | bytes 135200 | tf_op jit(solution)/shard_map/ppermute | solution.py:415
  29.7 4.1 %collective-permute-done.5 = f32[264,128]{1,0:T(8,128)S(1)} collective-permute-done((f32[264,128]{1,0:T(8,128)S(1)}, f32[264,128]{1,0:T(8,128)S(1)}, u32[]{:S(2)}, u32[]{:S(2)}) %collective-permute-start.5) | collective-permute-done | bytes 135200 | tf_op jit(solution)/shard_map/ppermute | solution.py:418
  33.9 2.4 %collective-permute-start.6 = (f32[264,128]{1,0:T(8,128)S(1)}, f32[264,128]{1,0:T(8,128)S(1)}, u32[]{:S(2)}, u32[]{:S(2)}) collective-permute-start(f32[264,128]{1,0:T(8,128)S(1)} %add.13), channel_id=1, source_target_pairs={{0,4},{1,9},{2,6},{3,11},{4,0},{5,13},{6,2},{7,15},{8,12},{9,1},{1... | collective-permute-start | bytes 405512 | tf_op jit(solution)/shard_map/ppermute | solution.py:418
  36.3 3.3 %collective-permute-done.6 = f32[264,128]{1,0:T(8,128)S(1)} collective-permute-done((f32[264,128]{1,0:T(8,128)S(1)}, f32[264,128]{1,0:T(8,128)S(1)}, u32[]{:S(2)}, u32[]{:S(2)}) %collective-permute-start.6) | collective-permute-done | bytes 135200 | tf_op jit(solution)/shard_map/ppermute | solution.py:418
  39.7 3.8 %collective-permute-done.7 = f32[264,128]{1,0:T(8,128)S(1)} collective-permute-done((f32[264,128]{1,0:T(8,128)S(1)}, f32[264,128]{1,0:T(8,128)S(1)}, u32[]{:S(2)}, u32[]{:S(2)}) %collective-permute-start.7) | collective-permute-done | bytes 135200 | tf_op jit(solution)/shard_map/ppermute | solution.py:418
  43.5 3.5 %collective-permute-start.8 = (f32[264,128]{1,0:T(8,128)S(1)}, f32[264,128]{1,0:T(8,128)S(1)}, u32[]{:S(2)}, u32[]{:S(2)}) collective-permute-start(f32[264,128]{1,0:T(8,128)S(1)} %add.15.mine_ref), channel_id=1, source_target_pairs={{0,1},{1,0},{2,3},{3,2},{4,5},{5,4},{6,7},{7,6},{8,9},{9,8},{10,11... | collective-permute-start | bytes 405512 | tf_op jit(solution)/shard_map/ppermute | solution.py:419
  47.1 1.0 %collective-permute-done.8.other_ref = f32[264,128]{1,0:T(8,128)S(1)} collective-permute-done((f32[264,128]{1,0:T(8,128)S(1)}, f32[264,128]{1,0:T(8,128)S(1)}, u32[]{:S(2)}, u32[]{:S(2)}) %collective-permute-start.8) | collective-permute-done | bytes 135200 | tf_op jit(solution)/shard_map/ppermute | solution.py:419
  48.1 11.7 %shard_map.73 = (bf16[256,256]{1,0:T(8,128)(2,1)S(1)}, bf16[256,256]{1,0:T(8,128)(2,1)S(1)}, bf16[256,256]{1,0:T(8,128)(2,1)S(1)}, bf16[256,256]{1,0:T(8,128)(2,1)S(1)}) custom-call(s32[1]{0:T(128)} %bitcast.2.core_ref, f32[264,128]{1,0:T(8,128)S(1)} %add.15.mine_ref, f32[264,128]{1,0:T(8,128)S(1)} %collective-permute-done.8.other_ref, f32[256,256]{1,0:T(8,128)S(1)} %copy-done.5), custom_call_target="tpu_custom_call" | custom-call | flops 1000000000 | bytes 1000000 | tf_op jit(solution)/shard_map/pallas_call | solution.py:23
  59.8 1.1 %shard_map.74 = (f32[2,2,384,128]{3,2,1,0:T(8,128)S(1)}, f32[2,384,128]{2,1,0:T(8,128)S(1)}, f32[2,384,128]{2,1,0:T(8,128)S(1)}) custom-call(f32[6,2,384]{2,1,0:T(2,128)S(1)} %copy-done.4, bf16[3072,256]{1,0:T(8,128)(2,1)S(1)} %get-tuple-element.36.qh_ref, bf16[3072,256]{1,0:T(8,128)(2,1)S(1)} %get-tuple-element.37.ql_ref, ...), custom_call_target="tpu_custom_call" | custom-call | flops 603979776 | bytes 6000000 | tf_op jit(solution)/shard_map/pallas_call | solution.py:23
  60.9 2.3 %collective-permute-start.10 = (f32[2,384,128]{2,1,0:T(8,128)S(1)}, f32[2,384,128]{2,1,0:T(8,128)S(1)}, u32[]{:S(2)}, u32[]{:S(2)}) collective-permute-start(f32[2,384,128]{2,1,0:T(8,128)S(1)} %get-tuple-element.61.jdown_ref), channel_id=1, source_target_pairs={{1,0},{2,1},{3,2},{4,3},{5,4},{6,5},{7,6},{8,7},{9,8},{10,9},{11,1... | collective-permute-start | bytes 1179656 | tf_op jit(solution)/shard_map/ppermute | solution.py:407
  63.2 3.3 %collective-permute-start.9 = (f32[2,384,128]{2,1,0:T(8,128)S(1)}, f32[2,384,128]{2,1,0:T(8,128)S(1)}, u32[]{:S(2)}, u32[]{:S(2)}) collective-permute-start(f32[2,384,128]{2,1,0:T(8,128)S(1)} %get-tuple-element.62.jup_ref), channel_id=1, source_target_pairs={{0,1},{1,2},{2,3},{3,4},{4,5},{5,6},{6,7},{7,8},{8,9},{9,10},{10,1... | collective-permute-start | bytes 1179656 | tf_op jit(solution)/shard_map/ppermute | solution.py:406
  66.5 1.4 %shard_map.75 = (f32[2,2,384,128]{3,2,1,0:T(8,128)S(1)}, f32[2,384,128]{2,1,0:T(8,128)S(1)}, f32[2,384,128]{2,1,0:T(8,128)S(1)}) custom-call(f32[6,2,384]{2,1,0:T(2,128)S(1)} %copy-done.4, f32[2,2,384,128]{3,2,1,0:T(8,128)S(1)} %get-tuple-element.60.light_ref, f32[2,384,128]{2,1,0:T(8,128)S(1)} %get-tuple-element.61.jdown_ref, ...), custom_call_target="tpu_custom_call" | custom-call | flops 603979776 | bytes 6000000 | tf_op jit(solution)/shard_map/pallas_call | solution.py:23
  67.9 1.9 %collective-permute-start.11 = (f32[2,384,128]{2,1,0:T(8,128)S(1)}, f32[2,384,128]{2,1,0:T(8,128)S(1)}, u32[]{:S(2)}, u32[]{:S(2)}) collective-permute-start(f32[2,384,128]{2,1,0:T(8,128)S(1)} %get-tuple-element.68), channel_id=1, source_target_pairs={{0,1},{1,2},{2,3},{3,4},{4,5},{5,6},{6,7},{7,8},{8,9},{9,10},{10,1... | collective-permute-start | bytes 1179656 | tf_op jit(solution)/shard_map/ppermute | solution.py:406
  69.9 2.4 %collective-permute-start.12 = (f32[2,384,128]{2,1,0:T(8,128)S(1)}, f32[2,384,128]{2,1,0:T(8,128)S(1)}, u32[]{:S(2)}, u32[]{:S(2)}) collective-permute-start(f32[2,384,128]{2,1,0:T(8,128)S(1)} %get-tuple-element.69), channel_id=1, source_target_pairs={{1,0},{2,1},{3,2},{4,3},{5,4},{6,5},{7,6},{8,7},{9,8},{10,9},{11,1... | collective-permute-start | bytes 1179656 | tf_op jit(solution)/shard_map/ppermute | solution.py:407
  72.3 3.0 %shard_map.78 = f32[4,2,384,128]{3,2,1,0:T(8,128)} custom-call(bf16[3072,256]{1,0:T(8,128)(2,1)S(1)} %get-tuple-element.36.qh_ref, bf16[3072,256]{1,0:T(8,128)(2,1)S(1)} %get-tuple-element.37.ql_ref, bf16[3072,128]{1,0:T(8,128)(2,1)S(1)} %get-tuple-element.38.nh_ref, bf16[3072,128]{1,0:T(8,128)(2,1)S(1)} %get-tuple-element.39.nl_ref, ...), custom_call_target="tpu_custom_call" | custom-call | flops 1207959552 | bytes 9000000 | tf_op jit(solution)/shard_map/pallas_call | solution.py:23
  75.3 3.1 %collective-permute-done.10.high_ref = f32[2,384,128]{2,1,0:T(8,128)S(1)} collective-permute-done((f32[2,384,128]{2,1,0:T(8,128)S(1)}, f32[2,384,128]{2,1,0:T(8,128)S(1)}, u32[]{:S(2)}, u32[]{:S(2)}) %collective-permute-start.10) | collective-permute-done | bytes 393248 | tf_op jit(solution)/shard_map/ppermute | solution.py:407
  78.4 2.2 %shard_map.76 = (f32[2,2,384,128]{3,2,1,0:T(8,128)S(1)}, f32[2,2,384,128]{3,2,1,0:T(8,128)S(1)}) custom-call(f32[6,2,384]{2,1,0:T(2,128)S(1)} %copy-done.4, f32[2,2,384,128]{3,2,1,0:T(8,128)S(1)} %get-tuple-element.60.light_ref, f32[2,2,384,128]{3,2,1,0:T(8,128)S(1)} %get-tuple-element.65.heavy_ref, f32[2,384,128]{2,1,0:T(8,128)S(1)} %get-tuple-element.61.jdown_ref, ...), custom_call_target="tpu_custom_call" | custom-call | flops 10000000 | bytes 6000000 | tf_op jit(solution)/shard_map/pallas_call | solution.py:23
  80.6 1.8 %collective-permute-done.11.low_ref = f32[2,384,128]{2,1,0:T(8,128)S(1)} collective-permute-done((f32[2,384,128]{2,1,0:T(8,128)S(1)}, f32[2,384,128]{2,1,0:T(8,128)S(1)}, u32[]{:S(2)}, u32[]{:S(2)}) %collective-permute-start.11) | collective-permute-done | bytes 393248 | tf_op jit(solution)/shard_map/ppermute | solution.py:406
  82.3 0.3 collective-permute-done.12.high_ref
  82.6 1.3 %shard_map.77 = f32[4,2,384,128]{3,2,1,0:T(8,128)} custom-call(f32[2,2,384,128]{3,2,1,0:T(8,128)S(1)} %get-tuple-element.66.light_ref, f32[2,2,384,128]{3,2,1,0:T(8,128)S(1)} %get-tuple-element.67.heavy_ref, f32[2,384,128]{2,1,0:T(8,128)S(1)} %collective-permute-done.11.low_ref, f32[2,384,128]{2,1,0:T(8,128)S(1)} %collective-permute-done.12.high_ref), custom_call_target="tpu_custom_call" | custom-call | flops 1000000 | bytes 6000000 | tf_op jit(solution)/shard_map/pallas_call | solution.py:23
  (21 shorter events, 0.3 us)
Async XLA Ops:
  0.6 7.7 %copy-start.4 = (f32[6,2,384]{2,1,0:T(2,128)S(1)}, f32[6,2,384]{2,1,0:T(2,128)}, u32[]{:S(2)}) copy-start(f32[6,2,384]{2,1,0:T(2,128)} %coeff_ref.11) | copy-start | bytes 55300
  2.7 18.0 %collective-permute-start.2 = (f32[2,384,128]{2,1,0:T(8,128)}, f32[2,384,128]{2,1,0:T(8,128)S(1)}, u32[]{:S(2)}, u32[]{:S(2)}) collective-permute-start(f32[2,384,128]{2,1,0:T(8,128)} %get-tuple-element.42), channel_id=1, source_target_pairs={{0,1},{1,2},{2,3},{3,4},{4,5},{5,6},{6,7},{7,8},{8,9},{9,10},{10,1... | collective-permute-start | bytes 1179656 | tf_op jit(solution)/shard_map/ppermute | solution.py:406
  6.4 14.3 %collective-permute-start.3 = (f32[2,384,128]{2,1,0:T(8,128)}, f32[2,384,128]{2,1,0:T(8,128)S(1)}, u32[]{:S(2)}, u32[]{:S(2)}) collective-permute-start(f32[2,384,128]{2,1,0:T(8,128)} %get-tuple-element.43), channel_id=1, source_target_pairs={{1,0},{2,1},{3,2},{4,3},{5,4},{6,5},{7,6},{8,7},{9,8},{10,9},{11,1... | collective-permute-start | bytes 1179656 | tf_op jit(solution)/shard_map/ppermute | solution.py:407
  8.3 1.4 %copy-start = (f32[4,2,384,128]{3,2,1,0:T(8,128)S(1)}, f32[4,2,384,128]{3,2,1,0:T(8,128)}, u32[]{:S(2)}) copy-start(f32[4,2,384,128]{3,2,1,0:T(8,128)} %z_ref.7) | copy-start | bytes 4718596
  9.7 7.2 %copy-start.3 = (f32[4,2,384,128]{3,2,1,0:T(8,128)S(1)}, f32[4,2,384,128]{3,2,1,0:T(8,128)}, u32[]{:S(2)}) copy-start(f32[4,2,384,128]{3,2,1,0:T(8,128)} %param.7) | copy-start | bytes 4718596
  11.3 12.0 %collective-permute-start = (f32[776,128]{1,0:T(8,128)}, f32[776,128]{1,0:T(8,128)S(1)}, u32[]{:S(2)}, u32[]{:S(2)}) collective-permute-start(f32[776,128]{1,0:T(8,128)} %get-tuple-element.40), channel_id=1, source_target_pairs={{0,1},{1,2},{2,3},{3,4},{4,5},{5,6},{6,7},{7,8},{8,9},{9,10},{10,1... | collective-permute-start | bytes 1191944 | tf_op jit(solution)/shard_map/ppermute | solution.py:406
  15.0 11.7 %collective-permute-start.1 = (f32[776,128]{1,0:T(8,128)}, f32[776,128]{1,0:T(8,128)S(1)}, u32[]{:S(2)}, u32[]{:S(2)}) collective-permute-start(f32[776,128]{1,0:T(8,128)} %get-tuple-element.41), channel_id=1, source_target_pairs={{1,0},{2,1},{3,2},{4,3},{5,4},{6,5},{7,6},{8,7},{9,8},{10,9},{11,1... | collective-permute-start | bytes 1191944 | tf_op jit(solution)/shard_map/ppermute | solution.py:407
  16.9 1.9 %copy-start.2 = (f32[4,2,384,256]{3,2,1,0:T(8,128)S(1)}, f32[4,2,384,256]{3,2,1,0:T(8,128)}, u32[]{:S(2)}) copy-start(f32[4,2,384,256]{3,2,1,0:T(8,128)} %param.8) | copy-start | bytes 9437188
  18.8 1.8 %copy-start.1 = (f32[4,2,384,128]{3,2,1,0:T(8,128)S(1)}, f32[4,2,384,128]{3,2,1,0:T(8,128)}, u32[]{:S(2)}) copy-start(f32[4,2,384,128]{3,2,1,0:T(8,128)} %z_ref.7) | copy-start | bytes 4718596
  28.2 19.9 %copy-start.5 = (f32[256,256]{1,0:T(8,128)S(1)}, f32[256,256]{1,0:T(8,128)}, u32[]{:S(2)}) copy-start(f32[256,256]{1,0:T(8,128)} %r_bar_ref.1) | copy-start | bytes 786436
  28.2 1.4 %collective-permute-start.4 = (f32[264,128]{1,0:T(8,128)S(1)}, f32[264,128]{1,0:T(8,128)S(1)}, u32[]{:S(2)}, u32[]{:S(2)}) collective-permute-start(f32[264,128]{1,0:T(8,128)S(1)} %get-tuple-element.55), channel_id=1, source_target_pairs={{0,1},{1,0},{2,3},{3,2},{4,5},{5,4},{6,7},{7,6},{8,9},{9,8},{10,11... | collective-permute-start | bytes 405512 | tf_op jit(solution)/shard_map/ppermute | solution.py:415
  29.7 4.2 %collective-permute-start.5 = (f32[264,128]{1,0:T(8,128)S(1)}, f32[264,128]{1,0:T(8,128)S(1)}, u32[]{:S(2)}, u32[]{:S(2)}) collective-permute-start(f32[264,128]{1,0:T(8,128)S(1)} %add.12), channel_id=1, source_target_pairs={{0,2},{1,5},{2,0},{3,7},{4,6},{5,1},{6,4},{7,3},{8,10},{9,13},{10,... | collective-permute-start | bytes 405512 | tf_op jit(solution)/shard_map/ppermute | solution.py:418
  33.9 5.7 %collective-permute-start.6 = (f32[264,128]{1,0:T(8,128)S(1)}, f32[264,128]{1,0:T(8,128)S(1)}, u32[]{:S(2)}, u32[]{:S(2)}) collective-permute-start(f32[264,128]{1,0:T(8,128)S(1)} %add.13), channel_id=1, source_target_pairs={{0,4},{1,9},{2,6},{3,11},{4,0},{5,13},{6,2},{7,15},{8,12},{9,1},{1... | collective-permute-start | bytes 405512 | tf_op jit(solution)/shard_map/ppermute | solution.py:418
  39.6 3.9 %collective-permute-start.7 = (f32[264,128]{1,0:T(8,128)S(1)}, f32[264,128]{1,0:T(8,128)S(1)}, u32[]{:S(2)}, u32[]{:S(2)}) collective-permute-start(f32[264,128]{1,0:T(8,128)S(1)} %add.14), channel_id=1, source_target_pairs={{0,8},{1,3},{2,10},{3,1},{4,12},{5,7},{6,14},{7,5},{8,0},{9,11},{1... | collective-permute-start | bytes 405512 | tf_op jit(solution)/shard_map/ppermute | solution.py:418
  43.5 4.5 %collective-permute-start.8 = (f32[264,128]{1,0:T(8,128)S(1)}, f32[264,128]{1,0:T(8,128)S(1)}, u32[]{:S(2)}, u32[]{:S(2)}) collective-permute-start(f32[264,128]{1,0:T(8,128)S(1)} %add.15.mine_ref), channel_id=1, source_target_pairs={{0,1},{1,0},{2,3},{3,2},{4,5},{5,4},{6,7},{7,6},{8,9},{9,8},{10,11... | collective-permute-start | bytes 405512 | tf_op jit(solution)/shard_map/ppermute | solution.py:419
  60.9 17.5 %collective-permute-start.10 = (f32[2,384,128]{2,1,0:T(8,128)S(1)}, f32[2,384,128]{2,1,0:T(8,128)S(1)}, u32[]{:S(2)}, u32[]{:S(2)}) collective-permute-start(f32[2,384,128]{2,1,0:T(8,128)S(1)} %get-tuple-element.61.jdown_ref), channel_id=1, source_target_pairs={{1,0},{2,1},{3,2},{4,3},{5,4},{6,5},{7,6},{8,7},{9,8},{10,9},{11,1... | collective-permute-start | bytes 1179656 | tf_op jit(solution)/shard_map/ppermute | solution.py:407
  63.2 15.2 %collective-permute-start.9 = (f32[2,384,128]{2,1,0:T(8,128)S(1)}, f32[2,384,128]{2,1,0:T(8,128)S(1)}, u32[]{:S(2)}, u32[]{:S(2)}) collective-permute-start(f32[2,384,128]{2,1,0:T(8,128)S(1)} %get-tuple-element.62.jup_ref), channel_id=1, source_target_pairs={{0,1},{1,2},{2,3},{3,4},{4,5},{5,6},{6,7},{7,8},{8,9},{9,10},{10,1... | collective-permute-start | bytes 1179656 | tf_op jit(solution)/shard_map/ppermute | solution.py:406
  67.9 14.4 %collective-permute-start.11 = (f32[2,384,128]{2,1,0:T(8,128)S(1)}, f32[2,384,128]{2,1,0:T(8,128)S(1)}, u32[]{:S(2)}, u32[]{:S(2)}) collective-permute-start(f32[2,384,128]{2,1,0:T(8,128)S(1)} %get-tuple-element.68), channel_id=1, source_target_pairs={{0,1},{1,2},{2,3},{3,4},{4,5},{5,6},{6,7},{7,8},{8,9},{9,10},{10,1... | collective-permute-start | bytes 1179656 | tf_op jit(solution)/shard_map/ppermute | solution.py:406
  69.9 12.8 %collective-permute-start.12 = (f32[2,384,128]{2,1,0:T(8,128)S(1)}, f32[2,384,128]{2,1,0:T(8,128)S(1)}, u32[]{:S(2)}, u32[]{:S(2)}) collective-permute-start(f32[2,384,128]{2,1,0:T(8,128)S(1)} %get-tuple-element.69), channel_id=1, source_target_pairs={{1,0},{2,1},{3,2},{4,3},{5,4},{6,5},{7,6},{8,7},{9,8},{10,9},{11,1... | collective-permute-start | bytes 1179656 | tf_op jit(solution)/shard_map/ppermute | solution.py:407

commit v5 on v4

--- a/solution.py
+++ b/solution.py
@@ -92,23 +92,24 @@
     return -2.0 * g * pa - w * pb, w * xb - 0.5 * m * pb
 
 
-def light_rows(z_ref, down_ref, up_ref, sems):
+def forward_rim(coeff_hbm, z_hbm, down1_ref, up1_ref, down2_ref, up2_ref, coeff_ref, xb_ref, sems):
     copies = [
-        pltpu.make_async_copy(z_ref.at[0:2, r], out, sems.at[r]) for r, out in ((0, down_ref), (1, up_ref))
+        pltpu.make_async_copy(z_hbm.at[0:2, 0], down1_ref, sems.at[0]),
+        pltpu.make_async_copy(z_hbm.at[0:2, 1], up1_ref, sems.at[1]),
+        pltpu.make_async_copy(coeff_hbm, coeff_ref, sems.at[2]),
+        pltpu.make_async_copy(z_hbm.at[2], xb_ref, sems.at[3]),
     ]
     for copy in copies:
         copy.start()
     for copy in copies:
         copy.wait()
-
-
-def forward_rim(coeff_ref, z_ref, down_ref, up_ref):
     c = coefficients(coeff_ref)
-    n = z_ref.shape[2]
-    for r, out in ((0, down_ref), (1, up_ref)):
-        xa, pa, xb = z_ref[0, r], z_ref[1, r], z_ref[2, r]
-        hop_x = z_ref[0, 1 - r] + side(xa)
-        hop_p = z_ref[1, 1 - r] + side(pa)
+    n = xb_ref.shape[1]
+    rows = (down1_ref, up1_ref)
+    for r, out in ((0, down2_ref), (1, up2_ref)):
+        xa, pa, xb = rows[r][0], rows[r][1], xb_ref[r]
+        hop_x = rows[1 - r][0] + side(xa)
+        hop_p = rows[1 - r][1] + side(pa)
         out[0:n], out[n : 2 * n] = forward_light(c[r], xa, pa, xb, hop_x, hop_p)
         hopping = coeff_ref[5, r : r + 1, :] * rate_scales[5]
         pieces = [hopping[:, k * 128 : (k + 1) * 128] for k in range(n // 128)]
@@ -428,13 +429,18 @@
     bar = q_bar.reshape(flat, -1)
     shape = jax.ShapeDtypeStruct
     hops = shape((2, n, rank), f32)
-    down, up = call(
-        light_rows, (hops, hops), 0, 2 * 10**6, [pltpu.SemaphoreType.DMA((2,))], far=True
-    )(z_factor)
+    rim = shape((2 * n + 8, rank), f32)
+    down, up, far_down, far_up = call(
+        forward_rim, (hops, hops, rim, rim), 10**6, 3 * 10**6,
+        [
+            pltpu.VMEM(cell_coeffs.shape, f32),
+            pltpu.VMEM(z_factor.shape[1:], f32),
+            pltpu.SemaphoreType.DMA((4,)),
+        ],
+        far=True,
+    )(coeffs, z_factor)
     low, high = exchange(up, down)
-    rim = shape((2 * n + 8, rank), f32)
-    down, up = call(forward_rim, (rim, rim), 10**6, 2 * 10**6)(coeffs, z_factor)
-    far_low, far_high = exchange(up, down)
+    far_low, far_high = exchange(far_up, far_down)
     wide, tall = shape((flat, 256), bf16), shape((flat, 128), bf16)
     wide_t, tall_t = shape((256, flat), bf16), shape((128, flat), bf16)
     work = 2 * flat * 128 * 128

time: 85.1 us -> 84.7 us (level)
    pallas_call x11 -> x10, Pallas kernels: 30.4 us -> 29.6 us  [run(): pl.pallas_call(kernel, out_shape=outs, in_specs=specs, scratch_shapes=lis...]
    unnamed x12 -> x10, local copies, waits for them, and re-layouts: 3.31 us -> 3.31 us
  transfers between devices with their start and end apart: 13 -> 13, of which waited for: 9 -> 10; matrix products, arithmetic and copies ran while one was open for 0% -> 0% of each run, Pallas kernels for 15% -> 13%
where the time goes in v5:
time: 84.7 us; the launch traced here: 83.7 us
  Pallas kernels  29.6 us (35%)
  starting transfers between devices  27.5 us (32%)
  waiting for transfers between devices  22.3 us (26%)
  local copies, waits for them, and re-layouts  3.31 us (4%)
    pallas_call x10, Pallas kernels, run(): pl.pallas_call(kernel, out_shape=outs, in_specs=specs, scratch_shapes=lis...  29.6 us
    ppermute x4, starting transfers between devices, exchange(): low = lax.ppermute(up, 'row', forward)  12.6 us
    ppermute x3, waiting for transfers between devices, sum_over_rows(): lax.ppermute(mine, 'row', [(i, i ^ 1 << turn[i & 1]) for i in range(count)])  10.9 us
    ppermute x4, starting transfers between devices, exchange(): high = lax.ppermute(down, 'row', backward)  8.43 us
    ppermute x4, waiting for transfers between devices, exchange(): high = lax.ppermute(down, 'row', backward)  6.5 us
    ppermute x1, starting transfers between devices, sum_over_rows(): return (mine, lax.ppermute(mine, 'row', swap))  3.53 us
    unnamed x10, local copies, waits for them, and re-layouts  3.31 us
    ppermute x3, starting transfers between devices, sum_over_rows(): lax.ppermute(mine, 'row', [(i, i ^ 1 << turn[i & 1]) for i in range(count)])  2.86 us
  transfers between devices with their start and end apart: 13, of which 10 were waited for; matrix products, arithmetic and copies ran while one was open for 0% of the time, Pallas kernels for 13%

profile of v5, /device:TPU:9, one launch (start us, length us, event | category | flops | bytes accessed | tf_op | source)
XLA Modules:
  0.0 83.7 jit_solution(7608282014043020125)
XLA Ops:
  0.6 2.8 %shard_map.69 = (f32[2,384,128]{2,1,0:T(8,128)}, f32[2,384,128]{2,1,0:T(8,128)}, f32[776,128]{1,0:T(8,128)}, f32[776,128]{1,0:T(8,128)}) custom-call(f32[6,2,384]{2,1,0:T(2,128)} %coeff_ref.9, f32[4,2,384,128]{3,2,1,0:T(8,128)} %z_ref.3), custom_call_target="tpu_custom_call" | custom-call | flops 1000000 | bytes 3000000 | tf_op jit(solution)/shard_map/pallas_call | solution.py:23
  3.4 3.7 %collective-permute-start.2 = (f32[2,384,128]{2,1,0:T(8,128)}, f32[2,384,128]{2,1,0:T(8,128)S(1)}, u32[]{:S(2)}, u32[]{:S(2)}) collective-permute-start(f32[2,384,128]{2,1,0:T(8,128)} %get-tuple-element.42), channel_id=1, source_target_pairs={{0,1},{1,2},{2,3},{3,4},{4,5},{5,6},{6,7},{7,8},{8,9},{9,10},{10,1... | collective-permute-start | bytes 1179656 | tf_op jit(solution)/shard_map/ppermute | solution.py:407
  7.2 1.9 %collective-permute-start.3 = (f32[2,384,128]{2,1,0:T(8,128)}, f32[2,384,128]{2,1,0:T(8,128)S(1)}, u32[]{:S(2)}, u32[]{:S(2)}) collective-permute-start(f32[2,384,128]{2,1,0:T(8,128)} %get-tuple-element.43), channel_id=1, source_target_pairs={{1,0},{2,1},{3,2},{4,3},{5,4},{6,5},{7,6},{8,7},{9,8},{10,9},{11,1... | collective-permute-start | bytes 1179656 | tf_op jit(solution)/shard_map/ppermute | solution.py:408
  9.1 3.6 %collective-permute-start = (f32[776,128]{1,0:T(8,128)}, f32[776,128]{1,0:T(8,128)S(1)}, u32[]{:S(2)}, u32[]{:S(2)}) collective-permute-start(f32[776,128]{1,0:T(8,128)} %get-tuple-element.40), channel_id=1, source_target_pairs={{0,1},{1,2},{2,3},{3,4},{4,5},{5,6},{6,7},{7,8},{8,9},{9,10},{10,1... | collective-permute-start | bytes 1191944 | tf_op jit(solution)/shard_map/ppermute | solution.py:407
  12.7 1.9 %collective-permute-start.1 = (f32[776,128]{1,0:T(8,128)}, f32[776,128]{1,0:T(8,128)S(1)}, u32[]{:S(2)}, u32[]{:S(2)}) collective-permute-start(f32[776,128]{1,0:T(8,128)} %get-tuple-element.41), channel_id=1, source_target_pairs={{1,0},{2,1},{3,2},{4,3},{5,4},{6,5},{7,6},{8,7},{9,8},{10,9},{11,1... | collective-permute-start | bytes 1191944 | tf_op jit(solution)/shard_map/ppermute | solution.py:408
  14.7 1.9 %copy-done.1 = f32[4,2,384,256]{3,2,1,0:T(8,128)S(1)} copy-done((f32[4,2,384,256]{3,2,1,0:T(8,128)S(1)}, f32[4,2,384,256]{3,2,1,0:T(8,128)}, u32[]{:S(2)}) %copy-start.1) | copy-done | bytes 3145752
  16.6 1.4 %copy-done.2 = f32[4,2,384,128]{3,2,1,0:T(8,128)S(1)} copy-done((f32[4,2,384,128]{3,2,1,0:T(8,128)S(1)}, f32[4,2,384,128]{3,2,1,0:T(8,128)}, u32[]{:S(2)}) %copy-start.2) | copy-done | bytes 1572888
  18.0 1.8 %shard_map.68 = (f32[136,128]{1,0:T(8,128)S(1)}, bf16[3072,128]{1,0:T(8,128)(2,1)S(1)}, bf16[3072,128]{1,0:T(8,128)(2,1)S(1)}, bf16[3072,256]{1,0:T(8,128)(2,1)S...) custom-call(f32[3072,128]{1,0:T(8,128)S(1)} %bitcast.4, ...), custom_call_target="tpu_custom_call" | custom-call | flops 503316480 | bytes 9000000 | tf_op jit(solution)/shard_map/pallas_call | solution.py:23
  19.8 2.3 %collective-permute-done.3.high_ref = f32[2,384,128]{2,1,0:T(8,128)S(1)} collective-permute-done((f32[2,384,128]{2,1,0:T(8,128)}, f32[2,384,128]{2,1,0:T(8,128)S(1)}, u32[]{:S(2)}, u32[]{:S(2)}) %collective-permute-start.3) | collective-permute-done | bytes 393248 | tf_op jit(solution)/shard_map/ppermute | solution.py:408
  22.1 2.7 %shard_map.70 = (f32[2,2,384,128]{3,2,1,0:T(8,128)S(1)}, bf16[1536,128]{1,0:T(8,128)(2,1)S(1)}, bf16[1536,128]{1,0:T(8,128)(2,1)S(1)}, f32[128,128]{1,0:T(8,128)S(1)}, f32[384,128]{1,0:T(8,128)S(1)}) custom-call(f32[6,2,384]{2,1,0:T(2,128)S(1)} %copy-done.3, f32[4,2,384,128]{3,2,1,0:T(8,128)S(1)} %copy-done, ...), custom_call_target="tpu_custom_call" | custom-call | flops 603979776 | bytes 9000000 | tf_op jit(solution)/shard_map/pallas_call | solution.py:23
  24.8 0.5 collective-permute-done.low_ref.flow_ref
  25.3 1.0 %collective-permute-done.1.high_ref.fhigh_ref = f32[776,128]{1,0:T(8,128)S(1)} collective-permute-done((f32[776,128]{1,0:T(8,128)}, f32[776,128]{1,0:T(8,128)S(1)}, u32[]{:S(2)}, u32[]{:S(2)}) %collective-permute-start.1) | collective-permute-done | bytes 397344 | tf_op jit(solution)/shard_map/ppermute | solution.py:408
  26.4 1.5 %shard_map.71 = (f32[264,128]{1,0:T(8,128)S(1)}, f32[264,128]{1,0:T(8,128)S(1)}, bf16[1536,128]{1,0:T(8,128)(2,1)S(1)}, bf16[1536,128]{1,0:T(8,128)(2,1)S(1)}) custom-call(s32[1]{0:T(128)} %bitcast.2.core_ref, f32[6,2,384]{2,1,0:T(2,128)S(1)} %copy-done.3, f32[4,2,384,128]{3,2,1,0:T(8,128)S(1)} %copy-done, ...), custom_call_target="tpu_custom_call" | custom-call | flops 603979776 | bytes 9000000 | tf_op jit(solution)/shard_map/pallas_call | solution.py:23
  28.0 1.3 %collective-permute-done.4 = f32[264,128]{1,0:T(8,128)S(1)} collective-permute-done((f32[264,128]{1,0:T(8,128)S(1)}, f32[264,128]{1,0:T(8,128)S(1)}, u32[]{:S(2)}, u32[]{:S(2)}) %collective-permute-start.4) | collective-permute-done | bytes 135200 | tf_op jit(solution)/shard_map/ppermute | solution.py:416
  29.4 4.1 %collective-permute-done.5 = f32[264,128]{1,0:T(8,128)S(1)} collective-permute-done((f32[264,128]{1,0:T(8,128)S(1)}, f32[264,128]{1,0:T(8,128)S(1)}, u32[]{:S(2)}, u32[]{:S(2)}) %collective-permute-start.5) | collective-permute-done | bytes 135200 | tf_op jit(solution)/shard_map/ppermute | solution.py:419
  33.6 2.4 %collective-permute-start.6 = (f32[264,128]{1,0:T(8,128)S(1)}, f32[264,128]{1,0:T(8,128)S(1)}, u32[]{:S(2)}, u32[]{:S(2)}) collective-permute-start(f32[264,128]{1,0:T(8,128)S(1)} %add.13), channel_id=1, source_target_pairs={{0,4},{1,9},{2,6},{3,11},{4,0},{5,13},{6,2},{7,15},{8,12},{9,1},{1... | collective-permute-start | bytes 405512 | tf_op jit(solution)/shard_map/ppermute | solution.py:419
  36.0 3.3 %collective-permute-done.6 = f32[264,128]{1,0:T(8,128)S(1)} collective-permute-done((f32[264,128]{1,0:T(8,128)S(1)}, f32[264,128]{1,0:T(8,128)S(1)}, u32[]{:S(2)}, u32[]{:S(2)}) %collective-permute-start.6) | collective-permute-done | bytes 135200 | tf_op jit(solution)/shard_map/ppermute | solution.py:419
  39.7 3.5 %collective-permute-done.7 = f32[264,128]{1,0:T(8,128)S(1)} collective-permute-done((f32[264,128]{1,0:T(8,128)S(1)}, f32[264,128]{1,0:T(8,128)S(1)}, u32[]{:S(2)}, u32[]{:S(2)}) %collective-permute-start.7) | collective-permute-done | bytes 135200 | tf_op jit(solution)/shard_map/ppermute | solution.py:419
  43.2 3.5 %collective-permute-start.8 = (f32[264,128]{1,0:T(8,128)S(1)}, f32[264,128]{1,0:T(8,128)S(1)}, u32[]{:S(2)}, u32[]{:S(2)}) collective-permute-start(f32[264,128]{1,0:T(8,128)S(1)} %add.15.mine_ref), channel_id=1, source_target_pairs={{0,1},{1,0},{2,3},{3,2},{4,5},{5,4},{6,7},{7,6},{8,9},{9,8},{10,11... | collective-permute-start | bytes 405512 | tf_op jit(solution)/shard_map/ppermute | solution.py:420
  46.8 1.0 %collective-permute-done.8.other_ref = f32[264,128]{1,0:T(8,128)S(1)} collective-permute-done((f32[264,128]{1,0:T(8,128)S(1)}, f32[264,128]{1,0:T(8,128)S(1)}, u32[]{:S(2)}, u32[]{:S(2)}) %collective-permute-start.8) | collective-permute-done | bytes 135200 | tf_op jit(solution)/shard_map/ppermute | solution.py:420
  47.8 11.7 %shard_map.72 = (bf16[256,256]{1,0:T(8,128)(2,1)S(1)}, bf16[256,256]{1,0:T(8,128)(2,1)S(1)}, bf16[256,256]{1,0:T(8,128)(2,1)S(1)}, bf16[256,256]{1,0:T(8,128)(2,1)S(1)}) custom-call(s32[1]{0:T(128)} %bitcast.2.core_ref, f32[264,128]{1,0:T(8,128)S(1)} %add.15.mine_ref, f32[264,128]{1,0:T(8,128)S(1)} %collective-permute-done.8.other_ref, f32[256,256]{1,0:T(8,128)S(1)} %copy-done.4), custom_call_target="tpu_custom_call" | custom-call | flops 1000000000 | bytes 1000000 | tf_op jit(solution)/shard_map/pallas_call | solution.py:23
  59.5 1.1 %shard_map.73 = (f32[2,2,384,128]{3,2,1,0:T(8,128)S(1)}, f32[2,384,128]{2,1,0:T(8,128)S(1)}, f32[2,384,128]{2,1,0:T(8,128)S(1)}) custom-call(f32[6,2,384]{2,1,0:T(2,128)S(1)} %copy-done.3, bf16[3072,256]{1,0:T(8,128)(2,1)S(1)} %get-tuple-element.36.qh_ref, bf16[3072,256]{1,0:T(8,128)(2,1)S(1)} %get-tuple-element.37.ql_ref, ...), custom_call_target="tpu_custom_call" | custom-call | flops 603979776 | bytes 6000000 | tf_op jit(solution)/shard_map/pallas_call | solution.py:23
  60.6 2.3 %collective-permute-start.10 = (f32[2,384,128]{2,1,0:T(8,128)S(1)}, f32[2,384,128]{2,1,0:T(8,128)S(1)}, u32[]{:S(2)}, u32[]{:S(2)}) collective-permute-start(f32[2,384,128]{2,1,0:T(8,128)S(1)} %get-tuple-element.61.jdown_ref), channel_id=1, source_target_pairs={{1,0},{2,1},{3,2},{4,3},{5,4},{6,5},{7,6},{8,7},{9,8},{10,9},{11,1... | collective-permute-start | bytes 1179656 | tf_op jit(solution)/shard_map/ppermute | solution.py:408
  62.9 3.3 %collective-permute-start.9 = (f32[2,384,128]{2,1,0:T(8,128)S(1)}, f32[2,384,128]{2,1,0:T(8,128)S(1)}, u32[]{:S(2)}, u32[]{:S(2)}) collective-permute-start(f32[2,384,128]{2,1,0:T(8,128)S(1)} %get-tuple-element.62.jup_ref), channel_id=1, source_target_pairs={{0,1},{1,2},{2,3},{3,4},{4,5},{5,6},{6,7},{7,8},{8,9},{9,10},{10,1... | collective-permute-start | bytes 1179656 | tf_op jit(solution)/shard_map/ppermute | solution.py:407
  66.2 1.5 %shard_map.74 = (f32[2,2,384,128]{3,2,1,0:T(8,128)S(1)}, f32[2,384,128]{2,1,0:T(8,128)S(1)}, f32[2,384,128]{2,1,0:T(8,128)S(1)}) custom-call(f32[6,2,384]{2,1,0:T(2,128)S(1)} %copy-done.3, f32[2,2,384,128]{3,2,1,0:T(8,128)S(1)} %get-tuple-element.60.light_ref, f32[2,384,128]{2,1,0:T(8,128)S(1)} %get-tuple-element.61.jdown_ref, ...), custom_call_target="tpu_custom_call" | custom-call | flops 603979776 | bytes 6000000 | tf_op jit(solution)/shard_map/pallas_call | solution.py:23
  67.6 2.0 %collective-permute-start.11 = (f32[2,384,128]{2,1,0:T(8,128)S(1)}, f32[2,384,128]{2,1,0:T(8,128)S(1)}, u32[]{:S(2)}, u32[]{:S(2)}) collective-permute-start(f32[2,384,128]{2,1,0:T(8,128)S(1)} %get-tuple-element.68), channel_id=1, source_target_pairs={{0,1},{1,2},{2,3},{3,4},{4,5},{5,6},{6,7},{7,8},{8,9},{9,10},{10,1... | collective-permute-start | bytes 1179656 | tf_op jit(solution)/shard_map/ppermute | solution.py:407
  69.6 2.3 %collective-permute-start.12 = (f32[2,384,128]{2,1,0:T(8,128)S(1)}, f32[2,384,128]{2,1,0:T(8,128)S(1)}, u32[]{:S(2)}, u32[]{:S(2)}) collective-permute-start(f32[2,384,128]{2,1,0:T(8,128)S(1)} %get-tuple-element.69), channel_id=1, source_target_pairs={{1,0},{2,1},{3,2},{4,3},{5,4},{6,5},{7,6},{8,7},{9,8},{10,9},{11,1... | collective-permute-start | bytes 1179656 | tf_op jit(solution)/shard_map/ppermute | solution.py:408
  72.0 3.0 %shard_map.77 = f32[4,2,384,128]{3,2,1,0:T(8,128)} custom-call(bf16[3072,256]{1,0:T(8,128)(2,1)S(1)} %get-tuple-element.36.qh_ref, bf16[3072,256]{1,0:T(8,128)(2,1)S(1)} %get-tuple-element.37.ql_ref, bf16[3072,128]{1,0:T(8,128)(2,1)S(1)} %get-tuple-element.38.nh_ref, bf16[3072,128]{1,0:T(8,128)(2,1)S(1)} %get-tuple-element.39.nl_ref, ...), custom_call_target="tpu_custom_call" | custom-call | flops 1207959552 | bytes 9000000 | tf_op jit(solution)/shard_map/pallas_call | solution.py:23
  75.0 3.1 %collective-permute-done.10.high_ref = f32[2,384,128]{2,1,0:T(8,128)S(1)} collective-permute-done((f32[2,384,128]{2,1,0:T(8,128)S(1)}, f32[2,384,128]{2,1,0:T(8,128)S(1)}, u32[]{:S(2)}, u32[]{:S(2)}) %collective-permute-start.10) | collective-permute-done | bytes 393248 | tf_op jit(solution)/shard_map/ppermute | solution.py:408
  78.1 2.2 %shard_map.75 = (f32[2,2,384,128]{3,2,1,0:T(8,128)S(1)}, f32[2,2,384,128]{3,2,1,0:T(8,128)S(1)}) custom-call(f32[6,2,384]{2,1,0:T(2,128)S(1)} %copy-done.3, f32[2,2,384,128]{3,2,1,0:T(8,128)S(1)} %get-tuple-element.60.light_ref, f32[2,2,384,128]{3,2,1,0:T(8,128)S(1)} %get-tuple-element.65.heavy_ref, f32[2,384,128]{2,1,0:T(8,128)S(1)} %get-tuple-element.61.jdown_ref, ...), custom_call_target="tpu_custom_call" | custom-call | flops 10000000 | bytes 6000000 | tf_op jit(solution)/shard_map/pallas_call | solution.py:23
  80.3 2.1 %collective-permute-done.11.low_ref = f32[2,384,128]{2,1,0:T(8,128)S(1)} collective-permute-done((f32[2,384,128]{2,1,0:T(8,128)S(1)}, f32[2,384,128]{2,1,0:T(8,128)S(1)}, u32[]{:S(2)}, u32[]{:S(2)}) %collective-permute-start.11) | collective-permute-done | bytes 393248 | tf_op jit(solution)/shard_map/ppermute | solution.py:407
  82.4 1.3 %shard_map.76 = f32[4,2,384,128]{3,2,1,0:T(8,128)} custom-call(f32[2,2,384,128]{3,2,1,0:T(8,128)S(1)} %get-tuple-element.66.light_ref, f32[2,2,384,128]{3,2,1,0:T(8,128)S(1)} %get-tuple-element.67.heavy_ref, f32[2,384,128]{2,1,0:T(8,128)S(1)} %collective-permute-done.11.low_ref, f32[2,384,128]{2,1,0:T(8,128)S(1)} %collective-permute-done.12.high_ref), custom_call_target="tpu_custom_call" | custom-call | flops 1000000 | bytes 6000000 | tf_op jit(solution)/shard_map/pallas_call | solution.py:23
  (18 shorter events, 0.7 us)
Async XLA Ops:
  3.4 16.3 %collective-permute-start.2 = (f32[2,384,128]{2,1,0:T(8,128)}, f32[2,384,128]{2,1,0:T(8,128)S(1)}, u32[]{:S(2)}, u32[]{:S(2)}) collective-permute-start(f32[2,384,128]{2,1,0:T(8,128)} %get-tuple-element.42), channel_id=1, source_target_pairs={{0,1},{1,2},{2,3},{3,4},{4,5},{5,6},{6,7},{7,8},{8,9},{9,10},{10,1... | collective-permute-start | bytes 1179656 | tf_op jit(solution)/shard_map/ppermute | solution.py:407
  7.2 14.9 %collective-permute-start.3 = (f32[2,384,128]{2,1,0:T(8,128)}, f32[2,384,128]{2,1,0:T(8,128)S(1)}, u32[]{:S(2)}, u32[]{:S(2)}) collective-permute-start(f32[2,384,128]{2,1,0:T(8,128)} %get-tuple-element.43), channel_id=1, source_target_pairs={{1,0},{2,1},{3,2},{4,3},{5,4},{6,5},{7,6},{8,7},{9,8},{10,9},{11,1... | collective-permute-start | bytes 1179656 | tf_op jit(solution)/shard_map/ppermute | solution.py:408
  9.1 16.2 %collective-permute-start = (f32[776,128]{1,0:T(8,128)}, f32[776,128]{1,0:T(8,128)S(1)}, u32[]{:S(2)}, u32[]{:S(2)}) collective-permute-start(f32[776,128]{1,0:T(8,128)} %get-tuple-element.40), channel_id=1, source_target_pairs={{0,1},{1,2},{2,3},{3,4},{4,5},{5,6},{6,7},{7,8},{8,9},{9,10},{10,1... | collective-permute-start | bytes 1191944 | tf_op jit(solution)/shard_map/ppermute | solution.py:407
  12.7 13.6 %collective-permute-start.1 = (f32[776,128]{1,0:T(8,128)}, f32[776,128]{1,0:T(8,128)S(1)}, u32[]{:S(2)}, u32[]{:S(2)}) collective-permute-start(f32[776,128]{1,0:T(8,128)} %get-tuple-element.41), channel_id=1, source_target_pairs={{1,0},{2,1},{3,2},{4,3},{5,4},{6,5},{7,6},{8,7},{9,8},{10,9},{11,1... | collective-permute-start | bytes 1191944 | tf_op jit(solution)/shard_map/ppermute | solution.py:408
  14.7 1.9 %copy-start.1 = (f32[4,2,384,256]{3,2,1,0:T(8,128)S(1)}, f32[4,2,384,256]{3,2,1,0:T(8,128)}, u32[]{:S(2)}) copy-start(f32[4,2,384,256]{3,2,1,0:T(8,128)} %param.8) | copy-start | bytes 9437188
  16.6 1.4 %copy-start.2 = (f32[4,2,384,128]{3,2,1,0:T(8,128)S(1)}, f32[4,2,384,128]{3,2,1,0:T(8,128)}, u32[]{:S(2)}) copy-start(f32[4,2,384,128]{3,2,1,0:T(8,128)} %param.7) | copy-start | bytes 4718596
  18.0 4.1 %copy-start = (f32[4,2,384,128]{3,2,1,0:T(8,128)S(1)}, f32[4,2,384,128]{3,2,1,0:T(8,128)}, u32[]{:S(2)}) copy-start(f32[4,2,384,128]{3,2,1,0:T(8,128)} %z_ref.3) | copy-start | bytes 4718596
  18.0 4.1 %copy-start.3 = (f32[6,2,384]{2,1,0:T(2,128)S(1)}, f32[6,2,384]{2,1,0:T(2,128)}, u32[]{:S(2)}) copy-start(f32[6,2,384]{2,1,0:T(2,128)} %coeff_ref.9) | copy-start | bytes 55300
  27.9 19.9 %copy-start.4 = (f32[256,256]{1,0:T(8,128)S(1)}, f32[256,256]{1,0:T(8,128)}, u32[]{:S(2)}) copy-start(f32[256,256]{1,0:T(8,128)} %r_bar_ref.1) | copy-start | bytes 786436
  27.9 1.4 %collective-permute-start.4 = (f32[264,128]{1,0:T(8,128)S(1)}, f32[264,128]{1,0:T(8,128)S(1)}, u32[]{:S(2)}, u32[]{:S(2)}) collective-permute-start(f32[264,128]{1,0:T(8,128)S(1)} %get-tuple-element.55), channel_id=1, source_target_pairs={{0,1},{1,0},{2,3},{3,2},{4,5},{5,4},{6,7},{7,6},{8,9},{9,8},{10,11... | collective-permute-start | bytes 405512 | tf_op jit(solution)/shard_map/ppermute | solution.py:416
  29.4 4.2 %collective-permute-start.5 = (f32[264,128]{1,0:T(8,128)S(1)}, f32[264,128]{1,0:T(8,128)S(1)}, u32[]{:S(2)}, u32[]{:S(2)}) collective-permute-start(f32[264,128]{1,0:T(8,128)S(1)} %add.12), channel_id=1, source_target_pairs={{0,2},{1,5},{2,0},{3,7},{4,6},{5,1},{6,4},{7,3},{8,10},{9,13},{10,... | collective-permute-start | bytes 405512 | tf_op jit(solution)/shard_map/ppermute | solution.py:419
  33.6 5.7 %collective-permute-start.6 = (f32[264,128]{1,0:T(8,128)S(1)}, f32[264,128]{1,0:T(8,128)S(1)}, u32[]{:S(2)}, u32[]{:S(2)}) collective-permute-start(f32[264,128]{1,0:T(8,128)S(1)} %add.13), channel_id=1, source_target_pairs={{0,4},{1,9},{2,6},{3,11},{4,0},{5,13},{6,2},{7,15},{8,12},{9,1},{1... | collective-permute-start | bytes 405512 | tf_op jit(solution)/shard_map/ppermute | solution.py:419
  39.3 3.9 %collective-permute-start.7 = (f32[264,128]{1,0:T(8,128)S(1)}, f32[264,128]{1,0:T(8,128)S(1)}, u32[]{:S(2)}, u32[]{:S(2)}) collective-permute-start(f32[264,128]{1,0:T(8,128)S(1)} %add.14), channel_id=1, source_target_pairs={{0,8},{1,3},{2,10},{3,1},{4,12},{5,7},{6,14},{7,5},{8,0},{9,11},{1... | collective-permute-start | bytes 405512 | tf_op jit(solution)/shard_map/ppermute | solution.py:419
  43.2 4.5 %collective-permute-start.8 = (f32[264,128]{1,0:T(8,128)S(1)}, f32[264,128]{1,0:T(8,128)S(1)}, u32[]{:S(2)}, u32[]{:S(2)}) collective-permute-start(f32[264,128]{1,0:T(8,128)S(1)} %add.15.mine_ref), channel_id=1, source_target_pairs={{0,1},{1,0},{2,3},{3,2},{4,5},{5,4},{6,7},{7,6},{8,9},{9,8},{10,11... | collective-permute-start | bytes 405512 | tf_op jit(solution)/shard_map/ppermute | solution.py:420
  60.6 17.5 %collective-permute-start.10 = (f32[2,384,128]{2,1,0:T(8,128)S(1)}, f32[2,384,128]{2,1,0:T(8,128)S(1)}, u32[]{:S(2)}, u32[]{:S(2)}) collective-permute-start(f32[2,384,128]{2,1,0:T(8,128)S(1)} %get-tuple-element.61.jdown_ref), channel_id=1, source_target_pairs={{1,0},{2,1},{3,2},{4,3},{5,4},{6,5},{7,6},{8,7},{9,8},{10,9},{11,1... | collective-permute-start | bytes 1179656 | tf_op jit(solution)/shard_map/ppermute | solution.py:408
  62.9 15.2 %collective-permute-start.9 = (f32[2,384,128]{2,1,0:T(8,128)S(1)}, f32[2,384,128]{2,1,0:T(8,128)S(1)}, u32[]{:S(2)}, u32[]{:S(2)}) collective-permute-start(f32[2,384,128]{2,1,0:T(8,128)S(1)} %get-tuple-element.62.jup_ref), channel_id=1, source_target_pairs={{0,1},{1,2},{2,3},{3,4},{4,5},{5,6},{6,7},{7,8},{8,9},{9,10},{10,1... | collective-permute-start | bytes 1179656 | tf_op jit(solution)/shard_map/ppermute | solution.py:407
  67.6 14.8 %collective-permute-start.11 = (f32[2,384,128]{2,1,0:T(8,128)S(1)}, f32[2,384,128]{2,1,0:T(8,128)S(1)}, u32[]{:S(2)}, u32[]{:S(2)}) collective-permute-start(f32[2,384,128]{2,1,0:T(8,128)S(1)} %get-tuple-element.68), channel_id=1, source_target_pairs={{0,1},{1,2},{2,3},{3,4},{4,5},{5,6},{6,7},{7,8},{8,9},{9,10},{10,1... | collective-permute-start | bytes 1179656 | tf_op jit(solution)/shard_map/ppermute | solution.py:407
  69.6 12.8 %collective-permute-start.12 = (f32[2,384,128]{2,1,0:T(8,128)S(1)}, f32[2,384,128]{2,1,0:T(8,128)S(1)}, u32[]{:S(2)}, u32[]{:S(2)}) collective-permute-start(f32[2,384,128]{2,1,0:T(8,128)S(1)} %get-tuple-element.69), channel_id=1, source_target_pairs={{1,0},{2,1},{3,2},{4,3},{5,4},{6,5},{7,6},{8,7},{9,8},{10,9},{11,1... | collective-permute-start | bytes 1179656 | tf_op jit(solution)/shard_map/ppermute | solution.py:408

commit v6 on v5

v6 whole, which is shorter than its diff:
```python
import jax
import jax.numpy as jnp
from jax import lax
from jax.experimental import pallas as pl
from jax.experimental.pallas import tpu as pltpu
from jax.sharding import PartitionSpec as P

rate_scales = (0.4, 0.4, 0.1, 0.2, 0.1, 0.1)
exact = lax.Precision.HIGHEST
f32 = jnp.float32
bf16 = jnp.bfloat16
VMEM = pl.BlockSpec(memory_space=pltpu.VMEM)
LIMIT = 24 * 1024 * 1024
FAR_LIMIT = 63 * 1024 * 1024
PANEL = 16


def call(kernel, outs, flops, moved, scratch=(), scalar=False, far=False):
    def run(*args):
        specs = [pl.BlockSpec(memory_space=pltpu.HBM) if far else pl.BlockSpec() for _ in args]
        if scalar:
            specs[0] = pl.BlockSpec(memory_space=pltpu.SMEM)
        return pl.pallas_call(
            kernel,
            out_shape=outs,
            in_specs=specs,
            scratch_shapes=list(scratch),
            compiler_params=pltpu.CompilerParams(vmem_limit_bytes=FAR_LIMIT if far else LIMIT),
            cost_estimate=pl.CostEstimate(flops=flops, bytes_accessed=moved, transcendentals=0),
        )(*args)

    return run


def split2(value):
    high = value.astype(bf16)
    low = (value - high.astype(f32)).astype(bf16)
    return high, low


def split3(value):
    high = value.astype(bf16)
    rest = value - high.astype(f32)
    mid = rest.astype(bf16)
    low = (rest - mid.astype(f32)).astype(bf16)
    return high, mid, low


def dot(a, b, contract):
    return lax.dot_general(a, b, ((contract[0], contract[1]), ((), ())), preferred_element_type=f32)


def coefficients(table_ref):
    return [[table_ref[:, 6 * s + k : 6 * s + k + 1] for k in range(6)] for s in range(2)]


def side(v):
    n = v.shape[0]
    place = lax.broadcasted_iota(jnp.int32, v.shape, 0)
    left = jnp.where(place == 0, 0.0, pltpu.roll(v, 1, 0))
    right = jnp.where(place == n - 1, 0.0, pltpu.roll(v, n - 1, 0))
    return left + right


def forward_light(c, xa, pa, xb, hop_x, hop_p):
    d, w, g, l, m, j = c
    return (
        -0.5 * l * xa - d * pa - j * hop_p,
        d * xa - 0.5 * l * pa - 2.0 * g * xb + j * hop_x,
    )


def forward_heavy(c, xa, xb, pb):
    d, w, g, l, m, j = c
    return w * pb, -w * xb - 0.5 * m * pb - 2.0 * g * xa


def backward_light(c, xa, pa, pb, hop_x, hop_p):
    d, w, g, l, m, j = c
    return (
        -0.5 * l * xa + d * pa - 2.0 * g * pb + hop_p,
        -d * xa - 0.5 * l * pa - hop_x,
    )


def backward_heavy(c, pa, xb, pb):
    d, w, g, l, m, j = c
    return -2.0 * g * pa - w * pb, w * xb - 0.5 * m * pb


def forward_rim(core_ref, coeff_hbm, z_hbm, outer1_ref, outer2_ref, inner_ref, table_ref, coeff_ref, z_ref, sems):
    n = z_ref.shape[2]
    core = core_ref[0]
    copies = [
        pltpu.make_async_copy(z_hbm.at[0:3, core], z_ref.at[0], sems.at[0]),
        pltpu.make_async_copy(z_hbm.at[0:3, 1 - core], z_ref.at[1], sems.at[1]),
        pltpu.make_async_copy(coeff_hbm, coeff_ref, sems.at[2]),
    ]
    for copy in copies:
        copy.start()
    for copy in copies:
        copy.wait()
    cols = jnp.transpose(jnp.concatenate([coeff_ref[k] for k in range(6)], axis=0))
    swapped = core == 1
    both = []
    for s in range(2):
        for k in range(6):
            column = jnp.where(swapped, cols[:, 2 * k + 1 - s : 2 * k + 2 - s], cols[:, 2 * k + s : 2 * k + s + 1])
            both.append(column * rate_scales[k])
    for place, column in enumerate(both):
        table_ref[:, place : place + 1] = column
    far = []
    for s in range(2):
        xa, pa, xb = z_ref[s, 0], z_ref[s, 1], z_ref[s, 2]
        hop_x = z_ref[1 - s, 0] + side(xa)
        hop_p = z_ref[1 - s, 1] + side(pa)
        far.append(forward_light(both[6 * s : 6 * s + 6], xa, pa, xb, hop_x, hop_p))
    outer1_ref[0:n] = z_ref[0, 0]
    outer1_ref[n : 2 * n] = z_ref[0, 1]
    inner_ref[0:n] = z_ref[1, 0]
    inner_ref[n : 2 * n] = z_ref[1, 1]
    for s, out, base in ((0, outer2_ref, 0), (1, inner_ref, 2 * n)):
        out[base : base + n], out[base + n : base + 2 * n] = far[s]
        hopping = jnp.where(swapped, coeff_ref[5, 1 - s : 2 - s, :], coeff_ref[5, s : s + 1, :]) * rate_scales[5]
        pieces = [hopping[:, k * 128 : (k + 1) * 128] for k in range(n // 128)]
        pieces.append(jnp.zeros((8 - n // 128, 128), f32))
        out[base + 2 * n :] = jnp.concatenate(pieces, axis=0)


def far_hopping(recv_ref, n):
    size = recv_ref.shape[0]
    tail = jnp.transpose(recv_ref[size - 8 : size])
    return jnp.concatenate([tail[:, k : k + 1] for k in range(n // 128)], axis=0)


def cells(row, k, n):
    return pl.ds(pl.multiple_of((2 * k + row) * n, 128), n)


def packed(gram, cross):
    row = lax.broadcasted_iota(jnp.int32, gram.shape, 0)
    col = lax.broadcasted_iota(jnp.int32, gram.shape, 1)
    diagonal = jnp.sum(jnp.where(row == col, cross, 0.0), axis=0, keepdims=True)
    return jnp.where(row <= col, gram, cross), jnp.broadcast_to(diagonal, (8, gram.shape[1]))


def noise_products(noise_ref, q_ref, pack_ref, nh_ref, nl_ref, qh_ref, ql_ref, nht_ref, nlt_ref, qht_ref, qlt_ref):
    nh, nl = split2(noise_ref[...])
    qh, ql = split2(q_ref[...])
    nh_ref[...] = nh
    nl_ref[...] = nl
    qh_ref[...] = qh
    ql_ref[...] = ql
    for value, out in ((nh, nht_ref), (nl, nlt_ref), (qh, qht_ref), (ql, qlt_ref)):
        out[...] = jnp.transpose(value)
    plain = ((1,), (0,))
    high = dot(jnp.concatenate([nht_ref[...], qht_ref[128:]], axis=0), jnp.concatenate([nh, nl], axis=1), plain)
    low = dot(qlt_ref[128:], nh, plain)
    mixed = high[:128, 128:]
    gram = high[:128, :128] + mixed + jnp.transpose(mixed)
    cross = high[128:, :128] + high[128:, 128:] + low
    pack_ref[0:128], pack_ref[128:] = packed(gram, cross)


def row_products(xh, xl, nht, nlt, qht, qlt):
    plain = ((1,), (0,))
    left = jnp.concatenate([jnp.transpose(xh), nht, qht], axis=0)
    high = dot(left, jnp.concatenate([xh, xl], axis=1), plain)
    low = dot(jnp.concatenate([nlt, qlt], axis=0), xh, plain)
    mixed = high[:128, 128:]
    return (
        high[:128, :128] + mixed + jnp.transpose(mixed),
        high[128:, :128] + high[128:, 128:] + low,
    )


def expand_first(
    core_ref, table_ref, z_ref, inner_ref, outer1_ref, nht_ref, nlt_ref, qht_ref, qlt_ref,
    light_ref, hh_ref, hl_ref, ih_ref, il_ref, gram_ref, rest_ref, first_ref,
):
    c = coefficients(table_ref)
    n = z_ref.shape[2]
    core = core_ref[0]
    rows = (core, 1 - core)
    z = [[z_ref[k, row] for k in range(4)] for row in rows]
    for s, beyond in enumerate((outer1_ref, inner_ref)):
        xa, pa, xb, pb = z[s]
        hop_x = z[1 - s][0] + beyond[0:n] + side(xa)
        hop_p = z[1 - s][1] + beyond[n : 2 * n] + side(pa)
        first_ref[0, s], first_ref[1, s] = forward_light(c[s], xa, pa, xb, hop_x, hop_p)
        first_ref[2, s], first_ref[3, s] = forward_heavy(c[s], xa, xb, pb)
    for s in range(2):
        xa, pa, xb, pb = (first_ref[k, s] for k in range(4))
        for k, (f, second) in enumerate(zip((xb, pb), forward_heavy(c[s], xa, xb, pb))):
            h, l = split2(z[s][2 + k] + f + 0.5 * second)
            hh_ref[cells(rows[s], k, n)] = h
            hl_ref[cells(rows[s], k, n)] = l
    jfar = far_hopping(inner_ref, n)
    for s in range(2):
        xa, pa, xb, pb = (first_ref[k, s] for k in range(4))
        hop_x = first_ref[0, 1 - s] + side(xa)
        hop_p = first_ref[1, 1 - s] + side(pa)
        if s == 1:
            hop_x = hop_x + inner_ref[2 * n : 3 * n] - jfar * z[s][1]
            hop_p = hop_p + inner_ref[3 * n : 4 * n] + jfar * z[s][0]
        second = forward_light(c[s], xa, pa, xb, hop_x, hop_p)
        for k in range(2):
            value = z[s][k] + first_ref[k, s] + 0.5 * second[k]
            if s == 0:
                light_ref[k] = value
            else:
                ih_ref[k * n : (k + 1) * n], il_ref[k * n : (k + 1) * n] = split2(value)
    half = 4 * n
    parts = (nht_ref, nlt_ref, qht_ref, qlt_ref)
    gram, rest = row_products(hh_ref[...], hl_ref[...], *(ref[:, half:] for ref in parts))
    for k in range(2):
        there = cells(1 - core, k, n)
        here = slice(k * n, (k + 1) * n)
        more = row_products(ih_ref[here], il_ref[here], *(ref[:, there] for ref in parts))
        gram = gram + more[0]
        rest = rest + more[1]
    gram_ref[...] = gram
    rest_ref[...] = rest


def expand_last(
    core_ref, table_ref, z_ref, outer2_ref, light_ref, gram_ref, rest_ref, pack_ref,
    nht_ref, nlt_ref, qht_ref, qlt_ref, mine_ref, other_ref, oh_ref, ol_ref, sums_ref,
):
    n = z_ref.shape[2]
    core = core_ref[0]
    jfar = far_hopping(outer2_ref, n)
    far_x = outer2_ref[0:n] - jfar * z_ref[1, core]
    far_p = outer2_ref[n : 2 * n] + jfar * z_ref[0, core]
    j = 0.5 * table_ref[:, 5:6]
    gram, rest = gram_ref[...], rest_ref[...]
    for k, value in enumerate((light_ref[0] - j * far_p, light_ref[1] + j * far_x)):
        h, l = split2(value)
        oh_ref[k * n : (k + 1) * n] = h
        ol_ref[k * n : (k + 1) * n] = l
        there = cells(core, k, n)
        more = row_products(h, l, *(ref[:, there] for ref in (nht_ref, nlt_ref, qht_ref, qlt_ref)))
        gram = gram + more[0]
        rest = rest + more[1]
    sums_ref[0:128], sums_ref[512:520] = packed(gram, rest[128:256])
    sums_ref[128:256] = jnp.transpose(rest[:128])
    sums_ref[256:384] = rest[256:]
    sums_ref[384:512] = pack_ref[0:128]
    sums_ref[520:528] = pack_ref[128:136]
    mine_ref[...] = sums_ref[pl.ds(pl.multiple_of(core * 264, 8), 264)]
    other_ref[...] = sums_ref[pl.ds(pl.multiple_of((1 - core) * 264, 8), 264)]


def factor(
    core_ref, mine_ref, other_ref, r_bar_ref, nh_ref, nl_ref, sh_ref, sl_ref, sums_ref, a_ref, u_ref, inv_ref
):
    size = 256
    tile = 128
    core = core_ref[0]
    sums_ref[pl.ds(pl.multiple_of(core * 264, 8), 264)] = mine_ref[...]
    sums_ref[pl.ds(pl.multiple_of((1 - core) * 264, 8), 264)] = other_ref[...]
    a_ref[0:tile, 0:tile] = sums_ref[0:tile]
    a_ref[0:tile, tile:size] = sums_ref[tile : 2 * tile]
    a_ref[tile:size, tile:size] = sums_ref[3 * tile : 4 * tile]
    row = lax.broadcasted_iota(jnp.int32, (size, size), 0)
    col = lax.broadcasted_iota(jnp.int32, (size, size), 1)
    a_ref[:, size : 2 * size] = jnp.where(row == col, 1.0, 0.0)
    u_ref[...] = jnp.zeros((size, size), f32)
    inv_ref[...] = jnp.zeros((size, size), f32)
    place = lax.broadcasted_iota(jnp.int32, (8, 3 * tile), 0)
    for start in range(0, size, PANEL):
        base = (start // tile) * tile
        lanes = slice(base, base + 3 * tile)
        offset = start - base
        rows = [jnp.broadcast_to(a_ref[start + i : start + i + 1, lanes], (8, 3 * tile)) for i in range(PANEL)]
        s = {}
        for i in range(PANEL):
            for m in range(i, PANEL):
                s[i, m] = jnp.broadcast_to(rows[i][:, offset + m : offset + m + 1], (8, tile))
        done = []
        for i in range(PANEL):
            inverse = pl.reciprocal(s[i, i])
            root = lax.rsqrt(s[i, i])
            root = root * (1.5 - 0.5 * s[i, i] * root * root)
            for k in range(i + 1, PANEL):
                factor_k = s[i, k] * inverse
                for m in range(k, PANEL):
                    s[k, m] = s[k, m] - factor_k * s[i, m]
                rows[k] = rows[k] - jnp.concatenate([factor_k] * 3, axis=1) * rows[i]
            done.append(rows[i] * jnp.concatenate([root] * 3, axis=1))
        groups = []
        for first in range(0, PANEL, 8):
            group = done[first]
            for i in range(1, 8):
                group = jnp.where(place == i, done[first + i], group)
            groups.append(group)
        panel = jnp.concatenate(groups, axis=0)
        stop = start + PANEL
        if base == 0:
            u_ref[start:stop, :] = panel[:, : 2 * tile]
            inv_ref[start:stop, :tile] = panel[:, 2 * tile :]
        else:
            u_ref[start:stop, tile:] = panel[:, :tile]
            inv_ref[start:stop, :] = panel[:, tile:]
        if stop < size:
            h, m, l = split3(panel)
            width = size - base
            left = jnp.concatenate([h, h, m, m, h, l], axis=0)[:, :width]
            right = jnp.concatenate([h, m, h, m, l, h], axis=0)
            change = dot(left, right, ((0,), (0,)))
            a_ref[stop:, lanes] = a_ref[stop:, lanes] - change[stop - base :]
    upper = jnp.where(row <= col, u_ref[...], 0.0)
    inv = jnp.where(row >= col, inv_ref[...], 0.0)
    bar = jnp.where(row <= col, r_bar_ref[...], 0.0)
    corner = jnp.zeros((tile, tile), f32)
    top = jnp.concatenate([sums_ref[0:tile], corner], axis=1)
    bottom = jnp.concatenate([sums_ref[2 * tile : 3 * tile], sums_ref[3 * tile : 4 * tile]], axis=1)
    cross = jnp.concatenate([top, bottom], axis=0)
    diagonal = jnp.concatenate([sums_ref[512:513], sums_ref[520:521]], axis=1)
    cross = jnp.where(row > col, cross, jnp.where(row == col, diagonal, 0.0))

    def product(a, b, contract):
        return lax.dot_general(a, b, ((contract[0], contract[1]), ((), ())), precision=exact, preferred_element_type=f32)

    across = ((1,), (1,))
    middle = product(upper, bar, across) - product(cross, inv, across)
    symmetric = jnp.where(row >= col, middle, 0.0) + jnp.transpose(jnp.where(row > col, middle, 0.0))
    spread = product(inv, product(symmetric, inv, ((1,), (0,))), ((0,), (0,)))
    nh_ref[...], nl_ref[...] = split2(inv)
    sh_ref[...], sl_ref[...] = split2(spread)


def columns(qh, ql, nh, nl, xh, xl, ih, il, sh, sl):
    plain = ((1,), (0,))
    xh = jnp.concatenate([xh, nh], axis=1)
    xl = jnp.concatenate([xl, nl], axis=1)
    high = dot(qh, jnp.concatenate([ih, il], axis=1), plain) + dot(xh, jnp.concatenate([sh, sl], axis=1), plain)
    return high[:, :128] + high[:, 128:] + dot(ql, ih, plain) + dot(xl, sh, plain)


def gradient_outer(
    core_ref, table_ref, qh_ref, ql_ref, nh_ref, nl_ref, oh_ref, ol_ref, ih_ref, il_ref, sh_ref, sl_ref,
    w_ref, outer1_ref,
):
    n = w_ref.shape[1]
    j = table_ref[:, 5:6]
    weights = [ref[:, :128] for ref in (ih_ref, il_ref, sh_ref, sl_ref)]
    for k in range(2):
        there = cells(core_ref[0], k, n)
        here = slice(k * n, (k + 1) * n)
        parts = [ref[there] for ref in (qh_ref, ql_ref, nh_ref, nl_ref)] + [oh_ref[here], ol_ref[here]]
        w = columns(*parts, *weights)
        w_ref[k] = w
        outer1_ref[here] = j * w


def gradient_rest(
    core_ref, table_ref, outer_ref, outer1_ref, qh_ref, ql_ref, nh_ref, nl_ref, lh_ref, ll_ref, hh_ref, hl_ref,
    ih_ref, il_ref, sh_ref, sl_ref, light_ref, heavy_ref, outer2_ref, inner_ref,
):
    c = coefficients(table_ref)
    n = outer_ref.shape[1]
    core = core_ref[0]
    weights = [ref[:, :128] for ref in (ih_ref, il_ref, sh_ref, sl_ref)]
    left = (qh_ref, ql_ref, nh_ref, nl_ref)
    for k in range(2):
        there = cells(1 - core, k, n)
        here = slice(k * n, (k + 1) * n)
        w = columns(*[ref[there] for ref in left], lh_ref[here], ll_ref[here], *weights)
        light_ref[k] = w
        inner_ref[here] = c[1][5] * w
    for k in (1, 0):
        for s, row in enumerate((core, 1 - core)):
            there = cells(row, 2 + k, n)
            here = cells(row, k, n)
            heavy_ref[k, s] = columns(*[ref[there] for ref in left], hh_ref[here], hl_ref[here], *weights)
    own = (outer1_ref, inner_ref)
    for s, w, out, base in ((0, outer_ref, outer2_ref, 0), (1, light_ref, inner_ref, 2 * n)):
        hop_x = own[1 - s][0:n] + side(own[s][0:n])
        hop_p = own[1 - s][n : 2 * n] + side(own[s][n : 2 * n])
        bx, bp = backward_light(c[s], w[0], w[1], heavy_ref[1, s], hop_x, hop_p)
        out[base : base + n] = c[s][5] * bx
        out[base + n : base + 2 * n] = c[s][5] * bp


def gradient_noise(
    core_ref, qh_ref, ql_ref, nh_ref, nl_ref, oh_ref, ol_ref, lh_ref, ll_ref, hh_ref, hl_ref,
    ih_ref, il_ref, sh_ref, sl_ref, out_ref,
):
    n = out_ref.shape[2]
    core = core_ref[0]
    weights = [ref[:, 128:] for ref in (ih_ref, il_ref, sh_ref, sl_ref)]
    for k in range(4):
        for s, row in enumerate((core, 1 - core)):
            there = cells(row, k, n)
            if k < 2:
                here = slice(k * n, (k + 1) * n)
                x = (oh_ref[here], ol_ref[here]) if s == 0 else (lh_ref[here], ll_ref[here])
            else:
                here = cells(row, k - 2, n)
                x = (hh_ref[here], hl_ref[here])
            out_ref[k, row] = columns(*[ref[there] for ref in (qh_ref, ql_ref, nh_ref, nl_ref)], *x, *weights)


def contract_first(
    table_ref, outer_ref, light_ref, heavy_ref, own1_ref, own_ref, outer1_ref, inner_ref, fouter2_ref, finner_ref,
    out_light_ref, out_heavy_ref, first_ref,
):
    c = coefficients(table_ref)
    n = outer_ref.shape[1]
    w = [
        (outer_ref[0], outer_ref[1], heavy_ref[0, 0], heavy_ref[1, 0]),
        (light_ref[0], light_ref[1], heavy_ref[0, 1], heavy_ref[1, 1]),
    ]
    own = [(ref[0:n], ref[n : 2 * n]) for ref in (own1_ref, own_ref)]
    for s, far in enumerate((outer1_ref, inner_ref)):
        xa, pa, xb, pb = w[s]
        hop_x = own[1 - s][0] + far[0:n] + side(own[s][0])
        hop_p = own[1 - s][1] + far[n : 2 * n] + side(own[s][1])
        first_ref[0, s], first_ref[1, s] = backward_light(c[s], xa, pa, pb, hop_x, hop_p)
        first_ref[2, s], first_ref[3, s] = backward_heavy(c[s], pa, xb, pb)
    for s, fref in enumerate((fouter2_ref, finner_ref)):
        xa, pa, xb, pb = (first_ref[k, s] for k in range(4))
        jfar = far_hopping(fref, n)
        j, jother = c[s][5], c[1 - s][5]
        hop_x = jother * first_ref[0, 1 - s] + jfar * own[s][1] + side(j * xa)
        hop_p = jother * first_ref[1, 1 - s] - jfar * own[s][0] + side(j * pa)
        if s == 1:
            hop_x = hop_x + inner_ref[2 * n : 3 * n]
            hop_p = hop_p + inner_ref[3 * n : 4 * n]
        light = backward_light(c[s], xa, pa, pb, hop_x, hop_p)
        heavy = backward_heavy(c[s], pa, xb, pb)
        for k in range(2):
            out_light_ref[k, s] = w[s][k] + first_ref[k, s] + 0.5 * light[k]
            out_heavy_ref[k, s] = w[s][2 + k] + first_ref[2 + k, s] + 0.5 * heavy[k]


def contract_last(core_ref, light_ref, heavy_ref, outer2_ref, out_ref):
    n = out_ref.shape[2]
    core = core_ref[0]
    out_ref[0, core] = light_ref[0, 0] + 0.5 * outer2_ref[n : 2 * n]
    out_ref[1, core] = light_ref[1, 0] - 0.5 * outer2_ref[0:n]
    for k in range(2):
        out_ref[k, 1 - core] = light_ref[k, 1]
        out_ref[2 + k, core] = heavy_ref[k, 0]
        out_ref[2 + k, 1 - core] = heavy_ref[k, 1]


def swap_inner(message):
    count = lax.axis_size("row")
    return lax.ppermute(message, "row", [(i, i ^ 1) for i in range(count)])


def swap_outer(message):
    count = lax.axis_size("row")
    pairs = [(i, i + 1) for i in range(1, count - 1, 2)]
    return lax.ppermute(message, "row", pairs + [(j, i) for i, j in pairs])


def sum_over_rows(mine, other):
    count = lax.axis_size("row")
    bits = count.bit_length() - 1
    swap = [(i, i ^ 1) for i in range(count)]
    mine = mine + lax.ppermute(other, "row", swap)
    for step in range(bits - 1):
        turn = [1 + step, 1 + (step + 1) % (bits - 1)]
        mine = mine + lax.ppermute(mine, "row", [(i, i ^ (1 << turn[i & 1])) for i in range(count)])
    return mine, lax.ppermute(mine, "row", swap)


def on_device(cell_coeffs, z_factor, noise_cols, q_bar, r_bar):
    quads, lattice, n, rank = z_factor.shape
    flat = quads * lattice * n
    coeffs = cell_coeffs
    core = (lax.axis_index("row") & 1).reshape(1)
    noise = noise_cols.reshape(flat, -1)
    bar = q_bar.reshape(flat, -1)
    shape = jax.ShapeDtypeStruct
    hops = shape((2 * n, rank), f32)
    rim = shape((2 * n + 8, rank), f32)
    table = shape((n, 16), f32)
    outer1, outer2, inner, table = call(
        forward_rim, (hops, rim, shape((4 * n + 8, rank), f32), table), 10**6, 3 * 10**6,
        [
            pltpu.VMEM(cell_coeffs.shape, f32),
            pltpu.VMEM((2, 3, n, rank), f32),
            pltpu.SemaphoreType.DMA((3,)),
        ],
        scalar=True, far=True,
    )(core, coeffs, z_factor)
    outer1, outer2, inner = swap_outer(outer1), swap_outer(outer2), swap_inner(inner)
    wide, tall = shape((flat, 256), bf16), shape((flat, 128), bf16)
    wide_t, tall_t = shape((256, flat), bf16), shape((128, flat), bf16)
    work = 2 * flat * 128 * 128
    pack, nh, nl, qh, ql, nht, nlt, qht, qlt = call(
        noise_products, (shape((136, 128), f32), tall, tall, wide, wide, tall_t, tall_t, wide_t, wide_t),
        work * 5, 9 * 10**6,
    )(noise, bar)
    transposed = (nht, nlt, qht, qlt)
    half, quarter = shape((flat // 2, 128), bf16), shape((flat // 4, 128), bf16)
    single, pair = shape((2, n, rank), f32), shape((2, lattice, n, rank), f32)
    light, hh, hl, lh, ll, gram, rest = call(
        expand_first,
        (single, half, half, quarter, quarter, shape((128, 128), f32), shape((384, 128), f32)),
        work * 8, 9 * 10**6, [pltpu.VMEM(z_factor.shape, f32)], scalar=True,
    )(core, table, z_factor, inner, outer1, *transposed)
    part = shape((264, 128), f32)
    mine, other, oh, ol = call(
        expand_last, (part, part, quarter, quarter), work * 3, 5 * 10**6, [pltpu.VMEM((528, 128), f32)], scalar=True
    )(core, table, z_factor, outer2, light, gram, rest, pack, *transposed)
    mine, other = sum_over_rows(mine, other)
    square = shape((256, 256), bf16)
    weights = call(
        factor, (square,) * 4, 10**9, 10**6,
        [
            pltpu.VMEM((528, 128), f32),
            pltpu.VMEM((256, 512), f32),
            pltpu.VMEM((256, 256), f32),
            pltpu.VMEM((256, 256), f32),
        ],
        scalar=True,
    )(core, mine, other, r_bar)
    left = (qh, ql, nh, nl)
    w_outer, own1 = call(gradient_outer, (single, hops), work * 3, 3 * 10**6, scalar=True)(
        core, table, *left, oh, ol, *weights
    )
    back1 = swap_outer(own1)
    w_inner, w_heavy, own2, own = call(
        gradient_rest, (single, pair, hops, shape((4 * n, rank), f32)), 10**10, 6 * 10**6, scalar=True
    )(core, table, w_outer, own1, *left, lh, ll, hh, hl, *weights)
    back2, back = swap_outer(own2), swap_inner(own)
    noise_grad = call(gradient_noise, shape(noise_cols.shape, f32), 0, 0, scalar=True)(
        core, *left, oh, ol, lh, ll, hh, hl, *weights
    )
    out_light, out_heavy = call(contract_first, (pair, pair), 10**7, 6 * 10**6, [pltpu.VMEM(z_factor.shape, f32)])(
        table, w_outer, w_inner, w_heavy, own1, own, back1, back, outer2, inner
    )
    z_grad = call(contract_last, shape(z_factor.shape, f32), 10**6, 6 * 10**6, scalar=True)(
        core, out_light, out_heavy, back2
    )
    return z_grad, noise_grad


def solution(mesh):
    return jax.shard_map(
        on_device,
        mesh=mesh,
        in_specs=(
            P(None, "row", None),
            P(None, ("grp", "row"), None, None),
            P(None, ("grp", "row"), None, None),
            P(None, ("grp", "row"), None, None),
            P("grp", None),
        ),
        out_specs=(P(None, ("grp", "row"), None, None), P(None, ("grp", "row"), None, None)),
        check_vma=False,
    )
```

time: 84.7 us -> 86.5 us (1.021)
  waiting for transfers between devices: 22.3 us -> 32.6 us
  starting transfers between devices: 27.5 us -> 18.5 us
    ppermute x8 -> x6, waiting for transfers between devices: 9.04 us -> 19.1 us  [the longest x4 19.1 us: swap_outer(): return lax.ppermute(message, 'row', pairs + [(j, i) for i, j in pairs])]
    ppermute x8 -> x6, starting transfers between devices: 21.1 us -> 12.3 us  [the longest x4 11.1 us: swap_outer(): return lax.ppermute(message, 'row', pairs + [(j, i) for i, j in pairs])]
  transfers between devices with their start and end apart: 13 -> 11, of which waited for: 10 -> 9; matrix products, arithmetic and copies ran while one was open for 0% -> 0% of each run, Pallas kernels for 13% -> 12%
where the time goes in v6:
time: 86.5 us; the launch traced here: 85.5 us
  waiting for transfers between devices  32.6 us (38%)
  Pallas kernels  30.2 us (35%)
  starting transfers between devices  18.5 us (21%)
  local copies, waits for them, and re-layouts  3.31 us (4%)
    pallas_call x10, Pallas kernels, run(): pl.pallas_call(kernel, out_shape=outs, in_specs=specs, scratch_shapes=lis...  30.2 us
    ppermute x4, waiting for transfers between devices, swap_outer(): return lax.ppermute(message, 'row', pairs + [(j, i) for i, j in pairs])  19.1 us
    ppermute x3, waiting for transfers between devices, sum_over_rows(): lax.ppermute(mine, 'row', [(i, i ^ 1 << turn[i & 1]) for i in range(count)])  11.1 us
    ppermute x4, starting transfers between devices, swap_outer(): return lax.ppermute(message, 'row', pairs + [(j, i) for i, j in pairs])  11.1 us
    ppermute x1, starting transfers between devices, sum_over_rows(): return (mine, lax.ppermute(mine, 'row', swap))  3.53 us
    unnamed x10, local copies, waits for them, and re-layouts  3.31 us
    ppermute x3, starting transfers between devices, sum_over_rows(): lax.ppermute(mine, 'row', [(i, i ^ 1 << turn[i & 1]) for i in range(count)])  2.67 us
  transfers between devices with their start and end apart: 11, of which 9 were waited for; matrix products, arithmetic and copies ran while one was open for 0% of the time, Pallas kernels for 12%

profile of v6, /device:TPU:9, one launch (start us, length us, event | category | flops | bytes accessed | tf_op | source)
XLA Modules:
  0.0 85.5 jit_solution(5876404641155127605)
XLA Ops:
  0.6 3.7 %shard_map.68 = (f32[768,128]{1,0:T(8,128)}, f32[776,128]{1,0:T(8,128)}, f32[1544,128]{1,0:T(8,128)}, f32[384,16]{1,0:T(8,128)}) custom-call(s32[1]{0:T(128)} %bitcast.core_ref, f32[6,2,384]{2,1,0:T(2,128)} %coeff_hbm.1, f32[4,2,384,128]{3,2,1,0:T(8,128)} %z_ref.3), custom_call_target="tpu_custom_call" | custom-call | flops 1000000 | bytes 3000000 | tf_op jit(solution)/shard_map/pallas_call | solution.py:23
  4.3 0.7 collective-permute-start.1
  5.1 3.0 %collective-permute-start.2 = (f32[768,128]{1,0:T(8,128)}, f32[768,128]{1,0:T(8,128)S(1)}, u32[]{:S(2)}, u32[]{:S(2)}) collective-permute-start(f32[768,128]{1,0:T(8,128)} %get-tuple-element.45), channel_id=1, source_target_pairs={{1,2},{3,4},{5,6},{7,8},{9,10},{11,12},{13,14},{2,1},{4,3},{6,5},{... | collective-permute-start | bytes 1179656 | tf_op jit(solution)/shard_map/ppermute | solution.py:457
  8.1 2.5 %collective-permute-start = (f32[776,128]{1,0:T(8,128)}, f32[776,128]{1,0:T(8,128)S(1)}, u32[]{:S(2)}, u32[]{:S(2)}) collective-permute-start(f32[776,128]{1,0:T(8,128)} %get-tuple-element.43), channel_id=1, source_target_pairs={{1,2},{3,4},{5,6},{7,8},{9,10},{11,12},{13,14},{2,1},{4,3},{6,5},{... | collective-permute-start | bytes 1191944 | tf_op jit(solution)/shard_map/ppermute | solution.py:457
  10.7 1.9 %copy-done.1 = f32[4,2,384,256]{3,2,1,0:T(8,128)S(1)} copy-done((f32[4,2,384,256]{3,2,1,0:T(8,128)S(1)}, f32[4,2,384,256]{3,2,1,0:T(8,128)}, u32[]{:S(2)}) %copy-start.1) | copy-done | bytes 3145752
  12.6 1.4 %copy-done.3 = f32[4,2,384,128]{3,2,1,0:T(8,128)S(1)} copy-done((f32[4,2,384,128]{3,2,1,0:T(8,128)S(1)}, f32[4,2,384,128]{3,2,1,0:T(8,128)}, u32[]{:S(2)}) %copy-start.3) | copy-done | bytes 1572888
  14.0 1.8 %shard_map.69 = (f32[136,128]{1,0:T(8,128)S(1)}, bf16[3072,128]{1,0:T(8,128)(2,1)S(1)}, bf16[3072,128]{1,0:T(8,128)(2,1)S(1)}, bf16[3072,256]{1,0:T(8,128)(2,1)S...) custom-call(f32[3072,128]{1,0:T(8,128)S(1)} %bitcast.4, ...), custom_call_target="tpu_custom_call" | custom-call | flops 503316480 | bytes 9000000 | tf_op jit(solution)/shard_map/pallas_call | solution.py:23
  15.8 7.1 %collective-permute-done.2.outer1_ref = f32[768,128]{1,0:T(8,128)S(1)} collective-permute-done((f32[768,128]{1,0:T(8,128)}, f32[768,128]{1,0:T(8,128)S(1)}, u32[]{:S(2)}, u32[]{:S(2)}) %collective-permute-start.2) | collective-permute-done | bytes 393248 | tf_op jit(solution)/shard_map/ppermute | solution.py:457
  22.9 3.2 %shard_map.70 = (f32[2,384,128]{2,1,0:T(8,128)S(1)}, bf16[1536,128]{1,0:T(8,128)(2,1)S(1)}, bf16[1536,128]{1,0:T(8,128)(2,1)S(1)}, bf16[768,128]{1,0:T(8,128)(2,...) custom-call(s32[1]{0:T(128)} %bitcast.core_ref, f32[384,16]{1,0:T(8,128)S(1)} %copy-done.2, ...), custom_call_target="tpu_custom_call" | custom-call | flops 805306368 | bytes 9000000 | tf_op jit(solution)/shard_map/pallas_call | solution.py:23
  26.1 1.0 %collective-permute-done.outer2_ref.fouter2_ref = f32[776,128]{1,0:T(8,128)S(1)} collective-permute-done((f32[776,128]{1,0:T(8,128)}, f32[776,128]{1,0:T(8,128)S(1)}, u32[]{:S(2)}, u32[]{:S(2)}) %collective-permute-start) | collective-permute-done | bytes 397344 | tf_op jit(solution)/shard_map/ppermute | solution.py:457
  27.1 1.0 %shard_map.71 = (f32[264,128]{1,0:T(8,128)S(1)}, f32[264,128]{1,0:T(8,128)S(1)}, bf16[768,128]{1,0:T(8,128)(2,1)S(1)}, bf16[768,128]{1,0:T(8,128)(2,1)S(1)}) custom-call(s32[1]{0:T(128)} %bitcast.core_ref, f32[384,16]{1,0:T(8,128)S(1)} %copy-done.2, f32[4,2,384,128]{3,2,1,0:T(8,128)S(1)} %copy-done, ...), custom_call_target="tpu_custom_call" | custom-call | flops 301989888 | bytes 5000000 | tf_op jit(solution)/shard_map/pallas_call | solution.py:23
  28.1 0.1 collective-permute-start.3
  28.2 1.3 %collective-permute-done.3 = f32[264,128]{1,0:T(8,128)S(1)} collective-permute-done((f32[264,128]{1,0:T(8,128)S(1)}, f32[264,128]{1,0:T(8,128)S(1)}, u32[]{:S(2)}, u32[]{:S(2)}) %collective-permute-start.3) | collective-permute-done | bytes 135200 | tf_op jit(solution)/shard_map/ppermute | solution.py:464
  29.6 0.1 collective-permute-start.4
  29.6 4.1 %collective-permute-done.4 = f32[264,128]{1,0:T(8,128)S(1)} collective-permute-done((f32[264,128]{1,0:T(8,128)S(1)}, f32[264,128]{1,0:T(8,128)S(1)}, u32[]{:S(2)}, u32[]{:S(2)}) %collective-permute-start.4) | collective-permute-done | bytes 135200 | tf_op jit(solution)/shard_map/ppermute | solution.py:467
  33.8 2.4 %collective-permute-start.5 = (f32[264,128]{1,0:T(8,128)S(1)}, f32[264,128]{1,0:T(8,128)S(1)}, u32[]{:S(2)}, u32[]{:S(2)}) collective-permute-start(f32[264,128]{1,0:T(8,128)S(1)} %add.13), channel_id=1, source_target_pairs={{0,4},{1,9},{2,6},{3,11},{4,0},{5,13},{6,2},{7,15},{8,12},{9,1},{1... | collective-permute-start | bytes 405512 | tf_op jit(solution)/shard_map/ppermute | solution.py:467
  36.2 3.3 %collective-permute-done.5 = f32[264,128]{1,0:T(8,128)S(1)} collective-permute-done((f32[264,128]{1,0:T(8,128)S(1)}, f32[264,128]{1,0:T(8,128)S(1)}, u32[]{:S(2)}, u32[]{:S(2)}) %collective-permute-start.5) | collective-permute-done | bytes 135200 | tf_op jit(solution)/shard_map/ppermute | solution.py:467
  39.5 0.2 collective-permute-start.6
  39.7 3.7 %collective-permute-done.6 = f32[264,128]{1,0:T(8,128)S(1)} collective-permute-done((f32[264,128]{1,0:T(8,128)S(1)}, f32[264,128]{1,0:T(8,128)S(1)}, u32[]{:S(2)}, u32[]{:S(2)}) %collective-permute-start.6) | collective-permute-done | bytes 135200 | tf_op jit(solution)/shard_map/ppermute | solution.py:467
  43.4 3.5 %collective-permute-start.7 = (f32[264,128]{1,0:T(8,128)S(1)}, f32[264,128]{1,0:T(8,128)S(1)}, u32[]{:S(2)}, u32[]{:S(2)}) collective-permute-start(f32[264,128]{1,0:T(8,128)S(1)} %add.15.mine_ref), channel_id=1, source_target_pairs={{0,1},{1,0},{2,3},{3,2},{4,5},{5,4},{6,7},{7,6},{8,9},{9,8},{10,11... | collective-permute-start | bytes 405512 | tf_op jit(solution)/shard_map/ppermute | solution.py:468
  47.0 1.0 %collective-permute-done.7.other_ref = f32[264,128]{1,0:T(8,128)S(1)} collective-permute-done((f32[264,128]{1,0:T(8,128)S(1)}, f32[264,128]{1,0:T(8,128)S(1)}, u32[]{:S(2)}, u32[]{:S(2)}) %collective-permute-start.7) | collective-permute-done | bytes 135200 | tf_op jit(solution)/shard_map/ppermute | solution.py:468
  48.0 11.7 %shard_map.72 = (bf16[256,256]{1,0:T(8,128)(2,1)S(1)}, bf16[256,256]{1,0:T(8,128)(2,1)S(1)}, bf16[256,256]{1,0:T(8,128)(2,1)S(1)}, bf16[256,256]{1,0:T(8,128)(2,1)S(1)}) custom-call(s32[1]{0:T(128)} %bitcast.core_ref, f32[264,128]{1,0:T(8,128)S(1)} %add.15.mine_ref, f32[264,128]{1,0:T(8,128)S(1)} %collective-permute-done.7.other_ref, f32[256,256]{1,0:T(8,128)S(1)} %copy-done.4), custom_call_target="tpu_custom_call" | custom-call | flops 1000000000 | bytes 1000000 | tf_op jit(solution)/shard_map/pallas_call | solution.py:23
  59.7 0.6 shard_map.73
  60.3 1.7 %shard_map.74 = (f32[2,384,128]{2,1,0:T(8,128)S(1)}, f32[2,2,384,128]{3,2,1,0:T(8,128)S(1)}, f32[768,128]{1,0:T(8,128)S(1)}, f32[1536,128]{1,0:T(8,128)S(1)}) custom-call(s32[1]{0:T(128)} %bitcast.core_ref, f32[384,16]{1,0:T(8,128)S(1)} %copy-done.2, f32[2,384,128]{2,1,0:T(8,128)S(1)} %get-tuple-element.62.outer_ref, ...), custom_call_target="tpu_custom_call" | custom-call | flops 10000000000 | bytes 6000000 | tf_op jit(solution)/shard_map/pallas_call | solution.py:23
  62.0 0.4 collective-permute-start.9
  62.5 2.8 %collective-permute-start.8 = (f32[768,128]{1,0:T(8,128)S(1)}, f32[768,128]{1,0:T(8,128)S(1)}, u32[]{:S(2)}, u32[]{:S(2)}) collective-permute-start(f32[768,128]{1,0:T(8,128)S(1)} %get-tuple-element.63.outer1_ref.own1_ref), channel_id=1, source_target_pairs={{1,2},{3,4},{5,6},{7,8},{9,10},{11,12},{13,14},{2,1},{4,3},{6,5},{... | collective-permute-start | bytes 1179656 | tf_op jit(solution)/shard_map/ppermute | solution.py:457
  65.3 2.7 %collective-permute-start.10 = (f32[768,128]{1,0:T(8,128)S(1)}, f32[768,128]{1,0:T(8,128)S(1)}, u32[]{:S(2)}, u32[]{:S(2)}) collective-permute-start(f32[768,128]{1,0:T(8,128)S(1)} %get-tuple-element.73), channel_id=1, source_target_pairs={{1,2},{3,4},{5,6},{7,8},{9,10},{11,12},{13,14},{2,1},{4,3},{6,5},{... | collective-permute-start | bytes 1179656 | tf_op jit(solution)/shard_map/ppermute | solution.py:457
  68.0 3.0 %shard_map.77 = f32[4,2,384,128]{3,2,1,0:T(8,128)} custom-call(s32[1]{0:T(128)} %bitcast.core_ref, bf16[3072,256]{1,0:T(8,128)(2,1)S(1)} %get-tuple-element.39.qh_ref, bf16[3072,256]{1,0:T(8,128)(2,1)S(1)} %get-tuple-element.40.ql_ref, bf16[3072,128]{1,0:T(8,128)(2,1)S(1)} %get-tuple-element.41.nh_ref, bf16[3072,128]{1,0:T(8,128)(2,1)S(1)} %get-tuple-element.42.nl_ref, ...), custom_call_target="tpu_custom_call" | custom-call | tf_op jit(solution)/shard_map/pallas_call | solution.py:23
  71.1 8.9 %collective-permute-done.8.outer1_ref = f32[768,128]{1,0:T(8,128)S(1)} collective-permute-done((f32[768,128]{1,0:T(8,128)S(1)}, f32[768,128]{1,0:T(8,128)S(1)}, u32[]{:S(2)}, u32[]{:S(2)}) %collective-permute-start.8) | collective-permute-done | bytes 393248 | tf_op jit(solution)/shard_map/ppermute | solution.py:457
  80.0 2.2 %shard_map.75 = (f32[2,2,384,128]{3,2,1,0:T(8,128)S(1)}, f32[2,2,384,128]{3,2,1,0:T(8,128)S(1)}) custom-call(f32[384,16]{1,0:T(8,128)S(1)} %copy-done.2, f32[2,384,128]{2,1,0:T(8,128)S(1)} %get-tuple-element.62.outer_ref, f32[2,384,128]{2,1,0:T(8,128)S(1)} %get-tuple-element.68.light_ref, f32[2,2,384,128]{3,2,1,0:T(8,128)S(1)} %get-tuple-element.69.heavy_ref, ...), custom_call_target="tpu_custom_call" | custom-call | flops 10000000 | bytes 6000000 | tf_op jit(solution)/shard_map/pallas_call | solution.py:23
  82.2 2.0 %collective-permute-done.10.outer2_ref = f32[768,128]{1,0:T(8,128)S(1)} collective-permute-done((f32[768,128]{1,0:T(8,128)S(1)}, f32[768,128]{1,0:T(8,128)S(1)}, u32[]{:S(2)}, u32[]{:S(2)}) %collective-permute-start.10) | collective-permute-done | bytes 393248 | tf_op jit(solution)/shard_map/ppermute | solution.py:457
  84.2 1.3 %shard_map.76 = f32[4,2,384,128]{3,2,1,0:T(8,128)} custom-call(s32[1]{0:T(128)} %bitcast.core_ref, f32[2,2,384,128]{3,2,1,0:T(8,128)S(1)} %get-tuple-element.71.light_ref, f32[2,2,384,128]{3,2,1,0:T(8,128)S(1)} %get-tuple-element.72.heavy_ref, f32[768,128]{1,0:T(8,128)S(1)} %collective-permute-done.10.outer2_ref), custom_call_target="tpu_custom_call" | custom-call | flops 1000000 | bytes 6000000 | tf_op jit(solution)/shard_map/pallas_call | solution.py:23
  (14 shorter events, 0.1 us)
Async XLA Ops:
  4.3 18.5 %collective-permute-start.1 = (f32[1544,128]{1,0:T(8,128)}, f32[1544,128]{1,0:T(8,128)S(1)}, u32[]{:S(2)}, u32[]{:S(2)}) collective-permute-start(f32[1544,128]{1,0:T(8,128)} %get-tuple-element.44), channel_id=1, source_target_pairs={{0,1},{1,0},{2,3},{3,2},{4,5},{5,4},{6,7},{7,6},{8,9},{9,8},{10,11... | collective-permute-start | bytes 2371592 | tf_op jit(solution)/shard_map/ppermute | solution.py:451
  5.1 17.8 %collective-permute-start.2 = (f32[768,128]{1,0:T(8,128)}, f32[768,128]{1,0:T(8,128)S(1)}, u32[]{:S(2)}, u32[]{:S(2)}) collective-permute-start(f32[768,128]{1,0:T(8,128)} %get-tuple-element.45), channel_id=1, source_target_pairs={{1,2},{3,4},{5,6},{7,8},{9,10},{11,12},{13,14},{2,1},{4,3},{6,5},{... | collective-permute-start | bytes 1179656 | tf_op jit(solution)/shard_map/ppermute | solution.py:457
  8.1 19.0 %collective-permute-start = (f32[776,128]{1,0:T(8,128)}, f32[776,128]{1,0:T(8,128)S(1)}, u32[]{:S(2)}, u32[]{:S(2)}) collective-permute-start(f32[776,128]{1,0:T(8,128)} %get-tuple-element.43), channel_id=1, source_target_pairs={{1,2},{3,4},{5,6},{7,8},{9,10},{11,12},{13,14},{2,1},{4,3},{6,5},{... | collective-permute-start | bytes 1191944 | tf_op jit(solution)/shard_map/ppermute | solution.py:457
  10.7 1.9 %copy-start.1 = (f32[4,2,384,256]{3,2,1,0:T(8,128)S(1)}, f32[4,2,384,256]{3,2,1,0:T(8,128)}, u32[]{:S(2)}) copy-start(f32[4,2,384,256]{3,2,1,0:T(8,128)} %param.8) | copy-start | bytes 9437188
  12.5 1.4 %copy-start.3 = (f32[4,2,384,128]{3,2,1,0:T(8,128)S(1)}, f32[4,2,384,128]{3,2,1,0:T(8,128)}, u32[]{:S(2)}) copy-start(f32[4,2,384,128]{3,2,1,0:T(8,128)} %param.7) | copy-start | bytes 4718596
  14.0 8.9 %copy-start = (f32[4,2,384,128]{3,2,1,0:T(8,128)S(1)}, f32[4,2,384,128]{3,2,1,0:T(8,128)}, u32[]{:S(2)}) copy-start(f32[4,2,384,128]{3,2,1,0:T(8,128)} %z_ref.3) | copy-start | bytes 4718596
  14.0 8.9 %copy-start.2 = (f32[384,16]{1,0:T(8,128)S(1)}, f32[384,16]{1,0:T(8,128)}, u32[]{:S(2)}) copy-start(f32[384,16]{1,0:T(8,128)} %get-tuple-element.38.table_ref) | copy-start | bytes 73732
  28.1 19.9 %copy-start.4 = (f32[256,256]{1,0:T(8,128)S(1)}, f32[256,256]{1,0:T(8,128)}, u32[]{:S(2)}) copy-start(f32[256,256]{1,0:T(8,128)} %r_bar_ref.1) | copy-start | bytes 786436
  28.1 1.4 %collective-permute-start.3 = (f32[264,128]{1,0:T(8,128)S(1)}, f32[264,128]{1,0:T(8,128)S(1)}, u32[]{:S(2)}, u32[]{:S(2)}) collective-permute-start(f32[264,128]{1,0:T(8,128)S(1)} %get-tuple-element.57), channel_id=1, source_target_pairs={{0,1},{1,0},{2,3},{3,2},{4,5},{5,4},{6,7},{7,6},{8,9},{9,8},{10,11... | collective-permute-start | bytes 405512 | tf_op jit(solution)/shard_map/ppermute | solution.py:464
  29.6 4.2 %collective-permute-start.4 = (f32[264,128]{1,0:T(8,128)S(1)}, f32[264,128]{1,0:T(8,128)S(1)}, u32[]{:S(2)}, u32[]{:S(2)}) collective-permute-start(f32[264,128]{1,0:T(8,128)S(1)} %add.12), channel_id=1, source_target_pairs={{0,2},{1,5},{2,0},{3,7},{4,6},{5,1},{6,4},{7,3},{8,10},{9,13},{10,... | collective-permute-start | bytes 405512 | tf_op jit(solution)/shard_map/ppermute | solution.py:467
  33.8 5.7 %collective-permute-start.5 = (f32[264,128]{1,0:T(8,128)S(1)}, f32[264,128]{1,0:T(8,128)S(1)}, u32[]{:S(2)}, u32[]{:S(2)}) collective-permute-start(f32[264,128]{1,0:T(8,128)S(1)} %add.13), channel_id=1, source_target_pairs={{0,4},{1,9},{2,6},{3,11},{4,0},{5,13},{6,2},{7,15},{8,12},{9,1},{1... | collective-permute-start | bytes 405512 | tf_op jit(solution)/shard_map/ppermute | solution.py:467
  39.5 3.9 %collective-permute-start.6 = (f32[264,128]{1,0:T(8,128)S(1)}, f32[264,128]{1,0:T(8,128)S(1)}, u32[]{:S(2)}, u32[]{:S(2)}) collective-permute-start(f32[264,128]{1,0:T(8,128)S(1)} %add.14), channel_id=1, source_target_pairs={{0,8},{1,3},{2,10},{3,1},{4,12},{5,7},{6,14},{7,5},{8,0},{9,11},{1... | collective-permute-start | bytes 405512 | tf_op jit(solution)/shard_map/ppermute | solution.py:467
  43.4 4.5 %collective-permute-start.7 = (f32[264,128]{1,0:T(8,128)S(1)}, f32[264,128]{1,0:T(8,128)S(1)}, u32[]{:S(2)}, u32[]{:S(2)}) collective-permute-start(f32[264,128]{1,0:T(8,128)S(1)} %add.15.mine_ref), channel_id=1, source_target_pairs={{0,1},{1,0},{2,3},{3,2},{4,5},{5,4},{6,7},{7,6},{8,9},{9,8},{10,11... | collective-permute-start | bytes 405512 | tf_op jit(solution)/shard_map/ppermute | solution.py:468
  62.0 17.9 %collective-permute-start.9 = (f32[1536,128]{1,0:T(8,128)S(1)}, f32[1536,128]{1,0:T(8,128)S(1)}, u32[]{:S(2)}, u32[]{:S(2)}) collective-permute-start(f32[1536,128]{1,0:T(8,128)S(1)} %get-tuple-element.70.own_ref), channel_id=1, source_target_pairs={{0,1},{1,0},{2,3},{3,2},{4,5},{5,4},{6,7},{7,6},{8,9},{9,8},{10,11... | collective-permute-start | bytes 2359304 | tf_op jit(solution)/shard_map/ppermute | solution.py:451
  62.5 17.5 %collective-permute-start.8 = (f32[768,128]{1,0:T(8,128)S(1)}, f32[768,128]{1,0:T(8,128)S(1)}, u32[]{:S(2)}, u32[]{:S(2)}) collective-permute-start(f32[768,128]{1,0:T(8,128)S(1)} %get-tuple-element.63.outer1_ref.own1_ref), channel_id=1, source_target_pairs={{1,2},{3,4},{5,6},{7,8},{9,10},{11,12},{13,14},{2,1},{4,3},{6,5},{... | collective-permute-start | bytes 1179656 | tf_op jit(solution)/shard_map/ppermute | solution.py:457
  65.3 18.9 %collective-permute-start.10 = (f32[768,128]{1,0:T(8,128)S(1)}, f32[768,128]{1,0:T(8,128)S(1)}, u32[]{:S(2)}, u32[]{:S(2)}) collective-permute-start(f32[768,128]{1,0:T(8,128)S(1)} %get-tuple-element.73), channel_id=1, source_target_pairs={{1,2},{3,4},{5,6},{7,8},{9,10},{11,12},{13,14},{2,1},{4,3},{6,5},{... | collective-permute-start | bytes 1179656 | tf_op jit(solution)/shard_map/ppermute | solution.py:457

commit v7 on v6

--- a/solution.py
+++ b/solution.py
@@ -453,8 +453,8 @@
 
 def swap_outer(message):
     count = lax.axis_size("row")
-    pairs = [(i, i + 1) for i in range(1, count - 1, 2)]
-    return lax.ppermute(message, "row", pairs + [(j, i) for i, j in pairs])
+    pairs = [(i, i + 2) for i in range(1, count - 2, 2)] + [(i, i - 2) for i in range(2, count, 2)]
+    return swap_inner(lax.ppermute(message, "row", pairs))
 
 
 def sum_over_rows(mine, other):

time: 86.5 us -> 99.5 us (1.15)
  starting transfers between devices: 18.5 us -> 29 us
  waiting for transfers between devices: 32.6 us -> 35 us
    ppermute x2 -> x6, starting transfers between devices: 1.17 us -> 10.9 us  [swap_inner(): return lax.ppermute(message, 'row', [(i, i ^ 1) for i in range(count)])]
    ppermute x4, waiting for transfers between devices: 19.1 us -> 21.4 us  [swap_outer(): return swap_inner(lax.ppermute(message, 'row', pairs))]
  transfers between devices with their start and end apart: 11 -> 15, of which waited for: 9 -> 9; matrix products, arithmetic and copies ran while one was open for 0% -> 0% of each run, Pallas kernels for 12% -> 12%
where the time goes in v7:
time: 99.5 us; the launch traced here: 98.4 us
  waiting for transfers between devices  35 us (35%)
  Pallas kernels  30.2 us (30%)
  starting transfers between devices  29 us (29%)
  local copies, waits for them, and re-layouts  3.31 us (3%)
    pallas_call x10, Pallas kernels, run(): pl.pallas_call(kernel, out_shape=outs, in_specs=specs, scratch_shapes=lis...  30.2 us
    ppermute x4, waiting for transfers between devices, swap_outer(): return swap_inner(lax.ppermute(message, 'row', pairs))  21.4 us
    ppermute x4, starting transfers between devices, swap_outer(): return swap_inner(lax.ppermute(message, 'row', pairs))  12 us
    ppermute x3, waiting for transfers between devices, sum_over_rows(): lax.ppermute(mine, 'row', [(i, i ^ 1 << turn[i & 1]) for i in range(count)])  11.3 us
    ppermute x6, starting transfers between devices, swap_inner(): return lax.ppermute(message, 'row', [(i, i ^ 1) for i in range(count)])  10.9 us
    ppermute x1, starting transfers between devices, sum_over_rows(): return (mine, lax.ppermute(mine, 'row', swap))  3.53 us
    unnamed x10, local copies, waits for them, and re-layouts  3.31 us
    ppermute x3, starting transfers between devices, sum_over_rows(): lax.ppermute(mine, 'row', [(i, i ^ 1 << turn[i & 1]) for i in range(count)])  2.52 us
  transfers between devices with their start and end apart: 15, of which 9 were waited for; matrix products, arithmetic and copies ran while one was open for 0% of the time, Pallas kernels for 12%

profile of v7, /device:TPU:9, one launch (start us, length us, event | category | flops | bytes accessed | tf_op | source)
XLA Modules:
  0.0 98.4 jit_solution(14334006122128641601)
XLA Ops:
  0.6 3.7 %shard_map.68 = (f32[768,128]{1,0:T(8,128)}, f32[776,128]{1,0:T(8,128)}, f32[1544,128]{1,0:T(8,128)}, f32[384,16]{1,0:T(8,128)}) custom-call(s32[1]{0:T(128)} %bitcast.core_ref, f32[6,2,384]{2,1,0:T(2,128)} %coeff_hbm.1, f32[4,2,384,128]{3,2,1,0:T(8,128)} %z_ref.3), custom_call_target="tpu_custom_call" | custom-call | flops 1000000 | bytes 3000000 | tf_op jit(solution)/shard_map/pallas_call | solution.py:23
  4.3 0.7 collective-permute-start.2
  5.1 3.1 %collective-permute-start.3 = (f32[768,128]{1,0:T(8,128)}, f32[768,128]{1,0:T(8,128)S(1)}, u32[]{:S(2)}, u32[]{:S(2)}) collective-permute-start(f32[768,128]{1,0:T(8,128)} %get-tuple-element.45), channel_id=1, source_target_pairs={{1,3},{3,5},{5,7},{7,9},{9,11},{11,13},{13,15},{2,0},{4,2},{6,4},{... | collective-permute-start | bytes 1179656 | tf_op jit(solution)/shard_map/ppermute | solution.py:457
  8.2 3.1 %collective-permute-start = (f32[776,128]{1,0:T(8,128)}, f32[776,128]{1,0:T(8,128)S(1)}, u32[]{:S(2)}, u32[]{:S(2)}) collective-permute-start(f32[776,128]{1,0:T(8,128)} %get-tuple-element.43), channel_id=1, source_target_pairs={{1,3},{3,5},{5,7},{7,9},{9,11},{11,13},{13,15},{2,0},{4,2},{6,4},{... | collective-permute-start | bytes 1191944 | tf_op jit(solution)/shard_map/ppermute | solution.py:457
  11.4 10.3 %collective-permute-done.3 = f32[768,128]{1,0:T(8,128)S(1)} collective-permute-done((f32[768,128]{1,0:T(8,128)}, f32[768,128]{1,0:T(8,128)S(1)}, u32[]{:S(2)}, u32[]{:S(2)}) %collective-permute-start.3) | collective-permute-done | bytes 393248 | tf_op jit(solution)/shard_map/ppermute | solution.py:457
  21.7 1.7 %collective-permute-start.4 = (f32[768,128]{1,0:T(8,128)S(1)}, f32[768,128]{1,0:T(8,128)S(1)}, u32[]{:S(2)}, u32[]{:S(2)}) collective-permute-start(f32[768,128]{1,0:T(8,128)S(1)} %collective-permute-done.3), channel_id=1, source_target_pairs={{0,1},{1,0},{2,3},{3,2},{4,5},{5,4},{6,7},{7,6},{8,9},{9,8},{10,11... | collective-permute-start | bytes 1179656 | tf_op jit(solution)/shard_map/ppermute | solution.py:451
  23.5 2.5 %collective-permute-done = f32[776,128]{1,0:T(8,128)S(1)} collective-permute-done((f32[776,128]{1,0:T(8,128)}, f32[776,128]{1,0:T(8,128)S(1)}, u32[]{:S(2)}, u32[]{:S(2)}) %collective-permute-start) | collective-permute-done | bytes 397344 | tf_op jit(solution)/shard_map/ppermute | solution.py:457
  26.0 1.7 %collective-permute-start.1 = (f32[776,128]{1,0:T(8,128)S(1)}, f32[776,128]{1,0:T(8,128)S(1)}, u32[]{:S(2)}, u32[]{:S(2)}) collective-permute-start(f32[776,128]{1,0:T(8,128)S(1)} %collective-permute-done), channel_id=1, source_target_pairs={{0,1},{1,0},{2,3},{3,2},{4,5},{5,4},{6,7},{7,6},{8,9},{9,8},{10,11... | collective-permute-start | bytes 1191944 | tf_op jit(solution)/shard_map/ppermute | solution.py:451
  27.7 1.9 %copy-done.1 = f32[4,2,384,256]{3,2,1,0:T(8,128)S(1)} copy-done((f32[4,2,384,256]{3,2,1,0:T(8,128)S(1)}, f32[4,2,384,256]{3,2,1,0:T(8,128)}, u32[]{:S(2)}) %copy-start.1) | copy-done | bytes 3145752
  29.6 1.4 %copy-done.3 = f32[4,2,384,128]{3,2,1,0:T(8,128)S(1)} copy-done((f32[4,2,384,128]{3,2,1,0:T(8,128)S(1)}, f32[4,2,384,128]{3,2,1,0:T(8,128)}, u32[]{:S(2)}) %copy-start.3) | copy-done | bytes 1572888
  31.0 1.8 %shard_map.69 = (f32[136,128]{1,0:T(8,128)S(1)}, bf16[3072,128]{1,0:T(8,128)(2,1)S(1)}, bf16[3072,128]{1,0:T(8,128)(2,1)S(1)}, bf16[3072,256]{1,0:T(8,128)(2,1)S...) custom-call(f32[3072,128]{1,0:T(8,128)S(1)} %bitcast.4, ...), custom_call_target="tpu_custom_call" | custom-call | flops 503316480 | bytes 9000000 | tf_op jit(solution)/shard_map/pallas_call | solution.py:23
  32.8 3.2 %shard_map.70 = (f32[2,384,128]{2,1,0:T(8,128)S(1)}, bf16[1536,128]{1,0:T(8,128)(2,1)S(1)}, bf16[1536,128]{1,0:T(8,128)(2,1)S(1)}, bf16[768,128]{1,0:T(8,128)(2,...) custom-call(s32[1]{0:T(128)} %bitcast.core_ref, f32[384,16]{1,0:T(8,128)S(1)} %copy-done.2, ...), custom_call_target="tpu_custom_call" | custom-call | flops 805306368 | bytes 9000000 | tf_op jit(solution)/shard_map/pallas_call | solution.py:23
  36.1 1.0 %shard_map.71 = (f32[264,128]{1,0:T(8,128)S(1)}, f32[264,128]{1,0:T(8,128)S(1)}, bf16[768,128]{1,0:T(8,128)(2,1)S(1)}, bf16[768,128]{1,0:T(8,128)(2,1)S(1)}) custom-call(s32[1]{0:T(128)} %bitcast.core_ref, f32[384,16]{1,0:T(8,128)S(1)} %copy-done.2, f32[4,2,384,128]{3,2,1,0:T(8,128)S(1)} %copy-done, ...), custom_call_target="tpu_custom_call" | custom-call | flops 301989888 | bytes 5000000 | tf_op jit(solution)/shard_map/pallas_call | solution.py:23
  37.2 1.3 %collective-permute-done.5 = f32[264,128]{1,0:T(8,128)S(1)} collective-permute-done((f32[264,128]{1,0:T(8,128)S(1)}, f32[264,128]{1,0:T(8,128)S(1)}, u32[]{:S(2)}, u32[]{:S(2)}) %collective-permute-start.5) | collective-permute-done | bytes 135200 | tf_op jit(solution)/shard_map/ppermute | solution.py:464
  38.6 4.1 %collective-permute-done.6 = f32[264,128]{1,0:T(8,128)S(1)} collective-permute-done((f32[264,128]{1,0:T(8,128)S(1)}, f32[264,128]{1,0:T(8,128)S(1)}, u32[]{:S(2)}, u32[]{:S(2)}) %collective-permute-start.6) | collective-permute-done | bytes 135200 | tf_op jit(solution)/shard_map/ppermute | solution.py:467
  42.8 2.4 %collective-permute-start.7 = (f32[264,128]{1,0:T(8,128)S(1)}, f32[264,128]{1,0:T(8,128)S(1)}, u32[]{:S(2)}, u32[]{:S(2)}) collective-permute-start(f32[264,128]{1,0:T(8,128)S(1)} %add.13), channel_id=1, source_target_pairs={{0,4},{1,9},{2,6},{3,11},{4,0},{5,13},{6,2},{7,15},{8,12},{9,1},{1... | collective-permute-start | bytes 405512 | tf_op jit(solution)/shard_map/ppermute | solution.py:467
  45.2 3.3 %collective-permute-done.7 = f32[264,128]{1,0:T(8,128)S(1)} collective-permute-done((f32[264,128]{1,0:T(8,128)S(1)}, f32[264,128]{1,0:T(8,128)S(1)}, u32[]{:S(2)}, u32[]{:S(2)}) %collective-permute-start.7) | collective-permute-done | bytes 135200 | tf_op jit(solution)/shard_map/ppermute | solution.py:467
  48.6 3.8 %collective-permute-done.8 = f32[264,128]{1,0:T(8,128)S(1)} collective-permute-done((f32[264,128]{1,0:T(8,128)S(1)}, f32[264,128]{1,0:T(8,128)S(1)}, u32[]{:S(2)}, u32[]{:S(2)}) %collective-permute-start.8) | collective-permute-done | bytes 135200 | tf_op jit(solution)/shard_map/ppermute | solution.py:467
  52.4 3.5 %collective-permute-start.9 = (f32[264,128]{1,0:T(8,128)S(1)}, f32[264,128]{1,0:T(8,128)S(1)}, u32[]{:S(2)}, u32[]{:S(2)}) collective-permute-start(f32[264,128]{1,0:T(8,128)S(1)} %add.15.mine_ref), channel_id=1, source_target_pairs={{0,1},{1,0},{2,3},{3,2},{4,5},{5,4},{6,7},{7,6},{8,9},{9,8},{10,11... | collective-permute-start | bytes 405512 | tf_op jit(solution)/shard_map/ppermute | solution.py:468
  56.0 1.0 %collective-permute-done.9.other_ref = f32[264,128]{1,0:T(8,128)S(1)} collective-permute-done((f32[264,128]{1,0:T(8,128)S(1)}, f32[264,128]{1,0:T(8,128)S(1)}, u32[]{:S(2)}, u32[]{:S(2)}) %collective-permute-start.9) | collective-permute-done | bytes 135200 | tf_op jit(solution)/shard_map/ppermute | solution.py:468
  57.0 11.7 %shard_map.72 = (bf16[256,256]{1,0:T(8,128)(2,1)S(1)}, bf16[256,256]{1,0:T(8,128)(2,1)S(1)}, bf16[256,256]{1,0:T(8,128)(2,1)S(1)}, bf16[256,256]{1,0:T(8,128)(2,1)S(1)}) custom-call(s32[1]{0:T(128)} %bitcast.core_ref, f32[264,128]{1,0:T(8,128)S(1)} %add.15.mine_ref, f32[264,128]{1,0:T(8,128)S(1)} %collective-permute-done.9.other_ref, f32[256,256]{1,0:T(8,128)S(1)} %copy-done.4), custom_call_target="tpu_custom_call" | custom-call | flops 1000000000 | bytes 1000000 | tf_op jit(solution)/shard_map/pallas_call | solution.py:23
  68.7 0.6 shard_map.73
  69.3 2.1 %collective-permute-start.10 = (f32[768,128]{1,0:T(8,128)S(1)}, f32[768,128]{1,0:T(8,128)S(1)}, u32[]{:S(2)}, u32[]{:S(2)}) collective-permute-start(f32[768,128]{1,0:T(8,128)S(1)} %get-tuple-element.63.outer1_ref.own1_ref), channel_id=1, source_target_pairs={{1,3},{3,5},{5,7},{7,9},{9,11},{11,13},{13,15},{2,0},{4,2},{6,4},{... | collective-permute-start | bytes 1179656 | tf_op jit(solution)/shard_map/ppermute | solution.py:457
  71.4 1.7 %shard_map.74 = (f32[2,384,128]{2,1,0:T(8,128)S(1)}, f32[2,2,384,128]{3,2,1,0:T(8,128)S(1)}, f32[768,128]{1,0:T(8,128)S(1)}, f32[1536,128]{1,0:T(8,128)S(1)}) custom-call(s32[1]{0:T(128)} %bitcast.core_ref, f32[384,16]{1,0:T(8,128)S(1)} %copy-done.2, f32[2,384,128]{2,1,0:T(8,128)S(1)} %get-tuple-element.62.outer_ref, ...), custom_call_target="tpu_custom_call" | custom-call | flops 10000000000 | bytes 6000000 | tf_op jit(solution)/shard_map/pallas_call | solution.py:23
  73.4 3.6 %collective-permute-start.13 = (f32[768,128]{1,0:T(8,128)S(1)}, f32[768,128]{1,0:T(8,128)S(1)}, u32[]{:S(2)}, u32[]{:S(2)}) collective-permute-start(f32[768,128]{1,0:T(8,128)S(1)} %get-tuple-element.73), channel_id=1, source_target_pairs={{1,3},{3,5},{5,7},{7,9},{9,11},{11,13},{13,15},{2,0},{4,2},{6,4},{... | collective-permute-start | bytes 1179656 | tf_op jit(solution)/shard_map/ppermute | solution.py:457
  77.0 7.5 %collective-permute-done.10 = f32[768,128]{1,0:T(8,128)S(1)} collective-permute-done((f32[768,128]{1,0:T(8,128)S(1)}, f32[768,128]{1,0:T(8,128)S(1)}, u32[]{:S(2)}, u32[]{:S(2)}) %collective-permute-start.10) | collective-permute-done | bytes 393248 | tf_op jit(solution)/shard_map/ppermute | solution.py:457
  84.6 3.2 %collective-permute-start.11 = (f32[768,128]{1,0:T(8,128)S(1)}, f32[768,128]{1,0:T(8,128)S(1)}, u32[]{:S(2)}, u32[]{:S(2)}) collective-permute-start(f32[768,128]{1,0:T(8,128)S(1)} %collective-permute-done.10), channel_id=1, source_target_pairs={{0,1},{1,0},{2,3},{3,2},{4,5},{5,4},{6,7},{7,6},{8,9},{9,8},{10,11... | collective-permute-start | bytes 1179656 | tf_op jit(solution)/shard_map/ppermute | solution.py:451
  87.8 1.0 %collective-permute-done.13 = f32[768,128]{1,0:T(8,128)S(1)} collective-permute-done((f32[768,128]{1,0:T(8,128)S(1)}, f32[768,128]{1,0:T(8,128)S(1)}, u32[]{:S(2)}, u32[]{:S(2)}) %collective-permute-start.13) | collective-permute-done | bytes 393248 | tf_op jit(solution)/shard_map/ppermute | solution.py:457
  88.8 3.2 %collective-permute-start.14 = (f32[768,128]{1,0:T(8,128)S(1)}, f32[768,128]{1,0:T(8,128)S(1)}, u32[]{:S(2)}, u32[]{:S(2)}) collective-permute-start(f32[768,128]{1,0:T(8,128)S(1)} %collective-permute-done.13), channel_id=1, source_target_pairs={{0,1},{1,0},{2,3},{3,2},{4,5},{5,4},{6,7},{7,6},{8,9},{9,8},{10,11... | collective-permute-start | bytes 1179656 | tf_op jit(solution)/shard_map/ppermute | solution.py:451
  92.0 3.0 %shard_map.77 = f32[4,2,384,128]{3,2,1,0:T(8,128)} custom-call(s32[1]{0:T(128)} %bitcast.core_ref, bf16[3072,256]{1,0:T(8,128)(2,1)S(1)} %get-tuple-element.39.qh_ref, bf16[3072,256]{1,0:T(8,128)(2,1)S(1)} %get-tuple-element.40.ql_ref, bf16[3072,128]{1,0:T(8,128)(2,1)S(1)} %get-tuple-element.41.nh_ref, bf16[3072,128]{1,0:T(8,128)(2,1)S(1)} %get-tuple-element.42.nl_ref, ...), custom_call_target="tpu_custom_call" | custom-call | tf_op jit(solution)/shard_map/pallas_call | solution.py:23
  95.0 2.2 %shard_map.75 = (f32[2,2,384,128]{3,2,1,0:T(8,128)S(1)}, f32[2,2,384,128]{3,2,1,0:T(8,128)S(1)}) custom-call(f32[384,16]{1,0:T(8,128)S(1)} %copy-done.2, f32[2,384,128]{2,1,0:T(8,128)S(1)} %get-tuple-element.62.outer_ref, f32[2,384,128]{2,1,0:T(8,128)S(1)} %get-tuple-element.68.light_ref, f32[2,2,384,128]{3,2,1,0:T(8,128)S(1)} %get-tuple-element.69.heavy_ref, ...), custom_call_target="tpu_custom_call" | custom-call | flops 10000000 | bytes 6000000 | tf_op jit(solution)/shard_map/pallas_call | solution.py:23
  97.2 1.3 %shard_map.76 = f32[4,2,384,128]{3,2,1,0:T(8,128)} custom-call(s32[1]{0:T(128)} %bitcast.core_ref, f32[2,2,384,128]{3,2,1,0:T(8,128)S(1)} %get-tuple-element.71.light_ref, f32[2,2,384,128]{3,2,1,0:T(8,128)S(1)} %get-tuple-element.72.heavy_ref, f32[768,128]{1,0:T(8,128)S(1)} %collective-permute-done.14.outer2_ref), custom_call_target="tpu_custom_call" | custom-call | flops 1000000 | bytes 6000000 | tf_op jit(solution)/shard_map/pallas_call | solution.py:23
  (22 shorter events, 0.6 us)
Async XLA Ops:
  4.3 28.5 %collective-permute-start.2 = (f32[1544,128]{1,0:T(8,128)}, f32[1544,128]{1,0:T(8,128)S(1)}, u32[]{:S(2)}, u32[]{:S(2)}) collective-permute-start(f32[1544,128]{1,0:T(8,128)} %get-tuple-element.44), channel_id=1, source_target_pairs={{0,1},{1,0},{2,3},{3,2},{4,5},{5,4},{6,7},{7,6},{8,9},{9,8},{10,11... | collective-permute-start | bytes 2371592 | tf_op jit(solution)/shard_map/ppermute | solution.py:451
  5.1 16.6 %collective-permute-start.3 = (f32[768,128]{1,0:T(8,128)}, f32[768,128]{1,0:T(8,128)S(1)}, u32[]{:S(2)}, u32[]{:S(2)}) collective-permute-start(f32[768,128]{1,0:T(8,128)} %get-tuple-element.45), channel_id=1, source_target_pairs={{1,3},{3,5},{5,7},{7,9},{9,11},{11,13},{13,15},{2,0},{4,2},{6,4},{... | collective-permute-start | bytes 1179656 | tf_op jit(solution)/shard_map/ppermute | solution.py:457
  8.2 17.7 %collective-permute-start = (f32[776,128]{1,0:T(8,128)}, f32[776,128]{1,0:T(8,128)S(1)}, u32[]{:S(2)}, u32[]{:S(2)}) collective-permute-start(f32[776,128]{1,0:T(8,128)} %get-tuple-element.43), channel_id=1, source_target_pairs={{1,3},{3,5},{5,7},{7,9},{9,11},{11,13},{13,15},{2,0},{4,2},{6,4},{... | collective-permute-start | bytes 1191944 | tf_op jit(solution)/shard_map/ppermute | solution.py:457
  21.7 11.1 %collective-permute-start.4 = (f32[768,128]{1,0:T(8,128)S(1)}, f32[768,128]{1,0:T(8,128)S(1)}, u32[]{:S(2)}, u32[]{:S(2)}) collective-permute-start(f32[768,128]{1,0:T(8,128)S(1)} %collective-permute-done.3), channel_id=1, source_target_pairs={{0,1},{1,0},{2,3},{3,2},{4,5},{5,4},{6,7},{7,6},{8,9},{9,8},{10,11... | collective-permute-start | bytes 1179656 | tf_op jit(solution)/shard_map/ppermute | solution.py:451
  26.0 10.1 %collective-permute-start.1 = (f32[776,128]{1,0:T(8,128)S(1)}, f32[776,128]{1,0:T(8,128)S(1)}, u32[]{:S(2)}, u32[]{:S(2)}) collective-permute-start(f32[776,128]{1,0:T(8,128)S(1)} %collective-permute-done), channel_id=1, source_target_pairs={{0,1},{1,0},{2,3},{3,2},{4,5},{5,4},{6,7},{7,6},{8,9},{9,8},{10,11... | collective-permute-start | bytes 1191944 | tf_op jit(solution)/shard_map/ppermute | solution.py:451
  27.7 1.9 %copy-start.1 = (f32[4,2,384,256]{3,2,1,0:T(8,128)S(1)}, f32[4,2,384,256]{3,2,1,0:T(8,128)}, u32[]{:S(2)}) copy-start(f32[4,2,384,256]{3,2,1,0:T(8,128)} %param.8) | copy-start | bytes 9437188
  29.6 1.4 %copy-start.3 = (f32[4,2,384,128]{3,2,1,0:T(8,128)S(1)}, f32[4,2,384,128]{3,2,1,0:T(8,128)}, u32[]{:S(2)}) copy-start(f32[4,2,384,128]{3,2,1,0:T(8,128)} %param.7) | copy-start | bytes 4718596
  31.0 1.8 %copy-start = (f32[4,2,384,128]{3,2,1,0:T(8,128)S(1)}, f32[4,2,384,128]{3,2,1,0:T(8,128)}, u32[]{:S(2)}) copy-start(f32[4,2,384,128]{3,2,1,0:T(8,128)} %z_ref.3) | copy-start | bytes 4718596
  31.0 1.8 %copy-start.2 = (f32[384,16]{1,0:T(8,128)S(1)}, f32[384,16]{1,0:T(8,128)}, u32[]{:S(2)}) copy-start(f32[384,16]{1,0:T(8,128)} %get-tuple-element.38.table_ref) | copy-start | bytes 73732
  37.1 19.9 %copy-start.4 = (f32[256,256]{1,0:T(8,128)S(1)}, f32[256,256]{1,0:T(8,128)}, u32[]{:S(2)}) copy-start(f32[256,256]{1,0:T(8,128)} %r_bar_ref.1) | copy-start | bytes 786436
  37.1 1.4 %collective-permute-start.5 = (f32[264,128]{1,0:T(8,128)S(1)}, f32[264,128]{1,0:T(8,128)S(1)}, u32[]{:S(2)}, u32[]{:S(2)}) collective-permute-start(f32[264,128]{1,0:T(8,128)S(1)} %get-tuple-element.57), channel_id=1, source_target_pairs={{0,1},{1,0},{2,3},{3,2},{4,5},{5,4},{6,7},{7,6},{8,9},{9,8},{10,11... | collective-permute-start | bytes 405512 | tf_op jit(solution)/shard_map/ppermute | solution.py:464
  38.6 4.2 %collective-permute-start.6 = (f32[264,128]{1,0:T(8,128)S(1)}, f32[264,128]{1,0:T(8,128)S(1)}, u32[]{:S(2)}, u32[]{:S(2)}) collective-permute-start(f32[264,128]{1,0:T(8,128)S(1)} %add.12), channel_id=1, source_target_pairs={{0,2},{1,5},{2,0},{3,7},{4,6},{5,1},{6,4},{7,3},{8,10},{9,13},{10,... | collective-permute-start | bytes 405512 | tf_op jit(solution)/shard_map/ppermute | solution.py:467
  42.8 5.7 %collective-permute-start.7 = (f32[264,128]{1,0:T(8,128)S(1)}, f32[264,128]{1,0:T(8,128)S(1)}, u32[]{:S(2)}, u32[]{:S(2)}) collective-permute-start(f32[264,128]{1,0:T(8,128)S(1)} %add.13), channel_id=1, source_target_pairs={{0,4},{1,9},{2,6},{3,11},{4,0},{5,13},{6,2},{7,15},{8,12},{9,1},{1... | collective-permute-start | bytes 405512 | tf_op jit(solution)/shard_map/ppermute | solution.py:467
  48.5 3.9 %collective-permute-start.8 = (f32[264,128]{1,0:T(8,128)S(1)}, f32[264,128]{1,0:T(8,128)S(1)}, u32[]{:S(2)}, u32[]{:S(2)}) collective-permute-start(f32[264,128]{1,0:T(8,128)S(1)} %add.14), channel_id=1, source_target_pairs={{0,8},{1,3},{2,10},{3,1},{4,12},{5,7},{6,14},{7,5},{8,0},{9,11},{1... | collective-permute-start | bytes 405512 | tf_op jit(solution)/shard_map/ppermute | solution.py:467
  52.4 4.5 %collective-permute-start.9 = (f32[264,128]{1,0:T(8,128)S(1)}, f32[264,128]{1,0:T(8,128)S(1)}, u32[]{:S(2)}, u32[]{:S(2)}) collective-permute-start(f32[264,128]{1,0:T(8,128)S(1)} %add.15.mine_ref), channel_id=1, source_target_pairs={{0,1},{1,0},{2,3},{3,2},{4,5},{5,4},{6,7},{7,6},{8,9},{9,8},{10,11... | collective-permute-start | bytes 405512 | tf_op jit(solution)/shard_map/ppermute | solution.py:468
  69.3 15.3 %collective-permute-start.10 = (f32[768,128]{1,0:T(8,128)S(1)}, f32[768,128]{1,0:T(8,128)S(1)}, u32[]{:S(2)}, u32[]{:S(2)}) collective-permute-start(f32[768,128]{1,0:T(8,128)S(1)} %get-tuple-element.63.outer1_ref.own1_ref), channel_id=1, source_target_pairs={{1,3},{3,5},{5,7},{7,9},{9,11},{11,13},{13,15},{2,0},{4,2},{6,4},{... | collective-permute-start | bytes 1179656 | tf_op jit(solution)/shard_map/ppermute | solution.py:457
  73.2 21.8 %collective-permute-start.12 = (f32[1536,128]{1,0:T(8,128)S(1)}, f32[1536,128]{1,0:T(8,128)S(1)}, u32[]{:S(2)}, u32[]{:S(2)}) collective-permute-start(f32[1536,128]{1,0:T(8,128)S(1)} %get-tuple-element.70.own_ref), channel_id=1, source_target_pairs={{0,1},{1,0},{2,3},{3,2},{4,5},{5,4},{6,7},{7,6},{8,9},{9,8},{10,11... | collective-permute-start | bytes 2359304 | tf_op jit(solution)/shard_map/ppermute | solution.py:451
  73.4 15.4 %collective-permute-start.13 = (f32[768,128]{1,0:T(8,128)S(1)}, f32[768,128]{1,0:T(8,128)S(1)}, u32[]{:S(2)}, u32[]{:S(2)}) collective-permute-start(f32[768,128]{1,0:T(8,128)S(1)} %get-tuple-element.73), channel_id=1, source_target_pairs={{1,3},{3,5},{5,7},{7,9},{9,11},{11,13},{13,15},{2,0},{4,2},{6,4},{... | collective-permute-start | bytes 1179656 | tf_op jit(solution)/shard_map/ppermute | solution.py:457
  84.6 10.4 %collective-permute-start.11 = (f32[768,128]{1,0:T(8,128)S(1)}, f32[768,128]{1,0:T(8,128)S(1)}, u32[]{:S(2)}, u32[]{:S(2)}) collective-permute-start(f32[768,128]{1,0:T(8,128)S(1)} %collective-permute-done.10), channel_id=1, source_target_pairs={{0,1},{1,0},{2,3},{3,2},{4,5},{5,4},{6,7},{7,6},{8,9},{9,8},{10,11... | collective-permute-start | bytes 1179656 | tf_op jit(solution)/shard_map/ppermute | solution.py:451
  88.8 8.4 %collective-permute-start.14 = (f32[768,128]{1,0:T(8,128)S(1)}, f32[768,128]{1,0:T(8,128)S(1)}, u32[]{:S(2)}, u32[]{:S(2)}) collective-permute-start(f32[768,128]{1,0:T(8,128)S(1)} %collective-permute-done.13), channel_id=1, source_target_pairs={{0,1},{1,0},{2,3},{3,2},{4,5},{5,4},{6,7},{7,6},{8,9},{9,8},{10,11... | collective-permute-start | bytes 1179656 | tf_op jit(solution)/shard_map/ppermute | solution.py:451

commit v8 on v6

--- a/solution.py
+++ b/solution.py
@@ -12,7 +12,6 @@
 VMEM = pl.BlockSpec(memory_space=pltpu.VMEM)
 LIMIT = 24 * 1024 * 1024
 FAR_LIMIT = 63 * 1024 * 1024
-PANEL = 16
 
 
 def call(kernel, outs, flops, moved, scratch=(), scalar=False, far=False):
@@ -251,81 +250,114 @@
     other_ref[...] = sums_ref[pl.ds(pl.multiple_of((1 - core) * 264, 8), 264)]
 
 
+def inverse_factor(w_ref, out_ref):
+    size = w_ref.shape[0]
+    step = 8
+    lane = lax.broadcasted_iota(jnp.int32, (step, size), 1)
+    place = lax.broadcasted_iota(jnp.int32, (step, size), 0)
+
+    def load(start):
+        return [jnp.broadcast_to(w_ref[start + i : start + i + 1, :], (step, size)) for i in range(step)]
+
+    rows = load(0)
+    for start in range(0, size, step):
+        last = start + step >= size
+        reach = step if last else 2 * step
+        s = {
+            (i, m): jnp.broadcast_to(rows[i][:, start + m : start + m + 1], (step, size))
+            for i in range(step)
+            for m in range(i, reach)
+        }
+        inside = (lane >= start) & (lane < start + step)
+        rows = [jnp.where(lane == start + i, 1.0, jnp.where(inside, 0.0, rows[i])) for i in range(step)]
+        if not last:
+            following = [jnp.where(inside, 0.0, row) for row in load(start + step)]
+        done = []
+        for i in range(step):
+            inverse = pl.reciprocal(s[i, i])
+            root = lax.rsqrt(s[i, i])
+            for k in range(i + 1, step):
+                ratio = s[i, k] * inverse
+                for m in range(k, reach):
+                    s[k, m] = s[k, m] - ratio * s[i, m]
+                rows[k] = rows[k] - ratio * rows[i]
+            if not last:
+                scaled = rows[i] * inverse
+                for k in range(step):
+                    following[k] = following[k] - s[i, step + k] * scaled
+            done.append(rows[i] * root)
+        panel = done[0]
+        for i in range(1, step):
+            panel = jnp.where(place == i, done[i], panel)
+        out_ref[start : start + step, :] = panel
+        beyond = start + 2 * step
+        if beyond < size:
+            high, mid, low = (part.astype(f32) for part in split3(panel))
+            left = jnp.concatenate([high, high, mid, mid, high, low], axis=0).astype(bf16)
+            right = jnp.concatenate([high, mid, high, mid, low, high], axis=0).astype(bf16)
+            change = dot(left, right, ((0,), (0,)))[beyond:]
+            old = w_ref[beyond:, :]
+            column = lax.broadcasted_iota(jnp.int32, old.shape, 1)
+            old = jnp.where((column >= start) & (column < start + step), 0.0, old)
+            w_ref[beyond:, :] = old - change
+        if not last:
+            rows = following
+    value = out_ref[...]
+    row = lax.broadcasted_iota(jnp.int32, value.shape, 0)
+    column = lax.broadcasted_iota(jnp.int32, value.shape, 1)
+    out_ref[...] = jnp.where(row >= column, value, 0.0)
+
+
 def factor(
-    core_ref, mine_ref, other_ref, r_bar_ref, nh_ref, nl_ref, sh_ref, sl_ref, sums_ref, a_ref, u_ref, inv_ref
-):
-    size = 256
+    core_ref, mine_ref, other_ref, r_bar_ref, nh_ref, nl_ref, sh_ref, sl_ref, sums_ref, w_ref, inv1_ref, inv2_ref
+):
     tile = 128
     core = core_ref[0]
     sums_ref[pl.ds(pl.multiple_of(core * 264, 8), 264)] = mine_ref[...]
     sums_ref[pl.ds(pl.multiple_of((1 - core) * 264, 8), 264)] = other_ref[...]
-    a_ref[0:tile, 0:tile] = sums_ref[0:tile]
-    a_ref[0:tile, tile:size] = sums_ref[tile : 2 * tile]
-    a_ref[tile:size, tile:size] = sums_ref[3 * tile : 4 * tile]
-    row = lax.broadcasted_iota(jnp.int32, (size, size), 0)
-    col = lax.broadcasted_iota(jnp.int32, (size, size), 1)
-    a_ref[:, size : 2 * size] = jnp.where(row == col, 1.0, 0.0)
-    u_ref[...] = jnp.zeros((size, size), f32)
-    inv_ref[...] = jnp.zeros((size, size), f32)
-    place = lax.broadcasted_iota(jnp.int32, (8, 3 * tile), 0)
-    for start in range(0, size, PANEL):
-        base = (start // tile) * tile
-        lanes = slice(base, base + 3 * tile)
-        offset = start - base
-        rows = [jnp.broadcast_to(a_ref[start + i : start + i + 1, lanes], (8, 3 * tile)) for i in range(PANEL)]
-        s = {}
-        for i in range(PANEL):
-            for m in range(i, PANEL):
-                s[i, m] = jnp.broadcast_to(rows[i][:, offset + m : offset + m + 1], (8, tile))
-        done = []
-        for i in range(PANEL):
-            inverse = pl.reciprocal(s[i, i])
-            root = lax.rsqrt(s[i, i])
-            root = root * (1.5 - 0.5 * s[i, i] * root * root)
-            for k in range(i + 1, PANEL):
-                factor_k = s[i, k] * inverse
-                for m in range(k, PANEL):
-                    s[k, m] = s[k, m] - factor_k * s[i, m]
-                rows[k] = rows[k] - jnp.concatenate([factor_k] * 3, axis=1) * rows[i]
-            done.append(rows[i] * jnp.concatenate([root] * 3, axis=1))
-        groups = []
-        for first in range(0, PANEL, 8):
-            group = done[first]
-            for i in range(1, 8):
-                group = jnp.where(place == i, done[first + i], group)
-            groups.append(group)
-        panel = jnp.concatenate(groups, axis=0)
-        stop = start + PANEL
-        if base == 0:
-            u_ref[start:stop, :] = panel[:, : 2 * tile]
-            inv_ref[start:stop, :tile] = panel[:, 2 * tile :]
-        else:
-            u_ref[start:stop, tile:] = panel[:, :tile]
-            inv_ref[start:stop, :] = panel[:, tile:]
-        if stop < size:
-            h, m, l = split3(panel)
-            width = size - base
-            left = jnp.concatenate([h, h, m, m, h, l], axis=0)[:, :width]
-            right = jnp.concatenate([h, m, h, m, l, h], axis=0)
-            change = dot(left, right, ((0,), (0,)))
-            a_ref[stop:, lanes] = a_ref[stop:, lanes] - change[stop - base :]
-    upper = jnp.where(row <= col, u_ref[...], 0.0)
-    inv = jnp.where(row >= col, inv_ref[...], 0.0)
+
+    def product(a, b, contract):
+        return lax.dot_general(a, b, ((contract[0], contract[1]), ((), ())), precision=exact, preferred_element_type=f32)
+
+    down, across, plain = ((0,), (0,)), ((1,), (1,)), ((1,), (0,))
+    row = lax.broadcasted_iota(jnp.int32, (2 * tile, 2 * tile), 0)
+    col = lax.broadcasted_iota(jnp.int32, (2 * tile, 2 * tile), 1)
+
+    def corner(value, keep):
+        return jnp.where(keep[:tile, :tile], value, 0.0)
+
+    def whole(value):
+        return corner(value, row <= col) + jnp.transpose(corner(value, row < col))
+
+    pack1, g12, pack2 = sums_ref[0:tile], sums_ref[tile : 2 * tile], sums_ref[3 * tile : 4 * tile]
+    w_ref[...] = corner(pack1, row <= col)
+    inverse_factor(w_ref, inv1_ref)
+    inv1 = inv1_ref[...]
+    u12 = product(inv1, g12, plain)
+    w_ref[...] = corner(pack2, row <= col) - product(u12, u12, down)
+    inverse_factor(w_ref, inv2_ref)
+    inv2 = inv2_ref[...]
+    inv21 = -product(inv2, product(u12, inv1, down), plain)
+    zero = jnp.zeros((tile, tile), f32)
+    inv = jnp.concatenate(
+        [jnp.concatenate([inv1, zero], axis=1), jnp.concatenate([inv21, inv2], axis=1)], axis=0
+    )
+    gram = jnp.concatenate(
+        [
+            jnp.concatenate([whole(pack1), g12], axis=1),
+            jnp.concatenate([jnp.transpose(g12), whole(pack2)], axis=1),
+        ],
+        axis=0,
+    )
     bar = jnp.where(row <= col, r_bar_ref[...], 0.0)
-    corner = jnp.zeros((tile, tile), f32)
-    top = jnp.concatenate([sums_ref[0:tile], corner], axis=1)
-    bottom = jnp.concatenate([sums_ref[2 * tile : 3 * tile], sums_ref[3 * tile : 4 * tile]], axis=1)
+    top = jnp.concatenate([pack1, zero], axis=1)
+    bottom = jnp.concatenate([sums_ref[2 * tile : 3 * tile], pack2], axis=1)
     cross = jnp.concatenate([top, bottom], axis=0)
     diagonal = jnp.concatenate([sums_ref[512:513], sums_ref[520:521]], axis=1)
     cross = jnp.where(row > col, cross, jnp.where(row == col, diagonal, 0.0))
-
-    def product(a, b, contract):
-        return lax.dot_general(a, b, ((contract[0], contract[1]), ((), ())), precision=exact, preferred_element_type=f32)
-
-    across = ((1,), (1,))
-    middle = product(upper, bar, across) - product(cross, inv, across)
+    middle = product(inv, product(gram, bar, across), plain) - product(cross, inv, across)
     symmetric = jnp.where(row >= col, middle, 0.0) + jnp.transpose(jnp.where(row > col, middle, 0.0))
-    spread = product(inv, product(symmetric, inv, ((1,), (0,))), ((0,), (0,)))
+    spread = product(inv, product(symmetric, inv, plain), down)
     nh_ref[...], nl_ref[...] = split2(inv)
     sh_ref[...], sl_ref[...] = split2(spread)
 
@@ -514,9 +546,9 @@
         factor, (square,) * 4, 10**9, 10**6,
         [
             pltpu.VMEM((528, 128), f32),
-            pltpu.VMEM((256, 512), f32),
-            pltpu.VMEM((256, 256), f32),
-            pltpu.VMEM((256, 256), f32),
+            pltpu.VMEM((128, 128), f32),
+            pltpu.VMEM((128, 128), f32),
+            pltpu.VMEM((128, 128), f32),
         ],
         scalar=True,
     )(core, mine, other, r_bar)

time: 86.5 us -> 85.1 us (0.984)
  Pallas kernels: 30.2 us -> 28.8 us
    pallas_call x10, Pallas kernels: 30.2 us -> 28.8 us  [run(): pl.pallas_call(kernel, out_shape=outs, in_specs=specs, scratch_shapes=lis...]
where the time goes in v8:
time: 85.1 us; the launch traced here: 84.1 us
  waiting for transfers between devices  32.6 us (38%)
  Pallas kernels  28.8 us (34%)
  starting transfers between devices  18.5 us (22%)
  local copies, waits for them, and re-layouts  3.31 us (4%)
    pallas_call x10, Pallas kernels, run(): pl.pallas_call(kernel, out_shape=outs, in_specs=specs, scratch_shapes=lis...  28.8 us
    ppermute x4, waiting for transfers between devices, swap_outer(): return lax.ppermute(message, 'row', pairs + [(j, i) for i, j in pairs])  19.1 us
    ppermute x3, waiting for transfers between devices, sum_over_rows(): lax.ppermute(mine, 'row', [(i, i ^ 1 << turn[i & 1]) for i in range(count)])  11.1 us
    ppermute x4, starting transfers between devices, swap_outer(): return lax.ppermute(message, 'row', pairs + [(j, i) for i, j in pairs])  11.1 us
    ppermute x1, starting transfers between devices, sum_over_rows(): return (mine, lax.ppermute(mine, 'row', swap))  3.53 us
    unnamed x10, local copies, waits for them, and re-layouts  3.31 us
    ppermute x3, starting transfers between devices, sum_over_rows(): lax.ppermute(mine, 'row', [(i, i ^ 1 << turn[i & 1]) for i in range(count)])  2.67 us
  transfers between devices with their start and end apart: 11, of which 9 were waited for; matrix products, arithmetic and copies ran while one was open for 0% of the time, Pallas kernels for 12%

profile of v8, /device:TPU:9, one launch (start us, length us, event | category | flops | bytes accessed | tf_op | source)
XLA Modules:
  0.0 84.1 jit_solution(14133236640206739424)
XLA Ops:
  0.6 3.7 %shard_map.68 = (f32[768,128]{1,0:T(8,128)}, f32[776,128]{1,0:T(8,128)}, f32[1544,128]{1,0:T(8,128)}, f32[384,16]{1,0:T(8,128)}) custom-call(s32[1]{0:T(128)} %bitcast.core_ref, f32[6,2,384]{2,1,0:T(2,128)} %coeff_hbm.1, f32[4,2,384,128]{3,2,1,0:T(8,128)} %z_ref.3), custom_call_target="tpu_custom_call" | custom-call | flops 1000000 | bytes 3000000 | tf_op jit(solution)/shard_map/pallas_call | solution.py:22
  4.3 0.7 collective-permute-start.1
  5.1 3.0 %collective-permute-start.2 = (f32[768,128]{1,0:T(8,128)}, f32[768,128]{1,0:T(8,128)S(1)}, u32[]{:S(2)}, u32[]{:S(2)}) collective-permute-start(f32[768,128]{1,0:T(8,128)} %get-tuple-element.45), channel_id=1, source_target_pairs={{1,2},{3,4},{5,6},{7,8},{9,10},{11,12},{13,14},{2,1},{4,3},{6,5},{... | collective-permute-start | bytes 1179656 | tf_op jit(solution)/shard_map/ppermute | solution.py:489
  8.1 2.5 %collective-permute-start = (f32[776,128]{1,0:T(8,128)}, f32[776,128]{1,0:T(8,128)S(1)}, u32[]{:S(2)}, u32[]{:S(2)}) collective-permute-start(f32[776,128]{1,0:T(8,128)} %get-tuple-element.43), channel_id=1, source_target_pairs={{1,2},{3,4},{5,6},{7,8},{9,10},{11,12},{13,14},{2,1},{4,3},{6,5},{... | collective-permute-start | bytes 1191944 | tf_op jit(solution)/shard_map/ppermute | solution.py:489
  10.7 1.9 %copy-done.1 = f32[4,2,384,256]{3,2,1,0:T(8,128)S(1)} copy-done((f32[4,2,384,256]{3,2,1,0:T(8,128)S(1)}, f32[4,2,384,256]{3,2,1,0:T(8,128)}, u32[]{:S(2)}) %copy-start.1) | copy-done | bytes 3145752
  12.6 1.4 %copy-done.3 = f32[4,2,384,128]{3,2,1,0:T(8,128)S(1)} copy-done((f32[4,2,384,128]{3,2,1,0:T(8,128)S(1)}, f32[4,2,384,128]{3,2,1,0:T(8,128)}, u32[]{:S(2)}) %copy-start.3) | copy-done | bytes 1572888
  14.0 1.8 %shard_map.69 = (f32[136,128]{1,0:T(8,128)S(1)}, bf16[3072,128]{1,0:T(8,128)(2,1)S(1)}, bf16[3072,128]{1,0:T(8,128)(2,1)S(1)}, bf16[3072,256]{1,0:T(8,128)(2,1)S...) custom-call(f32[3072,128]{1,0:T(8,128)S(1)} %bitcast.4, ...), custom_call_target="tpu_custom_call" | custom-call | flops 503316480 | bytes 9000000 | tf_op jit(solution)/shard_map/pallas_call | solution.py:22
  15.8 7.1 %collective-permute-done.2.outer1_ref = f32[768,128]{1,0:T(8,128)S(1)} collective-permute-done((f32[768,128]{1,0:T(8,128)}, f32[768,128]{1,0:T(8,128)S(1)}, u32[]{:S(2)}, u32[]{:S(2)}) %collective-permute-start.2) | collective-permute-done | bytes 393248 | tf_op jit(solution)/shard_map/ppermute | solution.py:489
  22.9 3.2 %shard_map.70 = (f32[2,384,128]{2,1,0:T(8,128)S(1)}, bf16[1536,128]{1,0:T(8,128)(2,1)S(1)}, bf16[1536,128]{1,0:T(8,128)(2,1)S(1)}, bf16[768,128]{1,0:T(8,128)(2,...) custom-call(s32[1]{0:T(128)} %bitcast.core_ref, f32[384,16]{1,0:T(8,128)S(1)} %copy-done.2, ...), custom_call_target="tpu_custom_call" | custom-call | flops 805306368 | bytes 9000000 | tf_op jit(solution)/shard_map/pallas_call | solution.py:22
  26.1 1.0 %collective-permute-done.outer2_ref.fouter2_ref = f32[776,128]{1,0:T(8,128)S(1)} collective-permute-done((f32[776,128]{1,0:T(8,128)}, f32[776,128]{1,0:T(8,128)S(1)}, u32[]{:S(2)}, u32[]{:S(2)}) %collective-permute-start) | collective-permute-done | bytes 397344 | tf_op jit(solution)/shard_map/ppermute | solution.py:489
  27.1 1.0 %shard_map.71 = (f32[264,128]{1,0:T(8,128)S(1)}, f32[264,128]{1,0:T(8,128)S(1)}, bf16[768,128]{1,0:T(8,128)(2,1)S(1)}, bf16[768,128]{1,0:T(8,128)(2,1)S(1)}) custom-call(s32[1]{0:T(128)} %bitcast.core_ref, f32[384,16]{1,0:T(8,128)S(1)} %copy-done.2, f32[4,2,384,128]{3,2,1,0:T(8,128)S(1)} %copy-done, ...), custom_call_target="tpu_custom_call" | custom-call | flops 301989888 | bytes 5000000 | tf_op jit(solution)/shard_map/pallas_call | solution.py:22
  28.1 0.1 collective-permute-start.3
  28.2 1.3 %collective-permute-done.3 = f32[264,128]{1,0:T(8,128)S(1)} collective-permute-done((f32[264,128]{1,0:T(8,128)S(1)}, f32[264,128]{1,0:T(8,128)S(1)}, u32[]{:S(2)}, u32[]{:S(2)}) %collective-permute-start.3) | collective-permute-done | bytes 135200 | tf_op jit(solution)/shard_map/ppermute | solution.py:496
  29.6 0.1 collective-permute-start.4
  29.6 4.1 %collective-permute-done.4 = f32[264,128]{1,0:T(8,128)S(1)} collective-permute-done((f32[264,128]{1,0:T(8,128)S(1)}, f32[264,128]{1,0:T(8,128)S(1)}, u32[]{:S(2)}, u32[]{:S(2)}) %collective-permute-start.4) | collective-permute-done | bytes 135200 | tf_op jit(solution)/shard_map/ppermute | solution.py:499
  33.8 2.4 %collective-permute-start.5 = (f32[264,128]{1,0:T(8,128)S(1)}, f32[264,128]{1,0:T(8,128)S(1)}, u32[]{:S(2)}, u32[]{:S(2)}) collective-permute-start(f32[264,128]{1,0:T(8,128)S(1)} %add.13), channel_id=1, source_target_pairs={{0,4},{1,9},{2,6},{3,11},{4,0},{5,13},{6,2},{7,15},{8,12},{9,1},{1... | collective-permute-start | bytes 405512 | tf_op jit(solution)/shard_map/ppermute | solution.py:499
  36.2 3.3 %collective-permute-done.5 = f32[264,128]{1,0:T(8,128)S(1)} collective-permute-done((f32[264,128]{1,0:T(8,128)S(1)}, f32[264,128]{1,0:T(8,128)S(1)}, u32[]{:S(2)}, u32[]{:S(2)}) %collective-permute-start.5) | collective-permute-done | bytes 135200 | tf_op jit(solution)/shard_map/ppermute | solution.py:499
  39.5 0.2 collective-permute-start.6
  39.7 3.7 %collective-permute-done.6 = f32[264,128]{1,0:T(8,128)S(1)} collective-permute-done((f32[264,128]{1,0:T(8,128)S(1)}, f32[264,128]{1,0:T(8,128)S(1)}, u32[]{:S(2)}, u32[]{:S(2)}) %collective-permute-start.6) | collective-permute-done | bytes 135200 | tf_op jit(solution)/shard_map/ppermute | solution.py:499
  43.4 3.5 %collective-permute-start.7 = (f32[264,128]{1,0:T(8,128)S(1)}, f32[264,128]{1,0:T(8,128)S(1)}, u32[]{:S(2)}, u32[]{:S(2)}) collective-permute-start(f32[264,128]{1,0:T(8,128)S(1)} %add.15.mine_ref), channel_id=1, source_target_pairs={{0,1},{1,0},{2,3},{3,2},{4,5},{5,4},{6,7},{7,6},{8,9},{9,8},{10,11... | collective-permute-start | bytes 405512 | tf_op jit(solution)/shard_map/ppermute | solution.py:500
  47.0 1.0 %collective-permute-done.7.other_ref = f32[264,128]{1,0:T(8,128)S(1)} collective-permute-done((f32[264,128]{1,0:T(8,128)S(1)}, f32[264,128]{1,0:T(8,128)S(1)}, u32[]{:S(2)}, u32[]{:S(2)}) %collective-permute-start.7) | collective-permute-done | bytes 135200 | tf_op jit(solution)/shard_map/ppermute | solution.py:500
  48.0 10.3 %shard_map.72 = (bf16[256,256]{1,0:T(8,128)(2,1)S(1)}, bf16[256,256]{1,0:T(8,128)(2,1)S(1)}, bf16[256,256]{1,0:T(8,128)(2,1)S(1)}, bf16[256,256]{1,0:T(8,128)(2,1)S(1)}) custom-call(s32[1]{0:T(128)} %bitcast.core_ref, f32[264,128]{1,0:T(8,128)S(1)} %add.15.mine_ref, f32[264,128]{1,0:T(8,128)S(1)} %collective-permute-done.7.other_ref, f32[256,256]{1,0:T(8,128)S(1)} %copy-done.4), custom_call_target="tpu_custom_call" | custom-call | flops 1000000000 | bytes 1000000 | tf_op jit(solution)/shard_map/pallas_call | solution.py:22
  58.3 0.6 shard_map.73
  58.9 1.7 %shard_map.74 = (f32[2,384,128]{2,1,0:T(8,128)S(1)}, f32[2,2,384,128]{3,2,1,0:T(8,128)S(1)}, f32[768,128]{1,0:T(8,128)S(1)}, f32[1536,128]{1,0:T(8,128)S(1)}) custom-call(s32[1]{0:T(128)} %bitcast.core_ref, f32[384,16]{1,0:T(8,128)S(1)} %copy-done.2, f32[2,384,128]{2,1,0:T(8,128)S(1)} %get-tuple-element.62.outer_ref, ...), custom_call_target="tpu_custom_call" | custom-call | flops 10000000000 | bytes 6000000 | tf_op jit(solution)/shard_map/pallas_call | solution.py:22
  60.6 0.4 collective-permute-start.9
  61.1 2.8 %collective-permute-start.8 = (f32[768,128]{1,0:T(8,128)S(1)}, f32[768,128]{1,0:T(8,128)S(1)}, u32[]{:S(2)}, u32[]{:S(2)}) collective-permute-start(f32[768,128]{1,0:T(8,128)S(1)} %get-tuple-element.63.outer1_ref.own1_ref), channel_id=1, source_target_pairs={{1,2},{3,4},{5,6},{7,8},{9,10},{11,12},{13,14},{2,1},{4,3},{6,5},{... | collective-permute-start | bytes 1179656 | tf_op jit(solution)/shard_map/ppermute | solution.py:489
  63.9 2.7 %collective-permute-start.10 = (f32[768,128]{1,0:T(8,128)S(1)}, f32[768,128]{1,0:T(8,128)S(1)}, u32[]{:S(2)}, u32[]{:S(2)}) collective-permute-start(f32[768,128]{1,0:T(8,128)S(1)} %get-tuple-element.73), channel_id=1, source_target_pairs={{1,2},{3,4},{5,6},{7,8},{9,10},{11,12},{13,14},{2,1},{4,3},{6,5},{... | collective-permute-start | bytes 1179656 | tf_op jit(solution)/shard_map/ppermute | solution.py:489
  66.6 3.0 %shard_map.77 = f32[4,2,384,128]{3,2,1,0:T(8,128)} custom-call(s32[1]{0:T(128)} %bitcast.core_ref, bf16[3072,256]{1,0:T(8,128)(2,1)S(1)} %get-tuple-element.39.qh_ref, bf16[3072,256]{1,0:T(8,128)(2,1)S(1)} %get-tuple-element.40.ql_ref, bf16[3072,128]{1,0:T(8,128)(2,1)S(1)} %get-tuple-element.41.nh_ref, bf16[3072,128]{1,0:T(8,128)(2,1)S(1)} %get-tuple-element.42.nl_ref, ...), custom_call_target="tpu_custom_call" | custom-call | tf_op jit(solution)/shard_map/pallas_call | solution.py:22
  69.6 8.9 %collective-permute-done.8.outer1_ref = f32[768,128]{1,0:T(8,128)S(1)} collective-permute-done((f32[768,128]{1,0:T(8,128)S(1)}, f32[768,128]{1,0:T(8,128)S(1)}, u32[]{:S(2)}, u32[]{:S(2)}) %collective-permute-start.8) | collective-permute-done | bytes 393248 | tf_op jit(solution)/shard_map/ppermute | solution.py:489
  78.6 2.2 %shard_map.75 = (f32[2,2,384,128]{3,2,1,0:T(8,128)S(1)}, f32[2,2,384,128]{3,2,1,0:T(8,128)S(1)}) custom-call(f32[384,16]{1,0:T(8,128)S(1)} %copy-done.2, f32[2,384,128]{2,1,0:T(8,128)S(1)} %get-tuple-element.62.outer_ref, f32[2,384,128]{2,1,0:T(8,128)S(1)} %get-tuple-element.68.light_ref, f32[2,2,384,128]{3,2,1,0:T(8,128)S(1)} %get-tuple-element.69.heavy_ref, ...), custom_call_target="tpu_custom_call" | custom-call | flops 10000000 | bytes 6000000 | tf_op jit(solution)/shard_map/pallas_call | solution.py:22
  80.7 2.0 %collective-permute-done.10.outer2_ref = f32[768,128]{1,0:T(8,128)S(1)} collective-permute-done((f32[768,128]{1,0:T(8,128)S(1)}, f32[768,128]{1,0:T(8,128)S(1)}, u32[]{:S(2)}, u32[]{:S(2)}) %collective-permute-start.10) | collective-permute-done | bytes 393248 | tf_op jit(solution)/shard_map/ppermute | solution.py:489
  82.8 1.3 %shard_map.76 = f32[4,2,384,128]{3,2,1,0:T(8,128)} custom-call(s32[1]{0:T(128)} %bitcast.core_ref, f32[2,2,384,128]{3,2,1,0:T(8,128)S(1)} %get-tuple-element.71.light_ref, f32[2,2,384,128]{3,2,1,0:T(8,128)S(1)} %get-tuple-element.72.heavy_ref, f32[768,128]{1,0:T(8,128)S(1)} %collective-permute-done.10.outer2_ref), custom_call_target="tpu_custom_call" | custom-call | flops 1000000 | bytes 6000000 | tf_op jit(solution)/shard_map/pallas_call | solution.py:22
  (14 shorter events, 0.1 us)
Async XLA Ops:
  4.3 18.5 %collective-permute-start.1 = (f32[1544,128]{1,0:T(8,128)}, f32[1544,128]{1,0:T(8,128)S(1)}, u32[]{:S(2)}, u32[]{:S(2)}) collective-permute-start(f32[1544,128]{1,0:T(8,128)} %get-tuple-element.44), channel_id=1, source_target_pairs={{0,1},{1,0},{2,3},{3,2},{4,5},{5,4},{6,7},{7,6},{8,9},{9,8},{10,11... | collective-permute-start | bytes 2371592 | tf_op jit(solution)/shard_map/ppermute | solution.py:483
  5.1 17.8 %collective-permute-start.2 = (f32[768,128]{1,0:T(8,128)}, f32[768,128]{1,0:T(8,128)S(1)}, u32[]{:S(2)}, u32[]{:S(2)}) collective-permute-start(f32[768,128]{1,0:T(8,128)} %get-tuple-element.45), channel_id=1, source_target_pairs={{1,2},{3,4},{5,6},{7,8},{9,10},{11,12},{13,14},{2,1},{4,3},{6,5},{... | collective-permute-start | bytes 1179656 | tf_op jit(solution)/shard_map/ppermute | solution.py:489
  8.1 19.0 %collective-permute-start = (f32[776,128]{1,0:T(8,128)}, f32[776,128]{1,0:T(8,128)S(1)}, u32[]{:S(2)}, u32[]{:S(2)}) collective-permute-start(f32[776,128]{1,0:T(8,128)} %get-tuple-element.43), channel_id=1, source_target_pairs={{1,2},{3,4},{5,6},{7,8},{9,10},{11,12},{13,14},{2,1},{4,3},{6,5},{... | collective-permute-start | bytes 1191944 | tf_op jit(solution)/shard_map/ppermute | solution.py:489
  10.7 1.9 %copy-start.1 = (f32[4,2,384,256]{3,2,1,0:T(8,128)S(1)}, f32[4,2,384,256]{3,2,1,0:T(8,128)}, u32[]{:S(2)}) copy-start(f32[4,2,384,256]{3,2,1,0:T(8,128)} %param.8) | copy-start | bytes 9437188
  12.5 1.4 %copy-start.3 = (f32[4,2,384,128]{3,2,1,0:T(8,128)S(1)}, f32[4,2,384,128]{3,2,1,0:T(8,128)}, u32[]{:S(2)}) copy-start(f32[4,2,384,128]{3,2,1,0:T(8,128)} %param.7) | copy-start | bytes 4718596
  14.0 8.9 %copy-start = (f32[4,2,384,128]{3,2,1,0:T(8,128)S(1)}, f32[4,2,384,128]{3,2,1,0:T(8,128)}, u32[]{:S(2)}) copy-start(f32[4,2,384,128]{3,2,1,0:T(8,128)} %z_ref.3) | copy-start | bytes 4718596
  14.0 8.9 %copy-start.2 = (f32[384,16]{1,0:T(8,128)S(1)}, f32[384,16]{1,0:T(8,128)}, u32[]{:S(2)}) copy-start(f32[384,16]{1,0:T(8,128)} %get-tuple-element.38.table_ref) | copy-start | bytes 73732
  28.1 19.9 %copy-start.4 = (f32[256,256]{1,0:T(8,128)S(1)}, f32[256,256]{1,0:T(8,128)}, u32[]{:S(2)}) copy-start(f32[256,256]{1,0:T(8,128)} %r_bar_ref.1) | copy-start | bytes 786436
  28.1 1.4 %collective-permute-start.3 = (f32[264,128]{1,0:T(8,128)S(1)}, f32[264,128]{1,0:T(8,128)S(1)}, u32[]{:S(2)}, u32[]{:S(2)}) collective-permute-start(f32[264,128]{1,0:T(8,128)S(1)} %get-tuple-element.57), channel_id=1, source_target_pairs={{0,1},{1,0},{2,3},{3,2},{4,5},{5,4},{6,7},{7,6},{8,9},{9,8},{10,11... | collective-permute-start | bytes 405512 | tf_op jit(solution)/shard_map/ppermute | solution.py:496
  29.6 4.2 %collective-permute-start.4 = (f32[264,128]{1,0:T(8,128)S(1)}, f32[264,128]{1,0:T(8,128)S(1)}, u32[]{:S(2)}, u32[]{:S(2)}) collective-permute-start(f32[264,128]{1,0:T(8,128)S(1)} %add.12), channel_id=1, source_target_pairs={{0,2},{1,5},{2,0},{3,7},{4,6},{5,1},{6,4},{7,3},{8,10},{9,13},{10,... | collective-permute-start | bytes 405512 | tf_op jit(solution)/shard_map/ppermute | solution.py:499
  33.8 5.7 %collective-permute-start.5 = (f32[264,128]{1,0:T(8,128)S(1)}, f32[264,128]{1,0:T(8,128)S(1)}, u32[]{:S(2)}, u32[]{:S(2)}) collective-permute-start(f32[264,128]{1,0:T(8,128)S(1)} %add.13), channel_id=1, source_target_pairs={{0,4},{1,9},{2,6},{3,11},{4,0},{5,13},{6,2},{7,15},{8,12},{9,1},{1... | collective-permute-start | bytes 405512 | tf_op jit(solution)/shard_map/ppermute | solution.py:499
  39.5 3.9 %collective-permute-start.6 = (f32[264,128]{1,0:T(8,128)S(1)}, f32[264,128]{1,0:T(8,128)S(1)}, u32[]{:S(2)}, u32[]{:S(2)}) collective-permute-start(f32[264,128]{1,0:T(8,128)S(1)} %add.14), channel_id=1, source_target_pairs={{0,8},{1,3},{2,10},{3,1},{4,12},{5,7},{6,14},{7,5},{8,0},{9,11},{1... | collective-permute-start | bytes 405512 | tf_op jit(solution)/shard_map/ppermute | solution.py:499
  43.4 4.5 %collective-permute-start.7 = (f32[264,128]{1,0:T(8,128)S(1)}, f32[264,128]{1,0:T(8,128)S(1)}, u32[]{:S(2)}, u32[]{:S(2)}) collective-permute-start(f32[264,128]{1,0:T(8,128)S(1)} %add.15.mine_ref), channel_id=1, source_target_pairs={{0,1},{1,0},{2,3},{3,2},{4,5},{5,4},{6,7},{7,6},{8,9},{9,8},{10,11... | collective-permute-start | bytes 405512 | tf_op jit(solution)/shard_map/ppermute | solution.py:500
  60.6 17.9 %collective-permute-start.9 = (f32[1536,128]{1,0:T(8,128)S(1)}, f32[1536,128]{1,0:T(8,128)S(1)}, u32[]{:S(2)}, u32[]{:S(2)}) collective-permute-start(f32[1536,128]{1,0:T(8,128)S(1)} %get-tuple-element.70.own_ref), channel_id=1, source_target_pairs={{0,1},{1,0},{2,3},{3,2},{4,5},{5,4},{6,7},{7,6},{8,9},{9,8},{10,11... | collective-permute-start | bytes 2359304 | tf_op jit(solution)/shard_map/ppermute | solution.py:483
  61.1 17.5 %collective-permute-start.8 = (f32[768,128]{1,0:T(8,128)S(1)}, f32[768,128]{1,0:T(8,128)S(1)}, u32[]{:S(2)}, u32[]{:S(2)}) collective-permute-start(f32[768,128]{1,0:T(8,128)S(1)} %get-tuple-element.63.outer1_ref.own1_ref), channel_id=1, source_target_pairs={{1,2},{3,4},{5,6},{7,8},{9,10},{11,12},{13,14},{2,1},{4,3},{6,5},{... | collective-permute-start | bytes 1179656 | tf_op jit(solution)/shard_map/ppermute | solution.py:489
  63.9 18.9 %collective-permute-start.10 = (f32[768,128]{1,0:T(8,128)S(1)}, f32[768,128]{1,0:T(8,128)S(1)}, u32[]{:S(2)}, u32[]{:S(2)}) collective-permute-start(f32[768,128]{1,0:T(8,128)S(1)} %get-tuple-element.73), channel_id=1, source_target_pairs={{1,2},{3,4},{5,6},{7,8},{9,10},{11,12},{13,14},{2,1},{4,3},{6,5},{... | collective-permute-start | bytes 1179656 | tf_op jit(solution)/shard_map/ppermute | solution.py:489

commit v9 on v8

--- a/solution.py
+++ b/solution.py
@@ -222,9 +222,17 @@
     rest_ref[...] = rest
 
 
+def quarters(core):
+    parts = []
+    for owner in (core, 1 - core):
+        first = pl.multiple_of(owner * 264, 8)
+        parts += [pl.ds(first, 136), pl.ds(pl.multiple_of(first + 136, 8), 128)]
+    return parts
+
+
 def expand_last(
     core_ref, table_ref, z_ref, outer2_ref, light_ref, gram_ref, rest_ref, pack_ref,
-    nht_ref, nlt_ref, qht_ref, qlt_ref, mine_ref, other_ref, oh_ref, ol_ref, sums_ref,
+    nht_ref, nlt_ref, qht_ref, qlt_ref, mine1_ref, mine2_ref, other1_ref, other2_ref, oh_ref, ol_ref, sums_ref,
 ):
     n = z_ref.shape[2]
     core = core_ref[0]
@@ -246,8 +254,8 @@
     sums_ref[256:384] = rest[256:]
     sums_ref[384:512] = pack_ref[0:128]
     sums_ref[520:528] = pack_ref[128:136]
-    mine_ref[...] = sums_ref[pl.ds(pl.multiple_of(core * 264, 8), 264)]
-    other_ref[...] = sums_ref[pl.ds(pl.multiple_of((1 - core) * 264, 8), 264)]
+    for part, out in zip(quarters(core), (mine1_ref, mine2_ref, other1_ref, other2_ref)):
+        out[...] = sums_ref[part]
 
 
 def inverse_factor(w_ref, out_ref):
@@ -309,12 +317,12 @@
 
 
 def factor(
-    core_ref, mine_ref, other_ref, r_bar_ref, nh_ref, nl_ref, sh_ref, sl_ref, sums_ref, w_ref, inv1_ref, inv2_ref
+    core_ref, mine1_ref, mine2_ref, other1_ref, other2_ref, r_bar_ref, nh_ref, nl_ref, sh_ref, sl_ref, sums_ref, w_ref, inv1_ref, inv2_ref
 ):
     tile = 128
     core = core_ref[0]
-    sums_ref[pl.ds(pl.multiple_of(core * 264, 8), 264)] = mine_ref[...]
-    sums_ref[pl.ds(pl.multiple_of((1 - core) * 264, 8), 264)] = other_ref[...]
+    for part, value in zip(quarters(core), (mine1_ref, mine2_ref, other1_ref, other2_ref)):
+        sums_ref[part] = value[...]
 
     def product(a, b, contract):
         return lax.dot_general(a, b, ((contract[0], contract[1]), ((), ())), precision=exact, preferred_element_type=f32)
@@ -492,12 +500,13 @@
 def sum_over_rows(mine, other):
     count = lax.axis_size("row")
     bits = count.bit_length() - 1
-    swap = [(i, i ^ 1) for i in range(count)]
-    mine = mine + lax.ppermute(other, "row", swap)
+    mine = [m + swap_inner(o) for m, o in zip(mine, other)]
     for step in range(bits - 1):
-        turn = [1 + step, 1 + (step + 1) % (bits - 1)]
-        mine = mine + lax.ppermute(mine, "row", [(i, i ^ (1 << turn[i & 1])) for i in range(count)])
-    return mine, lax.ppermute(mine, "row", swap)
+        for stream in range(2):
+            turn = [1 + (step + (core ^ stream)) % (bits - 1) for core in range(2)]
+            pairs = [(i, i ^ (1 << turn[i & 1])) for i in range(count)]
+            mine[stream] = mine[stream] + lax.ppermute(mine[stream], "row", pairs)
+    return mine + [swap_inner(m) for m in mine]
 
 
 def on_device(cell_coeffs, z_factor, noise_cols, q_bar, r_bar):
@@ -536,11 +545,11 @@
         (single, half, half, quarter, quarter, shape((128, 128), f32), shape((384, 128), f32)),
         work * 8, 9 * 10**6, [pltpu.VMEM(z_factor.shape, f32)], scalar=True,
     )(core, table, z_factor, inner, outer1, *transposed)
-    part = shape((264, 128), f32)
-    mine, other, oh, ol = call(
-        expand_last, (part, part, quarter, quarter), work * 3, 5 * 10**6, [pltpu.VMEM((528, 128), f32)], scalar=True
+    part1, part2 = shape((136, 128), f32), shape((128, 128), f32)
+    *parts, oh, ol = call(
+        expand_last, (part1, part2, part1, part2, quarter, quarter), work * 3, 5 * 10**6, [pltpu.VMEM((528, 128), f32)], scalar=True
     )(core, table, z_factor, outer2, light, gram, rest, pack, *transposed)
-    mine, other = sum_over_rows(mine, other)
+    parts = sum_over_rows(parts[:2], parts[2:])
     square = shape((256, 256), bf16)
     weights = call(
         factor, (square,) * 4, 10**9, 10**6,
@@ -551,7 +560,7 @@
             pltpu.VMEM((128, 128), f32),
         ],
         scalar=True,
-    )(core, mine, other, r_bar)
+    )(core, *parts, r_bar)
     left = (qh, ql, nh, nl)
     w_outer, own1 = call(gradient_outer, (single, hops), work * 3, 3 * 10**6, scalar=True)(
         core, table, *left, oh, ol, *weights

time: 85.1 us -> 84.2 us (0.989)
  waiting for transfers between devices: 32.6 us -> 25.7 us
  starting transfers between devices: 18.5 us -> 25.3 us
    ppermute x5 -> x6, waiting for transfers between devices: 13.5 us -> 4.91 us  [sum_over_rows(): mine[stream] = mine[stream] + lax.ppermute(mine[stream], 'row', pairs)]
    ppermute x2 -> x6, starting transfers between devices: 1.17 us -> 8.19 us  [swap_inner(): return lax.ppermute(message, 'row', [(i, i ^ 1) for i in range(count)])]
    ppermute x2 -> x6, waiting for transfers between devices: 0.01 us -> 1.72 us  [swap_inner(): return lax.ppermute(message, 'row', [(i, i ^ 1) for i in range(count)])]
    ppermute x5 -> x6, starting transfers between devices: 6.27 us -> 5.99 us  [sum_over_rows(): mine[stream] = mine[stream] + lax.ppermute(mine[stream], 'row', pairs)]
  transfers between devices with their start and end apart: 11 -> 16, of which waited for: 9 -> 11; matrix products, arithmetic and copies ran while one was open for 0% -> 0% of each run, Pallas kernels for 12% -> 12%
where the time goes in v9:
time: 84.2 us; the launch traced here: 83.9 us
  Pallas kernels  28.8 us (34%)
  waiting for transfers between devices  25.7 us (31%)
  starting transfers between devices  25.3 us (30%)
  local copies, waits for them, and re-layouts  3.31 us (4%)
    pallas_call x10, Pallas kernels, run(): pl.pallas_call(kernel, out_shape=outs, in_specs=specs, scratch_shapes=lis...  28.8 us
    ppermute x4, waiting for transfers between devices, swap_outer(): return lax.ppermute(message, 'row', pairs + [(j, i) for i, j in pairs])  19.1 us
    ppermute x4, starting transfers between devices, swap_outer(): return lax.ppermute(message, 'row', pairs + [(j, i) for i, j in pairs])  11.1 us
    ppermute x6, starting transfers between devices, swap_inner(): return lax.ppermute(message, 'row', [(i, i ^ 1) for i in range(count)])  8.19 us
    ppermute x6, starting transfers between devices, sum_over_rows(): mine[stream] = mine[stream] + lax.ppermute(mine[stream], 'row', pairs)  5.99 us
    ppermute x6, waiting for transfers between devices, sum_over_rows(): mine[stream] = mine[stream] + lax.ppermute(mine[stream], 'row', pairs)  4.91 us
    unnamed x10, local copies, waits for them, and re-layouts  3.31 us
    ppermute x6, waiting for transfers between devices, swap_inner(): return lax.ppermute(message, 'row', [(i, i ^ 1) for i in range(count)])  1.72 us
  transfers between devices with their start and end apart: 16, of which 11 were waited for; matrix products, arithmetic and copies ran while one was open for 0% of the time, Pallas kernels for 12%

profile of v9, /device:TPU:9, one launch (start us, length us, event | category | flops | bytes accessed | tf_op | source)
XLA Modules:
  0.0 83.9 jit_solution(16035020588558665094)
XLA Ops:
  0.6 3.7 %shard_map.68 = (f32[768,128]{1,0:T(8,128)}, f32[776,128]{1,0:T(8,128)}, f32[1544,128]{1,0:T(8,128)}, f32[384,16]{1,0:T(8,128)}) custom-call(s32[1]{0:T(128)} %bitcast.core_ref, f32[6,2,384]{2,1,0:T(2,128)} %coeff_hbm.1, f32[4,2,384,128]{3,2,1,0:T(8,128)} %z_ref.3), custom_call_target="tpu_custom_call" | custom-call | flops 1000000 | bytes 3000000 | tf_op jit(solution)/shard_map/pallas_call | solution.py:22
  4.3 0.7 collective-permute-start.1
  5.1 3.0 %collective-permute-start.2 = (f32[768,128]{1,0:T(8,128)}, f32[768,128]{1,0:T(8,128)S(1)}, u32[]{:S(2)}, u32[]{:S(2)}) collective-permute-start(f32[768,128]{1,0:T(8,128)} %get-tuple-element.47), channel_id=1, source_target_pairs={{1,2},{3,4},{5,6},{7,8},{9,10},{11,12},{13,14},{2,1},{4,3},{6,5},{... | collective-permute-start | bytes 1179656 | tf_op jit(solution)/shard_map/ppermute | solution.py:497
  8.1 2.5 %collective-permute-start = (f32[776,128]{1,0:T(8,128)}, f32[776,128]{1,0:T(8,128)S(1)}, u32[]{:S(2)}, u32[]{:S(2)}) collective-permute-start(f32[776,128]{1,0:T(8,128)} %get-tuple-element.45), channel_id=1, source_target_pairs={{1,2},{3,4},{5,6},{7,8},{9,10},{11,12},{13,14},{2,1},{4,3},{6,5},{... | collective-permute-start | bytes 1191944 | tf_op jit(solution)/shard_map/ppermute | solution.py:497
  10.7 1.9 %copy-done.1 = f32[4,2,384,256]{3,2,1,0:T(8,128)S(1)} copy-done((f32[4,2,384,256]{3,2,1,0:T(8,128)S(1)}, f32[4,2,384,256]{3,2,1,0:T(8,128)}, u32[]{:S(2)}) %copy-start.1) | copy-done | bytes 3145752
  12.6 1.4 %copy-done.3 = f32[4,2,384,128]{3,2,1,0:T(8,128)S(1)} copy-done((f32[4,2,384,128]{3,2,1,0:T(8,128)S(1)}, f32[4,2,384,128]{3,2,1,0:T(8,128)}, u32[]{:S(2)}) %copy-start.3) | copy-done | bytes 1572888
  14.0 1.8 %shard_map.69 = (f32[136,128]{1,0:T(8,128)S(1)}, bf16[3072,128]{1,0:T(8,128)(2,1)S(1)}, bf16[3072,128]{1,0:T(8,128)(2,1)S(1)}, bf16[3072,256]{1,0:T(8,128)(2,1)S...) custom-call(f32[3072,128]{1,0:T(8,128)S(1)} %bitcast.4, ...), custom_call_target="tpu_custom_call" | custom-call | flops 503316480 | bytes 9000000 | tf_op jit(solution)/shard_map/pallas_call | solution.py:22
  15.8 7.1 %collective-permute-done.2.outer1_ref = f32[768,128]{1,0:T(8,128)S(1)} collective-permute-done((f32[768,128]{1,0:T(8,128)}, f32[768,128]{1,0:T(8,128)S(1)}, u32[]{:S(2)}, u32[]{:S(2)}) %collective-permute-start.2) | collective-permute-done | bytes 393248 | tf_op jit(solution)/shard_map/ppermute | solution.py:497
  22.9 3.2 %shard_map.70 = (f32[2,384,128]{2,1,0:T(8,128)S(1)}, bf16[1536,128]{1,0:T(8,128)(2,1)S(1)}, bf16[1536,128]{1,0:T(8,128)(2,1)S(1)}, bf16[768,128]{1,0:T(8,128)(2,...) custom-call(s32[1]{0:T(128)} %bitcast.core_ref, f32[384,16]{1,0:T(8,128)S(1)} %copy-done.2, ...), custom_call_target="tpu_custom_call" | custom-call | flops 805306368 | bytes 9000000 | tf_op jit(solution)/shard_map/pallas_call | solution.py:22
  26.1 1.0 %collective-permute-done.outer2_ref.fouter2_ref = f32[776,128]{1,0:T(8,128)S(1)} collective-permute-done((f32[776,128]{1,0:T(8,128)}, f32[776,128]{1,0:T(8,128)S(1)}, u32[]{:S(2)}, u32[]{:S(2)}) %collective-permute-start) | collective-permute-done | bytes 397344 | tf_op jit(solution)/shard_map/ppermute | solution.py:497
  27.1 1.0 %shard_map.71 = (f32[136,128]{1,0:T(8,128)S(1)}, f32[128,128]{1,0:T(8,128)S(1)}, f32[136,128]{1,0:T(8,128)S(1)}, f32[128,128]{1,0:T(8,128)S(1)}, bf16[768,128]{1...) custom-call(s32[1]{0:T(128)} %bitcast.core_ref, f32[384,16]{1,0:T(8,128)S(1)} %copy-done.2, f32[4,2,384,128]{3,2,1,0:T(8,128)S(1)} %copy-done, ...), custom_call_target="tpu_custom_call" | custom-call | flops 301989888 | bytes 5000000 | tf_op jit(solution)/shard_map/pallas_call | solution.py:22
  28.7 0.7 collective-permute-done.3
  29.6 1.2 %collective-permute-start.8 = (f32[128,128]{1,0:T(8,128)S(1)}, f32[128,128]{1,0:T(8,128)S(1)}, u32[]{:S(2)}, u32[]{:S(2)}) collective-permute-start(f32[128,128]{1,0:T(8,128)S(1)} %add.28), channel_id=1, source_target_pairs={{0,4},{1,3},{2,6},{3,1},{4,0},{5,7},{6,2},{7,5},{8,12},{9,11},{10,... | collective-permute-start | bytes 196616 | tf_op jit(solution)/shard_map/ppermute | solution.py:508
  30.8 2.2 %collective-permute-done.4 = f32[136,128]{1,0:T(8,128)S(1)} collective-permute-done((f32[136,128]{1,0:T(8,128)S(1)}, f32[136,128]{1,0:T(8,128)S(1)}, u32[]{:S(2)}, u32[]{:S(2)}) %collective-permute-start.4) | collective-permute-done | bytes 69664 | tf_op jit(solution)/shard_map/ppermute | solution.py:508
  33.0 2.4 %collective-permute-start.5 = (f32[136,128]{1,0:T(8,128)S(1)}, f32[136,128]{1,0:T(8,128)S(1)}, u32[]{:S(2)}, u32[]{:S(2)}) collective-permute-start(f32[136,128]{1,0:T(8,128)S(1)} %add.25), channel_id=1, source_target_pairs={{0,4},{1,9},{2,6},{3,11},{4,0},{5,13},{6,2},{7,15},{8,12},{9,1},{1... | collective-permute-start | bytes 208904 | tf_op jit(solution)/shard_map/ppermute | solution.py:508
  35.6 1.6 %collective-permute-done.5 = f32[136,128]{1,0:T(8,128)S(1)} collective-permute-done((f32[136,128]{1,0:T(8,128)S(1)}, f32[136,128]{1,0:T(8,128)S(1)}, u32[]{:S(2)}, u32[]{:S(2)}) %collective-permute-start.5) | collective-permute-done | bytes 69664 | tf_op jit(solution)/shard_map/ppermute | solution.py:508
  37.3 0.5 collective-permute-start.6
  37.8 0.9 %collective-permute-done.9 = f32[128,128]{1,0:T(8,128)S(1)} collective-permute-done((f32[128,128]{1,0:T(8,128)S(1)}, f32[128,128]{1,0:T(8,128)S(1)}, u32[]{:S(2)}, u32[]{:S(2)}) %collective-permute-start.9) | collective-permute-done | bytes 65568 | tf_op jit(solution)/shard_map/ppermute | solution.py:508
  38.7 1.6 %collective-permute-start.10 = (f32[128,128]{1,0:T(8,128)S(1)}, f32[128,128]{1,0:T(8,128)S(1)}, u32[]{:S(2)}, u32[]{:S(2)}) collective-permute-start(f32[128,128]{1,0:T(8,128)S(1)} %add.30), channel_id=1, source_target_pairs={{0,2},{1,9},{2,0},{3,11},{4,6},{5,13},{6,4},{7,15},{8,10},{9,1},{1... | collective-permute-start | bytes 196616 | tf_op jit(solution)/shard_map/ppermute | solution.py:508
  40.5 4.4 %collective-permute-start.11 = (f32[136,128]{1,0:T(8,128)S(1)}, f32[136,128]{1,0:T(8,128)S(1)}, u32[]{:S(2)}, u32[]{:S(2)}) collective-permute-start(f32[136,128]{1,0:T(8,128)S(1)} %add.27.mine1_ref), channel_id=1, source_target_pairs={{0,1},{1,0},{2,3},{3,2},{4,5},{5,4},{6,7},{7,6},{8,9},{9,8},{10,11... | collective-permute-start | bytes 208904 | tf_op jit(solution)/shard_map/ppermute | solution.py:491
  44.9 2.0 %collective-permute-start.12 = (f32[128,128]{1,0:T(8,128)S(1)}, f32[128,128]{1,0:T(8,128)S(1)}, u32[]{:S(2)}, u32[]{:S(2)}) collective-permute-start(f32[128,128]{1,0:T(8,128)S(1)} %add.31.mine2_ref), channel_id=1, source_target_pairs={{0,1},{1,0},{2,3},{3,2},{4,5},{5,4},{6,7},{7,6},{8,9},{9,8},{10,11... | collective-permute-start | bytes 196616 | tf_op jit(solution)/shard_map/ppermute | solution.py:491
  47.0 0.9 %collective-permute-done.12.other2_ref = f32[128,128]{1,0:T(8,128)S(1)} collective-permute-done((f32[128,128]{1,0:T(8,128)S(1)}, f32[128,128]{1,0:T(8,128)S(1)}, u32[]{:S(2)}, u32[]{:S(2)}) %collective-permute-start.12) | collective-permute-done | bytes 65568 | tf_op jit(solution)/shard_map/ppermute | solution.py:491
  47.9 10.3 %shard_map.72 = (bf16[256,256]{1,0:T(8,128)(2,1)S(1)}, bf16[256,256]{1,0:T(8,128)(2,1)S(1)}, bf16[256,256]{1,0:T(8,128)(2,1)S(1)}, bf16[256,256]{1,0:T(8,128)(2,1)S(1)}) custom-call(s32[1]{0:T(128)} %bitcast.core_ref, f32[136,128]{1,0:T(8,128)S(1)} %add.27.mine1_ref, f32[128,128]{1,0:T(8,128)S(1)} %add.31.mine2_ref, ...), custom_call_target="tpu_custom_call" | custom-call | flops 1000000000 | bytes 1000000 | tf_op jit(solution)/shard_map/pallas_call | solution.py:22
  58.2 0.6 shard_map.73
  58.8 1.7 %shard_map.74 = (f32[2,384,128]{2,1,0:T(8,128)S(1)}, f32[2,2,384,128]{3,2,1,0:T(8,128)S(1)}, f32[768,128]{1,0:T(8,128)S(1)}, f32[1536,128]{1,0:T(8,128)S(1)}) custom-call(s32[1]{0:T(128)} %bitcast.core_ref, f32[384,16]{1,0:T(8,128)S(1)} %copy-done.2, f32[2,384,128]{2,1,0:T(8,128)S(1)} %get-tuple-element.66.outer_ref, ...), custom_call_target="tpu_custom_call" | custom-call | flops 10000000000 | bytes 6000000 | tf_op jit(solution)/shard_map/pallas_call | solution.py:22
  61.0 1.9 %collective-permute-start.13 = (f32[768,128]{1,0:T(8,128)S(1)}, f32[768,128]{1,0:T(8,128)S(1)}, u32[]{:S(2)}, u32[]{:S(2)}) collective-permute-start(f32[768,128]{1,0:T(8,128)S(1)} %get-tuple-element.67.outer1_ref.own1_ref), channel_id=1, source_target_pairs={{1,2},{3,4},{5,6},{7,8},{9,10},{11,12},{13,14},{2,1},{4,3},{6,5},{... | collective-permute-start | bytes 1179656 | tf_op jit(solution)/shard_map/ppermute | solution.py:497
  62.9 3.6 %collective-permute-start.15 = (f32[768,128]{1,0:T(8,128)S(1)}, f32[768,128]{1,0:T(8,128)S(1)}, u32[]{:S(2)}, u32[]{:S(2)}) collective-permute-start(f32[768,128]{1,0:T(8,128)S(1)} %get-tuple-element.77), channel_id=1, source_target_pairs={{1,2},{3,4},{5,6},{7,8},{9,10},{11,12},{13,14},{2,1},{4,3},{6,5},{... | collective-permute-start | bytes 1179656 | tf_op jit(solution)/shard_map/ppermute | solution.py:497
  66.5 3.0 %shard_map.77 = f32[4,2,384,128]{3,2,1,0:T(8,128)} custom-call(s32[1]{0:T(128)} %bitcast.core_ref, bf16[3072,256]{1,0:T(8,128)(2,1)S(1)} %get-tuple-element.41.qh_ref, bf16[3072,256]{1,0:T(8,128)(2,1)S(1)} %get-tuple-element.42.ql_ref, bf16[3072,128]{1,0:T(8,128)(2,1)S(1)} %get-tuple-element.43.nh_ref, bf16[3072,128]{1,0:T(8,128)(2,1)S(1)} %get-tuple-element.44.nl_ref, ...), custom_call_target="tpu_custom_call" | custom-call | tf_op jit(solution)/shard_map/pallas_call | solution.py:22
  69.5 8.9 %collective-permute-done.13.outer1_ref = f32[768,128]{1,0:T(8,128)S(1)} collective-permute-done((f32[768,128]{1,0:T(8,128)S(1)}, f32[768,128]{1,0:T(8,128)S(1)}, u32[]{:S(2)}, u32[]{:S(2)}) %collective-permute-start.13) | collective-permute-done | bytes 393248 | tf_op jit(solution)/shard_map/ppermute | solution.py:497
  78.5 2.2 %shard_map.75 = (f32[2,2,384,128]{3,2,1,0:T(8,128)S(1)}, f32[2,2,384,128]{3,2,1,0:T(8,128)S(1)}) custom-call(f32[384,16]{1,0:T(8,128)S(1)} %copy-done.2, f32[2,384,128]{2,1,0:T(8,128)S(1)} %get-tuple-element.66.outer_ref, f32[2,384,128]{2,1,0:T(8,128)S(1)} %get-tuple-element.72.light_ref, f32[2,2,384,128]{3,2,1,0:T(8,128)S(1)} %get-tuple-element.73.heavy_ref, ...), custom_call_target="tpu_custom_call" | custom-call | flops 10000000 | bytes 6000000 | tf_op jit(solution)/shard_map/pallas_call | solution.py:22
  80.6 2.0 %collective-permute-done.15.outer2_ref = f32[768,128]{1,0:T(8,128)S(1)} collective-permute-done((f32[768,128]{1,0:T(8,128)S(1)}, f32[768,128]{1,0:T(8,128)S(1)}, u32[]{:S(2)}, u32[]{:S(2)}) %collective-permute-start.15) | collective-permute-done | bytes 393248 | tf_op jit(solution)/shard_map/ppermute | solution.py:497
  82.7 1.3 %shard_map.76 = f32[4,2,384,128]{3,2,1,0:T(8,128)} custom-call(s32[1]{0:T(128)} %bitcast.core_ref, f32[2,2,384,128]{3,2,1,0:T(8,128)S(1)} %get-tuple-element.75.light_ref, f32[2,2,384,128]{3,2,1,0:T(8,128)S(1)} %get-tuple-element.76.heavy_ref, f32[768,128]{1,0:T(8,128)S(1)} %collective-permute-done.15.outer2_ref), custom_call_target="tpu_custom_call" | custom-call | flops 1000000 | bytes 6000000 | tf_op jit(solution)/shard_map/pallas_call | solution.py:22
  (28 shorter events, 1.7 us)
Async XLA Ops:
  4.3 18.5 %collective-permute-start.1 = (f32[1544,128]{1,0:T(8,128)}, f32[1544,128]{1,0:T(8,128)S(1)}, u32[]{:S(2)}, u32[]{:S(2)}) collective-permute-start(f32[1544,128]{1,0:T(8,128)} %get-tuple-element.46), channel_id=1, source_target_pairs={{0,1},{1,0},{2,3},{3,2},{4,5},{5,4},{6,7},{7,6},{8,9},{9,8},{10,11... | collective-permute-start | bytes 2371592 | tf_op jit(solution)/shard_map/ppermute | solution.py:491
  5.1 17.8 %collective-permute-start.2 = (f32[768,128]{1,0:T(8,128)}, f32[768,128]{1,0:T(8,128)S(1)}, u32[]{:S(2)}, u32[]{:S(2)}) collective-permute-start(f32[768,128]{1,0:T(8,128)} %get-tuple-element.47), channel_id=1, source_target_pairs={{1,2},{3,4},{5,6},{7,8},{9,10},{11,12},{13,14},{2,1},{4,3},{6,5},{... | collective-permute-start | bytes 1179656 | tf_op jit(solution)/shard_map/ppermute | solution.py:497
  8.1 19.0 %collective-permute-start = (f32[776,128]{1,0:T(8,128)}, f32[776,128]{1,0:T(8,128)S(1)}, u32[]{:S(2)}, u32[]{:S(2)}) collective-permute-start(f32[776,128]{1,0:T(8,128)} %get-tuple-element.45), channel_id=1, source_target_pairs={{1,2},{3,4},{5,6},{7,8},{9,10},{11,12},{13,14},{2,1},{4,3},{6,5},{... | collective-permute-start | bytes 1191944 | tf_op jit(solution)/shard_map/ppermute | solution.py:497
  10.7 1.9 %copy-start.1 = (f32[4,2,384,256]{3,2,1,0:T(8,128)S(1)}, f32[4,2,384,256]{3,2,1,0:T(8,128)}, u32[]{:S(2)}) copy-start(f32[4,2,384,256]{3,2,1,0:T(8,128)} %param.8) | copy-start | bytes 9437188
  12.5 1.4 %copy-start.3 = (f32[4,2,384,128]{3,2,1,0:T(8,128)S(1)}, f32[4,2,384,128]{3,2,1,0:T(8,128)}, u32[]{:S(2)}) copy-start(f32[4,2,384,128]{3,2,1,0:T(8,128)} %param.7) | copy-start | bytes 4718596
  14.0 8.9 %copy-start = (f32[4,2,384,128]{3,2,1,0:T(8,128)S(1)}, f32[4,2,384,128]{3,2,1,0:T(8,128)}, u32[]{:S(2)}) copy-start(f32[4,2,384,128]{3,2,1,0:T(8,128)} %z_ref.3) | copy-start | bytes 4718596
  14.0 8.9 %copy-start.2 = (f32[384,16]{1,0:T(8,128)S(1)}, f32[384,16]{1,0:T(8,128)}, u32[]{:S(2)}) copy-start(f32[384,16]{1,0:T(8,128)} %get-tuple-element.40.table_ref) | copy-start | bytes 73732
  28.1 19.8 %copy-start.4 = (f32[256,256]{1,0:T(8,128)S(1)}, f32[256,256]{1,0:T(8,128)}, u32[]{:S(2)}) copy-start(f32[256,256]{1,0:T(8,128)} %r_bar_ref.1) | copy-start | bytes 786436
  28.1 1.3 %collective-permute-start.3 = (f32[136,128]{1,0:T(8,128)S(1)}, f32[136,128]{1,0:T(8,128)S(1)}, u32[]{:S(2)}, u32[]{:S(2)}) collective-permute-start(f32[136,128]{1,0:T(8,128)S(1)} %get-tuple-element.59), channel_id=1, source_target_pairs={{0,1},{1,0},{2,3},{3,2},{4,5},{5,4},{6,7},{7,6},{8,9},{9,8},{10,11... | collective-permute-start | bytes 208904 | tf_op jit(solution)/shard_map/ppermute | solution.py:491
  28.2 1.4 %collective-permute-start.7 = (f32[128,128]{1,0:T(8,128)S(1)}, f32[128,128]{1,0:T(8,128)S(1)}, u32[]{:S(2)}, u32[]{:S(2)}) collective-permute-start(f32[128,128]{1,0:T(8,128)S(1)} %get-tuple-element.61), channel_id=1, source_target_pairs={{0,1},{1,0},{2,3},{3,2},{4,5},{5,4},{6,7},{7,6},{8,9},{9,8},{10,11... | collective-permute-start | bytes 196616 | tf_op jit(solution)/shard_map/ppermute | solution.py:491
  29.5 3.5 %collective-permute-start.4 = (f32[136,128]{1,0:T(8,128)S(1)}, f32[136,128]{1,0:T(8,128)S(1)}, u32[]{:S(2)}, u32[]{:S(2)}) collective-permute-start(f32[136,128]{1,0:T(8,128)S(1)} %add.24), channel_id=1, source_target_pairs={{0,2},{1,5},{2,0},{3,7},{4,6},{5,1},{6,4},{7,3},{8,10},{9,13},{10,... | collective-permute-start | bytes 208904 | tf_op jit(solution)/shard_map/ppermute | solution.py:508
  29.6 5.8 %collective-permute-start.8 = (f32[128,128]{1,0:T(8,128)S(1)}, f32[128,128]{1,0:T(8,128)S(1)}, u32[]{:S(2)}, u32[]{:S(2)}) collective-permute-start(f32[128,128]{1,0:T(8,128)S(1)} %add.28), channel_id=1, source_target_pairs={{0,4},{1,3},{2,6},{3,1},{4,0},{5,7},{6,2},{7,5},{8,12},{9,11},{10,... | collective-permute-start | bytes 196616 | tf_op jit(solution)/shard_map/ppermute | solution.py:508
  33.0 4.3 %collective-permute-start.5 = (f32[136,128]{1,0:T(8,128)S(1)}, f32[136,128]{1,0:T(8,128)S(1)}, u32[]{:S(2)}, u32[]{:S(2)}) collective-permute-start(f32[136,128]{1,0:T(8,128)S(1)} %add.25), channel_id=1, source_target_pairs={{0,4},{1,9},{2,6},{3,11},{4,0},{5,13},{6,2},{7,15},{8,12},{9,1},{1... | collective-permute-start | bytes 208904 | tf_op jit(solution)/shard_map/ppermute | solution.py:508
  35.4 3.3 %collective-permute-start.9 = (f32[128,128]{1,0:T(8,128)S(1)}, f32[128,128]{1,0:T(8,128)S(1)}, u32[]{:S(2)}, u32[]{:S(2)}) collective-permute-start(f32[128,128]{1,0:T(8,128)S(1)} %add.29), channel_id=1, source_target_pairs={{0,8},{1,5},{2,10},{3,7},{4,12},{5,1},{6,14},{7,3},{8,0},{9,13},{1... | collective-permute-start | bytes 196616 | tf_op jit(solution)/shard_map/ppermute | solution.py:508
  37.3 3.2 %collective-permute-start.6 = (f32[136,128]{1,0:T(8,128)S(1)}, f32[136,128]{1,0:T(8,128)S(1)}, u32[]{:S(2)}, u32[]{:S(2)}) collective-permute-start(f32[136,128]{1,0:T(8,128)S(1)} %add.26), channel_id=1, source_target_pairs={{0,8},{1,3},{2,10},{3,1},{4,12},{5,7},{6,14},{7,5},{8,0},{9,11},{1... | collective-permute-start | bytes 208904 | tf_op jit(solution)/shard_map/ppermute | solution.py:508
  38.7 6.2 %collective-permute-start.10 = (f32[128,128]{1,0:T(8,128)S(1)}, f32[128,128]{1,0:T(8,128)S(1)}, u32[]{:S(2)}, u32[]{:S(2)}) collective-permute-start(f32[128,128]{1,0:T(8,128)S(1)} %add.30), channel_id=1, source_target_pairs={{0,2},{1,9},{2,0},{3,11},{4,6},{5,13},{6,4},{7,15},{8,10},{9,1},{1... | collective-permute-start | bytes 196616 | tf_op jit(solution)/shard_map/ppermute | solution.py:508
  40.5 7.4 %collective-permute-start.11 = (f32[136,128]{1,0:T(8,128)S(1)}, f32[136,128]{1,0:T(8,128)S(1)}, u32[]{:S(2)}, u32[]{:S(2)}) collective-permute-start(f32[136,128]{1,0:T(8,128)S(1)} %add.27.mine1_ref), channel_id=1, source_target_pairs={{0,1},{1,0},{2,3},{3,2},{4,5},{5,4},{6,7},{7,6},{8,9},{9,8},{10,11... | collective-permute-start | bytes 208904 | tf_op jit(solution)/shard_map/ppermute | solution.py:491
  44.9 2.9 %collective-permute-start.12 = (f32[128,128]{1,0:T(8,128)S(1)}, f32[128,128]{1,0:T(8,128)S(1)}, u32[]{:S(2)}, u32[]{:S(2)}) collective-permute-start(f32[128,128]{1,0:T(8,128)S(1)} %add.31.mine2_ref), channel_id=1, source_target_pairs={{0,1},{1,0},{2,3},{3,2},{4,5},{5,4},{6,7},{7,6},{8,9},{9,8},{10,11... | collective-permute-start | bytes 196616 | tf_op jit(solution)/shard_map/ppermute | solution.py:491
  60.5 17.9 %collective-permute-start.14 = (f32[1536,128]{1,0:T(8,128)S(1)}, f32[1536,128]{1,0:T(8,128)S(1)}, u32[]{:S(2)}, u32[]{:S(2)}) collective-permute-start(f32[1536,128]{1,0:T(8,128)S(1)} %get-tuple-element.74.own_ref), channel_id=1, source_target_pairs={{0,1},{1,0},{2,3},{3,2},{4,5},{5,4},{6,7},{7,6},{8,9},{9,8},{10,11... | collective-permute-start | bytes 2359304 | tf_op jit(solution)/shard_map/ppermute | solution.py:491
  61.0 17.5 %collective-permute-start.13 = (f32[768,128]{1,0:T(8,128)S(1)}, f32[768,128]{1,0:T(8,128)S(1)}, u32[]{:S(2)}, u32[]{:S(2)}) collective-permute-start(f32[768,128]{1,0:T(8,128)S(1)} %get-tuple-element.67.outer1_ref.own1_ref), channel_id=1, source_target_pairs={{1,2},{3,4},{5,6},{7,8},{9,10},{11,12},{13,14},{2,1},{4,3},{6,5},{... | collective-permute-start | bytes 1179656 | tf_op jit(solution)/shard_map/ppermute | solution.py:497
  62.9 19.8 %collective-permute-start.15 = (f32[768,128]{1,0:T(8,128)S(1)}, f32[768,128]{1,0:T(8,128)S(1)}, u32[]{:S(2)}, u32[]{:S(2)}) collective-permute-start(f32[768,128]{1,0:T(8,128)S(1)} %get-tuple-element.77), channel_id=1, source_target_pairs={{1,2},{3,4},{5,6},{7,8},{9,10},{11,12},{13,14},{2,1},{4,3},{6,5},{... | collective-permute-start | bytes 1179656 | tf_op jit(solution)/shard_map/ppermute | solution.py:497

commit v10 on v9

--- a/solution.py
+++ b/solution.py
@@ -87,18 +87,22 @@
     return -2.0 * g * pa - w * pb, w * xb - 0.5 * m * pb
 
 
-def forward_rim(core_ref, coeff_hbm, z_hbm, outer1_ref, outer2_ref, inner_ref, table_ref, coeff_ref, z_ref, sems):
-    n = z_ref.shape[2]
-    core = core_ref[0]
+def forward_sources(core_ref, z_hbm, outer1_ref, sems):
+    n = z_hbm.shape[2]
     copies = [
-        pltpu.make_async_copy(z_hbm.at[0:3, core], z_ref.at[0], sems.at[0]),
-        pltpu.make_async_copy(z_hbm.at[0:3, 1 - core], z_ref.at[1], sems.at[1]),
-        pltpu.make_async_copy(coeff_hbm, coeff_ref, sems.at[2]),
+        pltpu.make_async_copy(z_hbm.at[k, core_ref[0]], outer1_ref.at[pl.ds(k * n, n)], sems.at[k]) for k in range(2)
     ]
     for copy in copies:
         copy.start()
+    outer1_ref[2 * n :] = jnp.zeros((16, z_hbm.shape[3]), f32)
     for copy in copies:
         copy.wait()
+
+
+def forward_rim(core_ref, coeff_ref, z_ref, outer2_ref, inner1_ref, inner2_ref, table_ref):
+    n = z_ref.shape[2]
+    core = core_ref[0]
+    z = [[z_ref[k, row] for k in range(3)] for row in (core, 1 - core)]
     cols = jnp.transpose(jnp.concatenate([coeff_ref[k] for k in range(6)], axis=0))
     swapped = core == 1
     both = []
@@ -110,20 +114,18 @@
         table_ref[:, place : place + 1] = column
     far = []
     for s in range(2):
-        xa, pa, xb = z_ref[s, 0], z_ref[s, 1], z_ref[s, 2]
-        hop_x = z_ref[1 - s, 0] + side(xa)
-        hop_p = z_ref[1 - s, 1] + side(pa)
+        xa, pa, xb = z[s]
+        hop_x = z[1 - s][0] + side(xa)
+        hop_p = z[1 - s][1] + side(pa)
         far.append(forward_light(both[6 * s : 6 * s + 6], xa, pa, xb, hop_x, hop_p))
-    outer1_ref[0:n] = z_ref[0, 0]
-    outer1_ref[n : 2 * n] = z_ref[0, 1]
-    inner_ref[0:n] = z_ref[1, 0]
-    inner_ref[n : 2 * n] = z_ref[1, 1]
-    for s, out, base in ((0, outer2_ref, 0), (1, inner_ref, 2 * n)):
-        out[base : base + n], out[base + n : base + 2 * n] = far[s]
+    inner1_ref[0:n] = z[1][0]
+    inner1_ref[n : 2 * n] = z[1][1]
+    for s, out in ((0, outer2_ref), (1, inner2_ref)):
+        out[0:n], out[n : 2 * n] = far[s]
         hopping = jnp.where(swapped, coeff_ref[5, 1 - s : 2 - s, :], coeff_ref[5, s : s + 1, :]) * rate_scales[5]
         pieces = [hopping[:, k * 128 : (k + 1) * 128] for k in range(n // 128)]
         pieces.append(jnp.zeros((8 - n // 128, 128), f32))
-        out[base + 2 * n :] = jnp.concatenate(pieces, axis=0)
+        out[2 * n :] = jnp.concatenate(pieces, axis=0)
 
 
 def far_hopping(recv_ref, n):
@@ -174,7 +176,7 @@
 
 
 def expand_first(
-    core_ref, table_ref, z_ref, inner_ref, outer1_ref, nht_ref, nlt_ref, qht_ref, qlt_ref,
+    core_ref, table_ref, z_ref, outer1_ref, inner1_ref, inner2_ref, nht_ref, nlt_ref, qht_ref, qlt_ref,
     light_ref, hh_ref, hl_ref, ih_ref, il_ref, gram_ref, rest_ref, first_ref,
 ):
     c = coefficients(table_ref)
@@ -182,7 +184,7 @@
     core = core_ref[0]
     rows = (core, 1 - core)
     z = [[z_ref[k, row] for k in range(4)] for row in rows]
-    for s, beyond in enumerate((outer1_ref, inner_ref)):
+    for s, beyond in enumerate((outer1_ref, inner1_ref)):
         xa, pa, xb, pb = z[s]
         hop_x = z[1 - s][0] + beyond[0:n] + side(xa)
         hop_p = z[1 - s][1] + beyond[n : 2 * n] + side(pa)
@@ -194,14 +196,14 @@
             h, l = split2(z[s][2 + k] + f + 0.5 * second)
             hh_ref[cells(rows[s], k, n)] = h
             hl_ref[cells(rows[s], k, n)] = l
-    jfar = far_hopping(inner_ref, n)
+    jfar = far_hopping(inner2_ref, n)
     for s in range(2):
         xa, pa, xb, pb = (first_ref[k, s] for k in range(4))
         hop_x = first_ref[0, 1 - s] + side(xa)
         hop_p = first_ref[1, 1 - s] + side(pa)
         if s == 1:
-            hop_x = hop_x + inner_ref[2 * n : 3 * n] - jfar * z[s][1]
-            hop_p = hop_p + inner_ref[3 * n : 4 * n] + jfar * z[s][0]
+            hop_x = hop_x + inner2_ref[0:n] - jfar * z[s][1]
+            hop_p = hop_p + inner2_ref[n : 2 * n] + jfar * z[s][0]
         second = forward_light(c[s], xa, pa, xb, hop_x, hop_p)
         for k in range(2):
             value = z[s][k] + first_ref[k, s] + 0.5 * second[k]
@@ -392,11 +394,12 @@
         w = columns(*parts, *weights)
         w_ref[k] = w
         outer1_ref[here] = j * w
+    outer1_ref[2 * n :] = jnp.zeros((8, w_ref.shape[2]), f32)
 
 
 def gradient_rest(
     core_ref, table_ref, outer_ref, outer1_ref, qh_ref, ql_ref, nh_ref, nl_ref, lh_ref, ll_ref, hh_ref, hl_ref,
-    ih_ref, il_ref, sh_ref, sl_ref, light_ref, heavy_ref, outer2_ref, inner_ref,
+    ih_ref, il_ref, sh_ref, sl_ref, light_ref, heavy_ref, outer2_ref, inner1_ref, inner2_ref,
 ):
     c = coefficients(table_ref)
     n = outer_ref.shape[1]
@@ -408,19 +411,19 @@
         here = slice(k * n, (k + 1) * n)
         w = columns(*[ref[there] for ref in left], lh_ref[here], ll_ref[here], *weights)
         light_ref[k] = w
-        inner_ref[here] = c[1][5] * w
+        inner1_ref[here] = c[1][5] * w
     for k in (1, 0):
         for s, row in enumerate((core, 1 - core)):
             there = cells(row, 2 + k, n)
             here = cells(row, k, n)
             heavy_ref[k, s] = columns(*[ref[there] for ref in left], hh_ref[here], hl_ref[here], *weights)
-    own = (outer1_ref, inner_ref)
-    for s, w, out, base in ((0, outer_ref, outer2_ref, 0), (1, light_ref, inner_ref, 2 * n)):
+    own = (outer1_ref, inner1_ref)
+    for s, w, out in ((0, outer_ref, outer2_ref), (1, light_ref, inner2_ref)):
         hop_x = own[1 - s][0:n] + side(own[s][0:n])
         hop_p = own[1 - s][n : 2 * n] + side(own[s][n : 2 * n])
         bx, bp = backward_light(c[s], w[0], w[1], heavy_ref[1, s], hop_x, hop_p)
-        out[base : base + n] = c[s][5] * bx
-        out[base + n : base + 2 * n] = c[s][5] * bp
+        out[0:n] = c[s][5] * bx
+        out[n : 2 * n] = c[s][5] * bp
 
 
 def gradient_noise(
@@ -443,7 +446,8 @@
 
 
 def contract_first(
-    table_ref, outer_ref, light_ref, heavy_ref, own1_ref, own_ref, outer1_ref, inner_ref, fouter2_ref, finner_ref,
+    outer1_ref, table_ref, outer_ref, light_ref, heavy_ref, own1_ref, own2_ref, inner1_ref, inner2_ref,
+    fouter2_ref, finner_ref,
     out_light_ref, out_heavy_ref, first_ref,
 ):
     c = coefficients(table_ref)
@@ -452,8 +456,8 @@
         (outer_ref[0], outer_ref[1], heavy_ref[0, 0], heavy_ref[1, 0]),
         (light_ref[0], light_ref[1], heavy_ref[0, 1], heavy_ref[1, 1]),
     ]
-    own = [(ref[0:n], ref[n : 2 * n]) for ref in (own1_ref, own_ref)]
-    for s, far in enumerate((outer1_ref, inner_ref)):
+    own = [(ref[0:n], ref[n : 2 * n]) for ref in (own1_ref, own2_ref)]
+    for s, far in enumerate((outer1_ref, inner1_ref)):
         xa, pa, xb, pb = w[s]
         hop_x = own[1 - s][0] + far[0:n] + side(own[s][0])
         hop_p = own[1 - s][1] + far[n : 2 * n] + side(own[s][1])
@@ -466,8 +470,8 @@
         hop_x = jother * first_ref[0, 1 - s] + jfar * own[s][1] + side(j * xa)
         hop_p = jother * first_ref[1, 1 - s] - jfar * own[s][0] + side(j * pa)
         if s == 1:
-            hop_x = hop_x + inner_ref[2 * n : 3 * n]
-            hop_p = hop_p + inner_ref[3 * n : 4 * n]
+            hop_x = hop_x + inner2_ref[0:n]
+            hop_p = hop_p + inner2_ref[n : 2 * n]
         light = backward_light(c[s], xa, pa, pb, hop_x, hop_p)
         heavy = backward_heavy(c[s], pa, xb, pb)
         for k in range(2):
@@ -520,16 +524,15 @@
     hops = shape((2 * n, rank), f32)
     rim = shape((2 * n + 8, rank), f32)
     table = shape((n, 16), f32)
-    outer1, outer2, inner, table = call(
-        forward_rim, (hops, rim, shape((4 * n + 8, rank), f32), table), 10**6, 3 * 10**6,
-        [
-            pltpu.VMEM(cell_coeffs.shape, f32),
-            pltpu.VMEM((2, 3, n, rank), f32),
-            pltpu.SemaphoreType.DMA((3,)),
-        ],
-        scalar=True, far=True,
-    )(core, coeffs, z_factor)
-    outer1, outer2, inner = swap_outer(outer1), swap_outer(outer2), swap_inner(inner)
+    outer1 = call(
+        forward_sources, shape((2 * n + 16, rank), f32), 0, 10**6, [pltpu.SemaphoreType.DMA((2,))], scalar=True, far=True
+    )(core, z_factor)
+    outer1, behind = lax.optimization_barrier((outer1, core))
+    outer2, inner1, inner2, table = call(
+        forward_rim, (rim, hops, rim, table), 10**6, 3 * 10**6, scalar=True
+    )(behind, coeffs, z_factor)
+    outer1, outer2 = swap_outer(outer1), swap_outer(outer2)
+    inner1, inner2 = swap_inner(inner1), swap_inner(inner2)
     wide, tall = shape((flat, 256), bf16), shape((flat, 128), bf16)
     wide_t, tall_t = shape((256, flat), bf16), shape((128, flat), bf16)
     work = 2 * flat * 128 * 128
@@ -544,7 +547,7 @@
         expand_first,
         (single, half, half, quarter, quarter, shape((128, 128), f32), shape((384, 128), f32)),
         work * 8, 9 * 10**6, [pltpu.VMEM(z_factor.shape, f32)], scalar=True,
-    )(core, table, z_factor, inner, outer1, *transposed)
+    )(core, table, z_factor, outer1, inner1, inner2, *transposed)
     part1, part2 = shape((136, 128), f32), shape((128, 128), f32)
     *parts, oh, ol = call(
         expand_last, (part1, part2, part1, part2, quarter, quarter), work * 3, 5 * 10**6, [pltpu.VMEM((528, 128), f32)], scalar=True
@@ -562,19 +565,19 @@
         scalar=True,
     )(core, *parts, r_bar)
     left = (qh, ql, nh, nl)
-    w_outer, own1 = call(gradient_outer, (single, hops), work * 3, 3 * 10**6, scalar=True)(
+    w_outer, own1 = call(gradient_outer, (single, rim), work * 3, 3 * 10**6, scalar=True)(
         core, table, *left, oh, ol, *weights
     )
     back1 = swap_outer(own1)
-    w_inner, w_heavy, own2, own = call(
-        gradient_rest, (single, pair, hops, shape((4 * n, rank), f32)), 10**10, 6 * 10**6, scalar=True
+    w_inner, w_heavy, last, own2, own3 = call(
+        gradient_rest, (single, pair, hops, hops, hops), 10**10, 6 * 10**6, scalar=True
     )(core, table, w_outer, own1, *left, lh, ll, hh, hl, *weights)
-    back2, back = swap_outer(own2), swap_inner(own)
+    back2, near1, near2 = swap_outer(last), swap_inner(own2), swap_inner(own3)
     noise_grad = call(gradient_noise, shape(noise_cols.shape, f32), 0, 0, scalar=True)(
         core, *left, oh, ol, lh, ll, hh, hl, *weights
     )
     out_light, out_heavy = call(contract_first, (pair, pair), 10**7, 6 * 10**6, [pltpu.VMEM(z_factor.shape, f32)])(
-        table, w_outer, w_inner, w_heavy, own1, own, back1, back, outer2, inner
+        back1, table, w_outer, w_inner, w_heavy, own1, own2, near1, near2, outer2, inner2
     )
     z_grad = call(contract_last, shape(z_factor.shape, f32), 10**6, 6 * 10**6, scalar=True)(
         core, out_light, out_heavy, back2

time: 84.2 us -> 79.8 us (0.948)
  waiting for transfers between devices: 25.7 us -> 19.6 us
  starting transfers between devices: 25.3 us -> 27.2 us
    ppermute x4, waiting for transfers between devices: 19.1 us -> 13.7 us  [swap_outer(): return lax.ppermute(message, 'row', pairs + [(j, i) for i, j in pairs])]
    ppermute x6, starting transfers between devices: 5.99 us -> 6.98 us  [sum_over_rows(): mine[stream] = mine[stream] + lax.ppermute(mine[stream], 'row', pairs)]
    ppermute x6 -> x8, starting transfers between devices: 8.19 us -> 8.69 us  [swap_inner(): return lax.ppermute(message, 'row', [(i, i ^ 1) for i in range(count)])]
    pallas_call x10 -> x11, Pallas kernels: 28.8 us -> 28.4 us  [run(): pl.pallas_call(kernel, out_shape=outs, in_specs=specs, scratch_shapes=lis...]
    ppermute x6 -> x8, waiting for transfers between devices: 1.72 us -> 1.73 us  [swap_inner(): return lax.ppermute(message, 'row', [(i, i ^ 1) for i in range(count)])]
    unnamed x10 -> x12, local copies, waits for them, and re-layouts: 3.31 us -> 3.31 us
  transfers between devices with their start and end apart: 16 -> 18, of which waited for: 11 -> 11; matrix products, arithmetic and copies ran while one was open for 0% -> 0% of each run, Pallas kernels for 12% -> 17%
where the time goes in v10:
time: 79.8 us; the launch traced here: 79.5 us
  Pallas kernels  28.4 us (36%)
  starting transfers between devices  27.2 us (34%)
  waiting for transfers between devices  19.6 us (25%)
  local copies, waits for them, and re-layouts  3.31 us (4%)
  between operations  0.85 us (1%)
    pallas_call x11, Pallas kernels, run(): pl.pallas_call(kernel, out_shape=outs, in_specs=specs, scratch_shapes=lis...  28.4 us
    ppermute x4, waiting for transfers between devices, swap_outer(): return lax.ppermute(message, 'row', pairs + [(j, i) for i, j in pairs])  13.7 us
    ppermute x4, starting transfers between devices, swap_outer(): return lax.ppermute(message, 'row', pairs + [(j, i) for i, j in pairs])  11.5 us
    ppermute x8, starting transfers between devices, swap_inner(): return lax.ppermute(message, 'row', [(i, i ^ 1) for i in range(count)])  8.69 us
    ppermute x6, starting transfers between devices, sum_over_rows(): mine[stream] = mine[stream] + lax.ppermute(mine[stream], 'row', pairs)  6.98 us
    ppermute x6, waiting for transfers between devices, sum_over_rows(): mine[stream] = mine[stream] + lax.ppermute(mine[stream], 'row', pairs)  4.22 us
    unnamed x12, local copies, waits for them, and re-layouts  3.31 us
    ppermute x8, waiting for transfers between devices, swap_inner(): return lax.ppermute(message, 'row', [(i, i ^ 1) for i in range(count)])  1.73 us
  transfers between devices with their start and end apart: 18, of which 11 were waited for; matrix products, arithmetic and copies ran while one was open for 0% of the time, Pallas kernels for 17%

profile of v10, /device:TPU:9, one launch (start us, length us, event | category | flops | bytes accessed | tf_op | source)
XLA Modules:
  0.0 79.5 jit_solution(3159908832088954835)
XLA Ops:
  0.6 1.8 %shard_map.68 = f32[784,128]{1,0:T(8,128)} custom-call(s32[1]{0:T(128)} %bitcast.core_ref, f32[4,2,384,128]{3,2,1,0:T(8,128)} %z_ref.5), custom_call_target="tpu_custom_call" | custom-call | bytes 1000000 | tf_op jit(solution)/shard_map/pallas_call | solution.py:22
  2.4 3.7 %collective-permute-start.1 = (f32[784,128]{1,0:T(8,128)}, f32[784,128]{1,0:T(8,128)S(1)}, u32[]{:S(2)}, u32[]{:S(2)}) collective-permute-start(f32[784,128]{1,0:T(8,128)} %shard_map.68), channel_id=1, source_target_pairs={{1,2},{3,4},{5,6},{7,8},{9,10},{11,12},{13,14},{2,1},{4,3},{6,5},{... | collective-permute-start | bytes 1204232 | tf_op jit(solution)/shard_map/ppermute | solution.py:501
  6.2 1.4 %copy-done = f32[4,2,384,128]{3,2,1,0:T(8,128)S(1)} copy-done((f32[4,2,384,128]{3,2,1,0:T(8,128)S(1)}, f32[4,2,384,128]{3,2,1,0:T(8,128)}, u32[]{:S(2)}) %copy-start) | copy-done | bytes 1572888
  7.6 1.6 %shard_map.69 = (f32[776,128]{1,0:T(8,128)S(1)}, f32[768,128]{1,0:T(8,128)S(1)}, f32[776,128]{1,0:T(8,128)S(1)}, f32[384,16]{1,0:T(8,128)S(1)}) custom-call(s32[1]{0:T(128)} %bitcast.core_ref, f32[6,2,384]{2,1,0:T(2,128)S(1)} %copy-done.4, f32[4,2,384,128]{3,2,1,0:T(8,128)S(1)} %copy-done), custom_call_target="tpu_custom_call" | custom-call | flops 1000000 | bytes 3000000 | tf_op jit(solution)/shard_map/pallas_call | solution.py:22
  9.7 3.1 %collective-permute-start = (f32[776,128]{1,0:T(8,128)S(1)}, f32[776,128]{1,0:T(8,128)S(1)}, u32[]{:S(2)}, u32[]{:S(2)}) collective-permute-start(f32[776,128]{1,0:T(8,128)S(1)} %get-tuple-element.49), channel_id=1, source_target_pairs={{1,2},{3,4},{5,6},{7,8},{9,10},{11,12},{13,14},{2,1},{4,3},{6,5},{... | collective-permute-start | bytes 1191944 | tf_op jit(solution)/shard_map/ppermute | solution.py:501
  12.8 1.9 %copy-done.2 = f32[4,2,384,256]{3,2,1,0:T(8,128)S(1)} copy-done((f32[4,2,384,256]{3,2,1,0:T(8,128)S(1)}, f32[4,2,384,256]{3,2,1,0:T(8,128)}, u32[]{:S(2)}) %copy-start.2) | copy-done | bytes 3145752
  14.7 1.8 %shard_map.70 = (f32[136,128]{1,0:T(8,128)S(1)}, bf16[3072,128]{1,0:T(8,128)(2,1)S(1)}, bf16[3072,128]{1,0:T(8,128)(2,1)S(1)}, bf16[3072,256]{1,0:T(8,128)(2,1)S...) custom-call(f32[3072,128]{1,0:T(8,128)S(1)} %bitcast.4, ...), custom_call_target="tpu_custom_call" | custom-call | flops 503316480 | bytes 9000000 | tf_op jit(solution)/shard_map/pallas_call | solution.py:22
  16.5 3.9 %collective-permute-done.1.outer1_ref = f32[784,128]{1,0:T(8,128)S(1)} collective-permute-done((f32[784,128]{1,0:T(8,128)}, f32[784,128]{1,0:T(8,128)S(1)}, u32[]{:S(2)}, u32[]{:S(2)}) %collective-permute-start.1) | collective-permute-done | bytes 401440 | tf_op jit(solution)/shard_map/ppermute | solution.py:501
  20.5 3.2 %shard_map.71 = (f32[2,384,128]{2,1,0:T(8,128)S(1)}, bf16[1536,128]{1,0:T(8,128)(2,1)S(1)}, bf16[1536,128]{1,0:T(8,128)(2,1)S(1)}, bf16[768,128]{1,0:T(8,128)(2,...) custom-call(s32[1]{0:T(128)} %bitcast.core_ref, ...), custom_call_target="tpu_custom_call" | custom-call | flops 805306368 | bytes 9000000 | tf_op jit(solution)/shard_map/pallas_call | solution.py:22
  23.7 1.0 %collective-permute-done.outer2_ref.fouter2_ref = f32[776,128]{1,0:T(8,128)S(1)} collective-permute-done((f32[776,128]{1,0:T(8,128)S(1)}, f32[776,128]{1,0:T(8,128)S(1)}, u32[]{:S(2)}, u32[]{:S(2)}) %collective-permute-start) | collective-permute-done | bytes 397344 | tf_op jit(solution)/shard_map/ppermute | solution.py:501
  24.7 1.0 %shard_map.72 = (f32[136,128]{1,0:T(8,128)S(1)}, f32[128,128]{1,0:T(8,128)S(1)}, f32[136,128]{1,0:T(8,128)S(1)}, f32[128,128]{1,0:T(8,128)S(1)}, bf16[768,128]{1...) custom-call(s32[1]{0:T(128)} %bitcast.core_ref, f32[384,16]{1,0:T(8,128)S(1)} %get-tuple-element.44.table_ref, ...), custom_call_target="tpu_custom_call" | custom-call | flops 301989888 | bytes 5000000 | tf_op jit(solution)/shard_map/pallas_call | solution.py:22
  26.3 0.7 collective-permute-done.4
  27.2 1.8 %collective-permute-start.9 = (f32[128,128]{1,0:T(8,128)S(1)}, f32[128,128]{1,0:T(8,128)S(1)}, u32[]{:S(2)}, u32[]{:S(2)}) collective-permute-start(f32[128,128]{1,0:T(8,128)S(1)} %add.28), channel_id=1, source_target_pairs={{0,4},{1,3},{2,6},{3,1},{4,0},{5,7},{6,2},{7,5},{8,12},{9,11},{10,... | collective-permute-start | bytes 196616 | tf_op jit(solution)/shard_map/ppermute | solution.py:512
  29.0 1.6 %collective-permute-done.5 = f32[136,128]{1,0:T(8,128)S(1)} collective-permute-done((f32[136,128]{1,0:T(8,128)S(1)}, f32[136,128]{1,0:T(8,128)S(1)}, u32[]{:S(2)}, u32[]{:S(2)}) %collective-permute-start.5) | collective-permute-done | bytes 69664 | tf_op jit(solution)/shard_map/ppermute | solution.py:512
  30.6 2.4 %collective-permute-start.6 = (f32[136,128]{1,0:T(8,128)S(1)}, f32[136,128]{1,0:T(8,128)S(1)}, u32[]{:S(2)}, u32[]{:S(2)}) collective-permute-start(f32[136,128]{1,0:T(8,128)S(1)} %add.25), channel_id=1, source_target_pairs={{0,4},{1,9},{2,6},{3,11},{4,0},{5,13},{6,2},{7,15},{8,12},{9,1},{1... | collective-permute-start | bytes 208904 | tf_op jit(solution)/shard_map/ppermute | solution.py:512
  33.2 1.6 %collective-permute-done.6 = f32[136,128]{1,0:T(8,128)S(1)} collective-permute-done((f32[136,128]{1,0:T(8,128)S(1)}, f32[136,128]{1,0:T(8,128)S(1)}, u32[]{:S(2)}, u32[]{:S(2)}) %collective-permute-start.6) | collective-permute-done | bytes 69664 | tf_op jit(solution)/shard_map/ppermute | solution.py:512
  34.9 1.1 %collective-permute-start.7 = (f32[136,128]{1,0:T(8,128)S(1)}, f32[136,128]{1,0:T(8,128)S(1)}, u32[]{:S(2)}, u32[]{:S(2)}) collective-permute-start(f32[136,128]{1,0:T(8,128)S(1)} %add.26), channel_id=1, source_target_pairs={{0,8},{1,3},{2,10},{3,1},{4,12},{5,7},{6,14},{7,5},{8,0},{9,11},{1... | collective-permute-start | bytes 208904 | tf_op jit(solution)/shard_map/ppermute | solution.py:512
  36.5 1.4 %collective-permute-start.11 = (f32[128,128]{1,0:T(8,128)S(1)}, f32[128,128]{1,0:T(8,128)S(1)}, u32[]{:S(2)}, u32[]{:S(2)}) collective-permute-start(f32[128,128]{1,0:T(8,128)S(1)} %add.30), channel_id=1, source_target_pairs={{0,2},{1,9},{2,0},{3,11},{4,6},{5,13},{6,4},{7,15},{8,10},{9,1},{1... | collective-permute-start | bytes 196616 | tf_op jit(solution)/shard_map/ppermute | solution.py:512
  38.4 4.1 %collective-permute-start.12 = (f32[136,128]{1,0:T(8,128)S(1)}, f32[136,128]{1,0:T(8,128)S(1)}, u32[]{:S(2)}, u32[]{:S(2)}) collective-permute-start(f32[136,128]{1,0:T(8,128)S(1)} %add.27.mine1_ref), channel_id=1, source_target_pairs={{0,1},{1,0},{2,3},{3,2},{4,5},{5,4},{6,7},{7,6},{8,9},{9,8},{10,11... | collective-permute-start | bytes 208904 | tf_op jit(solution)/shard_map/ppermute | solution.py:495
  42.6 2.0 %collective-permute-start.13 = (f32[128,128]{1,0:T(8,128)S(1)}, f32[128,128]{1,0:T(8,128)S(1)}, u32[]{:S(2)}, u32[]{:S(2)}) collective-permute-start(f32[128,128]{1,0:T(8,128)S(1)} %add.31.mine2_ref), channel_id=1, source_target_pairs={{0,1},{1,0},{2,3},{3,2},{4,5},{5,4},{6,7},{7,6},{8,9},{9,8},{10,11... | collective-permute-start | bytes 196616 | tf_op jit(solution)/shard_map/ppermute | solution.py:495
  44.6 0.9 %collective-permute-done.13.other2_ref = f32[128,128]{1,0:T(8,128)S(1)} collective-permute-done((f32[128,128]{1,0:T(8,128)S(1)}, f32[128,128]{1,0:T(8,128)S(1)}, u32[]{:S(2)}, u32[]{:S(2)}) %collective-permute-start.13) | collective-permute-done | bytes 65568 | tf_op jit(solution)/shard_map/ppermute | solution.py:495
  45.5 10.3 %shard_map.73 = (bf16[256,256]{1,0:T(8,128)(2,1)S(1)}, bf16[256,256]{1,0:T(8,128)(2,1)S(1)}, bf16[256,256]{1,0:T(8,128)(2,1)S(1)}, bf16[256,256]{1,0:T(8,128)(2,1)S(1)}) custom-call(s32[1]{0:T(128)} %bitcast.core_ref, f32[136,128]{1,0:T(8,128)S(1)} %add.27.mine1_ref, f32[128,128]{1,0:T(8,128)S(1)} %add.31.mine2_ref, ...), custom_call_target="tpu_custom_call" | custom-call | flops 1000000000 | bytes 1000000 | tf_op jit(solution)/shard_map/pallas_call | solution.py:22
  55.8 0.6 shard_map.74
  56.4 1.9 %collective-permute-start.14 = (f32[776,128]{1,0:T(8,128)S(1)}, f32[776,128]{1,0:T(8,128)S(1)}, u32[]{:S(2)}, u32[]{:S(2)}) collective-permute-start(f32[776,128]{1,0:T(8,128)S(1)} %get-tuple-element.71.outer1_ref.own1_ref), channel_id=1, source_target_pairs={{1,2},{3,4},{5,6},{7,8},{9,10},{11,12},{13,14},{2,1},{4,3},{6,5},{... | collective-permute-start | bytes 1191944 | tf_op jit(solution)/shard_map/ppermute | solution.py:501
  58.4 1.7 %shard_map.75 = (f32[2,384,128]{2,1,0:T(8,128)S(1)}, f32[2,2,384,128]{3,2,1,0:T(8,128)S(1)}, f32[768,128]{1,0:T(8,128)S(1)}, f32[768,128]{1,0:T(8,128)S(1)}, f32[768,128]{1,0:T(8,128)S(1)}) custom-call(s32[1]{0:T(128)} %bitcast.core_ref, f32[384,16]{1,0:T(8,128)S(1)} %get-tuple-element.44.table_ref, f32[2,384,128]{2,1,0:T(8,128)S(1)} %get-tuple-element.72.outer_ref, ...), custom_call_target="tpu_custom_call" | custom-call | flops 10000000000 | bytes 6000000 | tf_op jit(solution)/shard_map/pallas_call | solution.py:22
  60.1 1.3 %collective-permute-start.16 = (f32[768,128]{1,0:T(8,128)S(1)}, f32[768,128]{1,0:T(8,128)S(1)}, u32[]{:S(2)}, u32[]{:S(2)}) collective-permute-start(f32[768,128]{1,0:T(8,128)S(1)} %get-tuple-element.80), channel_id=1, source_target_pairs={{0,1},{1,0},{2,3},{3,2},{4,5},{5,4},{6,7},{7,6},{8,9},{9,8},{10,11... | collective-permute-start | bytes 1179656 | tf_op jit(solution)/shard_map/ppermute | solution.py:495
  61.5 2.8 %collective-permute-start.17 = (f32[768,128]{1,0:T(8,128)S(1)}, f32[768,128]{1,0:T(8,128)S(1)}, u32[]{:S(2)}, u32[]{:S(2)}) collective-permute-start(f32[768,128]{1,0:T(8,128)S(1)} %get-tuple-element.83), channel_id=1, source_target_pairs={{1,2},{3,4},{5,6},{7,8},{9,10},{11,12},{13,14},{2,1},{4,3},{6,5},{... | collective-permute-start | bytes 1179656 | tf_op jit(solution)/shard_map/ppermute | solution.py:501
  64.3 3.0 %shard_map.78 = f32[4,2,384,128]{3,2,1,0:T(8,128)} custom-call(s32[1]{0:T(128)} %bitcast.core_ref, bf16[3072,256]{1,0:T(8,128)(2,1)S(1)} %get-tuple-element.45.qh_ref, bf16[3072,256]{1,0:T(8,128)(2,1)S(1)} %get-tuple-element.46.ql_ref, bf16[3072,128]{1,0:T(8,128)(2,1)S(1)} %get-tuple-element.47.nh_ref, bf16[3072,128]{1,0:T(8,128)(2,1)S(1)} %get-tuple-element.48.nl_ref, ...), custom_call_target="tpu_custom_call" | custom-call | tf_op jit(solution)/shard_map/pallas_call | solution.py:22
  67.3 6.7 %collective-permute-done.14.outer1_ref = f32[776,128]{1,0:T(8,128)S(1)} collective-permute-done((f32[776,128]{1,0:T(8,128)S(1)}, f32[776,128]{1,0:T(8,128)S(1)}, u32[]{:S(2)}, u32[]{:S(2)}) %collective-permute-start.14) | collective-permute-done | bytes 397344 | tf_op jit(solution)/shard_map/ppermute | solution.py:501
  74.0 2.2 %shard_map.76 = (f32[2,2,384,128]{3,2,1,0:T(8,128)S(1)}, f32[2,2,384,128]{3,2,1,0:T(8,128)S(1)}) custom-call(f32[776,128]{1,0:T(8,128)S(1)} %collective-permute-done.14.outer1_ref, f32[384,16]{1,0:T(8,128)S(1)} %get-tuple-element.44.table_ref, f32[2,384,128]{2,1,0:T(8,128)S(1)} %get-tuple-element.72.outer_ref, ...), custom_call_target="tpu_custom_call" | custom-call | flops 10000000 | bytes 6000000 | tf_op jit(solution)/shard_map/pallas_call | solution.py:22
  76.2 2.0 %collective-permute-done.17.outer2_ref = f32[768,128]{1,0:T(8,128)S(1)} collective-permute-done((f32[768,128]{1,0:T(8,128)S(1)}, f32[768,128]{1,0:T(8,128)S(1)}, u32[]{:S(2)}, u32[]{:S(2)}) %collective-permute-start.17) | collective-permute-done | bytes 393248 | tf_op jit(solution)/shard_map/ppermute | solution.py:501
  78.2 1.3 %shard_map.77 = f32[4,2,384,128]{3,2,1,0:T(8,128)} custom-call(s32[1]{0:T(128)} %bitcast.core_ref, f32[2,2,384,128]{3,2,1,0:T(8,128)S(1)} %get-tuple-element.81.light_ref, f32[2,2,384,128]{3,2,1,0:T(8,128)S(1)} %get-tuple-element.82.heavy_ref, f32[768,128]{1,0:T(8,128)S(1)} %collective-permute-done.17.outer2_ref), custom_call_target="tpu_custom_call" | custom-call | flops 1000000 | bytes 6000000 | tf_op jit(solution)/shard_map/pallas_call | solution.py:22
  (35 shorter events, 2.7 us)
Async XLA Ops:
  0.6 5.5 %copy-start.4 = (f32[6,2,384]{2,1,0:T(2,128)S(1)}, f32[6,2,384]{2,1,0:T(2,128)}, u32[]{:S(2)}) copy-start(f32[6,2,384]{2,1,0:T(2,128)} %coeff_ref.1) | copy-start | bytes 55300
  2.4 18.0 %collective-permute-start.1 = (f32[784,128]{1,0:T(8,128)}, f32[784,128]{1,0:T(8,128)S(1)}, u32[]{:S(2)}, u32[]{:S(2)}) collective-permute-start(f32[784,128]{1,0:T(8,128)} %shard_map.68), channel_id=1, source_target_pairs={{1,2},{3,4},{5,6},{7,8},{9,10},{11,12},{13,14},{2,1},{4,3},{6,5},{... | collective-permute-start | bytes 1204232 | tf_op jit(solution)/shard_map/ppermute | solution.py:501
  6.2 1.4 %copy-start = (f32[4,2,384,128]{3,2,1,0:T(8,128)S(1)}, f32[4,2,384,128]{3,2,1,0:T(8,128)}, u32[]{:S(2)}) copy-start(f32[4,2,384,128]{3,2,1,0:T(8,128)} %z_ref.5) | copy-start | bytes 4718596
  7.6 5.2 %copy-start.3 = (f32[4,2,384,128]{3,2,1,0:T(8,128)S(1)}, f32[4,2,384,128]{3,2,1,0:T(8,128)}, u32[]{:S(2)}) copy-start(f32[4,2,384,128]{3,2,1,0:T(8,128)} %param.7) | copy-start | bytes 4718596
  9.1 7.4 %collective-permute-start.3 = (f32[776,128]{1,0:T(8,128)S(1)}, f32[776,128]{1,0:T(8,128)S(1)}, u32[]{:S(2)}, u32[]{:S(2)}) collective-permute-start(f32[776,128]{1,0:T(8,128)S(1)} %get-tuple-element.52), channel_id=1, source_target_pairs={{0,1},{1,0},{2,3},{3,2},{4,5},{5,4},{6,7},{7,6},{8,9},{9,8},{10,11... | collective-permute-start | bytes 1191944 | tf_op jit(solution)/shard_map/ppermute | solution.py:495
  9.2 7.3 %collective-permute-start.2 = (f32[768,128]{1,0:T(8,128)S(1)}, f32[768,128]{1,0:T(8,128)S(1)}, u32[]{:S(2)}, u32[]{:S(2)}) collective-permute-start(f32[768,128]{1,0:T(8,128)S(1)} %get-tuple-element.51), channel_id=1, source_target_pairs={{0,1},{1,0},{2,3},{3,2},{4,5},{5,4},{6,7},{7,6},{8,9},{9,8},{10,11... | collective-permute-start | bytes 1179656 | tf_op jit(solution)/shard_map/ppermute | solution.py:495
  9.7 15.0 %collective-permute-start = (f32[776,128]{1,0:T(8,128)S(1)}, f32[776,128]{1,0:T(8,128)S(1)}, u32[]{:S(2)}, u32[]{:S(2)}) collective-permute-start(f32[776,128]{1,0:T(8,128)S(1)} %get-tuple-element.49), channel_id=1, source_target_pairs={{1,2},{3,4},{5,6},{7,8},{9,10},{11,12},{13,14},{2,1},{4,3},{6,5},{... | collective-permute-start | bytes 1191944 | tf_op jit(solution)/shard_map/ppermute | solution.py:501
  12.8 1.9 %copy-start.2 = (f32[4,2,384,256]{3,2,1,0:T(8,128)S(1)}, f32[4,2,384,256]{3,2,1,0:T(8,128)}, u32[]{:S(2)}) copy-start(f32[4,2,384,256]{3,2,1,0:T(8,128)} %param.8) | copy-start | bytes 9437188
  14.7 5.7 %copy-start.1 = (f32[4,2,384,128]{3,2,1,0:T(8,128)S(1)}, f32[4,2,384,128]{3,2,1,0:T(8,128)}, u32[]{:S(2)}) copy-start(f32[4,2,384,128]{3,2,1,0:T(8,128)} %z_ref.5) | copy-start | bytes 4718596
  25.7 19.8 %copy-start.5 = (f32[256,256]{1,0:T(8,128)S(1)}, f32[256,256]{1,0:T(8,128)}, u32[]{:S(2)}) copy-start(f32[256,256]{1,0:T(8,128)} %r_bar_ref.1) | copy-start | bytes 786436
  25.7 1.3 %collective-permute-start.4 = (f32[136,128]{1,0:T(8,128)S(1)}, f32[136,128]{1,0:T(8,128)S(1)}, u32[]{:S(2)}, u32[]{:S(2)}) collective-permute-start(f32[136,128]{1,0:T(8,128)S(1)} %get-tuple-element.64), channel_id=1, source_target_pairs={{0,1},{1,0},{2,3},{3,2},{4,5},{5,4},{6,7},{7,6},{8,9},{9,8},{10,11... | collective-permute-start | bytes 208904 | tf_op jit(solution)/shard_map/ppermute | solution.py:495
  25.8 1.4 %collective-permute-start.8 = (f32[128,128]{1,0:T(8,128)S(1)}, f32[128,128]{1,0:T(8,128)S(1)}, u32[]{:S(2)}, u32[]{:S(2)}) collective-permute-start(f32[128,128]{1,0:T(8,128)S(1)} %get-tuple-element.66), channel_id=1, source_target_pairs={{0,1},{1,0},{2,3},{3,2},{4,5},{5,4},{6,7},{7,6},{8,9},{9,8},{10,11... | collective-permute-start | bytes 196616 | tf_op jit(solution)/shard_map/ppermute | solution.py:495
  27.1 3.5 %collective-permute-start.5 = (f32[136,128]{1,0:T(8,128)S(1)}, f32[136,128]{1,0:T(8,128)S(1)}, u32[]{:S(2)}, u32[]{:S(2)}) collective-permute-start(f32[136,128]{1,0:T(8,128)S(1)} %add.24), channel_id=1, source_target_pairs={{0,2},{1,5},{2,0},{3,7},{4,6},{5,1},{6,4},{7,3},{8,10},{9,13},{10,... | collective-permute-start | bytes 208904 | tf_op jit(solution)/shard_map/ppermute | solution.py:512
  27.2 5.8 %collective-permute-start.9 = (f32[128,128]{1,0:T(8,128)S(1)}, f32[128,128]{1,0:T(8,128)S(1)}, u32[]{:S(2)}, u32[]{:S(2)}) collective-permute-start(f32[128,128]{1,0:T(8,128)S(1)} %add.28), channel_id=1, source_target_pairs={{0,4},{1,3},{2,6},{3,1},{4,0},{5,7},{6,2},{7,5},{8,12},{9,11},{10,... | collective-permute-start | bytes 196616 | tf_op jit(solution)/shard_map/ppermute | solution.py:512
  30.6 4.3 %collective-permute-start.6 = (f32[136,128]{1,0:T(8,128)S(1)}, f32[136,128]{1,0:T(8,128)S(1)}, u32[]{:S(2)}, u32[]{:S(2)}) collective-permute-start(f32[136,128]{1,0:T(8,128)S(1)} %add.25), channel_id=1, source_target_pairs={{0,4},{1,9},{2,6},{3,11},{4,0},{5,13},{6,2},{7,15},{8,12},{9,1},{1... | collective-permute-start | bytes 208904 | tf_op jit(solution)/shard_map/ppermute | solution.py:512
  33.0 3.5 %collective-permute-start.10 = (f32[128,128]{1,0:T(8,128)S(1)}, f32[128,128]{1,0:T(8,128)S(1)}, u32[]{:S(2)}, u32[]{:S(2)}) collective-permute-start(f32[128,128]{1,0:T(8,128)S(1)} %add.29), channel_id=1, source_target_pairs={{0,8},{1,5},{2,10},{3,7},{4,12},{5,1},{6,14},{7,3},{8,0},{9,13},{1... | collective-permute-start | bytes 196616 | tf_op jit(solution)/shard_map/ppermute | solution.py:512
  34.9 3.5 %collective-permute-start.7 = (f32[136,128]{1,0:T(8,128)S(1)}, f32[136,128]{1,0:T(8,128)S(1)}, u32[]{:S(2)}, u32[]{:S(2)}) collective-permute-start(f32[136,128]{1,0:T(8,128)S(1)} %add.26), channel_id=1, source_target_pairs={{0,8},{1,3},{2,10},{3,1},{4,12},{5,7},{6,14},{7,5},{8,0},{9,11},{1... | collective-permute-start | bytes 208904 | tf_op jit(solution)/shard_map/ppermute | solution.py:512
  36.5 6.1 %collective-permute-start.11 = (f32[128,128]{1,0:T(8,128)S(1)}, f32[128,128]{1,0:T(8,128)S(1)}, u32[]{:S(2)}, u32[]{:S(2)}) collective-permute-start(f32[128,128]{1,0:T(8,128)S(1)} %add.30), channel_id=1, source_target_pairs={{0,2},{1,9},{2,0},{3,11},{4,6},{5,13},{6,4},{7,15},{8,10},{9,1},{1... | collective-permute-start | bytes 196616 | tf_op jit(solution)/shard_map/ppermute | solution.py:512
  38.4 7.1 %collective-permute-start.12 = (f32[136,128]{1,0:T(8,128)S(1)}, f32[136,128]{1,0:T(8,128)S(1)}, u32[]{:S(2)}, u32[]{:S(2)}) collective-permute-start(f32[136,128]{1,0:T(8,128)S(1)} %add.27.mine1_ref), channel_id=1, source_target_pairs={{0,1},{1,0},{2,3},{3,2},{4,5},{5,4},{6,7},{7,6},{8,9},{9,8},{10,11... | collective-permute-start | bytes 208904 | tf_op jit(solution)/shard_map/ppermute | solution.py:495
  42.6 2.9 %collective-permute-start.13 = (f32[128,128]{1,0:T(8,128)S(1)}, f32[128,128]{1,0:T(8,128)S(1)}, u32[]{:S(2)}, u32[]{:S(2)}) collective-permute-start(f32[128,128]{1,0:T(8,128)S(1)} %add.31.mine2_ref), channel_id=1, source_target_pairs={{0,1},{1,0},{2,3},{3,2},{4,5},{5,4},{6,7},{7,6},{8,9},{9,8},{10,11... | collective-permute-start | bytes 196616 | tf_op jit(solution)/shard_map/ppermute | solution.py:495
  56.4 17.6 %collective-permute-start.14 = (f32[776,128]{1,0:T(8,128)S(1)}, f32[776,128]{1,0:T(8,128)S(1)}, u32[]{:S(2)}, u32[]{:S(2)}) collective-permute-start(f32[776,128]{1,0:T(8,128)S(1)} %get-tuple-element.71.outer1_ref.own1_ref), channel_id=1, source_target_pairs={{1,2},{3,4},{5,6},{7,8},{9,10},{11,12},{13,14},{2,1},{4,3},{6,5},{... | collective-permute-start | bytes 1191944 | tf_op jit(solution)/shard_map/ppermute | solution.py:501
  60.1 7.2 %collective-permute-start.16 = (f32[768,128]{1,0:T(8,128)S(1)}, f32[768,128]{1,0:T(8,128)S(1)}, u32[]{:S(2)}, u32[]{:S(2)}) collective-permute-start(f32[768,128]{1,0:T(8,128)S(1)} %get-tuple-element.80), channel_id=1, source_target_pairs={{0,1},{1,0},{2,3},{3,2},{4,5},{5,4},{6,7},{7,6},{8,9},{9,8},{10,11... | collective-permute-start | bytes 1179656 | tf_op jit(solution)/shard_map/ppermute | solution.py:495
  61.4 5.9 %collective-permute-start.15 = (f32[768,128]{1,0:T(8,128)S(1)}, f32[768,128]{1,0:T(8,128)S(1)}, u32[]{:S(2)}, u32[]{:S(2)}) collective-permute-start(f32[768,128]{1,0:T(8,128)S(1)} %get-tuple-element.79.own2_ref), channel_id=1, source_target_pairs={{0,1},{1,0},{2,3},{3,2},{4,5},{5,4},{6,7},{7,6},{8,9},{9,8},{10,11... | collective-permute-start | bytes 1179656 | tf_op jit(solution)/shard_map/ppermute | solution.py:495
  61.5 16.8 %collective-permute-start.17 = (f32[768,128]{1,0:T(8,128)S(1)}, f32[768,128]{1,0:T(8,128)S(1)}, u32[]{:S(2)}, u32[]{:S(2)}) collective-permute-start(f32[768,128]{1,0:T(8,128)S(1)} %get-tuple-element.83), channel_id=1, source_target_pairs={{1,2},{3,4},{5,6},{7,8},{9,10},{11,12},{13,14},{2,1},{4,3},{6,5},{... | collective-permute-start | bytes 1179656 | tf_op jit(solution)/shard_map/ppermute | solution.py:501

commit v11 on v10

--- a/solution.py
+++ b/solution.py
@@ -506,9 +506,9 @@
     bits = count.bit_length() - 1
     mine = [m + swap_inner(o) for m, o in zip(mine, other)]
     for step in range(bits - 1):
+        turn = [1 + (step + core) % (bits - 1) for core in range(2)]
+        pairs = [(i, i ^ (1 << turn[i & 1])) for i in range(count)]
         for stream in range(2):
-            turn = [1 + (step + (core ^ stream)) % (bits - 1) for core in range(2)]
-            pairs = [(i, i ^ (1 << turn[i & 1])) for i in range(count)]
             mine[stream] = mine[stream] + lax.ppermute(mine[stream], "row", pairs)
     return mine + [swap_inner(m) for m in mine]
 

time: 79.8 us -> 79.9 us (level)
  starting transfers between devices: 27.2 us -> 26.1 us
  waiting for transfers between devices: 19.6 us -> 20.7 us
    ppermute x6, starting transfers between devices: 6.98 us -> 5.86 us  [sum_over_rows(): mine[stream] = mine[stream] + lax.ppermute(mine[stream], 'row', pairs)]
    ppermute x6, waiting for transfers between devices: 4.22 us -> 5.28 us  [sum_over_rows(): mine[stream] = mine[stream] + lax.ppermute(mine[stream], 'row', pairs)]
where the time goes in v11:
time: 79.9 us; the launch traced here: 79.5 us
  Pallas kernels  28.4 us (36%)
  starting transfers between devices  26.1 us (33%)
  waiting for transfers between devices  20.7 us (26%)
  local copies, waits for them, and re-layouts  3.31 us (4%)
  between operations  0.85 us (1%)
    pallas_call x11, Pallas kernels, run(): pl.pallas_call(kernel, out_shape=outs, in_specs=specs, scratch_shapes=lis...  28.4 us
    ppermute x4, waiting for transfers between devices, swap_outer(): return lax.ppermute(message, 'row', pairs + [(j, i) for i, j in pairs])  13.7 us
    ppermute x4, starting transfers between devices, swap_outer(): return lax.ppermute(message, 'row', pairs + [(j, i) for i, j in pairs])  11.1 us
    ppermute x8, starting transfers between devices, swap_inner(): return lax.ppermute(message, 'row', [(i, i ^ 1) for i in range(count)])  9.2 us
    ppermute x6, starting transfers between devices, sum_over_rows(): mine[stream] = mine[stream] + lax.ppermute(mine[stream], 'row', pairs)  5.86 us
    ppermute x6, waiting for transfers between devices, sum_over_rows(): mine[stream] = mine[stream] + lax.ppermute(mine[stream], 'row', pairs)  5.28 us
    unnamed x12, local copies, waits for them, and re-layouts  3.31 us
    ppermute x8, waiting for transfers between devices, swap_inner(): return lax.ppermute(message, 'row', [(i, i ^ 1) for i in range(count)])  1.73 us
  transfers between devices with their start and end apart: 18, of which 11 were waited for; matrix products, arithmetic and copies ran while one was open for 0% of the time, Pallas kernels for 17%

profile of v11, /device:TPU:9, one launch (start us, length us, event | category | flops | bytes accessed | tf_op | source)
XLA Modules:
  0.0 79.5 jit_solution(6960138287316780313)
XLA Ops:
  0.6 1.8 %shard_map.68 = f32[784,128]{1,0:T(8,128)} custom-call(s32[1]{0:T(128)} %bitcast.core_ref, f32[4,2,384,128]{3,2,1,0:T(8,128)} %z_ref.5), custom_call_target="tpu_custom_call" | custom-call | bytes 1000000 | tf_op jit(solution)/shard_map/pallas_call | solution.py:22
  2.4 3.7 %collective-permute-start.1 = (f32[784,128]{1,0:T(8,128)}, f32[784,128]{1,0:T(8,128)S(1)}, u32[]{:S(2)}, u32[]{:S(2)}) collective-permute-start(f32[784,128]{1,0:T(8,128)} %shard_map.68), channel_id=1, source_target_pairs={{1,2},{3,4},{5,6},{7,8},{9,10},{11,12},{13,14},{2,1},{4,3},{6,5},{... | collective-permute-start | bytes 1204232 | tf_op jit(solution)/shard_map/ppermute | solution.py:501
  6.2 1.4 %copy-done = f32[4,2,384,128]{3,2,1,0:T(8,128)S(1)} copy-done((f32[4,2,384,128]{3,2,1,0:T(8,128)S(1)}, f32[4,2,384,128]{3,2,1,0:T(8,128)}, u32[]{:S(2)}) %copy-start) | copy-done | bytes 1572888
  7.6 1.6 %shard_map.69 = (f32[776,128]{1,0:T(8,128)S(1)}, f32[768,128]{1,0:T(8,128)S(1)}, f32[776,128]{1,0:T(8,128)S(1)}, f32[384,16]{1,0:T(8,128)S(1)}) custom-call(s32[1]{0:T(128)} %bitcast.core_ref, f32[6,2,384]{2,1,0:T(2,128)S(1)} %copy-done.4, f32[4,2,384,128]{3,2,1,0:T(8,128)S(1)} %copy-done), custom_call_target="tpu_custom_call" | custom-call | flops 1000000 | bytes 3000000 | tf_op jit(solution)/shard_map/pallas_call | solution.py:22
  9.7 3.1 %collective-permute-start = (f32[776,128]{1,0:T(8,128)S(1)}, f32[776,128]{1,0:T(8,128)S(1)}, u32[]{:S(2)}, u32[]{:S(2)}) collective-permute-start(f32[776,128]{1,0:T(8,128)S(1)} %get-tuple-element.49), channel_id=1, source_target_pairs={{1,2},{3,4},{5,6},{7,8},{9,10},{11,12},{13,14},{2,1},{4,3},{6,5},{... | collective-permute-start | bytes 1191944 | tf_op jit(solution)/shard_map/ppermute | solution.py:501
  12.8 1.9 %copy-done.2 = f32[4,2,384,256]{3,2,1,0:T(8,128)S(1)} copy-done((f32[4,2,384,256]{3,2,1,0:T(8,128)S(1)}, f32[4,2,384,256]{3,2,1,0:T(8,128)}, u32[]{:S(2)}) %copy-start.2) | copy-done | bytes 3145752
  14.7 1.8 %shard_map.70 = (f32[136,128]{1,0:T(8,128)S(1)}, bf16[3072,128]{1,0:T(8,128)(2,1)S(1)}, bf16[3072,128]{1,0:T(8,128)(2,1)S(1)}, bf16[3072,256]{1,0:T(8,128)(2,1)S...) custom-call(f32[3072,128]{1,0:T(8,128)S(1)} %bitcast.4, ...), custom_call_target="tpu_custom_call" | custom-call | flops 503316480 | bytes 9000000 | tf_op jit(solution)/shard_map/pallas_call | solution.py:22
  16.5 3.9 %collective-permute-done.1.outer1_ref = f32[784,128]{1,0:T(8,128)S(1)} collective-permute-done((f32[784,128]{1,0:T(8,128)}, f32[784,128]{1,0:T(8,128)S(1)}, u32[]{:S(2)}, u32[]{:S(2)}) %collective-permute-start.1) | collective-permute-done | bytes 401440 | tf_op jit(solution)/shard_map/ppermute | solution.py:501
  20.5 3.2 %shard_map.71 = (f32[2,384,128]{2,1,0:T(8,128)S(1)}, bf16[1536,128]{1,0:T(8,128)(2,1)S(1)}, bf16[1536,128]{1,0:T(8,128)(2,1)S(1)}, bf16[768,128]{1,0:T(8,128)(2,...) custom-call(s32[1]{0:T(128)} %bitcast.core_ref, ...), custom_call_target="tpu_custom_call" | custom-call | flops 805306368 | bytes 9000000 | tf_op jit(solution)/shard_map/pallas_call | solution.py:22
  23.7 1.0 %collective-permute-done.outer2_ref.fouter2_ref = f32[776,128]{1,0:T(8,128)S(1)} collective-permute-done((f32[776,128]{1,0:T(8,128)S(1)}, f32[776,128]{1,0:T(8,128)S(1)}, u32[]{:S(2)}, u32[]{:S(2)}) %collective-permute-start) | collective-permute-done | bytes 397344 | tf_op jit(solution)/shard_map/ppermute | solution.py:501
  24.7 1.0 %shard_map.72 = (f32[136,128]{1,0:T(8,128)S(1)}, f32[128,128]{1,0:T(8,128)S(1)}, f32[136,128]{1,0:T(8,128)S(1)}, f32[128,128]{1,0:T(8,128)S(1)}, bf16[768,128]{1...) custom-call(s32[1]{0:T(128)} %bitcast.core_ref, f32[384,16]{1,0:T(8,128)S(1)} %get-tuple-element.44.table_ref, ...), custom_call_target="tpu_custom_call" | custom-call | flops 301989888 | bytes 5000000 | tf_op jit(solution)/shard_map/pallas_call | solution.py:22
  26.3 0.7 collective-permute-done.4
  27.2 1.5 %collective-permute-start.9 = (f32[128,128]{1,0:T(8,128)S(1)}, f32[128,128]{1,0:T(8,128)S(1)}, u32[]{:S(2)}, u32[]{:S(2)}) collective-permute-start(f32[128,128]{1,0:T(8,128)S(1)} %add.28), channel_id=1, source_target_pairs={{0,2},{1,5},{2,0},{3,7},{4,6},{5,1},{6,4},{7,3},{8,10},{9,13},{10,... | collective-permute-start | bytes 196616 | tf_op jit(solution)/shard_map/ppermute | solution.py:512
  28.7 1.9 %collective-permute-done.5 = f32[136,128]{1,0:T(8,128)S(1)} collective-permute-done((f32[136,128]{1,0:T(8,128)S(1)}, f32[136,128]{1,0:T(8,128)S(1)}, u32[]{:S(2)}, u32[]{:S(2)}) %collective-permute-start.5) | collective-permute-done | bytes 69664 | tf_op jit(solution)/shard_map/ppermute | solution.py:512
  30.6 2.4 %collective-permute-start.6 = (f32[136,128]{1,0:T(8,128)S(1)}, f32[136,128]{1,0:T(8,128)S(1)}, u32[]{:S(2)}, u32[]{:S(2)}) collective-permute-start(f32[136,128]{1,0:T(8,128)S(1)} %add.25), channel_id=1, source_target_pairs={{0,4},{1,9},{2,6},{3,11},{4,0},{5,13},{6,2},{7,15},{8,12},{9,1},{1... | collective-permute-start | bytes 208904 | tf_op jit(solution)/shard_map/ppermute | solution.py:512
  33.7 1.4 %collective-permute-done.6 = f32[136,128]{1,0:T(8,128)S(1)} collective-permute-done((f32[136,128]{1,0:T(8,128)S(1)}, f32[136,128]{1,0:T(8,128)S(1)}, u32[]{:S(2)}, u32[]{:S(2)}) %collective-permute-start.6) | collective-permute-done | bytes 69664 | tf_op jit(solution)/shard_map/ppermute | solution.py:512
  35.1 0.9 %collective-permute-start.7 = (f32[136,128]{1,0:T(8,128)S(1)}, f32[136,128]{1,0:T(8,128)S(1)}, u32[]{:S(2)}, u32[]{:S(2)}) collective-permute-start(f32[136,128]{1,0:T(8,128)S(1)} %add.26), channel_id=1, source_target_pairs={{0,8},{1,3},{2,10},{3,1},{4,12},{5,7},{6,14},{7,5},{8,0},{9,11},{1... | collective-permute-start | bytes 208904 | tf_op jit(solution)/shard_map/ppermute | solution.py:512
  36.0 1.1 %collective-permute-done.10 = f32[128,128]{1,0:T(8,128)S(1)} collective-permute-done((f32[128,128]{1,0:T(8,128)S(1)}, f32[128,128]{1,0:T(8,128)S(1)}, u32[]{:S(2)}, u32[]{:S(2)}) %collective-permute-start.10) | collective-permute-done | bytes 65568 | tf_op jit(solution)/shard_map/ppermute | solution.py:512
  37.5 0.9 %collective-permute-done.7 = f32[136,128]{1,0:T(8,128)S(1)} collective-permute-done((f32[136,128]{1,0:T(8,128)S(1)}, f32[136,128]{1,0:T(8,128)S(1)}, u32[]{:S(2)}, u32[]{:S(2)}) %collective-permute-start.7) | collective-permute-done | bytes 69664 | tf_op jit(solution)/shard_map/ppermute | solution.py:512
  38.4 3.7 %collective-permute-start.12 = (f32[136,128]{1,0:T(8,128)S(1)}, f32[136,128]{1,0:T(8,128)S(1)}, u32[]{:S(2)}, u32[]{:S(2)}) collective-permute-start(f32[136,128]{1,0:T(8,128)S(1)} %add.27.mine1_ref), channel_id=1, source_target_pairs={{0,1},{1,0},{2,3},{3,2},{4,5},{5,4},{6,7},{7,6},{8,9},{9,8},{10,11... | collective-permute-start | bytes 208904 | tf_op jit(solution)/shard_map/ppermute | solution.py:495
  42.0 2.5 %collective-permute-start.13 = (f32[128,128]{1,0:T(8,128)S(1)}, f32[128,128]{1,0:T(8,128)S(1)}, u32[]{:S(2)}, u32[]{:S(2)}) collective-permute-start(f32[128,128]{1,0:T(8,128)S(1)} %add.31.mine2_ref), channel_id=1, source_target_pairs={{0,1},{1,0},{2,3},{3,2},{4,5},{5,4},{6,7},{7,6},{8,9},{9,8},{10,11... | collective-permute-start | bytes 196616 | tf_op jit(solution)/shard_map/ppermute | solution.py:495
  44.6 0.9 %collective-permute-done.13.other2_ref = f32[128,128]{1,0:T(8,128)S(1)} collective-permute-done((f32[128,128]{1,0:T(8,128)S(1)}, f32[128,128]{1,0:T(8,128)S(1)}, u32[]{:S(2)}, u32[]{:S(2)}) %collective-permute-start.13) | collective-permute-done | bytes 65568 | tf_op jit(solution)/shard_map/ppermute | solution.py:495
  45.5 10.3 %shard_map.73 = (bf16[256,256]{1,0:T(8,128)(2,1)S(1)}, bf16[256,256]{1,0:T(8,128)(2,1)S(1)}, bf16[256,256]{1,0:T(8,128)(2,1)S(1)}, bf16[256,256]{1,0:T(8,128)(2,1)S(1)}) custom-call(s32[1]{0:T(128)} %bitcast.core_ref, f32[136,128]{1,0:T(8,128)S(1)} %add.27.mine1_ref, f32[128,128]{1,0:T(8,128)S(1)} %add.31.mine2_ref, ...), custom_call_target="tpu_custom_call" | custom-call | flops 1000000000 | bytes 1000000 | tf_op jit(solution)/shard_map/pallas_call | solution.py:22
  56.4 2.1 %collective-permute-start.14 = (f32[776,128]{1,0:T(8,128)S(1)}, f32[776,128]{1,0:T(8,128)S(1)}, u32[]{:S(2)}, u32[]{:S(2)}) collective-permute-start(f32[776,128]{1,0:T(8,128)S(1)} %get-tuple-element.71.outer1_ref.own1_ref), channel_id=1, source_target_pairs={{1,2},{3,4},{5,6},{7,8},{9,10},{11,12},{13,14},{2,1},{4,3},{6,5},{... | collective-permute-start | bytes 1191944 | tf_op jit(solution)/shard_map/ppermute | solution.py:501
  58.5 1.7 %shard_map.75 = (f32[2,384,128]{2,1,0:T(8,128)S(1)}, f32[2,2,384,128]{3,2,1,0:T(8,128)S(1)}, f32[768,128]{1,0:T(8,128)S(1)}, f32[768,128]{1,0:T(8,128)S(1)}, f32[768,128]{1,0:T(8,128)S(1)}) custom-call(s32[1]{0:T(128)} %bitcast.core_ref, f32[384,16]{1,0:T(8,128)S(1)} %get-tuple-element.44.table_ref, f32[2,384,128]{2,1,0:T(8,128)S(1)} %get-tuple-element.72.outer_ref, ...), custom_call_target="tpu_custom_call" | custom-call | flops 10000000000 | bytes 6000000 | tf_op jit(solution)/shard_map/pallas_call | solution.py:22
  60.2 1.8 %collective-permute-start.16 = (f32[768,128]{1,0:T(8,128)S(1)}, f32[768,128]{1,0:T(8,128)S(1)}, u32[]{:S(2)}, u32[]{:S(2)}) collective-permute-start(f32[768,128]{1,0:T(8,128)S(1)} %get-tuple-element.80), channel_id=1, source_target_pairs={{0,1},{1,0},{2,3},{3,2},{4,5},{5,4},{6,7},{7,6},{8,9},{9,8},{10,11... | collective-permute-start | bytes 1179656 | tf_op jit(solution)/shard_map/ppermute | solution.py:495
  62.1 2.2 %collective-permute-start.17 = (f32[768,128]{1,0:T(8,128)S(1)}, f32[768,128]{1,0:T(8,128)S(1)}, u32[]{:S(2)}, u32[]{:S(2)}) collective-permute-start(f32[768,128]{1,0:T(8,128)S(1)} %get-tuple-element.83), channel_id=1, source_target_pairs={{1,2},{3,4},{5,6},{7,8},{9,10},{11,12},{13,14},{2,1},{4,3},{6,5},{... | collective-permute-start | bytes 1179656 | tf_op jit(solution)/shard_map/ppermute | solution.py:501
  64.3 3.0 %shard_map.78 = f32[4,2,384,128]{3,2,1,0:T(8,128)} custom-call(s32[1]{0:T(128)} %bitcast.core_ref, bf16[3072,256]{1,0:T(8,128)(2,1)S(1)} %get-tuple-element.45.qh_ref, bf16[3072,256]{1,0:T(8,128)(2,1)S(1)} %get-tuple-element.46.ql_ref, bf16[3072,128]{1,0:T(8,128)(2,1)S(1)} %get-tuple-element.47.nh_ref, bf16[3072,128]{1,0:T(8,128)(2,1)S(1)} %get-tuple-element.48.nl_ref, ...), custom_call_target="tpu_custom_call" | custom-call | tf_op jit(solution)/shard_map/pallas_call | solution.py:22
  67.3 6.7 %collective-permute-done.14.outer1_ref = f32[776,128]{1,0:T(8,128)S(1)} collective-permute-done((f32[776,128]{1,0:T(8,128)S(1)}, f32[776,128]{1,0:T(8,128)S(1)}, u32[]{:S(2)}, u32[]{:S(2)}) %collective-permute-start.14) | collective-permute-done | bytes 397344 | tf_op jit(solution)/shard_map/ppermute | solution.py:501
  74.0 2.2 %shard_map.76 = (f32[2,2,384,128]{3,2,1,0:T(8,128)S(1)}, f32[2,2,384,128]{3,2,1,0:T(8,128)S(1)}) custom-call(f32[776,128]{1,0:T(8,128)S(1)} %collective-permute-done.14.outer1_ref, f32[384,16]{1,0:T(8,128)S(1)} %get-tuple-element.44.table_ref, f32[2,384,128]{2,1,0:T(8,128)S(1)} %get-tuple-element.72.outer_ref, ...), custom_call_target="tpu_custom_call" | custom-call | flops 10000000 | bytes 6000000 | tf_op jit(solution)/shard_map/pallas_call | solution.py:22
  76.2 2.0 %collective-permute-done.17.outer2_ref = f32[768,128]{1,0:T(8,128)S(1)} collective-permute-done((f32[768,128]{1,0:T(8,128)S(1)}, f32[768,128]{1,0:T(8,128)S(1)}, u32[]{:S(2)}, u32[]{:S(2)}) %collective-permute-start.17) | collective-permute-done | bytes 393248 | tf_op jit(solution)/shard_map/ppermute | solution.py:501
  78.2 1.3 %shard_map.77 = f32[4,2,384,128]{3,2,1,0:T(8,128)} custom-call(s32[1]{0:T(128)} %bitcast.core_ref, f32[2,2,384,128]{3,2,1,0:T(8,128)S(1)} %get-tuple-element.81.light_ref, f32[2,2,384,128]{3,2,1,0:T(8,128)S(1)} %get-tuple-element.82.heavy_ref, f32[768,128]{1,0:T(8,128)S(1)} %collective-permute-done.17.outer2_ref), custom_call_target="tpu_custom_call" | custom-call | flops 1000000 | bytes 6000000 | tf_op jit(solution)/shard_map/pallas_call | solution.py:22
  (35 shorter events, 3.1 us)
Async XLA Ops:
  0.6 5.5 %copy-start.4 = (f32[6,2,384]{2,1,0:T(2,128)S(1)}, f32[6,2,384]{2,1,0:T(2,128)}, u32[]{:S(2)}) copy-start(f32[6,2,384]{2,1,0:T(2,128)} %coeff_ref.1) | copy-start | bytes 55300
  2.4 18.0 %collective-permute-start.1 = (f32[784,128]{1,0:T(8,128)}, f32[784,128]{1,0:T(8,128)S(1)}, u32[]{:S(2)}, u32[]{:S(2)}) collective-permute-start(f32[784,128]{1,0:T(8,128)} %shard_map.68), channel_id=1, source_target_pairs={{1,2},{3,4},{5,6},{7,8},{9,10},{11,12},{13,14},{2,1},{4,3},{6,5},{... | collective-permute-start | bytes 1204232 | tf_op jit(solution)/shard_map/ppermute | solution.py:501
  6.2 1.4 %copy-start = (f32[4,2,384,128]{3,2,1,0:T(8,128)S(1)}, f32[4,2,384,128]{3,2,1,0:T(8,128)}, u32[]{:S(2)}) copy-start(f32[4,2,384,128]{3,2,1,0:T(8,128)} %z_ref.5) | copy-start | bytes 4718596
  7.6 5.2 %copy-start.3 = (f32[4,2,384,128]{3,2,1,0:T(8,128)S(1)}, f32[4,2,384,128]{3,2,1,0:T(8,128)}, u32[]{:S(2)}) copy-start(f32[4,2,384,128]{3,2,1,0:T(8,128)} %param.7) | copy-start | bytes 4718596
  9.1 7.4 %collective-permute-start.3 = (f32[776,128]{1,0:T(8,128)S(1)}, f32[776,128]{1,0:T(8,128)S(1)}, u32[]{:S(2)}, u32[]{:S(2)}) collective-permute-start(f32[776,128]{1,0:T(8,128)S(1)} %get-tuple-element.52), channel_id=1, source_target_pairs={{0,1},{1,0},{2,3},{3,2},{4,5},{5,4},{6,7},{7,6},{8,9},{9,8},{10,11... | collective-permute-start | bytes 1191944 | tf_op jit(solution)/shard_map/ppermute | solution.py:495
  9.2 7.3 %collective-permute-start.2 = (f32[768,128]{1,0:T(8,128)S(1)}, f32[768,128]{1,0:T(8,128)S(1)}, u32[]{:S(2)}, u32[]{:S(2)}) collective-permute-start(f32[768,128]{1,0:T(8,128)S(1)} %get-tuple-element.51), channel_id=1, source_target_pairs={{0,1},{1,0},{2,3},{3,2},{4,5},{5,4},{6,7},{7,6},{8,9},{9,8},{10,11... | collective-permute-start | bytes 1179656 | tf_op jit(solution)/shard_map/ppermute | solution.py:495
  9.7 15.0 %collective-permute-start = (f32[776,128]{1,0:T(8,128)S(1)}, f32[776,128]{1,0:T(8,128)S(1)}, u32[]{:S(2)}, u32[]{:S(2)}) collective-permute-start(f32[776,128]{1,0:T(8,128)S(1)} %get-tuple-element.49), channel_id=1, source_target_pairs={{1,2},{3,4},{5,6},{7,8},{9,10},{11,12},{13,14},{2,1},{4,3},{6,5},{... | collective-permute-start | bytes 1191944 | tf_op jit(solution)/shard_map/ppermute | solution.py:501
  12.8 1.9 %copy-start.2 = (f32[4,2,384,256]{3,2,1,0:T(8,128)S(1)}, f32[4,2,384,256]{3,2,1,0:T(8,128)}, u32[]{:S(2)}) copy-start(f32[4,2,384,256]{3,2,1,0:T(8,128)} %param.8) | copy-start | bytes 9437188
  14.7 5.7 %copy-start.1 = (f32[4,2,384,128]{3,2,1,0:T(8,128)S(1)}, f32[4,2,384,128]{3,2,1,0:T(8,128)}, u32[]{:S(2)}) copy-start(f32[4,2,384,128]{3,2,1,0:T(8,128)} %z_ref.5) | copy-start | bytes 4718596
  25.7 19.8 %copy-start.5 = (f32[256,256]{1,0:T(8,128)S(1)}, f32[256,256]{1,0:T(8,128)}, u32[]{:S(2)}) copy-start(f32[256,256]{1,0:T(8,128)} %r_bar_ref.1) | copy-start | bytes 786436
  25.7 1.3 %collective-permute-start.4 = (f32[136,128]{1,0:T(8,128)S(1)}, f32[136,128]{1,0:T(8,128)S(1)}, u32[]{:S(2)}, u32[]{:S(2)}) collective-permute-start(f32[136,128]{1,0:T(8,128)S(1)} %get-tuple-element.64), channel_id=1, source_target_pairs={{0,1},{1,0},{2,3},{3,2},{4,5},{5,4},{6,7},{7,6},{8,9},{9,8},{10,11... | collective-permute-start | bytes 208904 | tf_op jit(solution)/shard_map/ppermute | solution.py:495
  25.8 1.4 %collective-permute-start.8 = (f32[128,128]{1,0:T(8,128)S(1)}, f32[128,128]{1,0:T(8,128)S(1)}, u32[]{:S(2)}, u32[]{:S(2)}) collective-permute-start(f32[128,128]{1,0:T(8,128)S(1)} %get-tuple-element.66), channel_id=1, source_target_pairs={{0,1},{1,0},{2,3},{3,2},{4,5},{5,4},{6,7},{7,6},{8,9},{9,8},{10,11... | collective-permute-start | bytes 196616 | tf_op jit(solution)/shard_map/ppermute | solution.py:495
  27.1 3.5 %collective-permute-start.5 = (f32[136,128]{1,0:T(8,128)S(1)}, f32[136,128]{1,0:T(8,128)S(1)}, u32[]{:S(2)}, u32[]{:S(2)}) collective-permute-start(f32[136,128]{1,0:T(8,128)S(1)} %add.24), channel_id=1, source_target_pairs={{0,2},{1,5},{2,0},{3,7},{4,6},{5,1},{6,4},{7,3},{8,10},{9,13},{10,... | collective-permute-start | bytes 208904 | tf_op jit(solution)/shard_map/ppermute | solution.py:512
  27.2 5.8 %collective-permute-start.9 = (f32[128,128]{1,0:T(8,128)S(1)}, f32[128,128]{1,0:T(8,128)S(1)}, u32[]{:S(2)}, u32[]{:S(2)}) collective-permute-start(f32[128,128]{1,0:T(8,128)S(1)} %add.28), channel_id=1, source_target_pairs={{0,2},{1,5},{2,0},{3,7},{4,6},{5,1},{6,4},{7,3},{8,10},{9,13},{10,... | collective-permute-start | bytes 196616 | tf_op jit(solution)/shard_map/ppermute | solution.py:512
  30.6 4.5 %collective-permute-start.6 = (f32[136,128]{1,0:T(8,128)S(1)}, f32[136,128]{1,0:T(8,128)S(1)}, u32[]{:S(2)}, u32[]{:S(2)}) collective-permute-start(f32[136,128]{1,0:T(8,128)S(1)} %add.25), channel_id=1, source_target_pairs={{0,4},{1,9},{2,6},{3,11},{4,0},{5,13},{6,2},{7,15},{8,12},{9,1},{1... | collective-permute-start | bytes 208904 | tf_op jit(solution)/shard_map/ppermute | solution.py:512
  33.0 4.1 %collective-permute-start.10 = (f32[128,128]{1,0:T(8,128)S(1)}, f32[128,128]{1,0:T(8,128)S(1)}, u32[]{:S(2)}, u32[]{:S(2)}) collective-permute-start(f32[128,128]{1,0:T(8,128)S(1)} %add.29), channel_id=1, source_target_pairs={{0,4},{1,9},{2,6},{3,11},{4,0},{5,13},{6,2},{7,15},{8,12},{9,1},{1... | collective-permute-start | bytes 196616 | tf_op jit(solution)/shard_map/ppermute | solution.py:512
  35.1 3.2 %collective-permute-start.7 = (f32[136,128]{1,0:T(8,128)S(1)}, f32[136,128]{1,0:T(8,128)S(1)}, u32[]{:S(2)}, u32[]{:S(2)}) collective-permute-start(f32[136,128]{1,0:T(8,128)S(1)} %add.26), channel_id=1, source_target_pairs={{0,8},{1,3},{2,10},{3,1},{4,12},{5,7},{6,14},{7,5},{8,0},{9,11},{1... | collective-permute-start | bytes 208904 | tf_op jit(solution)/shard_map/ppermute | solution.py:512
  37.1 4.9 %collective-permute-start.11 = (f32[128,128]{1,0:T(8,128)S(1)}, f32[128,128]{1,0:T(8,128)S(1)}, u32[]{:S(2)}, u32[]{:S(2)}) collective-permute-start(f32[128,128]{1,0:T(8,128)S(1)} %add.30), channel_id=1, source_target_pairs={{0,8},{1,3},{2,10},{3,1},{4,12},{5,7},{6,14},{7,5},{8,0},{9,11},{1... | collective-permute-start | bytes 196616 | tf_op jit(solution)/shard_map/ppermute | solution.py:512
  38.4 7.1 %collective-permute-start.12 = (f32[136,128]{1,0:T(8,128)S(1)}, f32[136,128]{1,0:T(8,128)S(1)}, u32[]{:S(2)}, u32[]{:S(2)}) collective-permute-start(f32[136,128]{1,0:T(8,128)S(1)} %add.27.mine1_ref), channel_id=1, source_target_pairs={{0,1},{1,0},{2,3},{3,2},{4,5},{5,4},{6,7},{7,6},{8,9},{9,8},{10,11... | collective-permute-start | bytes 208904 | tf_op jit(solution)/shard_map/ppermute | solution.py:495
  42.0 3.4 %collective-permute-start.13 = (f32[128,128]{1,0:T(8,128)S(1)}, f32[128,128]{1,0:T(8,128)S(1)}, u32[]{:S(2)}, u32[]{:S(2)}) collective-permute-start(f32[128,128]{1,0:T(8,128)S(1)} %add.31.mine2_ref), channel_id=1, source_target_pairs={{0,1},{1,0},{2,3},{3,2},{4,5},{5,4},{6,7},{7,6},{8,9},{9,8},{10,11... | collective-permute-start | bytes 196616 | tf_op jit(solution)/shard_map/ppermute | solution.py:495
  56.4 17.6 %collective-permute-start.14 = (f32[776,128]{1,0:T(8,128)S(1)}, f32[776,128]{1,0:T(8,128)S(1)}, u32[]{:S(2)}, u32[]{:S(2)}) collective-permute-start(f32[776,128]{1,0:T(8,128)S(1)} %get-tuple-element.71.outer1_ref.own1_ref), channel_id=1, source_target_pairs={{1,2},{3,4},{5,6},{7,8},{9,10},{11,12},{13,14},{2,1},{4,3},{6,5},{... | collective-permute-start | bytes 1191944 | tf_op jit(solution)/shard_map/ppermute | solution.py:501
  60.2 7.1 %collective-permute-start.16 = (f32[768,128]{1,0:T(8,128)S(1)}, f32[768,128]{1,0:T(8,128)S(1)}, u32[]{:S(2)}, u32[]{:S(2)}) collective-permute-start(f32[768,128]{1,0:T(8,128)S(1)} %get-tuple-element.80), channel_id=1, source_target_pairs={{0,1},{1,0},{2,3},{3,2},{4,5},{5,4},{6,7},{7,6},{8,9},{9,8},{10,11... | collective-permute-start | bytes 1179656 | tf_op jit(solution)/shard_map/ppermute | solution.py:495
  62.0 5.3 %collective-permute-start.15 = (f32[768,128]{1,0:T(8,128)S(1)}, f32[768,128]{1,0:T(8,128)S(1)}, u32[]{:S(2)}, u32[]{:S(2)}) collective-permute-start(f32[768,128]{1,0:T(8,128)S(1)} %get-tuple-element.79.own2_ref), channel_id=1, source_target_pairs={{0,1},{1,0},{2,3},{3,2},{4,5},{5,4},{6,7},{7,6},{8,9},{9,8},{10,11... | collective-permute-start | bytes 1179656 | tf_op jit(solution)/shard_map/ppermute | solution.py:495
  62.1 16.2 %collective-permute-start.17 = (f32[768,128]{1,0:T(8,128)S(1)}, f32[768,128]{1,0:T(8,128)S(1)}, u32[]{:S(2)}, u32[]{:S(2)}) collective-permute-start(f32[768,128]{1,0:T(8,128)S(1)} %get-tuple-element.83), channel_id=1, source_target_pairs={{1,2},{3,4},{5,6},{7,8},{9,10},{11,12},{13,14},{2,1},{4,3},{6,5},{... | collective-permute-start | bytes 1179656 | tf_op jit(solution)/shard_map/ppermute | solution.py:501

commit v12 on v11

--- a/solution.py
+++ b/solution.py
@@ -11,6 +11,7 @@
 bf16 = jnp.bfloat16
 VMEM = pl.BlockSpec(memory_space=pltpu.VMEM)
 LIMIT = 24 * 1024 * 1024
+FIRST_ROWS = 72
 FAR_LIMIT = 63 * 1024 * 1024
 
 
@@ -224,12 +225,12 @@
     rest_ref[...] = rest
 
 
-def quarters(core):
-    parts = []
-    for owner in (core, 1 - core):
-        first = pl.multiple_of(owner * 264, 8)
-        parts += [pl.ds(first, 136), pl.ds(pl.multiple_of(first + 136, 8), 128)]
-    return parts
+def first_part(core):
+    return pl.ds(pl.multiple_of(core * 64, 8), 64)
+
+
+def second_part(core):
+    return pl.ds(pl.multiple_of(128 + core * 200, 8), 200)
 
 
 def expand_last(
@@ -256,12 +257,15 @@
     sums_ref[256:384] = rest[256:]
     sums_ref[384:512] = pack_ref[0:128]
     sums_ref[520:528] = pack_ref[128:136]
-    for part, out in zip(quarters(core), (mine1_ref, mine2_ref, other1_ref, other2_ref)):
-        out[...] = sums_ref[part]
-
-
-def inverse_factor(w_ref, out_ref):
+    mine1_ref[...] = sums_ref[first_part(core)]
+    mine2_ref[...] = sums_ref[second_part(core)]
+    other1_ref[...] = sums_ref[first_part(1 - core)]
+    other2_ref[...] = sums_ref[second_part(1 - core)]
+
+
+def inverse_factor(w_ref, out_ref, begin=0, end=None):
     size = w_ref.shape[0]
+    end = size if end is None else end
     step = 8
     lane = lax.broadcasted_iota(jnp.int32, (step, size), 1)
     place = lax.broadcasted_iota(jnp.int32, (step, size), 0)
@@ -269,8 +273,8 @@
     def load(start):
         return [jnp.broadcast_to(w_ref[start + i : start + i + 1, :], (step, size)) for i in range(step)]
 
-    rows = load(0)
-    for start in range(0, size, step):
+    rows = load(begin)
+    for start in range(begin, end, step):
         last = start + step >= size
         reach = step if last else 2 * step
         s = {
@@ -312,19 +316,41 @@
             w_ref[beyond:, :] = old - change
         if not last:
             rows = following
+    if end < size:
+        for i in range(step):
+            w_ref[end + i : end + i + 1, :] = rows[i][0:1]
+        return
     value = out_ref[...]
     row = lax.broadcasted_iota(jnp.int32, value.shape, 0)
     column = lax.broadcasted_iota(jnp.int32, value.shape, 1)
     out_ref[...] = jnp.where(row >= column, value, 0.0)
 
 
-def factor(
-    core_ref, mine1_ref, mine2_ref, other1_ref, other2_ref, r_bar_ref, nh_ref, nl_ref, sh_ref, sl_ref, sums_ref, w_ref, inv1_ref, inv2_ref
+def factor_first(core_ref, mine_ref, other_ref, pack_ref, w_ref, inv_ref):
+    core = core_ref[0]
+    pack_ref[first_part(core)] = mine_ref[...]
+    pack_ref[first_part(1 - core)] = other_ref[...]
+    row = lax.broadcasted_iota(jnp.int32, w_ref.shape, 0)
+    col = lax.broadcasted_iota(jnp.int32, w_ref.shape, 1)
+    w_ref[...] = jnp.where(row <= col, pack_ref[...], 0.0)
+    inv_ref[...] = jnp.zeros(inv_ref.shape, f32)
+    inverse_factor(w_ref, inv_ref, end=FIRST_ROWS)
+
+
+def factor_second(w0_ref, inv0_ref, inv_ref, w_ref):
+    w_ref[...] = w0_ref[...]
+    inv_ref[...] = inv0_ref[...]
+    inverse_factor(w_ref, inv_ref, begin=FIRST_ROWS)
+
+
+def factor_last(
+    core_ref, mine_ref, other_ref, pack1_ref, inv1_ref, r_bar_ref, nh_ref, nl_ref, sh_ref, sl_ref,
+    sums_ref, w_ref, inv2_ref,
 ):
     tile = 128
     core = core_ref[0]
-    for part, value in zip(quarters(core), (mine1_ref, mine2_ref, other1_ref, other2_ref)):
-        sums_ref[part] = value[...]
+    sums_ref[second_part(core)] = mine_ref[...]
+    sums_ref[second_part(1 - core)] = other_ref[...]
 
     def product(a, b, contract):
         return lax.dot_general(a, b, ((contract[0], contract[1]), ((), ())), precision=exact, preferred_element_type=f32)
@@ -339,9 +365,7 @@
     def whole(value):
         return corner(value, row <= col) + jnp.transpose(corner(value, row < col))
 
-    pack1, g12, pack2 = sums_ref[0:tile], sums_ref[tile : 2 * tile], sums_ref[3 * tile : 4 * tile]
-    w_ref[...] = corner(pack1, row <= col)
-    inverse_factor(w_ref, inv1_ref)
+    pack1, g12, pack2 = pack1_ref[...], sums_ref[tile : 2 * tile], sums_ref[3 * tile : 4 * tile]
     inv1 = inv1_ref[...]
     u12 = product(inv1, g12, plain)
     w_ref[...] = corner(pack2, row <= col) - product(u12, u12, down)
@@ -501,16 +525,18 @@
     return lax.ppermute(message, "row", pairs + [(j, i) for i, j in pairs])
 
 
-def sum_over_rows(mine, other):
+def tied(first, second):
+    return first, lax.optimization_barrier((first, second))[1]
+
+
+def chip_rounds():
     count = lax.axis_size("row")
     bits = count.bit_length() - 1
-    mine = [m + swap_inner(o) for m, o in zip(mine, other)]
+    rounds = []
     for step in range(bits - 1):
         turn = [1 + (step + core) % (bits - 1) for core in range(2)]
-        pairs = [(i, i ^ (1 << turn[i & 1])) for i in range(count)]
-        for stream in range(2):
-            mine[stream] = mine[stream] + lax.ppermute(mine[stream], "row", pairs)
-    return mine + [swap_inner(m) for m in mine]
+        rounds.append([(i, i ^ (1 << turn[i & 1])) for i in range(count)])
+    return rounds
 
 
 def on_device(cell_coeffs, z_factor, noise_cols, q_bar, r_bar):
@@ -548,22 +574,34 @@
         (single, half, half, quarter, quarter, shape((128, 128), f32), shape((384, 128), f32)),
         work * 8, 9 * 10**6, [pltpu.VMEM(z_factor.shape, f32)], scalar=True,
     )(core, table, z_factor, outer1, inner1, inner2, *transposed)
-    part1, part2 = shape((136, 128), f32), shape((128, 128), f32)
-    *parts, oh, ol = call(
-        expand_last, (part1, part2, part1, part2, quarter, quarter), work * 3, 5 * 10**6, [pltpu.VMEM((528, 128), f32)], scalar=True
+    part1, part2 = shape((64, 128), f32), shape((200, 128), f32)
+    mine1, mine2, other1, other2, oh, ol = call(
+        expand_last, (part1, part2, part1, part2, quarter, quarter), work * 3, 5 * 10**6,
+        [pltpu.VMEM((528, 128), f32)], scalar=True,
     )(core, table, z_factor, outer2, light, gram, rest, pack, *transposed)
-    parts = sum_over_rows(parts[:2], parts[2:])
+    mine1, mine2 = mine1 + swap_inner(other1), mine2 + swap_inner(other2)
+    rounds = chip_rounds()
+    for pairs in rounds[:-1]:
+        mine1, mine2 = tied(mine1, mine2)
+        arriving = lax.ppermute(mine2, "row", pairs)
+        mine1 = mine1 + lax.ppermute(mine1, "row", pairs)
+        mine1, arriving = tied(mine1, arriving)
+        mine2 = mine2 + arriving
+    arriving = lax.ppermute(mine2, "row", rounds[-1])
+    mine1 = mine1 + lax.ppermute(mine1, "row", rounds[-1])
+    other1 = swap_inner(mine1)
+    tile = shape((128, 128), f32)
+    pack1, w1, inv1 = call(factor_first, (tile,) * 3, 10**8, 10**5, scalar=True)(core, mine1, other1)
+    arriving, w1 = lax.optimization_barrier((arriving, w1))
+    mine2 = mine2 + arriving
+    other2 = swap_inner(mine2)
+    inv1 = call(factor_second, tile, 10**8, 10**5, [pltpu.VMEM((128, 128), f32)])(w1, inv1)
     square = shape((256, 256), bf16)
     weights = call(
-        factor, (square,) * 4, 10**9, 10**6,
-        [
-            pltpu.VMEM((528, 128), f32),
-            pltpu.VMEM((128, 128), f32),
-            pltpu.VMEM((128, 128), f32),
-            pltpu.VMEM((128, 128), f32),
-        ],
+        factor_last, (square,) * 4, 10**9, 10**6,
+        [pltpu.VMEM((528, 128), f32), pltpu.VMEM((128, 128), f32), pltpu.VMEM((128, 128), f32)],
         scalar=True,
-    )(core, *parts, r_bar)
+    )(core, mine2, other2, pack1, inv1, r_bar)
     left = (qh, ql, nh, nl)
     w_outer, own1 = call(gradient_outer, (single, rim), work * 3, 3 * 10**6, scalar=True)(
         core, table, *left, oh, ol, *weights

time: 79.9 us -> 83.1 us (1.040)
  waiting for transfers between devices: 20.7 us -> 24.3 us
  starting transfers between devices: 26.1 us -> 24.8 us
  Pallas kernels: 28.4 us -> 29.5 us
    ppermute x6, waiting for transfers between devices: 5.28 us -> 8.88 us  [the longest x2 6.47 us: on_device(): mine1 = mine1 + lax.ppermute(mine1, 'row', pairs)]
    ppermute x8, starting transfers between devices: 9.2 us -> 7.9 us  [swap_inner(): return lax.ppermute(message, 'row', [(i, i ^ 1) for i in range(count)])]
    pallas_call x11 -> x13, Pallas kernels: 28.4 us -> 29.5 us  [run(): pl.pallas_call(kernel, out_shape=outs, in_specs=specs, scratch_shapes=lis...]
  transfers between devices with their start and end apart: 18 -> 18, of which waited for: 11 -> 9; matrix products, arithmetic and copies ran while one was open for 0% -> 0% of each run, Pallas kernels for 17% -> 22%
where the time goes in v12:
time: 83.1 us; the launch traced here: 82.9 us
  Pallas kernels  29.5 us (35%)
  starting transfers between devices  24.8 us (30%)
  waiting for transfers between devices  24.3 us (29%)
  local copies, waits for them, and re-layouts  3.31 us (4%)
  between operations  0.89 us (1%)
    pallas_call x13, Pallas kernels, run(): pl.pallas_call(kernel, out_shape=outs, in_specs=specs, scratch_shapes=lis...  29.5 us
    ppermute x4, waiting for transfers between devices, swap_outer(): return lax.ppermute(message, 'row', pairs + [(j, i) for i, j in pairs])  13.7 us
    ppermute x4, starting transfers between devices, swap_outer(): return lax.ppermute(message, 'row', pairs + [(j, i) for i, j in pairs])  11.4 us
    ppermute x8, starting transfers between devices, swap_inner(): return lax.ppermute(message, 'row', [(i, i ^ 1) for i in range(count)])  7.9 us
    ppermute x2, waiting for transfers between devices, on_device(): mine1 = mine1 + lax.ppermute(mine1, 'row', pairs)  6.47 us
    unnamed x12, local copies, waits for them, and re-layouts  3.31 us
    ppermute x2, starting transfers between devices, on_device(): arriving = lax.ppermute(mine2, 'row', pairs)  2.45 us
    ppermute x1, waiting for transfers between devices, on_device(): mine1 = mine1 + lax.ppermute(mine1, 'row', rounds[-1])  2.4 us
  transfers between devices with their start and end apart: 18, of which 9 were waited for; matrix products, arithmetic and copies ran while one was open for 0% of the time, Pallas kernels for 22%

profile of v12, /device:TPU:9, one launch (start us, length us, event | category | flops | bytes accessed | tf_op | source)
XLA Modules:
  0.0 82.9 jit_solution(4724024076133090350)
XLA Ops:
  0.6 1.8 %shard_map.68 = f32[784,128]{1,0:T(8,128)} custom-call(s32[1]{0:T(128)} %bitcast.core_ref, f32[4,2,384,128]{3,2,1,0:T(8,128)} %z_ref.5), custom_call_target="tpu_custom_call" | custom-call | bytes 1000000 | tf_op jit(solution)/shard_map/pallas_call | solution.py:23
  2.4 3.7 %collective-permute-start.1 = (f32[784,128]{1,0:T(8,128)}, f32[784,128]{1,0:T(8,128)S(1)}, u32[]{:S(2)}, u32[]{:S(2)}) collective-permute-start(f32[784,128]{1,0:T(8,128)} %shard_map.68), channel_id=1, source_target_pairs={{1,2},{3,4},{5,6},{7,8},{9,10},{11,12},{13,14},{2,1},{4,3},{6,5},{... | collective-permute-start | bytes 1204232 | tf_op jit(solution)/shard_map/ppermute | solution.py:525
  6.2 1.4 %copy-done = f32[4,2,384,128]{3,2,1,0:T(8,128)S(1)} copy-done((f32[4,2,384,128]{3,2,1,0:T(8,128)S(1)}, f32[4,2,384,128]{3,2,1,0:T(8,128)}, u32[]{:S(2)}) %copy-start) | copy-done | bytes 1572888
  7.6 1.6 %shard_map.69 = (f32[776,128]{1,0:T(8,128)S(1)}, f32[768,128]{1,0:T(8,128)S(1)}, f32[776,128]{1,0:T(8,128)S(1)}, f32[384,16]{1,0:T(8,128)S(1)}) custom-call(s32[1]{0:T(128)} %bitcast.core_ref, f32[6,2,384]{2,1,0:T(2,128)S(1)} %copy-done.4, f32[4,2,384,128]{3,2,1,0:T(8,128)S(1)} %copy-done), custom_call_target="tpu_custom_call" | custom-call | flops 1000000 | bytes 3000000 | tf_op jit(solution)/shard_map/pallas_call | solution.py:23
  9.7 3.1 %collective-permute-start = (f32[776,128]{1,0:T(8,128)S(1)}, f32[776,128]{1,0:T(8,128)S(1)}, u32[]{:S(2)}, u32[]{:S(2)}) collective-permute-start(f32[776,128]{1,0:T(8,128)S(1)} %get-tuple-element.58), channel_id=1, source_target_pairs={{1,2},{3,4},{5,6},{7,8},{9,10},{11,12},{13,14},{2,1},{4,3},{6,5},{... | collective-permute-start | bytes 1191944 | tf_op jit(solution)/shard_map/ppermute | solution.py:525
  12.8 1.9 %copy-done.2 = f32[4,2,384,256]{3,2,1,0:T(8,128)S(1)} copy-done((f32[4,2,384,256]{3,2,1,0:T(8,128)S(1)}, f32[4,2,384,256]{3,2,1,0:T(8,128)}, u32[]{:S(2)}) %copy-start.2) | copy-done | bytes 3145752
  14.7 1.8 %shard_map.70 = (f32[136,128]{1,0:T(8,128)S(1)}, bf16[3072,128]{1,0:T(8,128)(2,1)S(1)}, bf16[3072,128]{1,0:T(8,128)(2,1)S(1)}, bf16[3072,256]{1,0:T(8,128)(2,1)S...) custom-call(f32[3072,128]{1,0:T(8,128)S(1)} %bitcast.4, ...), custom_call_target="tpu_custom_call" | custom-call | flops 503316480 | bytes 9000000 | tf_op jit(solution)/shard_map/pallas_call | solution.py:23
  16.5 3.9 %collective-permute-done.1.outer1_ref = f32[784,128]{1,0:T(8,128)S(1)} collective-permute-done((f32[784,128]{1,0:T(8,128)}, f32[784,128]{1,0:T(8,128)S(1)}, u32[]{:S(2)}, u32[]{:S(2)}) %collective-permute-start.1) | collective-permute-done | bytes 401440 | tf_op jit(solution)/shard_map/ppermute | solution.py:525
  20.5 3.2 %shard_map.71 = (f32[2,384,128]{2,1,0:T(8,128)S(1)}, bf16[1536,128]{1,0:T(8,128)(2,1)S(1)}, bf16[1536,128]{1,0:T(8,128)(2,1)S(1)}, bf16[768,128]{1,0:T(8,128)(2,...) custom-call(s32[1]{0:T(128)} %bitcast.core_ref, ...), custom_call_target="tpu_custom_call" | custom-call | flops 805306368 | bytes 9000000 | tf_op jit(solution)/shard_map/pallas_call | solution.py:23
  23.7 1.0 %collective-permute-done.outer2_ref.fouter2_ref = f32[776,128]{1,0:T(8,128)S(1)} collective-permute-done((f32[776,128]{1,0:T(8,128)S(1)}, f32[776,128]{1,0:T(8,128)S(1)}, u32[]{:S(2)}, u32[]{:S(2)}) %collective-permute-start) | collective-permute-done | bytes 397344 | tf_op jit(solution)/shard_map/ppermute | solution.py:525
  24.7 1.0 %shard_map.72 = (f32[64,128]{1,0:T(8,128)S(1)}, f32[200,128]{1,0:T(8,128)S(1)}, f32[64,128]{1,0:T(8,128)S(1)}, f32[200,128]{1,0:T(8,128)S(1)}, bf16[768,128]{1,0...) custom-call(s32[1]{0:T(128)} %bitcast.core_ref, f32[384,16]{1,0:T(8,128)S(1)} %get-tuple-element.53.table_ref, ...), custom_call_target="tpu_custom_call" | custom-call | flops 301989888 | bytes 5000000 | tf_op jit(solution)/shard_map/pallas_call | solution.py:23
  26.3 0.9 %collective-permute-done.4 = f32[64,128]{1,0:T(8,128)S(1)} collective-permute-done((f32[64,128]{1,0:T(8,128)S(1)}, f32[64,128]{1,0:T(8,128)S(1)}, u32[]{:S(2)}, u32[]{:S(2)}) %collective-permute-start.4) | collective-permute-done | bytes 32800 | tf_op jit(solution)/shard_map/ppermute | solution.py:519
  27.3 1.5 %collective-permute-start.5 = (f32[64,128]{1,0:T(8,128)S(1)}, f32[64,128]{1,0:T(8,128)S(1)}, u32[]{:S(2)}, u32[]{:S(2)}) collective-permute-start(f32[64,128]{1,0:T(8,128)S(1)} %add.24), channel_id=1, source_target_pairs={{0,2},{1,5},{2,0},{3,7},{4,6},{5,1},{6,4},{7,3},{8,10},{9,13},{10,... | collective-permute-start | bytes 98312 | tf_op jit(solution)/shard_map/ppermute | solution.py:587
  28.7 2.7 %collective-permute-done.5 = f32[64,128]{1,0:T(8,128)S(1)} collective-permute-done((f32[64,128]{1,0:T(8,128)S(1)}, f32[64,128]{1,0:T(8,128)S(1)}, u32[]{:S(2)}, u32[]{:S(2)}) %collective-permute-start.5) | collective-permute-done | bytes 32800 | tf_op jit(solution)/shard_map/ppermute | solution.py:587
  31.5 2.4 %collective-permute-start.9 = (f32[200,128]{1,0:T(8,128)S(1)}, f32[200,128]{1,0:T(8,128)S(1)}, u32[]{:S(2)}, u32[]{:S(2)}) collective-permute-start(f32[200,128]{1,0:T(8,128)S(1)} %add.27), channel_id=1, source_target_pairs={{0,4},{1,9},{2,6},{3,11},{4,0},{5,13},{6,2},{7,15},{8,12},{9,1},{1... | collective-permute-start | bytes 307208 | tf_op jit(solution)/shard_map/ppermute | solution.py:586
  33.9 3.8 %collective-permute-done.8 = f32[64,128]{1,0:T(8,128)S(1)} collective-permute-done((f32[64,128]{1,0:T(8,128)S(1)}, f32[64,128]{1,0:T(8,128)S(1)}, u32[]{:S(2)}, u32[]{:S(2)}) %collective-permute-start.8) | collective-permute-done | bytes 32800 | tf_op jit(solution)/shard_map/ppermute | solution.py:587
  38.2 1.1 %collective-permute-start.11 = (f32[64,128]{1,0:T(8,128)S(1)}, f32[64,128]{1,0:T(8,128)S(1)}, u32[]{:S(2)}, u32[]{:S(2)}) collective-permute-start(f32[64,128]{1,0:T(8,128)S(1)} %add.28), channel_id=1, source_target_pairs={{0,8},{1,3},{2,10},{3,1},{4,12},{5,7},{6,14},{7,5},{8,0},{9,11},{1... | collective-permute-start | bytes 98312 | tf_op jit(solution)/shard_map/ppermute | solution.py:591
  39.3 2.4 %collective-permute-done.11 = f32[64,128]{1,0:T(8,128)S(1)} collective-permute-done((f32[64,128]{1,0:T(8,128)S(1)}, f32[64,128]{1,0:T(8,128)S(1)}, u32[]{:S(2)}, u32[]{:S(2)}) %collective-permute-start.11) | collective-permute-done | bytes 32800 | tf_op jit(solution)/shard_map/ppermute | solution.py:591
  41.7 4.8 %collective-permute-start.12 = (f32[64,128]{1,0:T(8,128)S(1)}, f32[64,128]{1,0:T(8,128)S(1)}, u32[]{:S(2)}, u32[]{:S(2)}) collective-permute-start(f32[64,128]{1,0:T(8,128)S(1)} %add.30.mine_ref), channel_id=1, source_target_pairs={{0,1},{1,0},{2,3},{3,2},{4,5},{5,4},{6,7},{7,6},{8,9},{9,8},{10,11... | collective-permute-start | bytes 98312 | tf_op jit(solution)/shard_map/ppermute | solution.py:519
  46.5 0.9 %collective-permute-done.12.other_ref = f32[64,128]{1,0:T(8,128)S(1)} collective-permute-done((f32[64,128]{1,0:T(8,128)S(1)}, f32[64,128]{1,0:T(8,128)S(1)}, u32[]{:S(2)}, u32[]{:S(2)}) %collective-permute-start.12) | collective-permute-done | bytes 32800 | tf_op jit(solution)/shard_map/ppermute | solution.py:519
  47.4 2.6 %shard_map.73 = (f32[128,128]{1,0:T(8,128)S(1)}, f32[128,128]{1,0:T(8,128)S(1)}, f32[128,128]{1,0:T(8,128)S(1)}) custom-call(s32[1]{0:T(128)} %bitcast.core_ref, f32[64,128]{1,0:T(8,128)S(1)} %add.30.mine_ref, f32[64,128]{1,0:T(8,128)S(1)} %collective-permute-done.12.other_ref), custom_call_target="tpu_custom_call" | custom-call | flops 100000000 | bytes 100000 | tf_op jit(solution)/shard_map/pallas_call | solution.py:23
  50.5 1.8 %shard_map.74.inv1_ref = f32[128,128]{1,0:T(8,128)S(1)} custom-call(f32[128,128]{1,0:T(8,128)S(1)} %get-tuple-element.83.w0_ref, f32[128,128]{1,0:T(8,128)S(1)} %get-tuple-element.84.inv0_ref), custom_call_target="tpu_custom_call" | custom-call | flops 100000000 | bytes 100000 | tf_op jit(solution)/shard_map/pallas_call | solution.py:23
  52.3 6.9 %shard_map.75 = (bf16[256,256]{1,0:T(8,128)(2,1)S(1)}, bf16[256,256]{1,0:T(8,128)(2,1)S(1)}, bf16[256,256]{1,0:T(8,128)(2,1)S(1)}, bf16[256,256]{1,0:T(8,128)(2,1)S(1)}) custom-call(s32[1]{0:T(128)} %bitcast.core_ref, f32[200,128]{1,0:T(8,128)S(1)} %add.31.mine_ref, f32[200,128]{1,0:T(8,128)S(1)} %collective-permute-done.13.other_ref, ...), custom_call_target="tpu_custom_call" | custom-call | flops 1000000000 | bytes 1000000 | tf_op jit(solution)/shard_map/pallas_call | solution.py:23
  59.8 1.9 %collective-permute-start.14 = (f32[776,128]{1,0:T(8,128)S(1)}, f32[776,128]{1,0:T(8,128)S(1)}, u32[]{:S(2)}, u32[]{:S(2)}) collective-permute-start(f32[776,128]{1,0:T(8,128)S(1)} %get-tuple-element.89.outer1_ref.own1_ref), channel_id=1, source_target_pairs={{1,2},{3,4},{5,6},{7,8},{9,10},{11,12},{13,14},{2,1},{4,3},{6,5},{... | collective-permute-start | bytes 1191944 | tf_op jit(solution)/shard_map/ppermute | solution.py:525
  61.7 1.7 %shard_map.77 = (f32[2,384,128]{2,1,0:T(8,128)S(1)}, f32[2,2,384,128]{3,2,1,0:T(8,128)S(1)}, f32[768,128]{1,0:T(8,128)S(1)}, f32[768,128]{1,0:T(8,128)S(1)}, f32[768,128]{1,0:T(8,128)S(1)}) custom-call(s32[1]{0:T(128)} %bitcast.core_ref, f32[384,16]{1,0:T(8,128)S(1)} %get-tuple-element.53.table_ref, f32[2,384,128]{2,1,0:T(8,128)S(1)} %get-tuple-element.90.outer_ref, ...), custom_call_target="tpu_custom_call" | custom-call | flops 10000000000 | bytes 6000000 | tf_op jit(solution)/shard_map/pallas_call | solution.py:23
  63.4 1.4 %collective-permute-start.16 = (f32[768,128]{1,0:T(8,128)S(1)}, f32[768,128]{1,0:T(8,128)S(1)}, u32[]{:S(2)}, u32[]{:S(2)}) collective-permute-start(f32[768,128]{1,0:T(8,128)S(1)} %get-tuple-element.98), channel_id=1, source_target_pairs={{0,1},{1,0},{2,3},{3,2},{4,5},{5,4},{6,7},{7,6},{8,9},{9,8},{10,11... | collective-permute-start | bytes 1179656 | tf_op jit(solution)/shard_map/ppermute | solution.py:519
  64.9 2.7 %collective-permute-start.17 = (f32[768,128]{1,0:T(8,128)S(1)}, f32[768,128]{1,0:T(8,128)S(1)}, u32[]{:S(2)}, u32[]{:S(2)}) collective-permute-start(f32[768,128]{1,0:T(8,128)S(1)} %get-tuple-element.101), channel_id=1, source_target_pairs={{1,2},{3,4},{5,6},{7,8},{9,10},{11,12},{13,14},{2,1},{4,3},{6,5},{... | collective-permute-start | bytes 1179656 | tf_op jit(solution)/shard_map/ppermute | solution.py:525
  67.7 3.0 %shard_map.80 = f32[4,2,384,128]{3,2,1,0:T(8,128)} custom-call(s32[1]{0:T(128)} %bitcast.core_ref, bf16[3072,256]{1,0:T(8,128)(2,1)S(1)} %get-tuple-element.54.qh_ref, bf16[3072,256]{1,0:T(8,128)(2,1)S(1)} %get-tuple-element.55.ql_ref, bf16[3072,128]{1,0:T(8,128)(2,1)S(1)} %get-tuple-element.56.nh_ref, bf16[3072,128]{1,0:T(8,128)(2,1)S(1)} %get-tuple-element.57.nl_ref, ...), custom_call_target="tpu_custom_call" | custom-call | tf_op jit(solution)/shard_map/pallas_call | solution.py:23
  70.7 6.7 %collective-permute-done.14.outer1_ref = f32[776,128]{1,0:T(8,128)S(1)} collective-permute-done((f32[776,128]{1,0:T(8,128)S(1)}, f32[776,128]{1,0:T(8,128)S(1)}, u32[]{:S(2)}, u32[]{:S(2)}) %collective-permute-start.14) | collective-permute-done | bytes 397344 | tf_op jit(solution)/shard_map/ppermute | solution.py:525
  77.4 2.2 %shard_map.78 = (f32[2,2,384,128]{3,2,1,0:T(8,128)S(1)}, f32[2,2,384,128]{3,2,1,0:T(8,128)S(1)}) custom-call(f32[776,128]{1,0:T(8,128)S(1)} %collective-permute-done.14.outer1_ref, f32[384,16]{1,0:T(8,128)S(1)} %get-tuple-element.53.table_ref, f32[2,384,128]{2,1,0:T(8,128)S(1)} %get-tuple-element.90.outer_ref, ...), custom_call_target="tpu_custom_call" | custom-call | flops 10000000 | bytes 6000000 | tf_op jit(solution)/shard_map/pallas_call | solution.py:23
  79.6 2.0 %collective-permute-done.17.outer2_ref = f32[768,128]{1,0:T(8,128)S(1)} collective-permute-done((f32[768,128]{1,0:T(8,128)S(1)}, f32[768,128]{1,0:T(8,128)S(1)}, u32[]{:S(2)}, u32[]{:S(2)}) %collective-permute-start.17) | collective-permute-done | bytes 393248 | tf_op jit(solution)/shard_map/ppermute | solution.py:525
  81.6 1.3 %shard_map.79 = f32[4,2,384,128]{3,2,1,0:T(8,128)} custom-call(s32[1]{0:T(128)} %bitcast.core_ref, f32[2,2,384,128]{3,2,1,0:T(8,128)S(1)} %get-tuple-element.99.light_ref, f32[2,2,384,128]{3,2,1,0:T(8,128)S(1)} %get-tuple-element.100.heavy_ref, f32[768,128]{1,0:T(8,128)S(1)} %collective-permute-done.17.outer2_ref), custom_call_target="tpu_custom_call" | custom-call | flops 1000000 | bytes 6000000 | tf_op jit(solution)/shard_map/pallas_call | solution.py:23
  (37 shorter events, 2.9 us)
Async XLA Ops:
  0.6 5.5 %copy-start.4 = (f32[6,2,384]{2,1,0:T(2,128)S(1)}, f32[6,2,384]{2,1,0:T(2,128)}, u32[]{:S(2)}) copy-start(f32[6,2,384]{2,1,0:T(2,128)} %coeff_ref.1) | copy-start | bytes 55300
  2.4 18.0 %collective-permute-start.1 = (f32[784,128]{1,0:T(8,128)}, f32[784,128]{1,0:T(8,128)S(1)}, u32[]{:S(2)}, u32[]{:S(2)}) collective-permute-start(f32[784,128]{1,0:T(8,128)} %shard_map.68), channel_id=1, source_target_pairs={{1,2},{3,4},{5,6},{7,8},{9,10},{11,12},{13,14},{2,1},{4,3},{6,5},{... | collective-permute-start | bytes 1204232 | tf_op jit(solution)/shard_map/ppermute | solution.py:525
  6.2 1.4 %copy-start = (f32[4,2,384,128]{3,2,1,0:T(8,128)S(1)}, f32[4,2,384,128]{3,2,1,0:T(8,128)}, u32[]{:S(2)}) copy-start(f32[4,2,384,128]{3,2,1,0:T(8,128)} %z_ref.5) | copy-start | bytes 4718596
  7.6 5.2 %copy-start.3 = (f32[4,2,384,128]{3,2,1,0:T(8,128)S(1)}, f32[4,2,384,128]{3,2,1,0:T(8,128)}, u32[]{:S(2)}) copy-start(f32[4,2,384,128]{3,2,1,0:T(8,128)} %param.7) | copy-start | bytes 4718596
  9.1 7.4 %collective-permute-start.3 = (f32[776,128]{1,0:T(8,128)S(1)}, f32[776,128]{1,0:T(8,128)S(1)}, u32[]{:S(2)}, u32[]{:S(2)}) collective-permute-start(f32[776,128]{1,0:T(8,128)S(1)} %get-tuple-element.61), channel_id=1, source_target_pairs={{0,1},{1,0},{2,3},{3,2},{4,5},{5,4},{6,7},{7,6},{8,9},{9,8},{10,11... | collective-permute-start | bytes 1191944 | tf_op jit(solution)/shard_map/ppermute | solution.py:519
  9.2 7.3 %collective-permute-start.2 = (f32[768,128]{1,0:T(8,128)S(1)}, f32[768,128]{1,0:T(8,128)S(1)}, u32[]{:S(2)}, u32[]{:S(2)}) collective-permute-start(f32[768,128]{1,0:T(8,128)S(1)} %get-tuple-element.60), channel_id=1, source_target_pairs={{0,1},{1,0},{2,3},{3,2},{4,5},{5,4},{6,7},{7,6},{8,9},{9,8},{10,11... | collective-permute-start | bytes 1179656 | tf_op jit(solution)/shard_map/ppermute | solution.py:519
  9.7 15.0 %collective-permute-start = (f32[776,128]{1,0:T(8,128)S(1)}, f32[776,128]{1,0:T(8,128)S(1)}, u32[]{:S(2)}, u32[]{:S(2)}) collective-permute-start(f32[776,128]{1,0:T(8,128)S(1)} %get-tuple-element.58), channel_id=1, source_target_pairs={{1,2},{3,4},{5,6},{7,8},{9,10},{11,12},{13,14},{2,1},{4,3},{6,5},{... | collective-permute-start | bytes 1191944 | tf_op jit(solution)/shard_map/ppermute | solution.py:525
  12.8 1.9 %copy-start.2 = (f32[4,2,384,256]{3,2,1,0:T(8,128)S(1)}, f32[4,2,384,256]{3,2,1,0:T(8,128)}, u32[]{:S(2)}) copy-start(f32[4,2,384,256]{3,2,1,0:T(8,128)} %param.8) | copy-start | bytes 9437188
  14.7 5.7 %copy-start.1 = (f32[4,2,384,128]{3,2,1,0:T(8,128)S(1)}, f32[4,2,384,128]{3,2,1,0:T(8,128)}, u32[]{:S(2)}) copy-start(f32[4,2,384,128]{3,2,1,0:T(8,128)} %z_ref.5) | copy-start | bytes 4718596
  25.7 26.5 %copy-start.5 = (f32[256,256]{1,0:T(8,128)S(1)}, f32[256,256]{1,0:T(8,128)}, u32[]{:S(2)}) copy-start(f32[256,256]{1,0:T(8,128)} %r_bar_ref.1) | copy-start | bytes 786436
  25.7 1.4 %collective-permute-start.6 = (f32[200,128]{1,0:T(8,128)S(1)}, f32[200,128]{1,0:T(8,128)S(1)}, u32[]{:S(2)}, u32[]{:S(2)}) collective-permute-start(f32[200,128]{1,0:T(8,128)S(1)} %get-tuple-element.75), channel_id=1, source_target_pairs={{0,1},{1,0},{2,3},{3,2},{4,5},{5,4},{6,7},{7,6},{8,9},{9,8},{10,11... | collective-permute-start | bytes 307208 | tf_op jit(solution)/shard_map/ppermute | solution.py:519
  25.8 1.4 %collective-permute-start.4 = (f32[64,128]{1,0:T(8,128)S(1)}, f32[64,128]{1,0:T(8,128)S(1)}, u32[]{:S(2)}, u32[]{:S(2)}) collective-permute-start(f32[64,128]{1,0:T(8,128)S(1)} %get-tuple-element.73), channel_id=1, source_target_pairs={{0,1},{1,0},{2,3},{3,2},{4,5},{5,4},{6,7},{7,6},{8,9},{9,8},{10,11... | collective-permute-start | bytes 98312 | tf_op jit(solution)/shard_map/ppermute | solution.py:519
  27.2 4.2 %collective-permute-start.7 = (f32[200,128]{1,0:T(8,128)S(1)}, f32[200,128]{1,0:T(8,128)S(1)}, u32[]{:S(2)}, u32[]{:S(2)}) collective-permute-start(f32[200,128]{1,0:T(8,128)S(1)} %add.26), channel_id=1, source_target_pairs={{0,2},{1,5},{2,0},{3,7},{4,6},{5,1},{6,4},{7,3},{8,10},{9,13},{10,... | collective-permute-start | bytes 307208 | tf_op jit(solution)/shard_map/ppermute | solution.py:586
  27.3 4.1 %collective-permute-start.5 = (f32[64,128]{1,0:T(8,128)S(1)}, f32[64,128]{1,0:T(8,128)S(1)}, u32[]{:S(2)}, u32[]{:S(2)}) collective-permute-start(f32[64,128]{1,0:T(8,128)S(1)} %add.24), channel_id=1, source_target_pairs={{0,2},{1,5},{2,0},{3,7},{4,6},{5,1},{6,4},{7,3},{8,10},{9,13},{10,... | collective-permute-start | bytes 98312 | tf_op jit(solution)/shard_map/ppermute | solution.py:587
  31.5 6.2 %collective-permute-start.9 = (f32[200,128]{1,0:T(8,128)S(1)}, f32[200,128]{1,0:T(8,128)S(1)}, u32[]{:S(2)}, u32[]{:S(2)}) collective-permute-start(f32[200,128]{1,0:T(8,128)S(1)} %add.27), channel_id=1, source_target_pairs={{0,4},{1,9},{2,6},{3,11},{4,0},{5,13},{6,2},{7,15},{8,12},{9,1},{1... | collective-permute-start | bytes 307208 | tf_op jit(solution)/shard_map/ppermute | solution.py:586
  33.8 3.9 %collective-permute-start.8 = (f32[64,128]{1,0:T(8,128)S(1)}, f32[64,128]{1,0:T(8,128)S(1)}, u32[]{:S(2)}, u32[]{:S(2)}) collective-permute-start(f32[64,128]{1,0:T(8,128)S(1)} %add.25), channel_id=1, source_target_pairs={{0,4},{1,9},{2,6},{3,11},{4,0},{5,13},{6,2},{7,15},{8,12},{9,1},{1... | collective-permute-start | bytes 98312 | tf_op jit(solution)/shard_map/ppermute | solution.py:587
  37.7 12.3 %collective-permute-start.10 = (f32[200,128]{1,0:T(8,128)S(1)}, f32[200,128]{1,0:T(8,128)S(1)}, u32[]{:S(2)}, u32[]{:S(2)}) collective-permute-start(f32[200,128]{1,0:T(8,128)S(1)} %add.29), channel_id=1, source_target_pairs={{0,8},{1,3},{2,10},{3,1},{4,12},{5,7},{6,14},{7,5},{8,0},{9,11},{1... | collective-permute-start | bytes 307208 | tf_op jit(solution)/shard_map/ppermute | solution.py:590
  38.2 3.5 %collective-permute-start.11 = (f32[64,128]{1,0:T(8,128)S(1)}, f32[64,128]{1,0:T(8,128)S(1)}, u32[]{:S(2)}, u32[]{:S(2)}) collective-permute-start(f32[64,128]{1,0:T(8,128)S(1)} %add.28), channel_id=1, source_target_pairs={{0,8},{1,3},{2,10},{3,1},{4,12},{5,7},{6,14},{7,5},{8,0},{9,11},{1... | collective-permute-start | bytes 98312 | tf_op jit(solution)/shard_map/ppermute | solution.py:591
  41.7 5.7 %collective-permute-start.12 = (f32[64,128]{1,0:T(8,128)S(1)}, f32[64,128]{1,0:T(8,128)S(1)}, u32[]{:S(2)}, u32[]{:S(2)}) collective-permute-start(f32[64,128]{1,0:T(8,128)S(1)} %add.30.mine_ref), channel_id=1, source_target_pairs={{0,1},{1,0},{2,3},{3,2},{4,5},{5,4},{6,7},{7,6},{8,9},{9,8},{10,11... | collective-permute-start | bytes 98312 | tf_op jit(solution)/shard_map/ppermute | solution.py:519
  50.1 2.2 %collective-permute-start.13 = (f32[200,128]{1,0:T(8,128)S(1)}, f32[200,128]{1,0:T(8,128)S(1)}, u32[]{:S(2)}, u32[]{:S(2)}) collective-permute-start(f32[200,128]{1,0:T(8,128)S(1)} %add.31.mine_ref), channel_id=1, source_target_pairs={{0,1},{1,0},{2,3},{3,2},{4,5},{5,4},{6,7},{7,6},{8,9},{9,8},{10,11... | collective-permute-start | bytes 307208 | tf_op jit(solution)/shard_map/ppermute | solution.py:519
  59.8 17.6 %collective-permute-start.14 = (f32[776,128]{1,0:T(8,128)S(1)}, f32[776,128]{1,0:T(8,128)S(1)}, u32[]{:S(2)}, u32[]{:S(2)}) collective-permute-start(f32[776,128]{1,0:T(8,128)S(1)} %get-tuple-element.89.outer1_ref.own1_ref), channel_id=1, source_target_pairs={{1,2},{3,4},{5,6},{7,8},{9,10},{11,12},{13,14},{2,1},{4,3},{6,5},{... | collective-permute-start | bytes 1191944 | tf_op jit(solution)/shard_map/ppermute | solution.py:525
  63.4 7.2 %collective-permute-start.16 = (f32[768,128]{1,0:T(8,128)S(1)}, f32[768,128]{1,0:T(8,128)S(1)}, u32[]{:S(2)}, u32[]{:S(2)}) collective-permute-start(f32[768,128]{1,0:T(8,128)S(1)} %get-tuple-element.98), channel_id=1, source_target_pairs={{0,1},{1,0},{2,3},{3,2},{4,5},{5,4},{6,7},{7,6},{8,9},{9,8},{10,11... | collective-permute-start | bytes 1179656 | tf_op jit(solution)/shard_map/ppermute | solution.py:519
  64.9 5.8 %collective-permute-start.15 = (f32[768,128]{1,0:T(8,128)S(1)}, f32[768,128]{1,0:T(8,128)S(1)}, u32[]{:S(2)}, u32[]{:S(2)}) collective-permute-start(f32[768,128]{1,0:T(8,128)S(1)} %get-tuple-element.97.own2_ref), channel_id=1, source_target_pairs={{0,1},{1,0},{2,3},{3,2},{4,5},{5,4},{6,7},{7,6},{8,9},{9,8},{10,11... | collective-permute-start | bytes 1179656 | tf_op jit(solution)/shard_map/ppermute | solution.py:519
  64.9 16.6 %collective-permute-start.17 = (f32[768,128]{1,0:T(8,128)S(1)}, f32[768,128]{1,0:T(8,128)S(1)}, u32[]{:S(2)}, u32[]{:S(2)}) collective-permute-start(f32[768,128]{1,0:T(8,128)S(1)} %get-tuple-element.101), channel_id=1, source_target_pairs={{1,2},{3,4},{5,6},{7,8},{9,10},{11,12},{13,14},{2,1},{4,3},{6,5},{... | collective-permute-start | bytes 1179656 | tf_op jit(solution)/shard_map/ppermute | solution.py:525

commit v13 on v10

--- a/solution.py
+++ b/solution.py
@@ -280,9 +280,8 @@
         }
         inside = (lane >= start) & (lane < start + step)
         rows = [jnp.where(lane == start + i, 1.0, jnp.where(inside, 0.0, rows[i])) for i in range(step)]
-        if not last:
-            following = [jnp.where(inside, 0.0, row) for row in load(start + step)]
         done = []
+        change = [None] * step
         for i in range(step):
             inverse = pl.reciprocal(s[i, i])
             root = lax.rsqrt(s[i, i])
@@ -294,24 +293,25 @@
             if not last:
                 scaled = rows[i] * inverse
                 for k in range(step):
-                    following[k] = following[k] - s[i, step + k] * scaled
+                    term = s[i, step + k] * scaled
+                    change[k] = term if i == 0 else change[k] + term
             done.append(rows[i] * root)
         panel = done[0]
         for i in range(1, step):
             panel = jnp.where(place == i, done[i], panel)
         out_ref[start : start + step, :] = panel
+        if not last:
+            rows = [jnp.where(inside, 0.0, row) - c for row, c in zip(load(start + step), change)]
         beyond = start + 2 * step
         if beyond < size:
             high, mid, low = (part.astype(f32) for part in split3(panel))
             left = jnp.concatenate([high, high, mid, mid, high, low], axis=0).astype(bf16)
             right = jnp.concatenate([high, mid, high, mid, low, high], axis=0).astype(bf16)
-            change = dot(left, right, ((0,), (0,)))[beyond:]
+            update = dot(left, right, ((0,), (0,)))[beyond:]
             old = w_ref[beyond:, :]
             column = lax.broadcasted_iota(jnp.int32, old.shape, 1)
             old = jnp.where((column >= start) & (column < start + step), 0.0, old)
-            w_ref[beyond:, :] = old - change
-        if not last:
-            rows = following
+            w_ref[beyond:, :] = old - update
     value = out_ref[...]
     row = lax.broadcasted_iota(jnp.int32, value.shape, 0)
     column = lax.broadcasted_iota(jnp.int32, value.shape, 1)
@@ -330,6 +330,18 @@
         return lax.dot_general(a, b, ((contract[0], contract[1]), ((), ())), precision=exact, preferred_element_type=f32)
 
     down, across, plain = ((0,), (0,)), ((1,), (1,)), ((1,), (0,))
+
+    def stacked(a, b, contract):
+        a, b = split3(a), split3(b)
+        left = jnp.concatenate([a[k] for k in (0, 0, 1, 1, 0, 2)], axis=contract[0][0])
+        right = jnp.concatenate([b[k] for k in (0, 1, 0, 1, 2, 0)], axis=contract[1][0])
+        return dot(left, right, contract)
+
+    def stacked2(a, b, contract):
+        left = jnp.concatenate([a[0], a[0], a[1]], axis=contract[0][0])
+        right = jnp.concatenate([b[0], b[1], b[0]], axis=contract[1][0])
+        return dot(left, right, contract)
+
     row = lax.broadcasted_iota(jnp.int32, (2 * tile, 2 * tile), 0)
     col = lax.broadcasted_iota(jnp.int32, (2 * tile, 2 * tile), 1)
 
@@ -343,11 +355,11 @@
     w_ref[...] = corner(pack1, row <= col)
     inverse_factor(w_ref, inv1_ref)
     inv1 = inv1_ref[...]
-    u12 = product(inv1, g12, plain)
-    w_ref[...] = corner(pack2, row <= col) - product(u12, u12, down)
+    u12 = stacked(inv1, g12, plain)
+    w_ref[...] = corner(pack2, row <= col) - stacked(u12, u12, down)
     inverse_factor(w_ref, inv2_ref)
     inv2 = inv2_ref[...]
-    inv21 = -product(inv2, product(u12, inv1, down), plain)
+    inv21 = -stacked(inv2, stacked(u12, inv1, down), plain)
     zero = jnp.zeros((tile, tile), f32)
     inv = jnp.concatenate(
         [jnp.concatenate([inv1, zero], axis=1), jnp.concatenate([inv21, inv2], axis=1)], axis=0
@@ -367,8 +379,9 @@
     cross = jnp.where(row > col, cross, jnp.where(row == col, diagonal, 0.0))
     middle = product(inv, product(gram, bar, across), plain) - product(cross, inv, across)
     symmetric = jnp.where(row >= col, middle, 0.0) + jnp.transpose(jnp.where(row > col, middle, 0.0))
-    spread = product(inv, product(symmetric, inv, plain), down)
-    nh_ref[...], nl_ref[...] = split2(inv)
+    parts = split2(inv)
+    spread = stacked2(parts, split2(stacked2(split2(symmetric), parts, plain)), down)
+    nh_ref[...], nl_ref[...] = parts
     sh_ref[...], sl_ref[...] = split2(spread)
 
 

time: 79.8 us -> 79.4 us (level)
  no operation moved by 1% of the time
where the time goes in v13:
time: 79.4 us; the launch traced here: 79.2 us
  Pallas kernels  28.1 us (35%)
  starting transfers between devices  27.2 us (34%)
  waiting for transfers between devices  19.6 us (25%)
  local copies, waits for them, and re-layouts  3.31 us (4%)
  between operations  0.85 us (1%)
    pallas_call x11, Pallas kernels, run(): pl.pallas_call(kernel, out_shape=outs, in_specs=specs, scratch_shapes=lis...  28.1 us
    ppermute x4, waiting for transfers between devices, swap_outer(): return lax.ppermute(message, 'row', pairs + [(j, i) for i, j in pairs])  13.7 us
    ppermute x4, starting transfers between devices, swap_outer(): return lax.ppermute(message, 'row', pairs + [(j, i) for i, j in pairs])  11.5 us
    ppermute x8, starting transfers between devices, swap_inner(): return lax.ppermute(message, 'row', [(i, i ^ 1) for i in range(count)])  8.69 us
    ppermute x6, starting transfers between devices, sum_over_rows(): mine[stream] = mine[stream] + lax.ppermute(mine[stream], 'row', pairs)  6.98 us
    ppermute x6, waiting for transfers between devices, sum_over_rows(): mine[stream] = mine[stream] + lax.ppermute(mine[stream], 'row', pairs)  4.22 us
    unnamed x12, local copies, waits for them, and re-layouts  3.31 us
    ppermute x8, waiting for transfers between devices, swap_inner(): return lax.ppermute(message, 'row', [(i, i ^ 1) for i in range(count)])  1.73 us
  transfers between devices with their start and end apart: 18, of which 11 were waited for; matrix products, arithmetic and copies ran while one was open for 0% of the time, Pallas kernels for 17%

profile of v13, /device:TPU:9, one launch (start us, length us, event | category | flops | bytes accessed | tf_op | source)
XLA Modules:
  0.0 79.2 jit_solution(7989738631449133086)
XLA Ops:
  0.6 1.8 %shard_map.68 = f32[784,128]{1,0:T(8,128)} custom-call(s32[1]{0:T(128)} %bitcast.core_ref, f32[4,2,384,128]{3,2,1,0:T(8,128)} %z_ref.5), custom_call_target="tpu_custom_call" | custom-call | bytes 1000000 | tf_op jit(solution)/shard_map/pallas_call | solution.py:22
  2.4 3.7 %collective-permute-start.1 = (f32[784,128]{1,0:T(8,128)}, f32[784,128]{1,0:T(8,128)S(1)}, u32[]{:S(2)}, u32[]{:S(2)}) collective-permute-start(f32[784,128]{1,0:T(8,128)} %shard_map.68), channel_id=1, source_target_pairs={{1,2},{3,4},{5,6},{7,8},{9,10},{11,12},{13,14},{2,1},{4,3},{6,5},{... | collective-permute-start | bytes 1204232 | tf_op jit(solution)/shard_map/ppermute | solution.py:514
  6.2 1.4 %copy-done = f32[4,2,384,128]{3,2,1,0:T(8,128)S(1)} copy-done((f32[4,2,384,128]{3,2,1,0:T(8,128)S(1)}, f32[4,2,384,128]{3,2,1,0:T(8,128)}, u32[]{:S(2)}) %copy-start) | copy-done | bytes 1572888
  7.6 1.6 %shard_map.69 = (f32[776,128]{1,0:T(8,128)S(1)}, f32[768,128]{1,0:T(8,128)S(1)}, f32[776,128]{1,0:T(8,128)S(1)}, f32[384,16]{1,0:T(8,128)S(1)}) custom-call(s32[1]{0:T(128)} %bitcast.core_ref, f32[6,2,384]{2,1,0:T(2,128)S(1)} %copy-done.4, f32[4,2,384,128]{3,2,1,0:T(8,128)S(1)} %copy-done), custom_call_target="tpu_custom_call" | custom-call | flops 1000000 | bytes 3000000 | tf_op jit(solution)/shard_map/pallas_call | solution.py:22
  9.7 3.1 %collective-permute-start = (f32[776,128]{1,0:T(8,128)S(1)}, f32[776,128]{1,0:T(8,128)S(1)}, u32[]{:S(2)}, u32[]{:S(2)}) collective-permute-start(f32[776,128]{1,0:T(8,128)S(1)} %get-tuple-element.49), channel_id=1, source_target_pairs={{1,2},{3,4},{5,6},{7,8},{9,10},{11,12},{13,14},{2,1},{4,3},{6,5},{... | collective-permute-start | bytes 1191944 | tf_op jit(solution)/shard_map/ppermute | solution.py:514
  12.8 1.9 %copy-done.2 = f32[4,2,384,256]{3,2,1,0:T(8,128)S(1)} copy-done((f32[4,2,384,256]{3,2,1,0:T(8,128)S(1)}, f32[4,2,384,256]{3,2,1,0:T(8,128)}, u32[]{:S(2)}) %copy-start.2) | copy-done | bytes 3145752
  14.7 1.8 %shard_map.70 = (f32[136,128]{1,0:T(8,128)S(1)}, bf16[3072,128]{1,0:T(8,128)(2,1)S(1)}, bf16[3072,128]{1,0:T(8,128)(2,1)S(1)}, bf16[3072,256]{1,0:T(8,128)(2,1)S...) custom-call(f32[3072,128]{1,0:T(8,128)S(1)} %bitcast.4, ...), custom_call_target="tpu_custom_call" | custom-call | flops 503316480 | bytes 9000000 | tf_op jit(solution)/shard_map/pallas_call | solution.py:22
  16.5 3.9 %collective-permute-done.1.outer1_ref = f32[784,128]{1,0:T(8,128)S(1)} collective-permute-done((f32[784,128]{1,0:T(8,128)}, f32[784,128]{1,0:T(8,128)S(1)}, u32[]{:S(2)}, u32[]{:S(2)}) %collective-permute-start.1) | collective-permute-done | bytes 401440 | tf_op jit(solution)/shard_map/ppermute | solution.py:514
  20.5 3.2 %shard_map.71 = (f32[2,384,128]{2,1,0:T(8,128)S(1)}, bf16[1536,128]{1,0:T(8,128)(2,1)S(1)}, bf16[1536,128]{1,0:T(8,128)(2,1)S(1)}, bf16[768,128]{1,0:T(8,128)(2,...) custom-call(s32[1]{0:T(128)} %bitcast.core_ref, ...), custom_call_target="tpu_custom_call" | custom-call | flops 805306368 | bytes 9000000 | tf_op jit(solution)/shard_map/pallas_call | solution.py:22
  23.7 1.0 %collective-permute-done.outer2_ref.fouter2_ref = f32[776,128]{1,0:T(8,128)S(1)} collective-permute-done((f32[776,128]{1,0:T(8,128)S(1)}, f32[776,128]{1,0:T(8,128)S(1)}, u32[]{:S(2)}, u32[]{:S(2)}) %collective-permute-start) | collective-permute-done | bytes 397344 | tf_op jit(solution)/shard_map/ppermute | solution.py:514
  24.7 1.0 %shard_map.72 = (f32[136,128]{1,0:T(8,128)S(1)}, f32[128,128]{1,0:T(8,128)S(1)}, f32[136,128]{1,0:T(8,128)S(1)}, f32[128,128]{1,0:T(8,128)S(1)}, bf16[768,128]{1...) custom-call(s32[1]{0:T(128)} %bitcast.core_ref, f32[384,16]{1,0:T(8,128)S(1)} %get-tuple-element.44.table_ref, ...), custom_call_target="tpu_custom_call" | custom-call | flops 301989888 | bytes 5000000 | tf_op jit(solution)/shard_map/pallas_call | solution.py:22
  26.3 0.7 collective-permute-done.4
  27.2 1.8 %collective-permute-start.9 = (f32[128,128]{1,0:T(8,128)S(1)}, f32[128,128]{1,0:T(8,128)S(1)}, u32[]{:S(2)}, u32[]{:S(2)}) collective-permute-start(f32[128,128]{1,0:T(8,128)S(1)} %add.28), channel_id=1, source_target_pairs={{0,4},{1,3},{2,6},{3,1},{4,0},{5,7},{6,2},{7,5},{8,12},{9,11},{10,... | collective-permute-start | bytes 196616 | tf_op jit(solution)/shard_map/ppermute | solution.py:525
  29.0 1.6 %collective-permute-done.5 = f32[136,128]{1,0:T(8,128)S(1)} collective-permute-done((f32[136,128]{1,0:T(8,128)S(1)}, f32[136,128]{1,0:T(8,128)S(1)}, u32[]{:S(2)}, u32[]{:S(2)}) %collective-permute-start.5) | collective-permute-done | bytes 69664 | tf_op jit(solution)/shard_map/ppermute | solution.py:525
  30.6 2.4 %collective-permute-start.6 = (f32[136,128]{1,0:T(8,128)S(1)}, f32[136,128]{1,0:T(8,128)S(1)}, u32[]{:S(2)}, u32[]{:S(2)}) collective-permute-start(f32[136,128]{1,0:T(8,128)S(1)} %add.25), channel_id=1, source_target_pairs={{0,4},{1,9},{2,6},{3,11},{4,0},{5,13},{6,2},{7,15},{8,12},{9,1},{1... | collective-permute-start | bytes 208904 | tf_op jit(solution)/shard_map/ppermute | solution.py:525
  33.2 1.6 %collective-permute-done.6 = f32[136,128]{1,0:T(8,128)S(1)} collective-permute-done((f32[136,128]{1,0:T(8,128)S(1)}, f32[136,128]{1,0:T(8,128)S(1)}, u32[]{:S(2)}, u32[]{:S(2)}) %collective-permute-start.6) | collective-permute-done | bytes 69664 | tf_op jit(solution)/shard_map/ppermute | solution.py:525
  34.9 1.1 %collective-permute-start.7 = (f32[136,128]{1,0:T(8,128)S(1)}, f32[136,128]{1,0:T(8,128)S(1)}, u32[]{:S(2)}, u32[]{:S(2)}) collective-permute-start(f32[136,128]{1,0:T(8,128)S(1)} %add.26), channel_id=1, source_target_pairs={{0,8},{1,3},{2,10},{3,1},{4,12},{5,7},{6,14},{7,5},{8,0},{9,11},{1... | collective-permute-start | bytes 208904 | tf_op jit(solution)/shard_map/ppermute | solution.py:525
  36.5 1.4 %collective-permute-start.11 = (f32[128,128]{1,0:T(8,128)S(1)}, f32[128,128]{1,0:T(8,128)S(1)}, u32[]{:S(2)}, u32[]{:S(2)}) collective-permute-start(f32[128,128]{1,0:T(8,128)S(1)} %add.30), channel_id=1, source_target_pairs={{0,2},{1,9},{2,0},{3,11},{4,6},{5,13},{6,4},{7,15},{8,10},{9,1},{1... | collective-permute-start | bytes 196616 | tf_op jit(solution)/shard_map/ppermute | solution.py:525
  38.4 4.1 %collective-permute-start.12 = (f32[136,128]{1,0:T(8,128)S(1)}, f32[136,128]{1,0:T(8,128)S(1)}, u32[]{:S(2)}, u32[]{:S(2)}) collective-permute-start(f32[136,128]{1,0:T(8,128)S(1)} %add.27.mine1_ref), channel_id=1, source_target_pairs={{0,1},{1,0},{2,3},{3,2},{4,5},{5,4},{6,7},{7,6},{8,9},{9,8},{10,11... | collective-permute-start | bytes 208904 | tf_op jit(solution)/shard_map/ppermute | solution.py:508
  42.6 2.0 %collective-permute-start.13 = (f32[128,128]{1,0:T(8,128)S(1)}, f32[128,128]{1,0:T(8,128)S(1)}, u32[]{:S(2)}, u32[]{:S(2)}) collective-permute-start(f32[128,128]{1,0:T(8,128)S(1)} %add.31.mine2_ref), channel_id=1, source_target_pairs={{0,1},{1,0},{2,3},{3,2},{4,5},{5,4},{6,7},{7,6},{8,9},{9,8},{10,11... | collective-permute-start | bytes 196616 | tf_op jit(solution)/shard_map/ppermute | solution.py:508
  44.6 0.9 %collective-permute-done.13.other2_ref = f32[128,128]{1,0:T(8,128)S(1)} collective-permute-done((f32[128,128]{1,0:T(8,128)S(1)}, f32[128,128]{1,0:T(8,128)S(1)}, u32[]{:S(2)}, u32[]{:S(2)}) %collective-permute-start.13) | collective-permute-done | bytes 65568 | tf_op jit(solution)/shard_map/ppermute | solution.py:508
  45.5 9.9 %shard_map.73 = (bf16[256,256]{1,0:T(8,128)(2,1)S(1)}, bf16[256,256]{1,0:T(8,128)(2,1)S(1)}, bf16[256,256]{1,0:T(8,128)(2,1)S(1)}, bf16[256,256]{1,0:T(8,128)(2,1)S(1)}) custom-call(s32[1]{0:T(128)} %bitcast.core_ref, f32[136,128]{1,0:T(8,128)S(1)} %add.27.mine1_ref, f32[128,128]{1,0:T(8,128)S(1)} %add.31.mine2_ref, ...), custom_call_target="tpu_custom_call" | custom-call | flops 1000000000 | bytes 1000000 | tf_op jit(solution)/shard_map/pallas_call | solution.py:22
  55.5 0.6 shard_map.74
  56.0 1.9 %collective-permute-start.14 = (f32[776,128]{1,0:T(8,128)S(1)}, f32[776,128]{1,0:T(8,128)S(1)}, u32[]{:S(2)}, u32[]{:S(2)}) collective-permute-start(f32[776,128]{1,0:T(8,128)S(1)} %get-tuple-element.71.outer1_ref.own1_ref), channel_id=1, source_target_pairs={{1,2},{3,4},{5,6},{7,8},{9,10},{11,12},{13,14},{2,1},{4,3},{6,5},{... | collective-permute-start | bytes 1191944 | tf_op jit(solution)/shard_map/ppermute | solution.py:514
  58.0 1.7 %shard_map.75 = (f32[2,384,128]{2,1,0:T(8,128)S(1)}, f32[2,2,384,128]{3,2,1,0:T(8,128)S(1)}, f32[768,128]{1,0:T(8,128)S(1)}, f32[768,128]{1,0:T(8,128)S(1)}, f32[768,128]{1,0:T(8,128)S(1)}) custom-call(s32[1]{0:T(128)} %bitcast.core_ref, f32[384,16]{1,0:T(8,128)S(1)} %get-tuple-element.44.table_ref, f32[2,384,128]{2,1,0:T(8,128)S(1)} %get-tuple-element.72.outer_ref, ...), custom_call_target="tpu_custom_call" | custom-call | flops 10000000000 | bytes 6000000 | tf_op jit(solution)/shard_map/pallas_call | solution.py:22
  59.7 1.3 %collective-permute-start.16 = (f32[768,128]{1,0:T(8,128)S(1)}, f32[768,128]{1,0:T(8,128)S(1)}, u32[]{:S(2)}, u32[]{:S(2)}) collective-permute-start(f32[768,128]{1,0:T(8,128)S(1)} %get-tuple-element.80), channel_id=1, source_target_pairs={{0,1},{1,0},{2,3},{3,2},{4,5},{5,4},{6,7},{7,6},{8,9},{9,8},{10,11... | collective-permute-start | bytes 1179656 | tf_op jit(solution)/shard_map/ppermute | solution.py:508
  61.1 2.8 %collective-permute-start.17 = (f32[768,128]{1,0:T(8,128)S(1)}, f32[768,128]{1,0:T(8,128)S(1)}, u32[]{:S(2)}, u32[]{:S(2)}) collective-permute-start(f32[768,128]{1,0:T(8,128)S(1)} %get-tuple-element.83), channel_id=1, source_target_pairs={{1,2},{3,4},{5,6},{7,8},{9,10},{11,12},{13,14},{2,1},{4,3},{6,5},{... | collective-permute-start | bytes 1179656 | tf_op jit(solution)/shard_map/ppermute | solution.py:514
  63.9 3.0 %shard_map.78 = f32[4,2,384,128]{3,2,1,0:T(8,128)} custom-call(s32[1]{0:T(128)} %bitcast.core_ref, bf16[3072,256]{1,0:T(8,128)(2,1)S(1)} %get-tuple-element.45.qh_ref, bf16[3072,256]{1,0:T(8,128)(2,1)S(1)} %get-tuple-element.46.ql_ref, bf16[3072,128]{1,0:T(8,128)(2,1)S(1)} %get-tuple-element.47.nh_ref, bf16[3072,128]{1,0:T(8,128)(2,1)S(1)} %get-tuple-element.48.nl_ref, ...), custom_call_target="tpu_custom_call" | custom-call | tf_op jit(solution)/shard_map/pallas_call | solution.py:22
  67.0 6.7 %collective-permute-done.14.outer1_ref = f32[776,128]{1,0:T(8,128)S(1)} collective-permute-done((f32[776,128]{1,0:T(8,128)S(1)}, f32[776,128]{1,0:T(8,128)S(1)}, u32[]{:S(2)}, u32[]{:S(2)}) %collective-permute-start.14) | collective-permute-done | bytes 397344 | tf_op jit(solution)/shard_map/ppermute | solution.py:514
  73.7 2.2 %shard_map.76 = (f32[2,2,384,128]{3,2,1,0:T(8,128)S(1)}, f32[2,2,384,128]{3,2,1,0:T(8,128)S(1)}) custom-call(f32[776,128]{1,0:T(8,128)S(1)} %collective-permute-done.14.outer1_ref, f32[384,16]{1,0:T(8,128)S(1)} %get-tuple-element.44.table_ref, f32[2,384,128]{2,1,0:T(8,128)S(1)} %get-tuple-element.72.outer_ref, ...), custom_call_target="tpu_custom_call" | custom-call | flops 10000000 | bytes 6000000 | tf_op jit(solution)/shard_map/pallas_call | solution.py:22
  75.8 2.0 %collective-permute-done.17.outer2_ref = f32[768,128]{1,0:T(8,128)S(1)} collective-permute-done((f32[768,128]{1,0:T(8,128)S(1)}, f32[768,128]{1,0:T(8,128)S(1)}, u32[]{:S(2)}, u32[]{:S(2)}) %collective-permute-start.17) | collective-permute-done | bytes 393248 | tf_op jit(solution)/shard_map/ppermute | solution.py:514
  77.9 1.3 %shard_map.77 = f32[4,2,384,128]{3,2,1,0:T(8,128)} custom-call(s32[1]{0:T(128)} %bitcast.core_ref, f32[2,2,384,128]{3,2,1,0:T(8,128)S(1)} %get-tuple-element.81.light_ref, f32[2,2,384,128]{3,2,1,0:T(8,128)S(1)} %get-tuple-element.82.heavy_ref, f32[768,128]{1,0:T(8,128)S(1)} %collective-permute-done.17.outer2_ref), custom_call_target="tpu_custom_call" | custom-call | flops 1000000 | bytes 6000000 | tf_op jit(solution)/shard_map/pallas_call | solution.py:22
  (35 shorter events, 2.7 us)
Async XLA Ops:
  0.6 5.5 %copy-start.4 = (f32[6,2,384]{2,1,0:T(2,128)S(1)}, f32[6,2,384]{2,1,0:T(2,128)}, u32[]{:S(2)}) copy-start(f32[6,2,384]{2,1,0:T(2,128)} %coeff_ref.1) | copy-start | bytes 55300
  2.4 18.0 %collective-permute-start.1 = (f32[784,128]{1,0:T(8,128)}, f32[784,128]{1,0:T(8,128)S(1)}, u32[]{:S(2)}, u32[]{:S(2)}) collective-permute-start(f32[784,128]{1,0:T(8,128)} %shard_map.68), channel_id=1, source_target_pairs={{1,2},{3,4},{5,6},{7,8},{9,10},{11,12},{13,14},{2,1},{4,3},{6,5},{... | collective-permute-start | bytes 1204232 | tf_op jit(solution)/shard_map/ppermute | solution.py:514
  6.2 1.4 %copy-start = (f32[4,2,384,128]{3,2,1,0:T(8,128)S(1)}, f32[4,2,384,128]{3,2,1,0:T(8,128)}, u32[]{:S(2)}) copy-start(f32[4,2,384,128]{3,2,1,0:T(8,128)} %z_ref.5) | copy-start | bytes 4718596
  7.6 5.2 %copy-start.3 = (f32[4,2,384,128]{3,2,1,0:T(8,128)S(1)}, f32[4,2,384,128]{3,2,1,0:T(8,128)}, u32[]{:S(2)}) copy-start(f32[4,2,384,128]{3,2,1,0:T(8,128)} %param.7) | copy-start | bytes 4718596
  9.1 7.4 %collective-permute-start.3 = (f32[776,128]{1,0:T(8,128)S(1)}, f32[776,128]{1,0:T(8,128)S(1)}, u32[]{:S(2)}, u32[]{:S(2)}) collective-permute-start(f32[776,128]{1,0:T(8,128)S(1)} %get-tuple-element.52), channel_id=1, source_target_pairs={{0,1},{1,0},{2,3},{3,2},{4,5},{5,4},{6,7},{7,6},{8,9},{9,8},{10,11... | collective-permute-start | bytes 1191944 | tf_op jit(solution)/shard_map/ppermute | solution.py:508
  9.2 7.3 %collective-permute-start.2 = (f32[768,128]{1,0:T(8,128)S(1)}, f32[768,128]{1,0:T(8,128)S(1)}, u32[]{:S(2)}, u32[]{:S(2)}) collective-permute-start(f32[768,128]{1,0:T(8,128)S(1)} %get-tuple-element.51), channel_id=1, source_target_pairs={{0,1},{1,0},{2,3},{3,2},{4,5},{5,4},{6,7},{7,6},{8,9},{9,8},{10,11... | collective-permute-start | bytes 1179656 | tf_op jit(solution)/shard_map/ppermute | solution.py:508
  9.7 15.0 %collective-permute-start = (f32[776,128]{1,0:T(8,128)S(1)}, f32[776,128]{1,0:T(8,128)S(1)}, u32[]{:S(2)}, u32[]{:S(2)}) collective-permute-start(f32[776,128]{1,0:T(8,128)S(1)} %get-tuple-element.49), channel_id=1, source_target_pairs={{1,2},{3,4},{5,6},{7,8},{9,10},{11,12},{13,14},{2,1},{4,3},{6,5},{... | collective-permute-start | bytes 1191944 | tf_op jit(solution)/shard_map/ppermute | solution.py:514
  12.8 1.9 %copy-start.2 = (f32[4,2,384,256]{3,2,1,0:T(8,128)S(1)}, f32[4,2,384,256]{3,2,1,0:T(8,128)}, u32[]{:S(2)}) copy-start(f32[4,2,384,256]{3,2,1,0:T(8,128)} %param.8) | copy-start | bytes 9437188
  14.7 5.7 %copy-start.1 = (f32[4,2,384,128]{3,2,1,0:T(8,128)S(1)}, f32[4,2,384,128]{3,2,1,0:T(8,128)}, u32[]{:S(2)}) copy-start(f32[4,2,384,128]{3,2,1,0:T(8,128)} %z_ref.5) | copy-start | bytes 4718596
  25.7 19.8 %copy-start.5 = (f32[256,256]{1,0:T(8,128)S(1)}, f32[256,256]{1,0:T(8,128)}, u32[]{:S(2)}) copy-start(f32[256,256]{1,0:T(8,128)} %r_bar_ref.1) | copy-start | bytes 786436
  25.7 1.3 %collective-permute-start.4 = (f32[136,128]{1,0:T(8,128)S(1)}, f32[136,128]{1,0:T(8,128)S(1)}, u32[]{:S(2)}, u32[]{:S(2)}) collective-permute-start(f32[136,128]{1,0:T(8,128)S(1)} %get-tuple-element.64), channel_id=1, source_target_pairs={{0,1},{1,0},{2,3},{3,2},{4,5},{5,4},{6,7},{7,6},{8,9},{9,8},{10,11... | collective-permute-start | bytes 208904 | tf_op jit(solution)/shard_map/ppermute | solution.py:508
  25.8 1.4 %collective-permute-start.8 = (f32[128,128]{1,0:T(8,128)S(1)}, f32[128,128]{1,0:T(8,128)S(1)}, u32[]{:S(2)}, u32[]{:S(2)}) collective-permute-start(f32[128,128]{1,0:T(8,128)S(1)} %get-tuple-element.66), channel_id=1, source_target_pairs={{0,1},{1,0},{2,3},{3,2},{4,5},{5,4},{6,7},{7,6},{8,9},{9,8},{10,11... | collective-permute-start | bytes 196616 | tf_op jit(solution)/shard_map/ppermute | solution.py:508
  27.1 3.5 %collective-permute-start.5 = (f32[136,128]{1,0:T(8,128)S(1)}, f32[136,128]{1,0:T(8,128)S(1)}, u32[]{:S(2)}, u32[]{:S(2)}) collective-permute-start(f32[136,128]{1,0:T(8,128)S(1)} %add.24), channel_id=1, source_target_pairs={{0,2},{1,5},{2,0},{3,7},{4,6},{5,1},{6,4},{7,3},{8,10},{9,13},{10,... | collective-permute-start | bytes 208904 | tf_op jit(solution)/shard_map/ppermute | solution.py:525
  27.2 5.8 %collective-permute-start.9 = (f32[128,128]{1,0:T(8,128)S(1)}, f32[128,128]{1,0:T(8,128)S(1)}, u32[]{:S(2)}, u32[]{:S(2)}) collective-permute-start(f32[128,128]{1,0:T(8,128)S(1)} %add.28), channel_id=1, source_target_pairs={{0,4},{1,3},{2,6},{3,1},{4,0},{5,7},{6,2},{7,5},{8,12},{9,11},{10,... | collective-permute-start | bytes 196616 | tf_op jit(solution)/shard_map/ppermute | solution.py:525
  30.6 4.3 %collective-permute-start.6 = (f32[136,128]{1,0:T(8,128)S(1)}, f32[136,128]{1,0:T(8,128)S(1)}, u32[]{:S(2)}, u32[]{:S(2)}) collective-permute-start(f32[136,128]{1,0:T(8,128)S(1)} %add.25), channel_id=1, source_target_pairs={{0,4},{1,9},{2,6},{3,11},{4,0},{5,13},{6,2},{7,15},{8,12},{9,1},{1... | collective-permute-start | bytes 208904 | tf_op jit(solution)/shard_map/ppermute | solution.py:525
  33.0 3.5 %collective-permute-start.10 = (f32[128,128]{1,0:T(8,128)S(1)}, f32[128,128]{1,0:T(8,128)S(1)}, u32[]{:S(2)}, u32[]{:S(2)}) collective-permute-start(f32[128,128]{1,0:T(8,128)S(1)} %add.29), channel_id=1, source_target_pairs={{0,8},{1,5},{2,10},{3,7},{4,12},{5,1},{6,14},{7,3},{8,0},{9,13},{1... | collective-permute-start | bytes 196616 | tf_op jit(solution)/shard_map/ppermute | solution.py:525
  34.9 3.5 %collective-permute-start.7 = (f32[136,128]{1,0:T(8,128)S(1)}, f32[136,128]{1,0:T(8,128)S(1)}, u32[]{:S(2)}, u32[]{:S(2)}) collective-permute-start(f32[136,128]{1,0:T(8,128)S(1)} %add.26), channel_id=1, source_target_pairs={{0,8},{1,3},{2,10},{3,1},{4,12},{5,7},{6,14},{7,5},{8,0},{9,11},{1... | collective-permute-start | bytes 208904 | tf_op jit(solution)/shard_map/ppermute | solution.py:525
  36.5 6.1 %collective-permute-start.11 = (f32[128,128]{1,0:T(8,128)S(1)}, f32[128,128]{1,0:T(8,128)S(1)}, u32[]{:S(2)}, u32[]{:S(2)}) collective-permute-start(f32[128,128]{1,0:T(8,128)S(1)} %add.30), channel_id=1, source_target_pairs={{0,2},{1,9},{2,0},{3,11},{4,6},{5,13},{6,4},{7,15},{8,10},{9,1},{1... | collective-permute-start | bytes 196616 | tf_op jit(solution)/shard_map/ppermute | solution.py:525
  38.4 7.1 %collective-permute-start.12 = (f32[136,128]{1,0:T(8,128)S(1)}, f32[136,128]{1,0:T(8,128)S(1)}, u32[]{:S(2)}, u32[]{:S(2)}) collective-permute-start(f32[136,128]{1,0:T(8,128)S(1)} %add.27.mine1_ref), channel_id=1, source_target_pairs={{0,1},{1,0},{2,3},{3,2},{4,5},{5,4},{6,7},{7,6},{8,9},{9,8},{10,11... | collective-permute-start | bytes 208904 | tf_op jit(solution)/shard_map/ppermute | solution.py:508
  42.6 2.9 %collective-permute-start.13 = (f32[128,128]{1,0:T(8,128)S(1)}, f32[128,128]{1,0:T(8,128)S(1)}, u32[]{:S(2)}, u32[]{:S(2)}) collective-permute-start(f32[128,128]{1,0:T(8,128)S(1)} %add.31.mine2_ref), channel_id=1, source_target_pairs={{0,1},{1,0},{2,3},{3,2},{4,5},{5,4},{6,7},{7,6},{8,9},{9,8},{10,11... | collective-permute-start | bytes 196616 | tf_op jit(solution)/shard_map/ppermute | solution.py:508
  56.0 17.6 %collective-permute-start.14 = (f32[776,128]{1,0:T(8,128)S(1)}, f32[776,128]{1,0:T(8,128)S(1)}, u32[]{:S(2)}, u32[]{:S(2)}) collective-permute-start(f32[776,128]{1,0:T(8,128)S(1)} %get-tuple-element.71.outer1_ref.own1_ref), channel_id=1, source_target_pairs={{1,2},{3,4},{5,6},{7,8},{9,10},{11,12},{13,14},{2,1},{4,3},{6,5},{... | collective-permute-start | bytes 1191944 | tf_op jit(solution)/shard_map/ppermute | solution.py:514
  59.7 7.2 %collective-permute-start.16 = (f32[768,128]{1,0:T(8,128)S(1)}, f32[768,128]{1,0:T(8,128)S(1)}, u32[]{:S(2)}, u32[]{:S(2)}) collective-permute-start(f32[768,128]{1,0:T(8,128)S(1)} %get-tuple-element.80), channel_id=1, source_target_pairs={{0,1},{1,0},{2,3},{3,2},{4,5},{5,4},{6,7},{7,6},{8,9},{9,8},{10,11... | collective-permute-start | bytes 1179656 | tf_op jit(solution)/shard_map/ppermute | solution.py:508
  61.0 5.9 %collective-permute-start.15 = (f32[768,128]{1,0:T(8,128)S(1)}, f32[768,128]{1,0:T(8,128)S(1)}, u32[]{:S(2)}, u32[]{:S(2)}) collective-permute-start(f32[768,128]{1,0:T(8,128)S(1)} %get-tuple-element.79.own2_ref), channel_id=1, source_target_pairs={{0,1},{1,0},{2,3},{3,2},{4,5},{5,4},{6,7},{7,6},{8,9},{9,8},{10,11... | collective-permute-start | bytes 1179656 | tf_op jit(solution)/shard_map/ppermute | solution.py:508
  61.1 16.8 %collective-permute-start.17 = (f32[768,128]{1,0:T(8,128)S(1)}, f32[768,128]{1,0:T(8,128)S(1)}, u32[]{:S(2)}, u32[]{:S(2)}) collective-permute-start(f32[768,128]{1,0:T(8,128)S(1)} %get-tuple-element.83), channel_id=1, source_target_pairs={{1,2},{3,4},{5,6},{7,8},{9,10},{11,12},{13,14},{2,1},{4,3},{6,5},{... | collective-permute-start | bytes 1179656 | tf_op jit(solution)/shard_map/ppermute | solution.py:514

commit v14 on v13

--- a/solution.py
+++ b/solution.py
@@ -6,7 +6,6 @@
 from jax.sharding import PartitionSpec as P
 
 rate_scales = (0.4, 0.4, 0.1, 0.2, 0.1, 0.1)
-exact = lax.Precision.HIGHEST
 f32 = jnp.float32
 bf16 = jnp.bfloat16
 VMEM = pl.BlockSpec(memory_space=pltpu.VMEM)
@@ -326,9 +325,6 @@
     for part, value in zip(quarters(core), (mine1_ref, mine2_ref, other1_ref, other2_ref)):
         sums_ref[part] = value[...]
 
-    def product(a, b, contract):
-        return lax.dot_general(a, b, ((contract[0], contract[1]), ((), ())), precision=exact, preferred_element_type=f32)
-
     down, across, plain = ((0,), (0,)), ((1,), (1,)), ((1,), (0,))
 
     def stacked(a, b, contract):
@@ -377,7 +373,7 @@
     cross = jnp.concatenate([top, bottom], axis=0)
     diagonal = jnp.concatenate([sums_ref[512:513], sums_ref[520:521]], axis=1)
     cross = jnp.where(row > col, cross, jnp.where(row == col, diagonal, 0.0))
-    middle = product(inv, product(gram, bar, across), plain) - product(cross, inv, across)
+    middle = stacked(inv, stacked(gram, bar, across), plain) - stacked(cross, inv, across)
     symmetric = jnp.where(row >= col, middle, 0.0) + jnp.transpose(jnp.where(row > col, middle, 0.0))
     parts = split2(inv)
     spread = stacked2(parts, split2(stacked2(split2(symmetric), parts, plain)), down)
@@ -459,9 +455,8 @@
 
 
 def contract_first(
-    outer1_ref, table_ref, outer_ref, light_ref, heavy_ref, own1_ref, own2_ref, inner1_ref, inner2_ref,
-    fouter2_ref, finner_ref,
-    out_light_ref, out_heavy_ref, first_ref,
+    core_ref, outer1_ref, table_ref, outer_ref, light_ref, heavy_ref, own1_ref, own2_ref, inner1_ref, inner2_ref,
+    fouter2_ref, finner_ref, out_ref, light_out_ref, first_ref,
 ):
     c = coefficients(table_ref)
     n = outer_ref.shape[1]
@@ -487,20 +482,26 @@
             hop_p = hop_p + inner2_ref[n : 2 * n]
         light = backward_light(c[s], xa, pa, pb, hop_x, hop_p)
         heavy = backward_heavy(c[s], pa, xb, pb)
+        row = core_ref[0] if s == 0 else 1 - core_ref[0]
         for k in range(2):
-            out_light_ref[k, s] = w[s][k] + first_ref[k, s] + 0.5 * light[k]
-            out_heavy_ref[k, s] = w[s][2 + k] + first_ref[2 + k, s] + 0.5 * heavy[k]
-
-
-def contract_last(core_ref, light_ref, heavy_ref, outer2_ref, out_ref):
-    n = out_ref.shape[2]
+            value = w[s][k] + first_ref[k, s] + 0.5 * light[k]
+            out_ref[k, row] = value
+            if s == 0:
+                light_out_ref[k] = value
+            out_ref[2 + k, row] = w[s][2 + k] + first_ref[2 + k, s] + 0.5 * heavy[k]
+
+
+def contract_last(core_ref, light_ref, outer2_ref, whole_hbm, out_hbm, value_ref, sems):
+    n = light_ref.shape[1]
     core = core_ref[0]
-    out_ref[0, core] = light_ref[0, 0] + 0.5 * outer2_ref[n : 2 * n]
-    out_ref[1, core] = light_ref[1, 0] - 0.5 * outer2_ref[0:n]
-    for k in range(2):
-        out_ref[k, 1 - core] = light_ref[k, 1]
-        out_ref[2 + k, core] = heavy_ref[k, 0]
-        out_ref[2 + k, 1 - core] = heavy_ref[k, 1]
+    value_ref[0] = light_ref[0] + 0.5 * outer2_ref[n : 2 * n]
+    first = pltpu.make_async_copy(value_ref.at[0], out_hbm.at[0, core], sems.at[0])
+    first.start()
+    value_ref[1] = light_ref[1] - 0.5 * outer2_ref[0:n]
+    second = pltpu.make_async_copy(value_ref.at[1], out_hbm.at[1, core], sems.at[1])
+    second.start()
+    first.wait()
+    second.wait()
 
 
 def swap_inner(message):
@@ -589,12 +590,25 @@
     noise_grad = call(gradient_noise, shape(noise_cols.shape, f32), 0, 0, scalar=True)(
         core, *left, oh, ol, lh, ll, hh, hl, *weights
     )
-    out_light, out_heavy = call(contract_first, (pair, pair), 10**7, 6 * 10**6, [pltpu.VMEM(z_factor.shape, f32)])(
-        back1, table, w_outer, w_inner, w_heavy, own1, own2, near1, near2, outer2, inner2
-    )
-    z_grad = call(contract_last, shape(z_factor.shape, f32), 10**6, 6 * 10**6, scalar=True)(
-        core, out_light, out_heavy, back2
-    )
+    whole, light = call(
+        contract_first, (shape(z_factor.shape, f32), single), 10**7, 6 * 10**6,
+        [pltpu.VMEM(z_factor.shape, f32)], scalar=True,
+    )(core, back1, table, w_outer, w_inner, w_heavy, own1, own2, near1, near2, outer2, inner2)
+    z_grad = pl.pallas_call(
+        contract_last,
+        out_shape=shape(z_factor.shape, f32),
+        in_specs=[
+            pl.BlockSpec(memory_space=pltpu.SMEM),
+            pl.BlockSpec(),
+            pl.BlockSpec(),
+            pl.BlockSpec(memory_space=pltpu.HBM),
+        ],
+        out_specs=pl.BlockSpec(memory_space=pltpu.HBM),
+        input_output_aliases={3: 0},
+        scratch_shapes=[pltpu.VMEM((2, n, rank), f32), pltpu.SemaphoreType.DMA((2,))],
+        compiler_params=pltpu.CompilerParams(vmem_limit_bytes=LIMIT),
+        cost_estimate=pl.CostEstimate(flops=10**6, bytes_accessed=10**6, transcendentals=0),
+    )(core, light, back2, whole)
     return z_grad, noise_grad
 
 

time: 79.4 us -> 79 us (level)
  waiting for transfers between devices: 19.6 us -> 18.6 us
    ppermute x4, waiting for transfers between devices: 13.7 us -> 12.6 us  [swap_outer(): return lax.ppermute(message, 'row', pairs + [(j, i) for i, j in pairs])]
    pallas_call x11 -> x10, Pallas kernels: 28.1 us -> 27.8 us  [run(): pl.pallas_call(kernel, out_shape=outs, in_specs=specs, scratch_shapes=lis...]
  transfers between devices with their start and end apart: 18 -> 18, of which waited for: 11 -> 11; matrix products, arithmetic and copies ran while one was open for 0% -> 0% of each run, Pallas kernels for 17% -> 18%
where the time goes in v14:
time: 79 us; the launch traced here: 78.7 us
  Pallas kernels  28.5 us (36%)
  starting transfers between devices  27.2 us (34%)
  waiting for transfers between devices  18.6 us (24%)
  local copies, waits for them, and re-layouts  3.31 us (4%)
  between operations  1 us (1%)
    pallas_call x10, Pallas kernels, run(): pl.pallas_call(kernel, out_shape=outs, in_specs=specs, scratch_shapes=lis...  27.8 us
    ppermute x4, waiting for transfers between devices, swap_outer(): return lax.ppermute(message, 'row', pairs + [(j, i) for i, j in pairs])  12.6 us
    ppermute x4, starting transfers between devices, swap_outer(): return lax.ppermute(message, 'row', pairs + [(j, i) for i, j in pairs])  11.6 us
    ppermute x8, starting transfers between devices, swap_inner(): return lax.ppermute(message, 'row', [(i, i ^ 1) for i in range(count)])  8.68 us
    ppermute x6, starting transfers between devices, sum_over_rows(): mine[stream] = mine[stream] + lax.ppermute(mine[stream], 'row', pairs)  6.97 us
    ppermute x6, waiting for transfers between devices, sum_over_rows(): mine[stream] = mine[stream] + lax.ppermute(mine[stream], 'row', pairs)  4.22 us
    unnamed x12, local copies, waits for them, and re-layouts  3.31 us
    ppermute x8, waiting for transfers between devices, swap_inner(): return lax.ppermute(message, 'row', [(i, i ^ 1) for i in range(count)])  1.73 us
  transfers between devices with their start and end apart: 18, of which 11 were waited for; matrix products, arithmetic and copies ran while one was open for 0% of the time, Pallas kernels for 18%

profile of v14, /device:TPU:9, one launch (start us, length us, event | category | flops | bytes accessed | tf_op | source)
XLA Modules:
  0.0 78.7 jit_solution(12928947692767879020)
XLA Ops:
  0.6 1.8 %shard_map.68 = f32[784,128]{1,0:T(8,128)} custom-call(s32[1]{0:T(128)} %bitcast.core_ref, f32[4,2,384,128]{3,2,1,0:T(8,128)} %z_ref.5), custom_call_target="tpu_custom_call" | custom-call | bytes 1000000 | tf_op jit(solution)/shard_map/pallas_call | solution.py:21
  2.4 3.7 %collective-permute-start.1 = (f32[784,128]{1,0:T(8,128)}, f32[784,128]{1,0:T(8,128)S(1)}, u32[]{:S(2)}, u32[]{:S(2)}) collective-permute-start(f32[784,128]{1,0:T(8,128)} %shard_map.68), channel_id=1, source_target_pairs={{1,2},{3,4},{5,6},{7,8},{9,10},{11,12},{13,14},{2,1},{4,3},{6,5},{... | collective-permute-start | bytes 1204232 | tf_op jit(solution)/shard_map/ppermute | solution.py:515
  6.2 1.4 %copy-done = f32[4,2,384,128]{3,2,1,0:T(8,128)S(1)} copy-done((f32[4,2,384,128]{3,2,1,0:T(8,128)S(1)}, f32[4,2,384,128]{3,2,1,0:T(8,128)}, u32[]{:S(2)}) %copy-start) | copy-done | bytes 1572888
  7.6 1.6 %shard_map.69 = (f32[776,128]{1,0:T(8,128)S(1)}, f32[768,128]{1,0:T(8,128)S(1)}, f32[776,128]{1,0:T(8,128)S(1)}, f32[384,16]{1,0:T(8,128)S(1)}) custom-call(s32[1]{0:T(128)} %bitcast.core_ref, f32[6,2,384]{2,1,0:T(2,128)S(1)} %copy-done.4, f32[4,2,384,128]{3,2,1,0:T(8,128)S(1)} %copy-done), custom_call_target="tpu_custom_call" | custom-call | flops 1000000 | bytes 3000000 | tf_op jit(solution)/shard_map/pallas_call | solution.py:21
  9.7 3.1 %collective-permute-start = (f32[776,128]{1,0:T(8,128)S(1)}, f32[776,128]{1,0:T(8,128)S(1)}, u32[]{:S(2)}, u32[]{:S(2)}) collective-permute-start(f32[776,128]{1,0:T(8,128)S(1)} %get-tuple-element.49), channel_id=1, source_target_pairs={{1,2},{3,4},{5,6},{7,8},{9,10},{11,12},{13,14},{2,1},{4,3},{6,5},{... | collective-permute-start | bytes 1191944 | tf_op jit(solution)/shard_map/ppermute | solution.py:515
  12.8 1.9 %copy-done.2 = f32[4,2,384,256]{3,2,1,0:T(8,128)S(1)} copy-done((f32[4,2,384,256]{3,2,1,0:T(8,128)S(1)}, f32[4,2,384,256]{3,2,1,0:T(8,128)}, u32[]{:S(2)}) %copy-start.2) | copy-done | bytes 3145752
  14.7 1.8 %shard_map.70 = (f32[136,128]{1,0:T(8,128)S(1)}, bf16[3072,128]{1,0:T(8,128)(2,1)S(1)}, bf16[3072,128]{1,0:T(8,128)(2,1)S(1)}, bf16[3072,256]{1,0:T(8,128)(2,1)S...) custom-call(f32[3072,128]{1,0:T(8,128)S(1)} %bitcast.4, ...), custom_call_target="tpu_custom_call" | custom-call | flops 503316480 | bytes 9000000 | tf_op jit(solution)/shard_map/pallas_call | solution.py:21
  16.5 3.9 %collective-permute-done.1.outer1_ref = f32[784,128]{1,0:T(8,128)S(1)} collective-permute-done((f32[784,128]{1,0:T(8,128)}, f32[784,128]{1,0:T(8,128)S(1)}, u32[]{:S(2)}, u32[]{:S(2)}) %collective-permute-start.1) | collective-permute-done | bytes 401440 | tf_op jit(solution)/shard_map/ppermute | solution.py:515
  20.5 3.2 %shard_map.71 = (f32[2,384,128]{2,1,0:T(8,128)S(1)}, bf16[1536,128]{1,0:T(8,128)(2,1)S(1)}, bf16[1536,128]{1,0:T(8,128)(2,1)S(1)}, bf16[768,128]{1,0:T(8,128)(2,...) custom-call(s32[1]{0:T(128)} %bitcast.core_ref, ...), custom_call_target="tpu_custom_call" | custom-call | flops 805306368 | bytes 9000000 | tf_op jit(solution)/shard_map/pallas_call | solution.py:21
  23.7 1.0 %collective-permute-done.outer2_ref.fouter2_ref = f32[776,128]{1,0:T(8,128)S(1)} collective-permute-done((f32[776,128]{1,0:T(8,128)S(1)}, f32[776,128]{1,0:T(8,128)S(1)}, u32[]{:S(2)}, u32[]{:S(2)}) %collective-permute-start) | collective-permute-done | bytes 397344 | tf_op jit(solution)/shard_map/ppermute | solution.py:515
  24.7 1.0 %shard_map.72 = (f32[136,128]{1,0:T(8,128)S(1)}, f32[128,128]{1,0:T(8,128)S(1)}, f32[136,128]{1,0:T(8,128)S(1)}, f32[128,128]{1,0:T(8,128)S(1)}, bf16[768,128]{1...) custom-call(s32[1]{0:T(128)} %bitcast.core_ref, f32[384,16]{1,0:T(8,128)S(1)} %get-tuple-element.44.table_ref, ...), custom_call_target="tpu_custom_call" | custom-call | flops 301989888 | bytes 5000000 | tf_op jit(solution)/shard_map/pallas_call | solution.py:21
  26.3 0.7 collective-permute-done.4
  27.2 1.8 %collective-permute-start.9 = (f32[128,128]{1,0:T(8,128)S(1)}, f32[128,128]{1,0:T(8,128)S(1)}, u32[]{:S(2)}, u32[]{:S(2)}) collective-permute-start(f32[128,128]{1,0:T(8,128)S(1)} %add.28), channel_id=1, source_target_pairs={{0,4},{1,3},{2,6},{3,1},{4,0},{5,7},{6,2},{7,5},{8,12},{9,11},{10,... | collective-permute-start | bytes 196616 | tf_op jit(solution)/shard_map/ppermute | solution.py:526
  29.0 1.6 %collective-permute-done.5 = f32[136,128]{1,0:T(8,128)S(1)} collective-permute-done((f32[136,128]{1,0:T(8,128)S(1)}, f32[136,128]{1,0:T(8,128)S(1)}, u32[]{:S(2)}, u32[]{:S(2)}) %collective-permute-start.5) | collective-permute-done | bytes 69664 | tf_op jit(solution)/shard_map/ppermute | solution.py:526
  30.6 2.4 %collective-permute-start.6 = (f32[136,128]{1,0:T(8,128)S(1)}, f32[136,128]{1,0:T(8,128)S(1)}, u32[]{:S(2)}, u32[]{:S(2)}) collective-permute-start(f32[136,128]{1,0:T(8,128)S(1)} %add.25), channel_id=1, source_target_pairs={{0,4},{1,9},{2,6},{3,11},{4,0},{5,13},{6,2},{7,15},{8,12},{9,1},{1... | collective-permute-start | bytes 208904 | tf_op jit(solution)/shard_map/ppermute | solution.py:526
  33.2 1.6 %collective-permute-done.6 = f32[136,128]{1,0:T(8,128)S(1)} collective-permute-done((f32[136,128]{1,0:T(8,128)S(1)}, f32[136,128]{1,0:T(8,128)S(1)}, u32[]{:S(2)}, u32[]{:S(2)}) %collective-permute-start.6) | collective-permute-done | bytes 69664 | tf_op jit(solution)/shard_map/ppermute | solution.py:526
  34.9 1.1 %collective-permute-start.7 = (f32[136,128]{1,0:T(8,128)S(1)}, f32[136,128]{1,0:T(8,128)S(1)}, u32[]{:S(2)}, u32[]{:S(2)}) collective-permute-start(f32[136,128]{1,0:T(8,128)S(1)} %add.26), channel_id=1, source_target_pairs={{0,8},{1,3},{2,10},{3,1},{4,12},{5,7},{6,14},{7,5},{8,0},{9,11},{1... | collective-permute-start | bytes 208904 | tf_op jit(solution)/shard_map/ppermute | solution.py:526
  36.5 1.4 %collective-permute-start.11 = (f32[128,128]{1,0:T(8,128)S(1)}, f32[128,128]{1,0:T(8,128)S(1)}, u32[]{:S(2)}, u32[]{:S(2)}) collective-permute-start(f32[128,128]{1,0:T(8,128)S(1)} %add.30), channel_id=1, source_target_pairs={{0,2},{1,9},{2,0},{3,11},{4,6},{5,13},{6,4},{7,15},{8,10},{9,1},{1... | collective-permute-start | bytes 196616 | tf_op jit(solution)/shard_map/ppermute | solution.py:526
  38.4 4.1 %collective-permute-start.12 = (f32[136,128]{1,0:T(8,128)S(1)}, f32[136,128]{1,0:T(8,128)S(1)}, u32[]{:S(2)}, u32[]{:S(2)}) collective-permute-start(f32[136,128]{1,0:T(8,128)S(1)} %add.27.mine1_ref), channel_id=1, source_target_pairs={{0,1},{1,0},{2,3},{3,2},{4,5},{5,4},{6,7},{7,6},{8,9},{9,8},{10,11... | collective-permute-start | bytes 208904 | tf_op jit(solution)/shard_map/ppermute | solution.py:509
  42.6 2.0 %collective-permute-start.13 = (f32[128,128]{1,0:T(8,128)S(1)}, f32[128,128]{1,0:T(8,128)S(1)}, u32[]{:S(2)}, u32[]{:S(2)}) collective-permute-start(f32[128,128]{1,0:T(8,128)S(1)} %add.31.mine2_ref), channel_id=1, source_target_pairs={{0,1},{1,0},{2,3},{3,2},{4,5},{5,4},{6,7},{7,6},{8,9},{9,8},{10,11... | collective-permute-start | bytes 196616 | tf_op jit(solution)/shard_map/ppermute | solution.py:509
  44.6 0.9 %collective-permute-done.13.other2_ref = f32[128,128]{1,0:T(8,128)S(1)} collective-permute-done((f32[128,128]{1,0:T(8,128)S(1)}, f32[128,128]{1,0:T(8,128)S(1)}, u32[]{:S(2)}, u32[]{:S(2)}) %collective-permute-start.13) | collective-permute-done | bytes 65568 | tf_op jit(solution)/shard_map/ppermute | solution.py:509
  45.5 9.8 %shard_map.73 = (bf16[256,256]{1,0:T(8,128)(2,1)S(1)}, bf16[256,256]{1,0:T(8,128)(2,1)S(1)}, bf16[256,256]{1,0:T(8,128)(2,1)S(1)}, bf16[256,256]{1,0:T(8,128)(2,1)S(1)}) custom-call(s32[1]{0:T(128)} %bitcast.core_ref, f32[136,128]{1,0:T(8,128)S(1)} %add.27.mine1_ref, f32[128,128]{1,0:T(8,128)S(1)} %add.31.mine2_ref, ...), custom_call_target="tpu_custom_call" | custom-call | flops 1000000000 | bytes 1000000 | tf_op jit(solution)/shard_map/pallas_call | solution.py:21
  55.4 0.6 shard_map.74
  56.0 1.9 %collective-permute-start.14 = (f32[776,128]{1,0:T(8,128)S(1)}, f32[776,128]{1,0:T(8,128)S(1)}, u32[]{:S(2)}, u32[]{:S(2)}) collective-permute-start(f32[776,128]{1,0:T(8,128)S(1)} %get-tuple-element.71.outer1_ref.own1_ref), channel_id=1, source_target_pairs={{1,2},{3,4},{5,6},{7,8},{9,10},{11,12},{13,14},{2,1},{4,3},{6,5},{... | collective-permute-start | bytes 1191944 | tf_op jit(solution)/shard_map/ppermute | solution.py:515
  57.9 1.7 %shard_map.75 = (f32[2,384,128]{2,1,0:T(8,128)S(1)}, f32[2,2,384,128]{3,2,1,0:T(8,128)S(1)}, f32[768,128]{1,0:T(8,128)S(1)}, f32[768,128]{1,0:T(8,128)S(1)}, f32[768,128]{1,0:T(8,128)S(1)}) custom-call(s32[1]{0:T(128)} %bitcast.core_ref, f32[384,16]{1,0:T(8,128)S(1)} %get-tuple-element.44.table_ref, f32[2,384,128]{2,1,0:T(8,128)S(1)} %get-tuple-element.72.outer_ref, ...), custom_call_target="tpu_custom_call" | custom-call | flops 10000000000 | bytes 6000000 | tf_op jit(solution)/shard_map/pallas_call | solution.py:21
  59.6 1.3 %collective-permute-start.16 = (f32[768,128]{1,0:T(8,128)S(1)}, f32[768,128]{1,0:T(8,128)S(1)}, u32[]{:S(2)}, u32[]{:S(2)}) collective-permute-start(f32[768,128]{1,0:T(8,128)S(1)} %get-tuple-element.80), channel_id=1, source_target_pairs={{0,1},{1,0},{2,3},{3,2},{4,5},{5,4},{6,7},{7,6},{8,9},{9,8},{10,11... | collective-permute-start | bytes 1179656 | tf_op jit(solution)/shard_map/ppermute | solution.py:509
  61.0 2.8 %collective-permute-start.17 = (f32[768,128]{1,0:T(8,128)S(1)}, f32[768,128]{1,0:T(8,128)S(1)}, u32[]{:S(2)}, u32[]{:S(2)}) collective-permute-start(f32[768,128]{1,0:T(8,128)S(1)} %get-tuple-element.82), channel_id=1, source_target_pairs={{1,2},{3,4},{5,6},{7,8},{9,10},{11,12},{13,14},{2,1},{4,3},{6,5},{... | collective-permute-start | bytes 1179656 | tf_op jit(solution)/shard_map/ppermute | solution.py:515
  63.8 3.0 %shard_map.78 = f32[4,2,384,128]{3,2,1,0:T(8,128)} custom-call(s32[1]{0:T(128)} %bitcast.core_ref, bf16[3072,256]{1,0:T(8,128)(2,1)S(1)} %get-tuple-element.45.qh_ref, bf16[3072,256]{1,0:T(8,128)(2,1)S(1)} %get-tuple-element.46.ql_ref, bf16[3072,128]{1,0:T(8,128)(2,1)S(1)} %get-tuple-element.47.nh_ref, bf16[3072,128]{1,0:T(8,128)(2,1)S(1)} %get-tuple-element.48.nl_ref, ...), custom_call_target="tpu_custom_call" | custom-call | tf_op jit(solution)/shard_map/pallas_call | solution.py:21
  66.8 6.7 %collective-permute-done.14.outer1_ref = f32[776,128]{1,0:T(8,128)S(1)} collective-permute-done((f32[776,128]{1,0:T(8,128)S(1)}, f32[776,128]{1,0:T(8,128)S(1)}, u32[]{:S(2)}, u32[]{:S(2)}) %collective-permute-start.14) | collective-permute-done | bytes 397344 | tf_op jit(solution)/shard_map/ppermute | solution.py:515
  73.6 3.3 %shard_map.76 = (f32[4,2,384,128]{3,2,1,0:T(8,128)}, f32[2,384,128]{2,1,0:T(8,128)S(1)}) custom-call(s32[1]{0:T(128)} %bitcast.core_ref, f32[776,128]{1,0:T(8,128)S(1)} %collective-permute-done.14.outer1_ref, f32[384,16]{1,0:T(8,128)S(1)} %get-tuple-element.44.table_ref, f32[2,384,128]{2,1,0:T(8,128)S(1)} %get-tuple-element.72.outer_ref, ...), custom_call_target="tpu_custom_call" | custom-call | flops 10000000 | bytes 6000000 | tf_op jit(solution)/shard_map/pallas_call | solution.py:21
  76.8 0.9 %collective-permute-done.17.outer2_ref = f32[768,128]{1,0:T(8,128)S(1)} collective-permute-done((f32[768,128]{1,0:T(8,128)S(1)}, f32[768,128]{1,0:T(8,128)S(1)}, u32[]{:S(2)}, u32[]{:S(2)}) %collective-permute-start.17) | collective-permute-done | bytes 393248 | tf_op jit(solution)/shard_map/ppermute | solution.py:515
  77.8 0.8 shard_map.77
  (35 shorter events, 2.7 us)
Async XLA Ops:
  0.6 5.5 %copy-start.4 = (f32[6,2,384]{2,1,0:T(2,128)S(1)}, f32[6,2,384]{2,1,0:T(2,128)}, u32[]{:S(2)}) copy-start(f32[6,2,384]{2,1,0:T(2,128)} %coeff_ref.1) | copy-start | bytes 55300
  2.4 18.0 %collective-permute-start.1 = (f32[784,128]{1,0:T(8,128)}, f32[784,128]{1,0:T(8,128)S(1)}, u32[]{:S(2)}, u32[]{:S(2)}) collective-permute-start(f32[784,128]{1,0:T(8,128)} %shard_map.68), channel_id=1, source_target_pairs={{1,2},{3,4},{5,6},{7,8},{9,10},{11,12},{13,14},{2,1},{4,3},{6,5},{... | collective-permute-start | bytes 1204232 | tf_op jit(solution)/shard_map/ppermute | solution.py:515
  6.2 1.4 %copy-start = (f32[4,2,384,128]{3,2,1,0:T(8,128)S(1)}, f32[4,2,384,128]{3,2,1,0:T(8,128)}, u32[]{:S(2)}) copy-start(f32[4,2,384,128]{3,2,1,0:T(8,128)} %z_ref.5) | copy-start | bytes 4718596
  7.6 5.2 %copy-start.3 = (f32[4,2,384,128]{3,2,1,0:T(8,128)S(1)}, f32[4,2,384,128]{3,2,1,0:T(8,128)}, u32[]{:S(2)}) copy-start(f32[4,2,384,128]{3,2,1,0:T(8,128)} %param.7) | copy-start | bytes 4718596
  9.1 7.4 %collective-permute-start.3 = (f32[776,128]{1,0:T(8,128)S(1)}, f32[776,128]{1,0:T(8,128)S(1)}, u32[]{:S(2)}, u32[]{:S(2)}) collective-permute-start(f32[776,128]{1,0:T(8,128)S(1)} %get-tuple-element.52), channel_id=1, source_target_pairs={{0,1},{1,0},{2,3},{3,2},{4,5},{5,4},{6,7},{7,6},{8,9},{9,8},{10,11... | collective-permute-start | bytes 1191944 | tf_op jit(solution)/shard_map/ppermute | solution.py:509
  9.2 7.3 %collective-permute-start.2 = (f32[768,128]{1,0:T(8,128)S(1)}, f32[768,128]{1,0:T(8,128)S(1)}, u32[]{:S(2)}, u32[]{:S(2)}) collective-permute-start(f32[768,128]{1,0:T(8,128)S(1)} %get-tuple-element.51), channel_id=1, source_target_pairs={{0,1},{1,0},{2,3},{3,2},{4,5},{5,4},{6,7},{7,6},{8,9},{9,8},{10,11... | collective-permute-start | bytes 1179656 | tf_op jit(solution)/shard_map/ppermute | solution.py:509
  9.7 15.0 %collective-permute-start = (f32[776,128]{1,0:T(8,128)S(1)}, f32[776,128]{1,0:T(8,128)S(1)}, u32[]{:S(2)}, u32[]{:S(2)}) collective-permute-start(f32[776,128]{1,0:T(8,128)S(1)} %get-tuple-element.49), channel_id=1, source_target_pairs={{1,2},{3,4},{5,6},{7,8},{9,10},{11,12},{13,14},{2,1},{4,3},{6,5},{... | collective-permute-start | bytes 1191944 | tf_op jit(solution)/shard_map/ppermute | solution.py:515
  12.8 1.9 %copy-start.2 = (f32[4,2,384,256]{3,2,1,0:T(8,128)S(1)}, f32[4,2,384,256]{3,2,1,0:T(8,128)}, u32[]{:S(2)}) copy-start(f32[4,2,384,256]{3,2,1,0:T(8,128)} %param.8) | copy-start | bytes 9437188
  14.7 5.7 %copy-start.1 = (f32[4,2,384,128]{3,2,1,0:T(8,128)S(1)}, f32[4,2,384,128]{3,2,1,0:T(8,128)}, u32[]{:S(2)}) copy-start(f32[4,2,384,128]{3,2,1,0:T(8,128)} %z_ref.5) | copy-start | bytes 4718596
  25.7 19.8 %copy-start.5 = (f32[256,256]{1,0:T(8,128)S(1)}, f32[256,256]{1,0:T(8,128)}, u32[]{:S(2)}) copy-start(f32[256,256]{1,0:T(8,128)} %r_bar_ref.1) | copy-start | bytes 786436
  25.7 1.3 %collective-permute-start.4 = (f32[136,128]{1,0:T(8,128)S(1)}, f32[136,128]{1,0:T(8,128)S(1)}, u32[]{:S(2)}, u32[]{:S(2)}) collective-permute-start(f32[136,128]{1,0:T(8,128)S(1)} %get-tuple-element.64), channel_id=1, source_target_pairs={{0,1},{1,0},{2,3},{3,2},{4,5},{5,4},{6,7},{7,6},{8,9},{9,8},{10,11... | collective-permute-start | bytes 208904 | tf_op jit(solution)/shard_map/ppermute | solution.py:509
  25.8 1.4 %collective-permute-start.8 = (f32[128,128]{1,0:T(8,128)S(1)}, f32[128,128]{1,0:T(8,128)S(1)}, u32[]{:S(2)}, u32[]{:S(2)}) collective-permute-start(f32[128,128]{1,0:T(8,128)S(1)} %get-tuple-element.66), channel_id=1, source_target_pairs={{0,1},{1,0},{2,3},{3,2},{4,5},{5,4},{6,7},{7,6},{8,9},{9,8},{10,11... | collective-permute-start | bytes 196616 | tf_op jit(solution)/shard_map/ppermute | solution.py:509
  27.1 3.5 %collective-permute-start.5 = (f32[136,128]{1,0:T(8,128)S(1)}, f32[136,128]{1,0:T(8,128)S(1)}, u32[]{:S(2)}, u32[]{:S(2)}) collective-permute-start(f32[136,128]{1,0:T(8,128)S(1)} %add.24), channel_id=1, source_target_pairs={{0,2},{1,5},{2,0},{3,7},{4,6},{5,1},{6,4},{7,3},{8,10},{9,13},{10,... | collective-permute-start | bytes 208904 | tf_op jit(solution)/shard_map/ppermute | solution.py:526
  27.2 5.8 %collective-permute-start.9 = (f32[128,128]{1,0:T(8,128)S(1)}, f32[128,128]{1,0:T(8,128)S(1)}, u32[]{:S(2)}, u32[]{:S(2)}) collective-permute-start(f32[128,128]{1,0:T(8,128)S(1)} %add.28), channel_id=1, source_target_pairs={{0,4},{1,3},{2,6},{3,1},{4,0},{5,7},{6,2},{7,5},{8,12},{9,11},{10,... | collective-permute-start | bytes 196616 | tf_op jit(solution)/shard_map/ppermute | solution.py:526
  30.6 4.3 %collective-permute-start.6 = (f32[136,128]{1,0:T(8,128)S(1)}, f32[136,128]{1,0:T(8,128)S(1)}, u32[]{:S(2)}, u32[]{:S(2)}) collective-permute-start(f32[136,128]{1,0:T(8,128)S(1)} %add.25), channel_id=1, source_target_pairs={{0,4},{1,9},{2,6},{3,11},{4,0},{5,13},{6,2},{7,15},{8,12},{9,1},{1... | collective-permute-start | bytes 208904 | tf_op jit(solution)/shard_map/ppermute | solution.py:526
  33.0 3.5 %collective-permute-start.10 = (f32[128,128]{1,0:T(8,128)S(1)}, f32[128,128]{1,0:T(8,128)S(1)}, u32[]{:S(2)}, u32[]{:S(2)}) collective-permute-start(f32[128,128]{1,0:T(8,128)S(1)} %add.29), channel_id=1, source_target_pairs={{0,8},{1,5},{2,10},{3,7},{4,12},{5,1},{6,14},{7,3},{8,0},{9,13},{1... | collective-permute-start | bytes 196616 | tf_op jit(solution)/shard_map/ppermute | solution.py:526
  34.9 3.5 %collective-permute-start.7 = (f32[136,128]{1,0:T(8,128)S(1)}, f32[136,128]{1,0:T(8,128)S(1)}, u32[]{:S(2)}, u32[]{:S(2)}) collective-permute-start(f32[136,128]{1,0:T(8,128)S(1)} %add.26), channel_id=1, source_target_pairs={{0,8},{1,3},{2,10},{3,1},{4,12},{5,7},{6,14},{7,5},{8,0},{9,11},{1... | collective-permute-start | bytes 208904 | tf_op jit(solution)/shard_map/ppermute | solution.py:526
  36.5 6.1 %collective-permute-start.11 = (f32[128,128]{1,0:T(8,128)S(1)}, f32[128,128]{1,0:T(8,128)S(1)}, u32[]{:S(2)}, u32[]{:S(2)}) collective-permute-start(f32[128,128]{1,0:T(8,128)S(1)} %add.30), channel_id=1, source_target_pairs={{0,2},{1,9},{2,0},{3,11},{4,6},{5,13},{6,4},{7,15},{8,10},{9,1},{1... | collective-permute-start | bytes 196616 | tf_op jit(solution)/shard_map/ppermute | solution.py:526
  38.4 7.1 %collective-permute-start.12 = (f32[136,128]{1,0:T(8,128)S(1)}, f32[136,128]{1,0:T(8,128)S(1)}, u32[]{:S(2)}, u32[]{:S(2)}) collective-permute-start(f32[136,128]{1,0:T(8,128)S(1)} %add.27.mine1_ref), channel_id=1, source_target_pairs={{0,1},{1,0},{2,3},{3,2},{4,5},{5,4},{6,7},{7,6},{8,9},{9,8},{10,11... | collective-permute-start | bytes 208904 | tf_op jit(solution)/shard_map/ppermute | solution.py:509
  42.6 2.9 %collective-permute-start.13 = (f32[128,128]{1,0:T(8,128)S(1)}, f32[128,128]{1,0:T(8,128)S(1)}, u32[]{:S(2)}, u32[]{:S(2)}) collective-permute-start(f32[128,128]{1,0:T(8,128)S(1)} %add.31.mine2_ref), channel_id=1, source_target_pairs={{0,1},{1,0},{2,3},{3,2},{4,5},{5,4},{6,7},{7,6},{8,9},{9,8},{10,11... | collective-permute-start | bytes 196616 | tf_op jit(solution)/shard_map/ppermute | solution.py:509
  56.0 17.6 %collective-permute-start.14 = (f32[776,128]{1,0:T(8,128)S(1)}, f32[776,128]{1,0:T(8,128)S(1)}, u32[]{:S(2)}, u32[]{:S(2)}) collective-permute-start(f32[776,128]{1,0:T(8,128)S(1)} %get-tuple-element.71.outer1_ref.own1_ref), channel_id=1, source_target_pairs={{1,2},{3,4},{5,6},{7,8},{9,10},{11,12},{13,14},{2,1},{4,3},{6,5},{... | collective-permute-start | bytes 1191944 | tf_op jit(solution)/shard_map/ppermute | solution.py:515
  59.6 7.2 %collective-permute-start.16 = (f32[768,128]{1,0:T(8,128)S(1)}, f32[768,128]{1,0:T(8,128)S(1)}, u32[]{:S(2)}, u32[]{:S(2)}) collective-permute-start(f32[768,128]{1,0:T(8,128)S(1)} %get-tuple-element.80), channel_id=1, source_target_pairs={{0,1},{1,0},{2,3},{3,2},{4,5},{5,4},{6,7},{7,6},{8,9},{9,8},{10,11... | collective-permute-start | bytes 1179656 | tf_op jit(solution)/shard_map/ppermute | solution.py:509
  60.9 5.9 %collective-permute-start.15 = (f32[768,128]{1,0:T(8,128)S(1)}, f32[768,128]{1,0:T(8,128)S(1)}, u32[]{:S(2)}, u32[]{:S(2)}) collective-permute-start(f32[768,128]{1,0:T(8,128)S(1)} %get-tuple-element.79.own2_ref), channel_id=1, source_target_pairs={{0,1},{1,0},{2,3},{3,2},{4,5},{5,4},{6,7},{7,6},{8,9},{9,8},{10,11... | collective-permute-start | bytes 1179656 | tf_op jit(solution)/shard_map/ppermute | solution.py:509
  61.0 16.8 %collective-permute-start.17 = (f32[768,128]{1,0:T(8,128)S(1)}, f32[768,128]{1,0:T(8,128)S(1)}, u32[]{:S(2)}, u32[]{:S(2)}) collective-permute-start(f32[768,128]{1,0:T(8,128)S(1)} %get-tuple-element.82), channel_id=1, source_target_pairs={{1,2},{3,4},{5,6},{7,8},{9,10},{11,12},{13,14},{2,1},{4,3},{6,5},{... | collective-permute-start | bytes 1179656 | tf_op jit(solution)/shard_map/ppermute | solution.py:515

commit v15 on v14

--- a/solution.py
+++ b/solution.py
@@ -84,18 +84,6 @@
 def backward_heavy(c, pa, xb, pb):
     d, w, g, l, m, j = c
     return -2.0 * g * pa - w * pb, w * xb - 0.5 * m * pb
-
-
-def forward_sources(core_ref, z_hbm, outer1_ref, sems):
-    n = z_hbm.shape[2]
-    copies = [
-        pltpu.make_async_copy(z_hbm.at[k, core_ref[0]], outer1_ref.at[pl.ds(k * n, n)], sems.at[k]) for k in range(2)
-    ]
-    for copy in copies:
-        copy.start()
-    outer1_ref[2 * n :] = jnp.zeros((16, z_hbm.shape[3]), f32)
-    for copy in copies:
-        copy.wait()
 
 
 def forward_rim(core_ref, coeff_ref, z_ref, outer2_ref, inner1_ref, inner2_ref, table_ref):
@@ -318,8 +306,9 @@
 
 
 def factor(
-    core_ref, mine1_ref, mine2_ref, other1_ref, other2_ref, r_bar_ref, nh_ref, nl_ref, sh_ref, sl_ref, sums_ref, w_ref, inv1_ref, inv2_ref
+    core_ref, mine1_ref, mine2_ref, other1_ref, other2_ref, r_bar_ref, *refs
 ):
+    *gradient_refs, nh_ref, nl_ref, sh_ref, sl_ref, grad_ref, outer1_ref, sums_ref, w_ref, inv1_ref, inv2_ref = refs
     tile = 128
     core = core_ref[0]
     for part, value in zip(quarters(core), (mine1_ref, mine2_ref, other1_ref, other2_ref)):
@@ -379,6 +368,7 @@
     spread = stacked2(parts, split2(stacked2(split2(symmetric), parts, plain)), down)
     nh_ref[...], nl_ref[...] = parts
     sh_ref[...], sl_ref[...] = split2(spread)
+    gradient_outer(core_ref, *gradient_refs, nh_ref, nl_ref, sh_ref, sl_ref, grad_ref, outer1_ref)
 
 
 def columns(qh, ql, nh, nl, xh, xl, ih, il, sh, sl):
@@ -538,9 +528,8 @@
     hops = shape((2 * n, rank), f32)
     rim = shape((2 * n + 8, rank), f32)
     table = shape((n, 16), f32)
-    outer1 = call(
-        forward_sources, shape((2 * n + 16, rank), f32), 0, 10**6, [pltpu.SemaphoreType.DMA((2,))], scalar=True, far=True
-    )(core, z_factor)
+    outer1 = lax.dynamic_index_in_dim(z_factor[0:2], core[0], axis=1, keepdims=False).reshape(2 * n, rank)
+    outer1 = jnp.pad(outer1, ((0, 16), (0, 0)))
     outer1, behind = lax.optimization_barrier((outer1, core))
     outer2, inner1, inner2, table = call(
         forward_rim, (rim, hops, rim, table), 10**6, 3 * 10**6, scalar=True
@@ -568,8 +557,9 @@
     )(core, table, z_factor, outer2, light, gram, rest, pack, *transposed)
     parts = sum_over_rows(parts[:2], parts[2:])
     square = shape((256, 256), bf16)
-    weights = call(
-        factor, (square,) * 4, 10**9, 10**6,
+    left = (qh, ql, nh, nl)
+    *weights, w_outer, own1 = call(
+        factor, (square,) * 4 + (single, rim), 10**9, 10**6,
         [
             pltpu.VMEM((528, 128), f32),
             pltpu.VMEM((128, 128), f32),
@@ -577,11 +567,7 @@
             pltpu.VMEM((128, 128), f32),
         ],
         scalar=True,
-    )(core, *parts, r_bar)
-    left = (qh, ql, nh, nl)
-    w_outer, own1 = call(gradient_outer, (single, rim), work * 3, 3 * 10**6, scalar=True)(
-        core, table, *left, oh, ol, *weights
-    )
+    )(core, *parts, r_bar, table, *left, oh, ol)
     back1 = swap_outer(own1)
     w_inner, w_heavy, last, own2, own3 = call(
         gradient_rest, (single, pair, hops, hops, hops), 10**10, 6 * 10**6, scalar=True

time: 79 us -> 78.2 us (0.990)
  Pallas kernels: 28.5 us -> 26.4 us
  waiting for transfers between devices: 18.6 us -> 20 us
    pallas_call x10 -> x8, Pallas kernels: 27.8 us -> 25.6 us  [run(): pl.pallas_call(kernel, out_shape=outs, in_specs=specs, scratch_shapes=lis...]
    ppermute x4, waiting for transfers between devices: 12.6 us -> 14.1 us  [swap_outer(): return lax.ppermute(message, 'row', pairs + [(j, i) for i, j in pairs])]
    unnamed x12 -> x10, local copies, waits for them, and re-layouts: 3.31 us -> 1.9 us
    slice x0 -> x2, local copies, waits for them, and re-layouts: none -> 1.1 us  [on_device(): z_factor[0:2]]
where the time goes in v15:
time: 78.2 us; the launch traced here: 77.9 us
  starting transfers between devices  27.3 us (35%)
  Pallas kernels  26.4 us (34%)
  waiting for transfers between devices  20 us (26%)
  local copies, waits for them, and re-layouts  3.06 us (4%)
  between operations  1.02 us (1%)
    pallas_call x8, Pallas kernels, run(): pl.pallas_call(kernel, out_shape=outs, in_specs=specs, scratch_shapes=lis...  25.6 us
    ppermute x4, waiting for transfers between devices, swap_outer(): return lax.ppermute(message, 'row', pairs + [(j, i) for i, j in pairs])  14.1 us
    ppermute x4, starting transfers between devices, swap_outer(): return lax.ppermute(message, 'row', pairs + [(j, i) for i, j in pairs])  11.7 us
    ppermute x8, starting transfers between devices, swap_inner(): return lax.ppermute(message, 'row', [(i, i ^ 1) for i in range(count)])  8.67 us
    ppermute x6, starting transfers between devices, sum_over_rows(): mine[stream] = mine[stream] + lax.ppermute(mine[stream], 'row', pairs)  6.97 us
    ppermute x6, waiting for transfers between devices, sum_over_rows(): mine[stream] = mine[stream] + lax.ppermute(mine[stream], 'row', pairs)  4.22 us
    unnamed x10, local copies, waits for them, and re-layouts  1.9 us
    ppermute x8, waiting for transfers between devices, swap_inner(): return lax.ppermute(message, 'row', [(i, i ^ 1) for i in range(count)])  1.73 us
  transfers between devices with their start and end apart: 18, of which 11 were waited for; matrix products, arithmetic and copies ran while one was open for 0% of the time, Pallas kernels for 18%

profile of v15, /device:TPU:9, one launch (start us, length us, event | category | flops | bytes accessed | tf_op | source)
XLA Modules:
  0.0 77.9 jit_solution(11108742409076323839)
XLA Ops:
  0.7 1.1 %slice-done = f32[2,2,384,128]{3,2,1,0:T(8,128)S(1)} async-done(((f32[4,2,384,128]{3,2,1,0:T(8,128)}), f32[2,2,384,128]{3,2,1,0:T(8,128)S(1)}, s32[]{:S(2)}) %slice-start) | async-done | bytes 786456 | tf_op jit(solution)/shard_map/slice | solution.py:531
  1.8 3.8 %collective-permute-start.1 = (f32[784,128]{1,0:T(8,128)S(1)}, f32[784,128]{1,0:T(8,128)S(1)}, u32[]{:S(2)}, u32[]{:S(2)}) collective-permute-start(f32[784,128]{1,0:T(8,128)S(1)} %pad.4), channel_id=1, source_target_pairs={{1,2},{3,4},{5,6},{7,8},{9,10},{11,12},{13,14},{2,1},{4,3},{6,5},{... | collective-permute-start | bytes 1204232 | tf_op jit(solution)/shard_map/ppermute | solution.py:505
  5.7 1.5 %shard_map.68 = (f32[776,128]{1,0:T(8,128)S(1)}, f32[768,128]{1,0:T(8,128)S(1)}, f32[776,128]{1,0:T(8,128)S(1)}, f32[384,16]{1,0:T(8,128)S(1)}) custom-call(s32[1]{0:T(128)} %bitcast.core_ref, f32[6,2,384]{2,1,0:T(2,128)S(1)} %copy-done.4, f32[4,2,384,128]{3,2,1,0:T(8,128)S(1)} %copy-done), custom_call_target="tpu_custom_call" | custom-call | flops 1000000 | bytes 3000000 | tf_op jit(solution)/shard_map/pallas_call | solution.py:21
  7.8 3.1 %collective-permute-start = (f32[776,128]{1,0:T(8,128)S(1)}, f32[776,128]{1,0:T(8,128)S(1)}, u32[]{:S(2)}, u32[]{:S(2)}) collective-permute-start(f32[776,128]{1,0:T(8,128)S(1)} %get-tuple-element.45), channel_id=1, source_target_pairs={{1,2},{3,4},{5,6},{7,8},{9,10},{11,12},{13,14},{2,1},{4,3},{6,5},{... | collective-permute-start | bytes 1191944 | tf_op jit(solution)/shard_map/ppermute | solution.py:505
  10.9 1.9 %copy-done.1 = f32[4,2,384,256]{3,2,1,0:T(8,128)S(1)} copy-done((f32[4,2,384,256]{3,2,1,0:T(8,128)S(1)}, f32[4,2,384,256]{3,2,1,0:T(8,128)}, u32[]{:S(2)}) %copy-start.1) | copy-done | bytes 3145752
  12.8 1.8 %shard_map.69 = (f32[136,128]{1,0:T(8,128)S(1)}, bf16[3072,128]{1,0:T(8,128)(2,1)S(1)}, bf16[3072,128]{1,0:T(8,128)(2,1)S(1)}, bf16[3072,256]{1,0:T(8,128)(2,1)S...) custom-call(f32[3072,128]{1,0:T(8,128)S(1)} %bitcast.5, ...), custom_call_target="tpu_custom_call" | custom-call | flops 503316480 | bytes 9000000 | tf_op jit(solution)/shard_map/pallas_call | solution.py:21
  14.6 5.2 %collective-permute-done.1.outer1_ref = f32[784,128]{1,0:T(8,128)S(1)} collective-permute-done((f32[784,128]{1,0:T(8,128)S(1)}, f32[784,128]{1,0:T(8,128)S(1)}, u32[]{:S(2)}, u32[]{:S(2)}) %collective-permute-start.1) | collective-permute-done | bytes 401440 | tf_op jit(solution)/shard_map/ppermute | solution.py:505
  19.8 3.1 %shard_map.70 = (f32[2,384,128]{2,1,0:T(8,128)S(1)}, bf16[1536,128]{1,0:T(8,128)(2,1)S(1)}, bf16[1536,128]{1,0:T(8,128)(2,1)S(1)}, bf16[768,128]{1,0:T(8,128)(2,...) custom-call(s32[1]{0:T(128)} %bitcast.core_ref, ...), custom_call_target="tpu_custom_call" | custom-call | flops 805306368 | bytes 9000000 | tf_op jit(solution)/shard_map/pallas_call | solution.py:21
  22.8 1.2 %collective-permute-done.outer2_ref.fouter2_ref = f32[776,128]{1,0:T(8,128)S(1)} collective-permute-done((f32[776,128]{1,0:T(8,128)S(1)}, f32[776,128]{1,0:T(8,128)S(1)}, u32[]{:S(2)}, u32[]{:S(2)}) %collective-permute-start) | collective-permute-done | bytes 397344 | tf_op jit(solution)/shard_map/ppermute | solution.py:505
  24.0 1.0 %shard_map.71 = (f32[136,128]{1,0:T(8,128)S(1)}, f32[128,128]{1,0:T(8,128)S(1)}, f32[136,128]{1,0:T(8,128)S(1)}, f32[128,128]{1,0:T(8,128)S(1)}, bf16[768,128]{1...) custom-call(s32[1]{0:T(128)} %bitcast.core_ref, f32[384,16]{1,0:T(8,128)S(1)} %get-tuple-element.44.table_ref.refs_0_, ...), custom_call_target="tpu_custom_call" | custom-call | flops 301989888 | bytes 5000000 | tf_op jit(solution)/shard_map/pallas_call | solution.py:21
  25.1 0.5 collective-permute-start.8
  25.6 0.7 collective-permute-done.4
  26.5 1.7 %collective-permute-start.9 = (f32[128,128]{1,0:T(8,128)S(1)}, f32[128,128]{1,0:T(8,128)S(1)}, u32[]{:S(2)}, u32[]{:S(2)}) collective-permute-start(f32[128,128]{1,0:T(8,128)S(1)} %add.35), channel_id=1, source_target_pairs={{0,4},{1,3},{2,6},{3,1},{4,0},{5,7},{6,2},{7,5},{8,12},{9,11},{10,... | collective-permute-start | bytes 196616 | tf_op jit(solution)/shard_map/ppermute | solution.py:516
  28.3 1.6 %collective-permute-done.5 = f32[136,128]{1,0:T(8,128)S(1)} collective-permute-done((f32[136,128]{1,0:T(8,128)S(1)}, f32[136,128]{1,0:T(8,128)S(1)}, u32[]{:S(2)}, u32[]{:S(2)}) %collective-permute-start.5) | collective-permute-done | bytes 69664 | tf_op jit(solution)/shard_map/ppermute | solution.py:516
  29.9 2.4 %collective-permute-start.6 = (f32[136,128]{1,0:T(8,128)S(1)}, f32[136,128]{1,0:T(8,128)S(1)}, u32[]{:S(2)}, u32[]{:S(2)}) collective-permute-start(f32[136,128]{1,0:T(8,128)S(1)} %add.32), channel_id=1, source_target_pairs={{0,4},{1,9},{2,6},{3,11},{4,0},{5,13},{6,2},{7,15},{8,12},{9,1},{1... | collective-permute-start | bytes 208904 | tf_op jit(solution)/shard_map/ppermute | solution.py:516
  32.5 1.6 %collective-permute-done.6 = f32[136,128]{1,0:T(8,128)S(1)} collective-permute-done((f32[136,128]{1,0:T(8,128)S(1)}, f32[136,128]{1,0:T(8,128)S(1)}, u32[]{:S(2)}, u32[]{:S(2)}) %collective-permute-start.6) | collective-permute-done | bytes 69664 | tf_op jit(solution)/shard_map/ppermute | solution.py:516
  34.2 1.1 %collective-permute-start.7 = (f32[136,128]{1,0:T(8,128)S(1)}, f32[136,128]{1,0:T(8,128)S(1)}, u32[]{:S(2)}, u32[]{:S(2)}) collective-permute-start(f32[136,128]{1,0:T(8,128)S(1)} %add.33), channel_id=1, source_target_pairs={{0,8},{1,3},{2,10},{3,1},{4,12},{5,7},{6,14},{7,5},{8,0},{9,11},{1... | collective-permute-start | bytes 208904 | tf_op jit(solution)/shard_map/ppermute | solution.py:516
  35.8 1.4 %collective-permute-start.11 = (f32[128,128]{1,0:T(8,128)S(1)}, f32[128,128]{1,0:T(8,128)S(1)}, u32[]{:S(2)}, u32[]{:S(2)}) collective-permute-start(f32[128,128]{1,0:T(8,128)S(1)} %add.37), channel_id=1, source_target_pairs={{0,2},{1,9},{2,0},{3,11},{4,6},{5,13},{6,4},{7,15},{8,10},{9,1},{1... | collective-permute-start | bytes 196616 | tf_op jit(solution)/shard_map/ppermute | solution.py:516
  37.2 0.5 collective-permute-done.7
  37.7 4.1 %collective-permute-start.12 = (f32[136,128]{1,0:T(8,128)S(1)}, f32[136,128]{1,0:T(8,128)S(1)}, u32[]{:S(2)}, u32[]{:S(2)}) collective-permute-start(f32[136,128]{1,0:T(8,128)S(1)} %add.34.mine1_ref), channel_id=1, source_target_pairs={{0,1},{1,0},{2,3},{3,2},{4,5},{5,4},{6,7},{7,6},{8,9},{9,8},{10,11... | collective-permute-start | bytes 208904 | tf_op jit(solution)/shard_map/ppermute | solution.py:499
  41.9 2.0 %collective-permute-start.13 = (f32[128,128]{1,0:T(8,128)S(1)}, f32[128,128]{1,0:T(8,128)S(1)}, u32[]{:S(2)}, u32[]{:S(2)}) collective-permute-start(f32[128,128]{1,0:T(8,128)S(1)} %add.38.mine2_ref), channel_id=1, source_target_pairs={{0,1},{1,0},{2,3},{3,2},{4,5},{5,4},{6,7},{7,6},{8,9},{9,8},{10,11... | collective-permute-start | bytes 196616 | tf_op jit(solution)/shard_map/ppermute | solution.py:499
  43.9 0.9 %collective-permute-done.13.other2_ref = f32[128,128]{1,0:T(8,128)S(1)} collective-permute-done((f32[128,128]{1,0:T(8,128)S(1)}, f32[128,128]{1,0:T(8,128)S(1)}, u32[]{:S(2)}, u32[]{:S(2)}) %collective-permute-start.13) | collective-permute-done | bytes 65568 | tf_op jit(solution)/shard_map/ppermute | solution.py:499
  44.8 10.3 %shard_map.72 = (bf16[256,256]{1,0:T(8,128)(2,1)S(1)}, bf16[256,256]{1,0:T(8,128)(2,1)S(1)}, bf16[256,256]{1,0:T(8,128)(2,1)S(1)}, bf16[256,256]{1,0:T(8,128)(2,...) custom-call(s32[1]{0:T(128)} %bitcast.core_ref, f32[136,128]{1,0:T(8,128)S(1)} %add.34.mine1_ref, ...), custom_call_target="tpu_custom_call" | custom-call | flops 1000000000 | bytes 1000000 | tf_op jit(solution)/shard_map/pallas_call | solution.py:21
  55.1 1.9 %collective-permute-start.14 = (f32[776,128]{1,0:T(8,128)S(1)}, f32[776,128]{1,0:T(8,128)S(1)}, u32[]{:S(2)}, u32[]{:S(2)}) collective-permute-start(f32[776,128]{1,0:T(8,128)S(1)} %get-tuple-element.67.outer1_ref.own1_ref), channel_id=1, source_target_pairs={{1,2},{3,4},{5,6},{7,8},{9,10},{11,12},{13,14},{2,1},{4,3},{6,5},{... | collective-permute-start | bytes 1191944 | tf_op jit(solution)/shard_map/ppermute | solution.py:505
  57.1 1.7 %shard_map.73 = (f32[2,384,128]{2,1,0:T(8,128)S(1)}, f32[2,2,384,128]{3,2,1,0:T(8,128)S(1)}, f32[768,128]{1,0:T(8,128)S(1)}, f32[768,128]{1,0:T(8,128)S(1)}, f32[768,128]{1,0:T(8,128)S(1)}) custom-call(s32[1]{0:T(128)} %bitcast.core_ref, f32[384,16]{1,0:T(8,128)S(1)} %get-tuple-element.44.table_ref.refs_0_, f32[2,384,128]{2,1,0:T(8,128)S(1)} %get-tuple-element.68.outer_ref, ...), custom_call_target="tpu_custom_call" | custom-call | flops 10000000000 | bytes 6000000 | tf_op jit(solution)/shard_map/pallas_call | solution.py:21
  58.8 1.3 %collective-permute-start.16 = (f32[768,128]{1,0:T(8,128)S(1)}, f32[768,128]{1,0:T(8,128)S(1)}, u32[]{:S(2)}, u32[]{:S(2)}) collective-permute-start(f32[768,128]{1,0:T(8,128)S(1)} %get-tuple-element.80), channel_id=1, source_target_pairs={{0,1},{1,0},{2,3},{3,2},{4,5},{5,4},{6,7},{7,6},{8,9},{9,8},{10,11... | collective-permute-start | bytes 1179656 | tf_op jit(solution)/shard_map/ppermute | solution.py:499
  60.2 2.8 %collective-permute-start.17 = (f32[768,128]{1,0:T(8,128)S(1)}, f32[768,128]{1,0:T(8,128)S(1)}, u32[]{:S(2)}, u32[]{:S(2)}) collective-permute-start(f32[768,128]{1,0:T(8,128)S(1)} %get-tuple-element.82), channel_id=1, source_target_pairs={{1,2},{3,4},{5,6},{7,8},{9,10},{11,12},{13,14},{2,1},{4,3},{6,5},{... | collective-permute-start | bytes 1179656 | tf_op jit(solution)/shard_map/ppermute | solution.py:505
  63.0 3.0 %shard_map.76 = f32[4,2,384,128]{3,2,1,0:T(8,128)} custom-call(s32[1]{0:T(128)} %bitcast.core_ref, bf16[3072,256]{1,0:T(8,128)(2,1)S(1)} %get-tuple-element.61.refs_1_.qh_ref, bf16[3072,256]{1,0:T(8,128)(2,1)S(1)} %get-tuple-element.62.refs_2_.ql_ref, bf16[3072,128]{1,0:T(8,128)(2,1)S(1)} %get-tuple-element.63.refs_3_.nh_ref, ...), custom_call_target="tpu_custom_call" | custom-call | tf_op jit(solution)/shard_map/pallas_call | solution.py:21
  66.0 6.7 %collective-permute-done.14.outer1_ref = f32[776,128]{1,0:T(8,128)S(1)} collective-permute-done((f32[776,128]{1,0:T(8,128)S(1)}, f32[776,128]{1,0:T(8,128)S(1)}, u32[]{:S(2)}, u32[]{:S(2)}) %collective-permute-start.14) | collective-permute-done | bytes 397344 | tf_op jit(solution)/shard_map/ppermute | solution.py:505
  72.8 3.3 %shard_map.74 = (f32[4,2,384,128]{3,2,1,0:T(8,128)}, f32[2,384,128]{2,1,0:T(8,128)S(1)}) custom-call(s32[1]{0:T(128)} %bitcast.core_ref, f32[776,128]{1,0:T(8,128)S(1)} %collective-permute-done.14.outer1_ref, f32[384,16]{1,0:T(8,128)S(1)} %get-tuple-element.44.table_ref.refs_0_, f32[2,384,128]{2,1,0:T(8,128)S(1)} %get-tuple-element.68.outer_ref, ...), custom_call_target="tpu_custom_call" | custom-call | flops 10000000 | bytes 6000000 | tf_op jit(solution)/shard_map/pallas_call | solution.py:21
  76.0 0.9 %collective-permute-done.17.outer2_ref = f32[768,128]{1,0:T(8,128)S(1)} collective-permute-done((f32[768,128]{1,0:T(8,128)S(1)}, f32[768,128]{1,0:T(8,128)S(1)}, u32[]{:S(2)}, u32[]{:S(2)}) %collective-permute-start.17) | collective-permute-done | bytes 393248 | tf_op jit(solution)/shard_map/ppermute | solution.py:505
  77.0 0.8 %shard_map.75 = f32[4,2,384,128]{3,2,1,0:T(8,128)} custom-call(s32[1]{0:T(128)} %bitcast.core_ref, f32[2,384,128]{2,1,0:T(8,128)S(1)} %get-tuple-element.81.light_ref, f32[768,128]{1,0:T(8,128)S(1)} %collective-permute-done.17.outer2_ref, f32[4,2,384,128]{3,2,1,0:T(8,128)} %get-tuple-element.83.whole_hbm), custom_call_target="tpu_custom_call", output_to_operand_aliasing={{}: (3, {})} | custom-call | flops 1000000 | bytes 1000000 | tf_op jit(solution)/shard_map/pallas_call | solution.py:583
  (35 shorter events, 1.7 us)
Async XLA Ops:
  0.6 1.1 %slice-start = ((f32[4,2,384,128]{3,2,1,0:T(8,128)}), f32[2,2,384,128]{3,2,1,0:T(8,128)S(1)}, s32[]{:S(2)}) async-start(f32[4,2,384,128]{3,2,1,0:T(8,128)} %z_ref.5), calls=%async_computation | async-start | bytes 1572864 | tf_op jit(solution)/shard_map/slice | solution.py:531
  0.6 5.0 %copy-start = (f32[4,2,384,128]{3,2,1,0:T(8,128)S(1)}, f32[4,2,384,128]{3,2,1,0:T(8,128)}, u32[]{:S(2)}) copy-start(f32[4,2,384,128]{3,2,1,0:T(8,128)} %z_ref.5) | copy-start | bytes 4718596
  0.7 5.0 %copy-start.4 = (f32[6,2,384]{2,1,0:T(2,128)S(1)}, f32[6,2,384]{2,1,0:T(2,128)}, u32[]{:S(2)}) copy-start(f32[6,2,384]{2,1,0:T(2,128)} %coeff_ref.1) | copy-start | bytes 55300
  1.8 9.1 %copy-start.2 = (f32[4,2,384,128]{3,2,1,0:T(8,128)S(1)}, f32[4,2,384,128]{3,2,1,0:T(8,128)}, u32[]{:S(2)}) copy-start(f32[4,2,384,128]{3,2,1,0:T(8,128)} %param.7) | copy-start | bytes 4718596
  1.8 17.9 %collective-permute-start.1 = (f32[784,128]{1,0:T(8,128)S(1)}, f32[784,128]{1,0:T(8,128)S(1)}, u32[]{:S(2)}, u32[]{:S(2)}) collective-permute-start(f32[784,128]{1,0:T(8,128)S(1)} %pad.4), channel_id=1, source_target_pairs={{1,2},{3,4},{5,6},{7,8},{9,10},{11,12},{13,14},{2,1},{4,3},{6,5},{... | collective-permute-start | bytes 1204232 | tf_op jit(solution)/shard_map/ppermute | solution.py:505
  7.2 7.4 %collective-permute-start.3 = (f32[776,128]{1,0:T(8,128)S(1)}, f32[776,128]{1,0:T(8,128)S(1)}, u32[]{:S(2)}, u32[]{:S(2)}) collective-permute-start(f32[776,128]{1,0:T(8,128)S(1)} %get-tuple-element.48), channel_id=1, source_target_pairs={{0,1},{1,0},{2,3},{3,2},{4,5},{5,4},{6,7},{7,6},{8,9},{9,8},{10,11... | collective-permute-start | bytes 1191944 | tf_op jit(solution)/shard_map/ppermute | solution.py:499
  7.3 7.3 %collective-permute-start.2 = (f32[768,128]{1,0:T(8,128)S(1)}, f32[768,128]{1,0:T(8,128)S(1)}, u32[]{:S(2)}, u32[]{:S(2)}) collective-permute-start(f32[768,128]{1,0:T(8,128)S(1)} %get-tuple-element.47), channel_id=1, source_target_pairs={{0,1},{1,0},{2,3},{3,2},{4,5},{5,4},{6,7},{7,6},{8,9},{9,8},{10,11... | collective-permute-start | bytes 1179656 | tf_op jit(solution)/shard_map/ppermute | solution.py:499
  7.8 16.3 %collective-permute-start = (f32[776,128]{1,0:T(8,128)S(1)}, f32[776,128]{1,0:T(8,128)S(1)}, u32[]{:S(2)}, u32[]{:S(2)}) collective-permute-start(f32[776,128]{1,0:T(8,128)S(1)} %get-tuple-element.45), channel_id=1, source_target_pairs={{1,2},{3,4},{5,6},{7,8},{9,10},{11,12},{13,14},{2,1},{4,3},{6,5},{... | collective-permute-start | bytes 1191944 | tf_op jit(solution)/shard_map/ppermute | solution.py:505
  10.9 1.9 %copy-start.1 = (f32[4,2,384,256]{3,2,1,0:T(8,128)S(1)}, f32[4,2,384,256]{3,2,1,0:T(8,128)}, u32[]{:S(2)}) copy-start(f32[4,2,384,256]{3,2,1,0:T(8,128)} %param.8) | copy-start | bytes 9437188
  25.0 19.8 %copy-start.3 = (f32[256,256]{1,0:T(8,128)S(1)}, f32[256,256]{1,0:T(8,128)}, u32[]{:S(2)}) copy-start(f32[256,256]{1,0:T(8,128)} %r_bar_ref.1) | copy-start | bytes 786436
  25.0 1.3 %collective-permute-start.4 = (f32[136,128]{1,0:T(8,128)S(1)}, f32[136,128]{1,0:T(8,128)S(1)}, u32[]{:S(2)}, u32[]{:S(2)}) collective-permute-start(f32[136,128]{1,0:T(8,128)S(1)} %get-tuple-element.58), channel_id=1, source_target_pairs={{0,1},{1,0},{2,3},{3,2},{4,5},{5,4},{6,7},{7,6},{8,9},{9,8},{10,11... | collective-permute-start | bytes 208904 | tf_op jit(solution)/shard_map/ppermute | solution.py:499
  25.1 1.4 %collective-permute-start.8 = (f32[128,128]{1,0:T(8,128)S(1)}, f32[128,128]{1,0:T(8,128)S(1)}, u32[]{:S(2)}, u32[]{:S(2)}) collective-permute-start(f32[128,128]{1,0:T(8,128)S(1)} %get-tuple-element.60), channel_id=1, source_target_pairs={{0,1},{1,0},{2,3},{3,2},{4,5},{5,4},{6,7},{7,6},{8,9},{9,8},{10,11... | collective-permute-start | bytes 196616 | tf_op jit(solution)/shard_map/ppermute | solution.py:499
  26.4 3.5 %collective-permute-start.5 = (f32[136,128]{1,0:T(8,128)S(1)}, f32[136,128]{1,0:T(8,128)S(1)}, u32[]{:S(2)}, u32[]{:S(2)}) collective-permute-start(f32[136,128]{1,0:T(8,128)S(1)} %add.31), channel_id=1, source_target_pairs={{0,2},{1,5},{2,0},{3,7},{4,6},{5,1},{6,4},{7,3},{8,10},{9,13},{10,... | collective-permute-start | bytes 208904 | tf_op jit(solution)/shard_map/ppermute | solution.py:516
  26.5 5.8 %collective-permute-start.9 = (f32[128,128]{1,0:T(8,128)S(1)}, f32[128,128]{1,0:T(8,128)S(1)}, u32[]{:S(2)}, u32[]{:S(2)}) collective-permute-start(f32[128,128]{1,0:T(8,128)S(1)} %add.35), channel_id=1, source_target_pairs={{0,4},{1,3},{2,6},{3,1},{4,0},{5,7},{6,2},{7,5},{8,12},{9,11},{10,... | collective-permute-start | bytes 196616 | tf_op jit(solution)/shard_map/ppermute | solution.py:516
  29.9 4.3 %collective-permute-start.6 = (f32[136,128]{1,0:T(8,128)S(1)}, f32[136,128]{1,0:T(8,128)S(1)}, u32[]{:S(2)}, u32[]{:S(2)}) collective-permute-start(f32[136,128]{1,0:T(8,128)S(1)} %add.32), channel_id=1, source_target_pairs={{0,4},{1,9},{2,6},{3,11},{4,0},{5,13},{6,2},{7,15},{8,12},{9,1},{1... | collective-permute-start | bytes 208904 | tf_op jit(solution)/shard_map/ppermute | solution.py:516
  32.3 3.5 %collective-permute-start.10 = (f32[128,128]{1,0:T(8,128)S(1)}, f32[128,128]{1,0:T(8,128)S(1)}, u32[]{:S(2)}, u32[]{:S(2)}) collective-permute-start(f32[128,128]{1,0:T(8,128)S(1)} %add.36), channel_id=1, source_target_pairs={{0,8},{1,5},{2,10},{3,7},{4,12},{5,1},{6,14},{7,3},{8,0},{9,13},{1... | collective-permute-start | bytes 196616 | tf_op jit(solution)/shard_map/ppermute | solution.py:516
  34.2 3.5 %collective-permute-start.7 = (f32[136,128]{1,0:T(8,128)S(1)}, f32[136,128]{1,0:T(8,128)S(1)}, u32[]{:S(2)}, u32[]{:S(2)}) collective-permute-start(f32[136,128]{1,0:T(8,128)S(1)} %add.33), channel_id=1, source_target_pairs={{0,8},{1,3},{2,10},{3,1},{4,12},{5,7},{6,14},{7,5},{8,0},{9,11},{1... | collective-permute-start | bytes 208904 | tf_op jit(solution)/shard_map/ppermute | solution.py:516
  35.8 6.1 %collective-permute-start.11 = (f32[128,128]{1,0:T(8,128)S(1)}, f32[128,128]{1,0:T(8,128)S(1)}, u32[]{:S(2)}, u32[]{:S(2)}) collective-permute-start(f32[128,128]{1,0:T(8,128)S(1)} %add.37), channel_id=1, source_target_pairs={{0,2},{1,9},{2,0},{3,11},{4,6},{5,13},{6,4},{7,15},{8,10},{9,1},{1... | collective-permute-start | bytes 196616 | tf_op jit(solution)/shard_map/ppermute | solution.py:516
  37.7 7.1 %collective-permute-start.12 = (f32[136,128]{1,0:T(8,128)S(1)}, f32[136,128]{1,0:T(8,128)S(1)}, u32[]{:S(2)}, u32[]{:S(2)}) collective-permute-start(f32[136,128]{1,0:T(8,128)S(1)} %add.34.mine1_ref), channel_id=1, source_target_pairs={{0,1},{1,0},{2,3},{3,2},{4,5},{5,4},{6,7},{7,6},{8,9},{9,8},{10,11... | collective-permute-start | bytes 208904 | tf_op jit(solution)/shard_map/ppermute | solution.py:499
  41.9 2.9 %collective-permute-start.13 = (f32[128,128]{1,0:T(8,128)S(1)}, f32[128,128]{1,0:T(8,128)S(1)}, u32[]{:S(2)}, u32[]{:S(2)}) collective-permute-start(f32[128,128]{1,0:T(8,128)S(1)} %add.38.mine2_ref), channel_id=1, source_target_pairs={{0,1},{1,0},{2,3},{3,2},{4,5},{5,4},{6,7},{7,6},{8,9},{9,8},{10,11... | collective-permute-start | bytes 196616 | tf_op jit(solution)/shard_map/ppermute | solution.py:499
  55.1 17.6 %collective-permute-start.14 = (f32[776,128]{1,0:T(8,128)S(1)}, f32[776,128]{1,0:T(8,128)S(1)}, u32[]{:S(2)}, u32[]{:S(2)}) collective-permute-start(f32[776,128]{1,0:T(8,128)S(1)} %get-tuple-element.67.outer1_ref.own1_ref), channel_id=1, source_target_pairs={{1,2},{3,4},{5,6},{7,8},{9,10},{11,12},{13,14},{2,1},{4,3},{6,5},{... | collective-permute-start | bytes 1191944 | tf_op jit(solution)/shard_map/ppermute | solution.py:505
  58.8 7.3 %collective-permute-start.16 = (f32[768,128]{1,0:T(8,128)S(1)}, f32[768,128]{1,0:T(8,128)S(1)}, u32[]{:S(2)}, u32[]{:S(2)}) collective-permute-start(f32[768,128]{1,0:T(8,128)S(1)} %get-tuple-element.80), channel_id=1, source_target_pairs={{0,1},{1,0},{2,3},{3,2},{4,5},{5,4},{6,7},{7,6},{8,9},{9,8},{10,11... | collective-permute-start | bytes 1179656 | tf_op jit(solution)/shard_map/ppermute | solution.py:499
  60.1 6.0 %collective-permute-start.15 = (f32[768,128]{1,0:T(8,128)S(1)}, f32[768,128]{1,0:T(8,128)S(1)}, u32[]{:S(2)}, u32[]{:S(2)}) collective-permute-start(f32[768,128]{1,0:T(8,128)S(1)} %get-tuple-element.79.own2_ref), channel_id=1, source_target_pairs={{0,1},{1,0},{2,3},{3,2},{4,5},{5,4},{6,7},{7,6},{8,9},{9,8},{10,11... | collective-permute-start | bytes 1179656 | tf_op jit(solution)/shard_map/ppermute | solution.py:499
  60.2 16.8 %collective-permute-start.17 = (f32[768,128]{1,0:T(8,128)S(1)}, f32[768,128]{1,0:T(8,128)S(1)}, u32[]{:S(2)}, u32[]{:S(2)}) collective-permute-start(f32[768,128]{1,0:T(8,128)S(1)} %get-tuple-element.82), channel_id=1, source_target_pairs={{1,2},{3,4},{5,6},{7,8},{9,10},{11,12},{13,14},{2,1},{4,3},{6,5},{... | collective-permute-start | bytes 1179656 | tf_op jit(solution)/shard_map/ppermute | solution.py:505

commit v16 on v15

--- a/solution.py
+++ b/solution.py
@@ -260,11 +260,9 @@
     for start in range(0, size, step):
         last = start + step >= size
         reach = step if last else 2 * step
-        s = {
-            (i, m): jnp.broadcast_to(rows[i][:, start + m : start + m + 1], (step, size))
-            for i in range(step)
-            for m in range(i, reach)
-        }
+        wanted = [(i, m) for i in range(step) for m in range(i, step)]
+        wanted += [(i, m) for i in range(step) for m in range(step, reach)]
+        s = {(i, m): jnp.broadcast_to(rows[i][:, start + m : start + m + 1], (step, size)) for i, m in wanted}
         inside = (lane >= start) & (lane < start + step)
         rows = [jnp.where(lane == start + i, 1.0, jnp.where(inside, 0.0, rows[i])) for i in range(step)]
         done = []
@@ -272,11 +270,14 @@
         for i in range(step):
             inverse = pl.reciprocal(s[i, i])
             root = lax.rsqrt(s[i, i])
+            ratio = {k: s[i, k] * inverse for k in range(i + 1, step)}
+            for part in (range(step), range(step, reach)):
+                for k in range(i + 1, step):
+                    for m in part:
+                        if m >= k:
+                            s[k, m] = s[k, m] - ratio[k] * s[i, m]
             for k in range(i + 1, step):
-                ratio = s[i, k] * inverse
-                for m in range(k, reach):
-                    s[k, m] = s[k, m] - ratio * s[i, m]
-                rows[k] = rows[k] - ratio * rows[i]
+                rows[k] = rows[k] - ratio[k] * rows[i]
             if not last:
                 scaled = rows[i] * inverse
                 for k in range(step):

time: 78.2 us -> 78.1 us (level)
  no operation moved by 1% of the time
where the time goes in v16:
time: 78.1 us; the launch traced here: 77.9 us
  starting transfers between devices  27.3 us (35%)
  Pallas kernels  26.4 us (34%)
  waiting for transfers between devices  20 us (26%)
  local copies, waits for them, and re-layouts  3.06 us (4%)
  between operations  1.02 us (1%)
    pallas_call x8, Pallas kernels, run(): pl.pallas_call(kernel, out_shape=outs, in_specs=specs, scratch_shapes=lis...  25.6 us
    ppermute x4, waiting for transfers between devices, swap_outer(): return lax.ppermute(message, 'row', pairs + [(j, i) for i, j in pairs])  14.1 us
    ppermute x4, starting transfers between devices, swap_outer(): return lax.ppermute(message, 'row', pairs + [(j, i) for i, j in pairs])  11.7 us
    ppermute x8, starting transfers between devices, swap_inner(): return lax.ppermute(message, 'row', [(i, i ^ 1) for i in range(count)])  8.67 us
    ppermute x6, starting transfers between devices, sum_over_rows(): mine[stream] = mine[stream] + lax.ppermute(mine[stream], 'row', pairs)  6.97 us
    ppermute x6, waiting for transfers between devices, sum_over_rows(): mine[stream] = mine[stream] + lax.ppermute(mine[stream], 'row', pairs)  4.22 us
    unnamed x10, local copies, waits for them, and re-layouts  1.9 us
    ppermute x8, waiting for transfers between devices, swap_inner(): return lax.ppermute(message, 'row', [(i, i ^ 1) for i in range(count)])  1.73 us
  transfers between devices with their start and end apart: 18, of which 11 were waited for; matrix products, arithmetic and copies ran while one was open for 0% of the time, Pallas kernels for 18%

profile of v16, /device:TPU:9, one launch (start us, length us, event | category | flops | bytes accessed | tf_op | source)
XLA Modules:
  0.0 77.9 jit_solution(2732069363758623883)
XLA Ops:
  0.7 1.1 %slice-done = f32[2,2,384,128]{3,2,1,0:T(8,128)S(1)} async-done(((f32[4,2,384,128]{3,2,1,0:T(8,128)}), f32[2,2,384,128]{3,2,1,0:T(8,128)S(1)}, s32[]{:S(2)}) %slice-start) | async-done | bytes 786456 | tf_op jit(solution)/shard_map/slice | solution.py:532
  1.8 3.8 %collective-permute-start.1 = (f32[784,128]{1,0:T(8,128)S(1)}, f32[784,128]{1,0:T(8,128)S(1)}, u32[]{:S(2)}, u32[]{:S(2)}) collective-permute-start(f32[784,128]{1,0:T(8,128)S(1)} %pad.4), channel_id=1, source_target_pairs={{1,2},{3,4},{5,6},{7,8},{9,10},{11,12},{13,14},{2,1},{4,3},{6,5},{... | collective-permute-start | bytes 1204232 | tf_op jit(solution)/shard_map/ppermute | solution.py:506
  5.7 1.5 %shard_map.68 = (f32[776,128]{1,0:T(8,128)S(1)}, f32[768,128]{1,0:T(8,128)S(1)}, f32[776,128]{1,0:T(8,128)S(1)}, f32[384,16]{1,0:T(8,128)S(1)}) custom-call(s32[1]{0:T(128)} %bitcast.core_ref, f32[6,2,384]{2,1,0:T(2,128)S(1)} %copy-done.4, f32[4,2,384,128]{3,2,1,0:T(8,128)S(1)} %copy-done), custom_call_target="tpu_custom_call" | custom-call | flops 1000000 | bytes 3000000 | tf_op jit(solution)/shard_map/pallas_call | solution.py:21
  7.3 0.5 collective-permute-start.2
  7.8 3.1 %collective-permute-start = (f32[776,128]{1,0:T(8,128)S(1)}, f32[776,128]{1,0:T(8,128)S(1)}, u32[]{:S(2)}, u32[]{:S(2)}) collective-permute-start(f32[776,128]{1,0:T(8,128)S(1)} %get-tuple-element.45), channel_id=1, source_target_pairs={{1,2},{3,4},{5,6},{7,8},{9,10},{11,12},{13,14},{2,1},{4,3},{6,5},{... | collective-permute-start | bytes 1191944 | tf_op jit(solution)/shard_map/ppermute | solution.py:506
  10.9 1.9 %copy-done.1 = f32[4,2,384,256]{3,2,1,0:T(8,128)S(1)} copy-done((f32[4,2,384,256]{3,2,1,0:T(8,128)S(1)}, f32[4,2,384,256]{3,2,1,0:T(8,128)}, u32[]{:S(2)}) %copy-start.1) | copy-done | bytes 3145752
  12.8 1.8 %shard_map.69 = (f32[136,128]{1,0:T(8,128)S(1)}, bf16[3072,128]{1,0:T(8,128)(2,1)S(1)}, bf16[3072,128]{1,0:T(8,128)(2,1)S(1)}, bf16[3072,256]{1,0:T(8,128)(2,1)S...) custom-call(f32[3072,128]{1,0:T(8,128)S(1)} %bitcast.5, ...), custom_call_target="tpu_custom_call" | custom-call | flops 503316480 | bytes 9000000 | tf_op jit(solution)/shard_map/pallas_call | solution.py:21
  14.6 5.2 %collective-permute-done.1.outer1_ref = f32[784,128]{1,0:T(8,128)S(1)} collective-permute-done((f32[784,128]{1,0:T(8,128)S(1)}, f32[784,128]{1,0:T(8,128)S(1)}, u32[]{:S(2)}, u32[]{:S(2)}) %collective-permute-start.1) | collective-permute-done | bytes 401440 | tf_op jit(solution)/shard_map/ppermute | solution.py:506
  19.8 3.1 %shard_map.70 = (f32[2,384,128]{2,1,0:T(8,128)S(1)}, bf16[1536,128]{1,0:T(8,128)(2,1)S(1)}, bf16[1536,128]{1,0:T(8,128)(2,1)S(1)}, bf16[768,128]{1,0:T(8,128)(2,...) custom-call(s32[1]{0:T(128)} %bitcast.core_ref, ...), custom_call_target="tpu_custom_call" | custom-call | flops 805306368 | bytes 9000000 | tf_op jit(solution)/shard_map/pallas_call | solution.py:21
  22.8 1.2 %collective-permute-done.outer2_ref.fouter2_ref = f32[776,128]{1,0:T(8,128)S(1)} collective-permute-done((f32[776,128]{1,0:T(8,128)S(1)}, f32[776,128]{1,0:T(8,128)S(1)}, u32[]{:S(2)}, u32[]{:S(2)}) %collective-permute-start) | collective-permute-done | bytes 397344 | tf_op jit(solution)/shard_map/ppermute | solution.py:506
  24.0 1.0 %shard_map.71 = (f32[136,128]{1,0:T(8,128)S(1)}, f32[128,128]{1,0:T(8,128)S(1)}, f32[136,128]{1,0:T(8,128)S(1)}, f32[128,128]{1,0:T(8,128)S(1)}, bf16[768,128]{1...) custom-call(s32[1]{0:T(128)} %bitcast.core_ref, f32[384,16]{1,0:T(8,128)S(1)} %get-tuple-element.44.table_ref.refs_0_, ...), custom_call_target="tpu_custom_call" | custom-call | flops 301989888 | bytes 5000000 | tf_op jit(solution)/shard_map/pallas_call | solution.py:21
  25.6 0.7 collective-permute-done.4
  26.5 1.7 %collective-permute-start.9 = (f32[128,128]{1,0:T(8,128)S(1)}, f32[128,128]{1,0:T(8,128)S(1)}, u32[]{:S(2)}, u32[]{:S(2)}) collective-permute-start(f32[128,128]{1,0:T(8,128)S(1)} %add.35), channel_id=1, source_target_pairs={{0,4},{1,3},{2,6},{3,1},{4,0},{5,7},{6,2},{7,5},{8,12},{9,11},{10,... | collective-permute-start | bytes 196616 | tf_op jit(solution)/shard_map/ppermute | solution.py:517
  28.3 1.6 %collective-permute-done.5 = f32[136,128]{1,0:T(8,128)S(1)} collective-permute-done((f32[136,128]{1,0:T(8,128)S(1)}, f32[136,128]{1,0:T(8,128)S(1)}, u32[]{:S(2)}, u32[]{:S(2)}) %collective-permute-start.5) | collective-permute-done | bytes 69664 | tf_op jit(solution)/shard_map/ppermute | solution.py:517
  29.9 2.4 %collective-permute-start.6 = (f32[136,128]{1,0:T(8,128)S(1)}, f32[136,128]{1,0:T(8,128)S(1)}, u32[]{:S(2)}, u32[]{:S(2)}) collective-permute-start(f32[136,128]{1,0:T(8,128)S(1)} %add.32), channel_id=1, source_target_pairs={{0,4},{1,9},{2,6},{3,11},{4,0},{5,13},{6,2},{7,15},{8,12},{9,1},{1... | collective-permute-start | bytes 208904 | tf_op jit(solution)/shard_map/ppermute | solution.py:517
  32.5 1.6 %collective-permute-done.6 = f32[136,128]{1,0:T(8,128)S(1)} collective-permute-done((f32[136,128]{1,0:T(8,128)S(1)}, f32[136,128]{1,0:T(8,128)S(1)}, u32[]{:S(2)}, u32[]{:S(2)}) %collective-permute-start.6) | collective-permute-done | bytes 69664 | tf_op jit(solution)/shard_map/ppermute | solution.py:517
  34.2 1.1 %collective-permute-start.7 = (f32[136,128]{1,0:T(8,128)S(1)}, f32[136,128]{1,0:T(8,128)S(1)}, u32[]{:S(2)}, u32[]{:S(2)}) collective-permute-start(f32[136,128]{1,0:T(8,128)S(1)} %add.33), channel_id=1, source_target_pairs={{0,8},{1,3},{2,10},{3,1},{4,12},{5,7},{6,14},{7,5},{8,0},{9,11},{1... | collective-permute-start | bytes 208904 | tf_op jit(solution)/shard_map/ppermute | solution.py:517
  35.8 1.4 %collective-permute-start.11 = (f32[128,128]{1,0:T(8,128)S(1)}, f32[128,128]{1,0:T(8,128)S(1)}, u32[]{:S(2)}, u32[]{:S(2)}) collective-permute-start(f32[128,128]{1,0:T(8,128)S(1)} %add.37), channel_id=1, source_target_pairs={{0,2},{1,9},{2,0},{3,11},{4,6},{5,13},{6,4},{7,15},{8,10},{9,1},{1... | collective-permute-start | bytes 196616 | tf_op jit(solution)/shard_map/ppermute | solution.py:517
  37.2 0.5 collective-permute-done.7
  37.7 4.1 %collective-permute-start.12 = (f32[136,128]{1,0:T(8,128)S(1)}, f32[136,128]{1,0:T(8,128)S(1)}, u32[]{:S(2)}, u32[]{:S(2)}) collective-permute-start(f32[136,128]{1,0:T(8,128)S(1)} %add.34.mine1_ref), channel_id=1, source_target_pairs={{0,1},{1,0},{2,3},{3,2},{4,5},{5,4},{6,7},{7,6},{8,9},{9,8},{10,11... | collective-permute-start | bytes 208904 | tf_op jit(solution)/shard_map/ppermute | solution.py:500
  41.9 2.0 %collective-permute-start.13 = (f32[128,128]{1,0:T(8,128)S(1)}, f32[128,128]{1,0:T(8,128)S(1)}, u32[]{:S(2)}, u32[]{:S(2)}) collective-permute-start(f32[128,128]{1,0:T(8,128)S(1)} %add.38.mine2_ref), channel_id=1, source_target_pairs={{0,1},{1,0},{2,3},{3,2},{4,5},{5,4},{6,7},{7,6},{8,9},{9,8},{10,11... | collective-permute-start | bytes 196616 | tf_op jit(solution)/shard_map/ppermute | solution.py:500
  43.9 0.9 %collective-permute-done.13.other2_ref = f32[128,128]{1,0:T(8,128)S(1)} collective-permute-done((f32[128,128]{1,0:T(8,128)S(1)}, f32[128,128]{1,0:T(8,128)S(1)}, u32[]{:S(2)}, u32[]{:S(2)}) %collective-permute-start.13) | collective-permute-done | bytes 65568 | tf_op jit(solution)/shard_map/ppermute | solution.py:500
  44.8 10.3 %shard_map.72 = (bf16[256,256]{1,0:T(8,128)(2,1)S(1)}, bf16[256,256]{1,0:T(8,128)(2,1)S(1)}, bf16[256,256]{1,0:T(8,128)(2,1)S(1)}, bf16[256,256]{1,0:T(8,128)(2,...) custom-call(s32[1]{0:T(128)} %bitcast.core_ref, f32[136,128]{1,0:T(8,128)S(1)} %add.34.mine1_ref, ...), custom_call_target="tpu_custom_call" | custom-call | flops 1000000000 | bytes 1000000 | tf_op jit(solution)/shard_map/pallas_call | solution.py:21
  55.1 1.9 %collective-permute-start.14 = (f32[776,128]{1,0:T(8,128)S(1)}, f32[776,128]{1,0:T(8,128)S(1)}, u32[]{:S(2)}, u32[]{:S(2)}) collective-permute-start(f32[776,128]{1,0:T(8,128)S(1)} %get-tuple-element.67.outer1_ref.own1_ref), channel_id=1, source_target_pairs={{1,2},{3,4},{5,6},{7,8},{9,10},{11,12},{13,14},{2,1},{4,3},{6,5},{... | collective-permute-start | bytes 1191944 | tf_op jit(solution)/shard_map/ppermute | solution.py:506
  57.0 1.7 %shard_map.73 = (f32[2,384,128]{2,1,0:T(8,128)S(1)}, f32[2,2,384,128]{3,2,1,0:T(8,128)S(1)}, f32[768,128]{1,0:T(8,128)S(1)}, f32[768,128]{1,0:T(8,128)S(1)}, f32[768,128]{1,0:T(8,128)S(1)}) custom-call(s32[1]{0:T(128)} %bitcast.core_ref, f32[384,16]{1,0:T(8,128)S(1)} %get-tuple-element.44.table_ref.refs_0_, f32[2,384,128]{2,1,0:T(8,128)S(1)} %get-tuple-element.68.outer_ref, ...), custom_call_target="tpu_custom_call" | custom-call | flops 10000000000 | bytes 6000000 | tf_op jit(solution)/shard_map/pallas_call | solution.py:21
  58.8 1.3 %collective-permute-start.16 = (f32[768,128]{1,0:T(8,128)S(1)}, f32[768,128]{1,0:T(8,128)S(1)}, u32[]{:S(2)}, u32[]{:S(2)}) collective-permute-start(f32[768,128]{1,0:T(8,128)S(1)} %get-tuple-element.80), channel_id=1, source_target_pairs={{0,1},{1,0},{2,3},{3,2},{4,5},{5,4},{6,7},{7,6},{8,9},{9,8},{10,11... | collective-permute-start | bytes 1179656 | tf_op jit(solution)/shard_map/ppermute | solution.py:500
  60.1 2.8 %collective-permute-start.17 = (f32[768,128]{1,0:T(8,128)S(1)}, f32[768,128]{1,0:T(8,128)S(1)}, u32[]{:S(2)}, u32[]{:S(2)}) collective-permute-start(f32[768,128]{1,0:T(8,128)S(1)} %get-tuple-element.82), channel_id=1, source_target_pairs={{1,2},{3,4},{5,6},{7,8},{9,10},{11,12},{13,14},{2,1},{4,3},{6,5},{... | collective-permute-start | bytes 1179656 | tf_op jit(solution)/shard_map/ppermute | solution.py:506
  63.0 3.0 %shard_map.76 = f32[4,2,384,128]{3,2,1,0:T(8,128)} custom-call(s32[1]{0:T(128)} %bitcast.core_ref, bf16[3072,256]{1,0:T(8,128)(2,1)S(1)} %get-tuple-element.61.refs_1_.qh_ref, bf16[3072,256]{1,0:T(8,128)(2,1)S(1)} %get-tuple-element.62.refs_2_.ql_ref, bf16[3072,128]{1,0:T(8,128)(2,1)S(1)} %get-tuple-element.63.refs_3_.nh_ref, ...), custom_call_target="tpu_custom_call" | custom-call | tf_op jit(solution)/shard_map/pallas_call | solution.py:21
  66.0 6.7 %collective-permute-done.14.outer1_ref = f32[776,128]{1,0:T(8,128)S(1)} collective-permute-done((f32[776,128]{1,0:T(8,128)S(1)}, f32[776,128]{1,0:T(8,128)S(1)}, u32[]{:S(2)}, u32[]{:S(2)}) %collective-permute-start.14) | collective-permute-done | bytes 397344 | tf_op jit(solution)/shard_map/ppermute | solution.py:506
  72.7 3.3 %shard_map.74 = (f32[4,2,384,128]{3,2,1,0:T(8,128)}, f32[2,384,128]{2,1,0:T(8,128)S(1)}) custom-call(s32[1]{0:T(128)} %bitcast.core_ref, f32[776,128]{1,0:T(8,128)S(1)} %collective-permute-done.14.outer1_ref, f32[384,16]{1,0:T(8,128)S(1)} %get-tuple-element.44.table_ref.refs_0_, f32[2,384,128]{2,1,0:T(8,128)S(1)} %get-tuple-element.68.outer_ref, ...), custom_call_target="tpu_custom_call" | custom-call | flops 10000000 | bytes 6000000 | tf_op jit(solution)/shard_map/pallas_call | solution.py:21
  76.0 0.9 %collective-permute-done.17.outer2_ref = f32[768,128]{1,0:T(8,128)S(1)} collective-permute-done((f32[768,128]{1,0:T(8,128)S(1)}, f32[768,128]{1,0:T(8,128)S(1)}, u32[]{:S(2)}, u32[]{:S(2)}) %collective-permute-start.17) | collective-permute-done | bytes 393248 | tf_op jit(solution)/shard_map/ppermute | solution.py:506
  76.9 0.8 %shard_map.75 = f32[4,2,384,128]{3,2,1,0:T(8,128)} custom-call(s32[1]{0:T(128)} %bitcast.core_ref, f32[2,384,128]{2,1,0:T(8,128)S(1)} %get-tuple-element.81.light_ref, f32[768,128]{1,0:T(8,128)S(1)} %collective-permute-done.17.outer2_ref, f32[4,2,384,128]{3,2,1,0:T(8,128)} %get-tuple-element.83.whole_hbm), custom_call_target="tpu_custom_call", output_to_operand_aliasing={{}: (3, {})} | custom-call | flops 1000000 | bytes 1000000 | tf_op jit(solution)/shard_map/pallas_call | solution.py:584
  (35 shorter events, 1.7 us)
Async XLA Ops:
  0.6 1.1 %slice-start = ((f32[4,2,384,128]{3,2,1,0:T(8,128)}), f32[2,2,384,128]{3,2,1,0:T(8,128)S(1)}, s32[]{:S(2)}) async-start(f32[4,2,384,128]{3,2,1,0:T(8,128)} %z_ref.5), calls=%async_computation | async-start | bytes 1572864 | tf_op jit(solution)/shard_map/slice | solution.py:532
  0.6 5.0 %copy-start = (f32[4,2,384,128]{3,2,1,0:T(8,128)S(1)}, f32[4,2,384,128]{3,2,1,0:T(8,128)}, u32[]{:S(2)}) copy-start(f32[4,2,384,128]{3,2,1,0:T(8,128)} %z_ref.5) | copy-start | bytes 4718596
  0.7 5.0 %copy-start.4 = (f32[6,2,384]{2,1,0:T(2,128)S(1)}, f32[6,2,384]{2,1,0:T(2,128)}, u32[]{:S(2)}) copy-start(f32[6,2,384]{2,1,0:T(2,128)} %coeff_ref.1) | copy-start | bytes 55300
  1.8 9.1 %copy-start.2 = (f32[4,2,384,128]{3,2,1,0:T(8,128)S(1)}, f32[4,2,384,128]{3,2,1,0:T(8,128)}, u32[]{:S(2)}) copy-start(f32[4,2,384,128]{3,2,1,0:T(8,128)} %param.7) | copy-start | bytes 4718596
  1.8 17.9 %collective-permute-start.1 = (f32[784,128]{1,0:T(8,128)S(1)}, f32[784,128]{1,0:T(8,128)S(1)}, u32[]{:S(2)}, u32[]{:S(2)}) collective-permute-start(f32[784,128]{1,0:T(8,128)S(1)} %pad.4), channel_id=1, source_target_pairs={{1,2},{3,4},{5,6},{7,8},{9,10},{11,12},{13,14},{2,1},{4,3},{6,5},{... | collective-permute-start | bytes 1204232 | tf_op jit(solution)/shard_map/ppermute | solution.py:506
  7.2 7.4 %collective-permute-start.3 = (f32[776,128]{1,0:T(8,128)S(1)}, f32[776,128]{1,0:T(8,128)S(1)}, u32[]{:S(2)}, u32[]{:S(2)}) collective-permute-start(f32[776,128]{1,0:T(8,128)S(1)} %get-tuple-element.48), channel_id=1, source_target_pairs={{0,1},{1,0},{2,3},{3,2},{4,5},{5,4},{6,7},{7,6},{8,9},{9,8},{10,11... | collective-permute-start | bytes 1191944 | tf_op jit(solution)/shard_map/ppermute | solution.py:500
  7.3 7.3 %collective-permute-start.2 = (f32[768,128]{1,0:T(8,128)S(1)}, f32[768,128]{1,0:T(8,128)S(1)}, u32[]{:S(2)}, u32[]{:S(2)}) collective-permute-start(f32[768,128]{1,0:T(8,128)S(1)} %get-tuple-element.47), channel_id=1, source_target_pairs={{0,1},{1,0},{2,3},{3,2},{4,5},{5,4},{6,7},{7,6},{8,9},{9,8},{10,11... | collective-permute-start | bytes 1179656 | tf_op jit(solution)/shard_map/ppermute | solution.py:500
  7.8 16.3 %collective-permute-start = (f32[776,128]{1,0:T(8,128)S(1)}, f32[776,128]{1,0:T(8,128)S(1)}, u32[]{:S(2)}, u32[]{:S(2)}) collective-permute-start(f32[776,128]{1,0:T(8,128)S(1)} %get-tuple-element.45), channel_id=1, source_target_pairs={{1,2},{3,4},{5,6},{7,8},{9,10},{11,12},{13,14},{2,1},{4,3},{6,5},{... | collective-permute-start | bytes 1191944 | tf_op jit(solution)/shard_map/ppermute | solution.py:506
  10.9 1.9 %copy-start.1 = (f32[4,2,384,256]{3,2,1,0:T(8,128)S(1)}, f32[4,2,384,256]{3,2,1,0:T(8,128)}, u32[]{:S(2)}) copy-start(f32[4,2,384,256]{3,2,1,0:T(8,128)} %param.8) | copy-start | bytes 9437188
  25.0 19.8 %copy-start.3 = (f32[256,256]{1,0:T(8,128)S(1)}, f32[256,256]{1,0:T(8,128)}, u32[]{:S(2)}) copy-start(f32[256,256]{1,0:T(8,128)} %r_bar_ref.1) | copy-start | bytes 786436
  25.0 1.3 %collective-permute-start.4 = (f32[136,128]{1,0:T(8,128)S(1)}, f32[136,128]{1,0:T(8,128)S(1)}, u32[]{:S(2)}, u32[]{:S(2)}) collective-permute-start(f32[136,128]{1,0:T(8,128)S(1)} %get-tuple-element.58), channel_id=1, source_target_pairs={{0,1},{1,0},{2,3},{3,2},{4,5},{5,4},{6,7},{7,6},{8,9},{9,8},{10,11... | collective-permute-start | bytes 208904 | tf_op jit(solution)/shard_map/ppermute | solution.py:500
  25.1 1.4 %collective-permute-start.8 = (f32[128,128]{1,0:T(8,128)S(1)}, f32[128,128]{1,0:T(8,128)S(1)}, u32[]{:S(2)}, u32[]{:S(2)}) collective-permute-start(f32[128,128]{1,0:T(8,128)S(1)} %get-tuple-element.60), channel_id=1, source_target_pairs={{0,1},{1,0},{2,3},{3,2},{4,5},{5,4},{6,7},{7,6},{8,9},{9,8},{10,11... | collective-permute-start | bytes 196616 | tf_op jit(solution)/shard_map/ppermute | solution.py:500
  26.4 3.5 %collective-permute-start.5 = (f32[136,128]{1,0:T(8,128)S(1)}, f32[136,128]{1,0:T(8,128)S(1)}, u32[]{:S(2)}, u32[]{:S(2)}) collective-permute-start(f32[136,128]{1,0:T(8,128)S(1)} %add.31), channel_id=1, source_target_pairs={{0,2},{1,5},{2,0},{3,7},{4,6},{5,1},{6,4},{7,3},{8,10},{9,13},{10,... | collective-permute-start | bytes 208904 | tf_op jit(solution)/shard_map/ppermute | solution.py:517
  26.5 5.8 %collective-permute-start.9 = (f32[128,128]{1,0:T(8,128)S(1)}, f32[128,128]{1,0:T(8,128)S(1)}, u32[]{:S(2)}, u32[]{:S(2)}) collective-permute-start(f32[128,128]{1,0:T(8,128)S(1)} %add.35), channel_id=1, source_target_pairs={{0,4},{1,3},{2,6},{3,1},{4,0},{5,7},{6,2},{7,5},{8,12},{9,11},{10,... | collective-permute-start | bytes 196616 | tf_op jit(solution)/shard_map/ppermute | solution.py:517
  29.9 4.3 %collective-permute-start.6 = (f32[136,128]{1,0:T(8,128)S(1)}, f32[136,128]{1,0:T(8,128)S(1)}, u32[]{:S(2)}, u32[]{:S(2)}) collective-permute-start(f32[136,128]{1,0:T(8,128)S(1)} %add.32), channel_id=1, source_target_pairs={{0,4},{1,9},{2,6},{3,11},{4,0},{5,13},{6,2},{7,15},{8,12},{9,1},{1... | collective-permute-start | bytes 208904 | tf_op jit(solution)/shard_map/ppermute | solution.py:517
  32.3 3.5 %collective-permute-start.10 = (f32[128,128]{1,0:T(8,128)S(1)}, f32[128,128]{1,0:T(8,128)S(1)}, u32[]{:S(2)}, u32[]{:S(2)}) collective-permute-start(f32[128,128]{1,0:T(8,128)S(1)} %add.36), channel_id=1, source_target_pairs={{0,8},{1,5},{2,10},{3,7},{4,12},{5,1},{6,14},{7,3},{8,0},{9,13},{1... | collective-permute-start | bytes 196616 | tf_op jit(solution)/shard_map/ppermute | solution.py:517
  34.2 3.5 %collective-permute-start.7 = (f32[136,128]{1,0:T(8,128)S(1)}, f32[136,128]{1,0:T(8,128)S(1)}, u32[]{:S(2)}, u32[]{:S(2)}) collective-permute-start(f32[136,128]{1,0:T(8,128)S(1)} %add.33), channel_id=1, source_target_pairs={{0,8},{1,3},{2,10},{3,1},{4,12},{5,7},{6,14},{7,5},{8,0},{9,11},{1... | collective-permute-start | bytes 208904 | tf_op jit(solution)/shard_map/ppermute | solution.py:517
  35.8 6.1 %collective-permute-start.11 = (f32[128,128]{1,0:T(8,128)S(1)}, f32[128,128]{1,0:T(8,128)S(1)}, u32[]{:S(2)}, u32[]{:S(2)}) collective-permute-start(f32[128,128]{1,0:T(8,128)S(1)} %add.37), channel_id=1, source_target_pairs={{0,2},{1,9},{2,0},{3,11},{4,6},{5,13},{6,4},{7,15},{8,10},{9,1},{1... | collective-permute-start | bytes 196616 | tf_op jit(solution)/shard_map/ppermute | solution.py:517
  37.7 7.1 %collective-permute-start.12 = (f32[136,128]{1,0:T(8,128)S(1)}, f32[136,128]{1,0:T(8,128)S(1)}, u32[]{:S(2)}, u32[]{:S(2)}) collective-permute-start(f32[136,128]{1,0:T(8,128)S(1)} %add.34.mine1_ref), channel_id=1, source_target_pairs={{0,1},{1,0},{2,3},{3,2},{4,5},{5,4},{6,7},{7,6},{8,9},{9,8},{10,11... | collective-permute-start | bytes 208904 | tf_op jit(solution)/shard_map/ppermute | solution.py:500
  41.9 2.9 %collective-permute-start.13 = (f32[128,128]{1,0:T(8,128)S(1)}, f32[128,128]{1,0:T(8,128)S(1)}, u32[]{:S(2)}, u32[]{:S(2)}) collective-permute-start(f32[128,128]{1,0:T(8,128)S(1)} %add.38.mine2_ref), channel_id=1, source_target_pairs={{0,1},{1,0},{2,3},{3,2},{4,5},{5,4},{6,7},{7,6},{8,9},{9,8},{10,11... | collective-permute-start | bytes 196616 | tf_op jit(solution)/shard_map/ppermute | solution.py:500
  55.1 17.6 %collective-permute-start.14 = (f32[776,128]{1,0:T(8,128)S(1)}, f32[776,128]{1,0:T(8,128)S(1)}, u32[]{:S(2)}, u32[]{:S(2)}) collective-permute-start(f32[776,128]{1,0:T(8,128)S(1)} %get-tuple-element.67.outer1_ref.own1_ref), channel_id=1, source_target_pairs={{1,2},{3,4},{5,6},{7,8},{9,10},{11,12},{13,14},{2,1},{4,3},{6,5},{... | collective-permute-start | bytes 1191944 | tf_op jit(solution)/shard_map/ppermute | solution.py:506
  58.8 7.3 %collective-permute-start.16 = (f32[768,128]{1,0:T(8,128)S(1)}, f32[768,128]{1,0:T(8,128)S(1)}, u32[]{:S(2)}, u32[]{:S(2)}) collective-permute-start(f32[768,128]{1,0:T(8,128)S(1)} %get-tuple-element.80), channel_id=1, source_target_pairs={{0,1},{1,0},{2,3},{3,2},{4,5},{5,4},{6,7},{7,6},{8,9},{9,8},{10,11... | collective-permute-start | bytes 1179656 | tf_op jit(solution)/shard_map/ppermute | solution.py:500
  60.0 6.0 %collective-permute-start.15 = (f32[768,128]{1,0:T(8,128)S(1)}, f32[768,128]{1,0:T(8,128)S(1)}, u32[]{:S(2)}, u32[]{:S(2)}) collective-permute-start(f32[768,128]{1,0:T(8,128)S(1)} %get-tuple-element.79.own2_ref), channel_id=1, source_target_pairs={{0,1},{1,0},{2,3},{3,2},{4,5},{5,4},{6,7},{7,6},{8,9},{9,8},{10,11... | collective-permute-start | bytes 1179656 | tf_op jit(solution)/shard_map/ppermute | solution.py:500
  60.1 16.8 %collective-permute-start.17 = (f32[768,128]{1,0:T(8,128)S(1)}, f32[768,128]{1,0:T(8,128)S(1)}, u32[]{:S(2)}, u32[]{:S(2)}) collective-permute-start(f32[768,128]{1,0:T(8,128)S(1)} %get-tuple-element.82), channel_id=1, source_target_pairs={{1,2},{3,4},{5,6},{7,8},{9,10},{11,12},{13,14},{2,1},{4,3},{6,5},{... | collective-permute-start | bytes 1179656 | tf_op jit(solution)/shard_map/ppermute | solution.py:506

commit v17 on v16

--- a/solution.py
+++ b/solution.py
@@ -306,10 +306,21 @@
     out_ref[...] = jnp.where(row >= column, value, 0.0)
 
 
+def stacked2(a, b, contract):
+    left = jnp.concatenate([a[0], a[0], a[1]], axis=contract[0][0])
+    right = jnp.concatenate([b[0], b[1], b[0]], axis=contract[1][0])
+    return dot(left, right, contract)
+
+
+def spread_columns(inv, symmetric, cols):
+    inner = stacked2(symmetric, [part[:, cols] for part in inv], ((1,), (0,)))
+    return split2(stacked2(inv, split2(inner), ((0,), (0,))))
+
+
 def factor(
     core_ref, mine1_ref, mine2_ref, other1_ref, other2_ref, r_bar_ref, *refs
 ):
-    *gradient_refs, nh_ref, nl_ref, sh_ref, sl_ref, grad_ref, outer1_ref, sums_ref, w_ref, inv1_ref, inv2_ref = refs
+    *gradient_refs, nh_ref, nl_ref, sh_ref, sl_ref, yh_ref, yl_ref, grad_ref, outer1_ref, sums_ref, w_ref, inv1_ref, inv2_ref = refs
     tile = 128
     core = core_ref[0]
     for part, value in zip(quarters(core), (mine1_ref, mine2_ref, other1_ref, other2_ref)):
@@ -321,11 +332,6 @@
         a, b = split3(a), split3(b)
         left = jnp.concatenate([a[k] for k in (0, 0, 1, 1, 0, 2)], axis=contract[0][0])
         right = jnp.concatenate([b[k] for k in (0, 1, 0, 1, 2, 0)], axis=contract[1][0])
-        return dot(left, right, contract)
-
-    def stacked2(a, b, contract):
-        left = jnp.concatenate([a[0], a[0], a[1]], axis=contract[0][0])
-        right = jnp.concatenate([b[0], b[1], b[0]], axis=contract[1][0])
         return dot(left, right, contract)
 
     row = lax.broadcasted_iota(jnp.int32, (2 * tile, 2 * tile), 0)
@@ -366,9 +372,10 @@
     middle = stacked(inv, stacked(gram, bar, across), plain) - stacked(cross, inv, across)
     symmetric = jnp.where(row >= col, middle, 0.0) + jnp.transpose(jnp.where(row > col, middle, 0.0))
     parts = split2(inv)
-    spread = stacked2(parts, split2(stacked2(split2(symmetric), parts, plain)), down)
+    symmetric = split2(symmetric)
     nh_ref[...], nl_ref[...] = parts
-    sh_ref[...], sl_ref[...] = split2(spread)
+    yh_ref[...], yl_ref[...] = symmetric
+    sh_ref[...], sl_ref[...] = spread_columns(parts, symmetric, slice(0, 128))
     gradient_outer(core_ref, *gradient_refs, nh_ref, nl_ref, sh_ref, sl_ref, grad_ref, outer1_ref)
 
 
@@ -428,11 +435,14 @@
 
 def gradient_noise(
     core_ref, qh_ref, ql_ref, nh_ref, nl_ref, oh_ref, ol_ref, lh_ref, ll_ref, hh_ref, hl_ref,
-    ih_ref, il_ref, sh_ref, sl_ref, out_ref,
+    ih_ref, il_ref, yh_ref, yl_ref, out_ref,
 ):
     n = out_ref.shape[2]
     core = core_ref[0]
-    weights = [ref[:, 128:] for ref in (ih_ref, il_ref, sh_ref, sl_ref)]
+    inv = (ih_ref[...], il_ref[...])
+    cols = slice(128, 256)
+    weights = [part[:, cols] for part in inv]
+    weights += spread_columns(inv, (yh_ref[...], yl_ref[...]), cols)
     for k in range(4):
         for s, row in enumerate((core, 1 - core)):
             there = cells(row, k, n)
@@ -559,8 +569,8 @@
     parts = sum_over_rows(parts[:2], parts[2:])
     square = shape((256, 256), bf16)
     left = (qh, ql, nh, nl)
-    *weights, w_outer, own1 = call(
-        factor, (square,) * 4 + (single, rim), 10**9, 10**6,
+    *weights, yh, yl, w_outer, own1 = call(
+        factor, (square,) * 2 + (shape((256, 128), bf16),) * 2 + (square,) * 2 + (single, rim), 10**9, 10**6,
         [
             pltpu.VMEM((528, 128), f32),
             pltpu.VMEM((128, 128), f32),
@@ -575,7 +585,7 @@
     )(core, table, w_outer, own1, *left, lh, ll, hh, hl, *weights)
     back2, near1, near2 = swap_outer(last), swap_inner(own2), swap_inner(own3)
     noise_grad = call(gradient_noise, shape(noise_cols.shape, f32), 0, 0, scalar=True)(
-        core, *left, oh, ol, lh, ll, hh, hl, *weights
+        core, *left, oh, ol, lh, ll, hh, hl, *weights[:2], yh, yl
     )
     whole, light = call(
         contract_first, (shape(z_factor.shape, f32), single), 10**7, 6 * 10**6,

time: 78.1 us -> 78.1 us (level)
  transfers between devices with their start and end apart: 18 -> 18, of which waited for: 11 -> 11; matrix products, arithmetic and copies ran while one was open for 0% -> 0% of each run, Pallas kernels for 18% -> 19%
where the time goes in v17:
time: 78.1 us; the launch traced here: 77.9 us
  starting transfers between devices  27.3 us (35%)
  Pallas kernels  27 us (35%)
  waiting for transfers between devices  19.4 us (25%)
  local copies, waits for them, and re-layouts  3.06 us (4%)
  between operations  1.02 us (1%)
    pallas_call x8, Pallas kernels, run(): pl.pallas_call(kernel, out_shape=outs, in_specs=specs, scratch_shapes=lis...  26.2 us
    ppermute x4, waiting for transfers between devices, swap_outer(): return lax.ppermute(message, 'row', pairs + [(j, i) for i, j in pairs])  13.5 us
    ppermute x4, starting transfers between devices, swap_outer(): return lax.ppermute(message, 'row', pairs + [(j, i) for i, j in pairs])  11.7 us
    ppermute x8, starting transfers between devices, swap_inner(): return lax.ppermute(message, 'row', [(i, i ^ 1) for i in range(count)])  8.7 us
    ppermute x6, starting transfers between devices, sum_over_rows(): mine[stream] = mine[stream] + lax.ppermute(mine[stream], 'row', pairs)  6.98 us
    ppermute x6, waiting for transfers between devices, sum_over_rows(): mine[stream] = mine[stream] + lax.ppermute(mine[stream], 'row', pairs)  4.22 us
    unnamed x10, local copies, waits for them, and re-layouts  1.9 us
    ppermute x8, waiting for transfers between devices, swap_inner(): return lax.ppermute(message, 'row', [(i, i ^ 1) for i in range(count)])  1.73 us
  transfers between devices with their start and end apart: 18, of which 11 were waited for; matrix products, arithmetic and copies ran while one was open for 0% of the time, Pallas kernels for 19%

profile of v17, /device:TPU:9, one launch (start us, length us, event | category | flops | bytes accessed | tf_op | source)
XLA Modules:
  0.0 77.9 jit_solution(14053616401284805796)
XLA Ops:
  0.7 1.1 %slice-done = f32[2,2,384,128]{3,2,1,0:T(8,128)S(1)} async-done(((f32[4,2,384,128]{3,2,1,0:T(8,128)}), f32[2,2,384,128]{3,2,1,0:T(8,128)S(1)}, s32[]{:S(2)}) %slice-start) | async-done | bytes 786456 | tf_op jit(solution)/shard_map/slice | solution.py:542
  1.8 3.8 %collective-permute-start.1 = (f32[784,128]{1,0:T(8,128)S(1)}, f32[784,128]{1,0:T(8,128)S(1)}, u32[]{:S(2)}, u32[]{:S(2)}) collective-permute-start(f32[784,128]{1,0:T(8,128)S(1)} %pad.4), channel_id=1, source_target_pairs={{1,2},{3,4},{5,6},{7,8},{9,10},{11,12},{13,14},{2,1},{4,3},{6,5},{... | collective-permute-start | bytes 1204232 | tf_op jit(solution)/shard_map/ppermute | solution.py:516
  5.7 1.5 %shard_map.68 = (f32[776,128]{1,0:T(8,128)S(1)}, f32[768,128]{1,0:T(8,128)S(1)}, f32[776,128]{1,0:T(8,128)S(1)}, f32[384,16]{1,0:T(8,128)S(1)}) custom-call(s32[1]{0:T(128)} %bitcast.core_ref, f32[6,2,384]{2,1,0:T(2,128)S(1)} %copy-done.4, f32[4,2,384,128]{3,2,1,0:T(8,128)S(1)} %copy-done), custom_call_target="tpu_custom_call" | custom-call | flops 1000000 | bytes 3000000 | tf_op jit(solution)/shard_map/pallas_call | solution.py:21
  7.8 3.1 %collective-permute-start = (f32[776,128]{1,0:T(8,128)S(1)}, f32[776,128]{1,0:T(8,128)S(1)}, u32[]{:S(2)}, u32[]{:S(2)}) collective-permute-start(f32[776,128]{1,0:T(8,128)S(1)} %get-tuple-element.47), channel_id=1, source_target_pairs={{1,2},{3,4},{5,6},{7,8},{9,10},{11,12},{13,14},{2,1},{4,3},{6,5},{... | collective-permute-start | bytes 1191944 | tf_op jit(solution)/shard_map/ppermute | solution.py:516
  10.9 1.9 %copy-done.1 = f32[4,2,384,256]{3,2,1,0:T(8,128)S(1)} copy-done((f32[4,2,384,256]{3,2,1,0:T(8,128)S(1)}, f32[4,2,384,256]{3,2,1,0:T(8,128)}, u32[]{:S(2)}) %copy-start.1) | copy-done | bytes 3145752
  12.8 1.8 %shard_map.69 = (f32[136,128]{1,0:T(8,128)S(1)}, bf16[3072,128]{1,0:T(8,128)(2,1)S(1)}, bf16[3072,128]{1,0:T(8,128)(2,1)S(1)}, bf16[3072,256]{1,0:T(8,128)(2,1)S...) custom-call(f32[3072,128]{1,0:T(8,128)S(1)} %bitcast.5, ...), custom_call_target="tpu_custom_call" | custom-call | flops 503316480 | bytes 9000000 | tf_op jit(solution)/shard_map/pallas_call | solution.py:21
  14.6 5.2 %collective-permute-done.1.outer1_ref = f32[784,128]{1,0:T(8,128)S(1)} collective-permute-done((f32[784,128]{1,0:T(8,128)S(1)}, f32[784,128]{1,0:T(8,128)S(1)}, u32[]{:S(2)}, u32[]{:S(2)}) %collective-permute-start.1) | collective-permute-done | bytes 401440 | tf_op jit(solution)/shard_map/ppermute | solution.py:516
  19.8 3.1 %shard_map.70 = (f32[2,384,128]{2,1,0:T(8,128)S(1)}, bf16[1536,128]{1,0:T(8,128)(2,1)S(1)}, bf16[1536,128]{1,0:T(8,128)(2,1)S(1)}, bf16[768,128]{1,0:T(8,128)(2,...) custom-call(s32[1]{0:T(128)} %bitcast.core_ref, ...), custom_call_target="tpu_custom_call" | custom-call | flops 805306368 | bytes 9000000 | tf_op jit(solution)/shard_map/pallas_call | solution.py:21
  22.9 1.2 %collective-permute-done.outer2_ref.fouter2_ref = f32[776,128]{1,0:T(8,128)S(1)} collective-permute-done((f32[776,128]{1,0:T(8,128)S(1)}, f32[776,128]{1,0:T(8,128)S(1)}, u32[]{:S(2)}, u32[]{:S(2)}) %collective-permute-start) | collective-permute-done | bytes 397344 | tf_op jit(solution)/shard_map/ppermute | solution.py:516
  24.0 1.0 %shard_map.71 = (f32[136,128]{1,0:T(8,128)S(1)}, f32[128,128]{1,0:T(8,128)S(1)}, f32[136,128]{1,0:T(8,128)S(1)}, f32[128,128]{1,0:T(8,128)S(1)}, bf16[768,128]{1...) custom-call(s32[1]{0:T(128)} %bitcast.core_ref, f32[384,16]{1,0:T(8,128)S(1)} %get-tuple-element.46.table_ref.refs_0_, ...), custom_call_target="tpu_custom_call" | custom-call | flops 301989888 | bytes 5000000 | tf_op jit(solution)/shard_map/pallas_call | solution.py:21
  25.1 0.5 collective-permute-start.8
  25.6 0.7 collective-permute-done.4
  26.5 1.8 %collective-permute-start.9 = (f32[128,128]{1,0:T(8,128)S(1)}, f32[128,128]{1,0:T(8,128)S(1)}, u32[]{:S(2)}, u32[]{:S(2)}) collective-permute-start(f32[128,128]{1,0:T(8,128)S(1)} %add.35), channel_id=1, source_target_pairs={{0,4},{1,3},{2,6},{3,1},{4,0},{5,7},{6,2},{7,5},{8,12},{9,11},{10,... | collective-permute-start | bytes 196616 | tf_op jit(solution)/shard_map/ppermute | solution.py:527
  28.3 1.6 %collective-permute-done.5 = f32[136,128]{1,0:T(8,128)S(1)} collective-permute-done((f32[136,128]{1,0:T(8,128)S(1)}, f32[136,128]{1,0:T(8,128)S(1)}, u32[]{:S(2)}, u32[]{:S(2)}) %collective-permute-start.5) | collective-permute-done | bytes 69664 | tf_op jit(solution)/shard_map/ppermute | solution.py:527
  29.9 2.4 %collective-permute-start.6 = (f32[136,128]{1,0:T(8,128)S(1)}, f32[136,128]{1,0:T(8,128)S(1)}, u32[]{:S(2)}, u32[]{:S(2)}) collective-permute-start(f32[136,128]{1,0:T(8,128)S(1)} %add.32), channel_id=1, source_target_pairs={{0,4},{1,9},{2,6},{3,11},{4,0},{5,13},{6,2},{7,15},{8,12},{9,1},{1... | collective-permute-start | bytes 208904 | tf_op jit(solution)/shard_map/ppermute | solution.py:527
  32.5 1.6 %collective-permute-done.6 = f32[136,128]{1,0:T(8,128)S(1)} collective-permute-done((f32[136,128]{1,0:T(8,128)S(1)}, f32[136,128]{1,0:T(8,128)S(1)}, u32[]{:S(2)}, u32[]{:S(2)}) %collective-permute-start.6) | collective-permute-done | bytes 69664 | tf_op jit(solution)/shard_map/ppermute | solution.py:527
  34.2 1.1 %collective-permute-start.7 = (f32[136,128]{1,0:T(8,128)S(1)}, f32[136,128]{1,0:T(8,128)S(1)}, u32[]{:S(2)}, u32[]{:S(2)}) collective-permute-start(f32[136,128]{1,0:T(8,128)S(1)} %add.33), channel_id=1, source_target_pairs={{0,8},{1,3},{2,10},{3,1},{4,12},{5,7},{6,14},{7,5},{8,0},{9,11},{1... | collective-permute-start | bytes 208904 | tf_op jit(solution)/shard_map/ppermute | solution.py:527
  35.8 1.4 %collective-permute-start.11 = (f32[128,128]{1,0:T(8,128)S(1)}, f32[128,128]{1,0:T(8,128)S(1)}, u32[]{:S(2)}, u32[]{:S(2)}) collective-permute-start(f32[128,128]{1,0:T(8,128)S(1)} %add.37), channel_id=1, source_target_pairs={{0,2},{1,9},{2,0},{3,11},{4,6},{5,13},{6,4},{7,15},{8,10},{9,1},{1... | collective-permute-start | bytes 196616 | tf_op jit(solution)/shard_map/ppermute | solution.py:527
  37.2 0.5 collective-permute-done.7
  37.7 4.1 %collective-permute-start.12 = (f32[136,128]{1,0:T(8,128)S(1)}, f32[136,128]{1,0:T(8,128)S(1)}, u32[]{:S(2)}, u32[]{:S(2)}) collective-permute-start(f32[136,128]{1,0:T(8,128)S(1)} %add.34.mine1_ref), channel_id=1, source_target_pairs={{0,1},{1,0},{2,3},{3,2},{4,5},{5,4},{6,7},{7,6},{8,9},{9,8},{10,11... | collective-permute-start | bytes 208904 | tf_op jit(solution)/shard_map/ppermute | solution.py:510
  41.9 2.0 %collective-permute-start.13 = (f32[128,128]{1,0:T(8,128)S(1)}, f32[128,128]{1,0:T(8,128)S(1)}, u32[]{:S(2)}, u32[]{:S(2)}) collective-permute-start(f32[128,128]{1,0:T(8,128)S(1)} %add.38.mine2_ref), channel_id=1, source_target_pairs={{0,1},{1,0},{2,3},{3,2},{4,5},{5,4},{6,7},{7,6},{8,9},{9,8},{10,11... | collective-permute-start | bytes 196616 | tf_op jit(solution)/shard_map/ppermute | solution.py:510
  43.9 0.9 %collective-permute-done.13.other2_ref = f32[128,128]{1,0:T(8,128)S(1)} collective-permute-done((f32[128,128]{1,0:T(8,128)S(1)}, f32[128,128]{1,0:T(8,128)S(1)}, u32[]{:S(2)}, u32[]{:S(2)}) %collective-permute-start.13) | collective-permute-done | bytes 65568 | tf_op jit(solution)/shard_map/ppermute | solution.py:510
  44.8 10.3 %shard_map.72 = (bf16[256,256]{1,0:T(8,128)(2,1)S(1)}, bf16[256,256]{1,0:T(8,128)(2,1)S(1)}, bf16[256,128]{1,0:T(8,128)(2,1)S(1)}, bf16[256,128]{1,0:T(8,128)(2,...) custom-call(s32[1]{0:T(128)} %bitcast.core_ref, ...), custom_call_target="tpu_custom_call" | custom-call | flops 1000000000 | bytes 1000000 | tf_op jit(solution)/shard_map/pallas_call | solution.py:21
  55.1 1.9 %collective-permute-start.14 = (f32[776,128]{1,0:T(8,128)S(1)}, f32[776,128]{1,0:T(8,128)S(1)}, u32[]{:S(2)}, u32[]{:S(2)}) collective-permute-start(f32[776,128]{1,0:T(8,128)S(1)} %get-tuple-element.69.outer1_ref.own1_ref), channel_id=1, source_target_pairs={{1,2},{3,4},{5,6},{7,8},{9,10},{11,12},{13,14},{2,1},{4,3},{6,5},{... | collective-permute-start | bytes 1191944 | tf_op jit(solution)/shard_map/ppermute | solution.py:516
  57.1 1.7 %shard_map.73 = (f32[2,384,128]{2,1,0:T(8,128)S(1)}, f32[2,2,384,128]{3,2,1,0:T(8,128)S(1)}, f32[768,128]{1,0:T(8,128)S(1)}, f32[768,128]{1,0:T(8,128)S(1)}, f32[768,128]{1,0:T(8,128)S(1)}) custom-call(s32[1]{0:T(128)} %bitcast.core_ref, f32[384,16]{1,0:T(8,128)S(1)} %get-tuple-element.46.table_ref.refs_0_, f32[2,384,128]{2,1,0:T(8,128)S(1)} %get-tuple-element.70.outer_ref, ...), custom_call_target="tpu_custom_call" | custom-call | flops 10000000000 | bytes 6000000 | tf_op jit(solution)/shard_map/pallas_call | solution.py:21
  58.8 1.3 %collective-permute-start.16 = (f32[768,128]{1,0:T(8,128)S(1)}, f32[768,128]{1,0:T(8,128)S(1)}, u32[]{:S(2)}, u32[]{:S(2)}) collective-permute-start(f32[768,128]{1,0:T(8,128)S(1)} %get-tuple-element.82), channel_id=1, source_target_pairs={{0,1},{1,0},{2,3},{3,2},{4,5},{5,4},{6,7},{7,6},{8,9},{9,8},{10,11... | collective-permute-start | bytes 1179656 | tf_op jit(solution)/shard_map/ppermute | solution.py:510
  60.2 2.8 %collective-permute-start.17 = (f32[768,128]{1,0:T(8,128)S(1)}, f32[768,128]{1,0:T(8,128)S(1)}, u32[]{:S(2)}, u32[]{:S(2)}) collective-permute-start(f32[768,128]{1,0:T(8,128)S(1)} %get-tuple-element.84), channel_id=1, source_target_pairs={{1,2},{3,4},{5,6},{7,8},{9,10},{11,12},{13,14},{2,1},{4,3},{6,5},{... | collective-permute-start | bytes 1179656 | tf_op jit(solution)/shard_map/ppermute | solution.py:516
  63.0 3.5 %shard_map.76 = f32[4,2,384,128]{3,2,1,0:T(8,128)} custom-call(s32[1]{0:T(128)} %bitcast.core_ref, bf16[3072,256]{1,0:T(8,128)(2,1)S(1)} %get-tuple-element.63.refs_1_.qh_ref, bf16[3072,256]{1,0:T(8,128)(2,1)S(1)} %get-tuple-element.64.refs_2_.ql_ref, bf16[3072,128]{1,0:T(8,128)(2,1)S(1)} %get-tuple-element.65.refs_3_.nh_ref, ...), custom_call_target="tpu_custom_call" | custom-call | tf_op jit(solution)/shard_map/pallas_call | solution.py:21
  66.5 6.2 %collective-permute-done.14.outer1_ref = f32[776,128]{1,0:T(8,128)S(1)} collective-permute-done((f32[776,128]{1,0:T(8,128)S(1)}, f32[776,128]{1,0:T(8,128)S(1)}, u32[]{:S(2)}, u32[]{:S(2)}) %collective-permute-start.14) | collective-permute-done | bytes 397344 | tf_op jit(solution)/shard_map/ppermute | solution.py:516
  72.7 3.3 %shard_map.74 = (f32[4,2,384,128]{3,2,1,0:T(8,128)}, f32[2,384,128]{2,1,0:T(8,128)S(1)}) custom-call(s32[1]{0:T(128)} %bitcast.core_ref, f32[776,128]{1,0:T(8,128)S(1)} %collective-permute-done.14.outer1_ref, f32[384,16]{1,0:T(8,128)S(1)} %get-tuple-element.46.table_ref.refs_0_, f32[2,384,128]{2,1,0:T(8,128)S(1)} %get-tuple-element.70.outer_ref, ...), custom_call_target="tpu_custom_call" | custom-call | flops 10000000 | bytes 6000000 | tf_op jit(solution)/shard_map/pallas_call | solution.py:21
  76.1 0.9 %collective-permute-done.17.outer2_ref = f32[768,128]{1,0:T(8,128)S(1)} collective-permute-done((f32[768,128]{1,0:T(8,128)S(1)}, f32[768,128]{1,0:T(8,128)S(1)}, u32[]{:S(2)}, u32[]{:S(2)}) %collective-permute-start.17) | collective-permute-done | bytes 393248 | tf_op jit(solution)/shard_map/ppermute | solution.py:516
  77.0 0.8 %shard_map.75 = f32[4,2,384,128]{3,2,1,0:T(8,128)} custom-call(s32[1]{0:T(128)} %bitcast.core_ref, f32[2,384,128]{2,1,0:T(8,128)S(1)} %get-tuple-element.83.light_ref, f32[768,128]{1,0:T(8,128)S(1)} %collective-permute-done.17.outer2_ref, f32[4,2,384,128]{3,2,1,0:T(8,128)} %get-tuple-element.85.whole_hbm), custom_call_target="tpu_custom_call", output_to_operand_aliasing={{}: (3, {})} | custom-call | flops 1000000 | bytes 1000000 | tf_op jit(solution)/shard_map/pallas_call | solution.py:594
  (35 shorter events, 1.7 us)
Async XLA Ops:
  0.6 1.1 %slice-start = ((f32[4,2,384,128]{3,2,1,0:T(8,128)}), f32[2,2,384,128]{3,2,1,0:T(8,128)S(1)}, s32[]{:S(2)}) async-start(f32[4,2,384,128]{3,2,1,0:T(8,128)} %z_ref.5), calls=%async_computation | async-start | bytes 1572864 | tf_op jit(solution)/shard_map/slice | solution.py:542
  0.6 5.0 %copy-start = (f32[4,2,384,128]{3,2,1,0:T(8,128)S(1)}, f32[4,2,384,128]{3,2,1,0:T(8,128)}, u32[]{:S(2)}) copy-start(f32[4,2,384,128]{3,2,1,0:T(8,128)} %z_ref.5) | copy-start | bytes 4718596
  0.7 5.0 %copy-start.4 = (f32[6,2,384]{2,1,0:T(2,128)S(1)}, f32[6,2,384]{2,1,0:T(2,128)}, u32[]{:S(2)}) copy-start(f32[6,2,384]{2,1,0:T(2,128)} %coeff_ref.1) | copy-start | bytes 55300
  1.8 9.2 %copy-start.2 = (f32[4,2,384,128]{3,2,1,0:T(8,128)S(1)}, f32[4,2,384,128]{3,2,1,0:T(8,128)}, u32[]{:S(2)}) copy-start(f32[4,2,384,128]{3,2,1,0:T(8,128)} %param.7) | copy-start | bytes 4718596
  1.8 17.9 %collective-permute-start.1 = (f32[784,128]{1,0:T(8,128)S(1)}, f32[784,128]{1,0:T(8,128)S(1)}, u32[]{:S(2)}, u32[]{:S(2)}) collective-permute-start(f32[784,128]{1,0:T(8,128)S(1)} %pad.4), channel_id=1, source_target_pairs={{1,2},{3,4},{5,6},{7,8},{9,10},{11,12},{13,14},{2,1},{4,3},{6,5},{... | collective-permute-start | bytes 1204232 | tf_op jit(solution)/shard_map/ppermute | solution.py:516
  7.2 7.4 %collective-permute-start.3 = (f32[776,128]{1,0:T(8,128)S(1)}, f32[776,128]{1,0:T(8,128)S(1)}, u32[]{:S(2)}, u32[]{:S(2)}) collective-permute-start(f32[776,128]{1,0:T(8,128)S(1)} %get-tuple-element.50), channel_id=1, source_target_pairs={{0,1},{1,0},{2,3},{3,2},{4,5},{5,4},{6,7},{7,6},{8,9},{9,8},{10,11... | collective-permute-start | bytes 1191944 | tf_op jit(solution)/shard_map/ppermute | solution.py:510
  7.3 7.3 %collective-permute-start.2 = (f32[768,128]{1,0:T(8,128)S(1)}, f32[768,128]{1,0:T(8,128)S(1)}, u32[]{:S(2)}, u32[]{:S(2)}) collective-permute-start(f32[768,128]{1,0:T(8,128)S(1)} %get-tuple-element.49), channel_id=1, source_target_pairs={{0,1},{1,0},{2,3},{3,2},{4,5},{5,4},{6,7},{7,6},{8,9},{9,8},{10,11... | collective-permute-start | bytes 1179656 | tf_op jit(solution)/shard_map/ppermute | solution.py:510
  7.8 16.2 %collective-permute-start = (f32[776,128]{1,0:T(8,128)S(1)}, f32[776,128]{1,0:T(8,128)S(1)}, u32[]{:S(2)}, u32[]{:S(2)}) collective-permute-start(f32[776,128]{1,0:T(8,128)S(1)} %get-tuple-element.47), channel_id=1, source_target_pairs={{1,2},{3,4},{5,6},{7,8},{9,10},{11,12},{13,14},{2,1},{4,3},{6,5},{... | collective-permute-start | bytes 1191944 | tf_op jit(solution)/shard_map/ppermute | solution.py:516
  10.9 1.9 %copy-start.1 = (f32[4,2,384,256]{3,2,1,0:T(8,128)S(1)}, f32[4,2,384,256]{3,2,1,0:T(8,128)}, u32[]{:S(2)}) copy-start(f32[4,2,384,256]{3,2,1,0:T(8,128)} %param.8) | copy-start | bytes 9437188
  25.0 19.8 %copy-start.3 = (f32[256,256]{1,0:T(8,128)S(1)}, f32[256,256]{1,0:T(8,128)}, u32[]{:S(2)}) copy-start(f32[256,256]{1,0:T(8,128)} %r_bar_ref.1) | copy-start | bytes 786436
  25.0 1.3 %collective-permute-start.4 = (f32[136,128]{1,0:T(8,128)S(1)}, f32[136,128]{1,0:T(8,128)S(1)}, u32[]{:S(2)}, u32[]{:S(2)}) collective-permute-start(f32[136,128]{1,0:T(8,128)S(1)} %get-tuple-element.60), channel_id=1, source_target_pairs={{0,1},{1,0},{2,3},{3,2},{4,5},{5,4},{6,7},{7,6},{8,9},{9,8},{10,11... | collective-permute-start | bytes 208904 | tf_op jit(solution)/shard_map/ppermute | solution.py:510
  25.1 1.4 %collective-permute-start.8 = (f32[128,128]{1,0:T(8,128)S(1)}, f32[128,128]{1,0:T(8,128)S(1)}, u32[]{:S(2)}, u32[]{:S(2)}) collective-permute-start(f32[128,128]{1,0:T(8,128)S(1)} %get-tuple-element.62), channel_id=1, source_target_pairs={{0,1},{1,0},{2,3},{3,2},{4,5},{5,4},{6,7},{7,6},{8,9},{9,8},{10,11... | collective-permute-start | bytes 196616 | tf_op jit(solution)/shard_map/ppermute | solution.py:510
  26.4 3.5 %collective-permute-start.5 = (f32[136,128]{1,0:T(8,128)S(1)}, f32[136,128]{1,0:T(8,128)S(1)}, u32[]{:S(2)}, u32[]{:S(2)}) collective-permute-start(f32[136,128]{1,0:T(8,128)S(1)} %add.31), channel_id=1, source_target_pairs={{0,2},{1,5},{2,0},{3,7},{4,6},{5,1},{6,4},{7,3},{8,10},{9,13},{10,... | collective-permute-start | bytes 208904 | tf_op jit(solution)/shard_map/ppermute | solution.py:527
  26.5 5.8 %collective-permute-start.9 = (f32[128,128]{1,0:T(8,128)S(1)}, f32[128,128]{1,0:T(8,128)S(1)}, u32[]{:S(2)}, u32[]{:S(2)}) collective-permute-start(f32[128,128]{1,0:T(8,128)S(1)} %add.35), channel_id=1, source_target_pairs={{0,4},{1,3},{2,6},{3,1},{4,0},{5,7},{6,2},{7,5},{8,12},{9,11},{10,... | collective-permute-start | bytes 196616 | tf_op jit(solution)/shard_map/ppermute | solution.py:527
  29.9 4.3 %collective-permute-start.6 = (f32[136,128]{1,0:T(8,128)S(1)}, f32[136,128]{1,0:T(8,128)S(1)}, u32[]{:S(2)}, u32[]{:S(2)}) collective-permute-start(f32[136,128]{1,0:T(8,128)S(1)} %add.32), channel_id=1, source_target_pairs={{0,4},{1,9},{2,6},{3,11},{4,0},{5,13},{6,2},{7,15},{8,12},{9,1},{1... | collective-permute-start | bytes 208904 | tf_op jit(solution)/shard_map/ppermute | solution.py:527
  32.3 3.5 %collective-permute-start.10 = (f32[128,128]{1,0:T(8,128)S(1)}, f32[128,128]{1,0:T(8,128)S(1)}, u32[]{:S(2)}, u32[]{:S(2)}) collective-permute-start(f32[128,128]{1,0:T(8,128)S(1)} %add.36), channel_id=1, source_target_pairs={{0,8},{1,5},{2,10},{3,7},{4,12},{5,1},{6,14},{7,3},{8,0},{9,13},{1... | collective-permute-start | bytes 196616 | tf_op jit(solution)/shard_map/ppermute | solution.py:527
  34.2 3.5 %collective-permute-start.7 = (f32[136,128]{1,0:T(8,128)S(1)}, f32[136,128]{1,0:T(8,128)S(1)}, u32[]{:S(2)}, u32[]{:S(2)}) collective-permute-start(f32[136,128]{1,0:T(8,128)S(1)} %add.33), channel_id=1, source_target_pairs={{0,8},{1,3},{2,10},{3,1},{4,12},{5,7},{6,14},{7,5},{8,0},{9,11},{1... | collective-permute-start | bytes 208904 | tf_op jit(solution)/shard_map/ppermute | solution.py:527
  35.8 6.1 %collective-permute-start.11 = (f32[128,128]{1,0:T(8,128)S(1)}, f32[128,128]{1,0:T(8,128)S(1)}, u32[]{:S(2)}, u32[]{:S(2)}) collective-permute-start(f32[128,128]{1,0:T(8,128)S(1)} %add.37), channel_id=1, source_target_pairs={{0,2},{1,9},{2,0},{3,11},{4,6},{5,13},{6,4},{7,15},{8,10},{9,1},{1... | collective-permute-start | bytes 196616 | tf_op jit(solution)/shard_map/ppermute | solution.py:527
  37.7 7.1 %collective-permute-start.12 = (f32[136,128]{1,0:T(8,128)S(1)}, f32[136,128]{1,0:T(8,128)S(1)}, u32[]{:S(2)}, u32[]{:S(2)}) collective-permute-start(f32[136,128]{1,0:T(8,128)S(1)} %add.34.mine1_ref), channel_id=1, source_target_pairs={{0,1},{1,0},{2,3},{3,2},{4,5},{5,4},{6,7},{7,6},{8,9},{9,8},{10,11... | collective-permute-start | bytes 208904 | tf_op jit(solution)/shard_map/ppermute | solution.py:510
  41.9 2.9 %collective-permute-start.13 = (f32[128,128]{1,0:T(8,128)S(1)}, f32[128,128]{1,0:T(8,128)S(1)}, u32[]{:S(2)}, u32[]{:S(2)}) collective-permute-start(f32[128,128]{1,0:T(8,128)S(1)} %add.38.mine2_ref), channel_id=1, source_target_pairs={{0,1},{1,0},{2,3},{3,2},{4,5},{5,4},{6,7},{7,6},{8,9},{9,8},{10,11... | collective-permute-start | bytes 196616 | tf_op jit(solution)/shard_map/ppermute | solution.py:510
  55.1 17.6 %collective-permute-start.14 = (f32[776,128]{1,0:T(8,128)S(1)}, f32[776,128]{1,0:T(8,128)S(1)}, u32[]{:S(2)}, u32[]{:S(2)}) collective-permute-start(f32[776,128]{1,0:T(8,128)S(1)} %get-tuple-element.69.outer1_ref.own1_ref), channel_id=1, source_target_pairs={{1,2},{3,4},{5,6},{7,8},{9,10},{11,12},{13,14},{2,1},{4,3},{6,5},{... | collective-permute-start | bytes 1191944 | tf_op jit(solution)/shard_map/ppermute | solution.py:516
  58.8 7.7 %collective-permute-start.16 = (f32[768,128]{1,0:T(8,128)S(1)}, f32[768,128]{1,0:T(8,128)S(1)}, u32[]{:S(2)}, u32[]{:S(2)}) collective-permute-start(f32[768,128]{1,0:T(8,128)S(1)} %get-tuple-element.82), channel_id=1, source_target_pairs={{0,1},{1,0},{2,3},{3,2},{4,5},{5,4},{6,7},{7,6},{8,9},{9,8},{10,11... | collective-permute-start | bytes 1179656 | tf_op jit(solution)/shard_map/ppermute | solution.py:510
  60.1 6.4 %collective-permute-start.15 = (f32[768,128]{1,0:T(8,128)S(1)}, f32[768,128]{1,0:T(8,128)S(1)}, u32[]{:S(2)}, u32[]{:S(2)}) collective-permute-start(f32[768,128]{1,0:T(8,128)S(1)} %get-tuple-element.81.own2_ref), channel_id=1, source_target_pairs={{0,1},{1,0},{2,3},{3,2},{4,5},{5,4},{6,7},{7,6},{8,9},{9,8},{10,11... | collective-permute-start | bytes 1179656 | tf_op jit(solution)/shard_map/ppermute | solution.py:510
  60.2 16.8 %collective-permute-start.17 = (f32[768,128]{1,0:T(8,128)S(1)}, f32[768,128]{1,0:T(8,128)S(1)}, u32[]{:S(2)}, u32[]{:S(2)}) collective-permute-start(f32[768,128]{1,0:T(8,128)S(1)} %get-tuple-element.84), channel_id=1, source_target_pairs={{1,2},{3,4},{5,6},{7,8},{9,10},{11,12},{13,14},{2,1},{4,3},{6,5},{... | collective-permute-start | bytes 1179656 | tf_op jit(solution)/shard_map/ppermute | solution.py:516
